TPU v7x, 128 devices: a whole 4x4x4 slice. The times are simulated.
128 devices in a mesh: row: 16 (over x, z), col: 8 (over y, core).
Axes of the slice: x: 4, y: 4, z: 4, core: 2. Of those that a mesh axis runs over, the one named last changes fastest.
Arguments:
- object_field: float32 [2, 8192, 3072], P(None, 'row', 'col'), may hold values from -6 to 6
- probe_field: float32 [2, 256, 256], replicated, may hold values from -6 to 6
- amplitudes: bfloat16 [2, 1536, 256, 256], P(None, ('row', 'col')), may hold values from 0.29882812 to 3
- positions: int32 [2, 2, 1536], P(None, None, ('row', 'col')), may hold values from 0 to 511, as said below
- live_counts: int32 [2, 8, 16], P(None, 'col', 'row'), may hold values from 1 to 12, 48 in all within a row
Outputs:
- object_out: float32 [2, 8192, 3072], P(None, 'row', 'col')
- probe_out: float32 [2, 256, 256], replicated
Inputs may be any that keep to these rules, and one draw needn't show every extreme that they name: `positions`: every offset is below 512 for rows and below 384 for columns; in the last block row the row offset is at most 256, in the last block column the column offset at most 128, so every patch lies inside the object. The live frames of a device are its first slots. For every iteration t and block column c, the 16 counts live_counts[t, c, :] of that block column's devices sum to 48, and one of them is 12; no such sum holds over the devices of a block row.
All inputs are finite; a program needn't handle non-finite values.
Results may differ from a plain program's by a relative error of at most 0.0019.
Values may be sent and summed in bfloat16 or wider, within the bound.
No kernel may reach another device: no remote copies, remote signals or barrier semaphores. Data moves between devices by JAX's collectives and lax.ppermute only.
A program may use at most 128 MiB of HBM per device.

v0:
```python
import math

import jax
import jax.numpy as jnp
from jax import lax
from jax.sharding import PartitionSpec as P

ITERS = 2


FLOOR = 0.3
ALPHA = 0.5


def passed_along(value, axis, steps):
    count = lax.axis_size(axis)
    first, last = (max(0, -steps), min(count, count - steps))
    return lax.ppermute(value, axis, [(source, source + steps) for source in range(first, last)])


def for_sending(value):

    def short(part):
        return part.astype(jnp.bfloat16) if part.dtype == jnp.float32 else part

    return jax.tree.map(short, value)


def chirp_tables(frame_size):
    offset = jnp.arange(frame_size, dtype=jnp.int32)
    differ = offset[:, None] - offset[None, :]
    phase_units = differ * differ % (2 * frame_size)
    phase = jnp.pi * phase_units.astype(jnp.float32) / frame_size
    scale = 1.0 / math.sqrt(frame_size)
    return (
        (jnp.cos(phase) * scale).astype(jnp.bfloat16),
        (jnp.sin(phase) * scale).astype(jnp.bfloat16),
    )


def left_product(real_table, imag_table, real_part, imag_part):

    def product(table, part):
        return jnp.einsum("ab,nbc->nac", table, part, preferred_element_type=jnp.float32)

    return (
        product(real_table, real_part) - product(imag_table, imag_part),
        product(real_table, imag_part) + product(imag_table, real_part),
    )


def right_product(real_table, imag_table, real_part, imag_part):

    def product(part, table):
        return jnp.einsum("nab,bc->nac", part, table, preferred_element_type=jnp.float32)

    return (
        product(real_part, real_table) - product(imag_part, imag_table),
        product(imag_part, real_table) + product(real_part, imag_table),
    )


def frame_terms(patches, frame_amps, probe_field, real_table, imag_table, weights):
    probe_real, probe_imag = (probe_field[0], probe_field[1])
    patch_real = patches[:, 0].astype(jnp.float32)
    patch_imag = patches[:, 1].astype(jnp.float32)
    wave_real = (probe_real * patch_real - probe_imag * patch_imag).astype(jnp.bfloat16)
    wave_imag = (probe_real * patch_imag + probe_imag * patch_real).astype(jnp.bfloat16)
    near_real, near_imag = left_product(real_table, imag_table, wave_real, wave_imag)
    near_real, near_imag = (near_real.astype(jnp.bfloat16), near_imag.astype(jnp.bfloat16))
    far_real, far_imag = right_product(real_table, imag_table, near_real, near_imag)
    magnitude = jnp.sqrt(far_real * far_real + far_imag * far_imag)
    factor = 1.0 - frame_amps.astype(jnp.float32) / jnp.maximum(magnitude, FLOOR)
    misfit_real = (far_real * factor).astype(jnp.bfloat16)
    misfit_imag = (far_imag * factor).astype(jnp.bfloat16)
    conj_table = -imag_table
    back_real, back_imag = left_product(real_table, conj_table, misfit_real, misfit_imag)
    back_real, back_imag = (back_real.astype(jnp.bfloat16), back_imag.astype(jnp.bfloat16))
    update_real, update_imag = right_product(real_table, conj_table, back_real, back_imag)
    weight_col = weights[:, None, None]
    grad_real = (probe_real * update_real + probe_imag * update_imag) * weight_col
    grad_imag = (probe_real * update_imag - probe_imag * update_real) * weight_col
    gradients = jnp.stack([grad_real, grad_imag], axis=1).astype(jnp.bfloat16)
    probe_real_term = jnp.sum(
        weight_col * (patch_real * update_real + patch_imag * update_imag), axis=0
    )
    probe_imag_term = jnp.sum(
        weight_col * (patch_real * update_imag - patch_imag * update_real), axis=0
    )
    weight_term = jnp.sum(weight_col * (patch_real * patch_real + patch_imag * patch_imag), axis=0)
    return (gradients, jnp.stack([probe_real_term, probe_imag_term], axis=0), weight_term)


def extend_block(object_field, frame_size):
    below = passed_along(object_field[:, :frame_size, :].astype(jnp.bfloat16), "row", -1).astype(
        jnp.float32
    )
    taller = jnp.concatenate([object_field, below], axis=1)
    beside = passed_along(for_sending(taller[:, :, :frame_size]), "col", -1)
    return jnp.concatenate([taller, beside], axis=2)


def fold_rims(gathered, block_rows, block_columns):
    from_left = passed_along(gathered[:, :, block_columns:].astype(jnp.bfloat16), "col", 1).astype(
        jnp.float32
    )
    narrow = gathered[:, :, :block_columns]
    narrow = narrow.at[:, :, : from_left.shape[2]].add(from_left)
    from_above = passed_along(narrow[:, block_rows:, :].astype(jnp.bfloat16), "row", 1).astype(
        jnp.float32
    )
    return narrow[:, :block_rows, :].at[:, : from_above.shape[1], :].add(from_above)


def place_patches(gradients, row_offsets, col_offsets, ext_rows, ext_columns):
    frame_size = gradients.shape[-1]
    inside = jnp.arange(frame_size, dtype=jnp.int32)
    column_ids = jnp.arange(ext_columns, dtype=jnp.int32)
    row_ids = jnp.arange(ext_rows, dtype=jnp.int32)
    column_select = (
        col_offsets[:, None, None] + inside[None, :, None] == column_ids[None, None, :]
    ).astype(jnp.bfloat16)
    row_select = (
        row_offsets[:, None, None] + inside[None, :, None] == row_ids[None, None, :]
    ).astype(jnp.bfloat16)
    widened = jnp.einsum(
        "fcab,fbs->fcas", gradients, column_select, preferred_element_type=jnp.float32
    ).astype(jnp.bfloat16)
    return jnp.einsum("far,fcas->crs", row_select, widened, preferred_element_type=jnp.float32)


def local(object_field, probe_field, amplitudes, positions, live_counts):
    frame_size = probe_field.shape[-1]
    block_rows, block_columns = (object_field.shape[1], object_field.shape[2])
    slots_dev = amplitudes.shape[1]
    real_table, imag_table = chirp_tables(frame_size)
    slot_range = jnp.arange(slots_dev, dtype=jnp.int32)
    anchor = jnp.zeros((), jnp.int32)
    for iteration in range(ITERS):
        extended = extend_block(object_field, frame_size)
        live_total = live_counts[iteration, 0, 0]
        row_offsets = positions[iteration, 0]
        col_offsets = positions[iteration, 1]

        def cut_patch(top_row, left_column):
            return lax.dynamic_slice(
                extended, (anchor, top_row, left_column), (2, frame_size, frame_size)
            )

        patches = jax.vmap(cut_patch)(row_offsets, col_offsets).astype(jnp.bfloat16)
        frame_amps = amplitudes[iteration]
        weights = (slot_range < live_total).astype(jnp.float32)
        gradients, probe_terms, weight_terms = frame_terms(
            patches, frame_amps, probe_field, real_table, imag_table, weights
        )
        gathered = place_patches(
            gradients, row_offsets, col_offsets, extended.shape[1], extended.shape[2]
        )
        object_sum = fold_rims(gathered, block_rows, block_columns)
        probe_sum, weight_sum = lax.psum((probe_terms, weight_terms), ("row", "col"))
        step_size = ALPHA / (
            jnp.max(probe_field[0] * probe_field[0] + probe_field[1] * probe_field[1]) + 1e-06
        )
        object_field = object_field - step_size * object_sum
        probe_field = probe_field - probe_sum / (weight_sum + 1.0)
    return (object_field, probe_field)


def solution(mesh):
    placed = (
        P(None, "row", "col"),
        P(),
        P(None, ("row", "col"), None, None),
        P(None, None, ("row", "col")),
        P(None, "col", "row"),
    )
    return jax.shard_map(
        local, mesh=mesh, in_specs=placed, out_specs=(P(None, "row", "col"), P()), check_vma=False
    )
```

profile of v0, /device:TPU:1, one launch (start us, length us, event | category | flops | bytes accessed | tf_op | source)
XLA Modules:
  0.0 564.1 jit_solution(16557437784425672466)
XLA Ops:
  12.0 9.7 %collective-permute-done = bf16[2,256,384]{2,1,0:T(8,128)(2,1)S(1)} collective-permute-done((bf16[2,256,384]{2,1,0:T(8,128)(2,1)S(1)}, bf16[2,256,384]{2,1,0:T(8,128)(2,1)S(1)}, u32[]{:S(2)}, u32[]{:S(2)}) %collective-permute-start) | collective-permute-done | bytes 393248 | tf_op jit(solution)/shard_map/ppermute | solution.py:18
  23.2 3.2 collective-permute-start.1
  29.1 8.1 %collective-permute-done.1 = bf16[2,768,256]{2,1,0:T(8,128)(2,1)S(1)} collective-permute-done((bf16[2,768,256]{2,1,0:T(8,128)(2,1)S(1)}, bf16[2,768,256]{2,1,0:T(8,128)(2,1)S(1)}, u32[]{:S(2)}, u32[]{:S(2)}) %collective-permute-start.1) | collective-permute-done | bytes 786464 | tf_op jit(solution)/shard_map/ppermute | solution.py:18
  38.4 2.0 broadcast.239.clone2
  40.4 33.4 %while.6 = (s32[]{:T(128)}, bf16[2,768,640]{2,1,0:T(8,128)(2,1)S(1)}, s32[12,3]{0,1:T(4,128)S(1)}, bf16[12,2,256,256]{3,2,0,1:T(8,128)(2,1)}, s32[]{:T(128)}) while((s32[]{:T(128)}, bf16[2,768,640]{2,1,0:T(8,128)(2,1)S(1)}, s32[12,3]{0,1:T(4,128)S(1)}, bf16[12,2,256,256]{3,2,0,1:T(8,128)(2,1)}, s32[]{:T(128)}) %tuple.79), condition=%wide.while_cond.4, body=%wide.while_body.4.sunk | while | flops 2 | bytes 525929 | solution.py:146
  41.0 2.2 bitcast_dynamic-update-slice_fusion.4
  43.8 2.2 bitcast_dynamic-update-slice_fusion.4
  46.6 2.2 bitcast_dynamic-update-slice_fusion.4
  49.3 2.1 bitcast_dynamic-update-slice_fusion.4
  52.1 2.2 bitcast_dynamic-update-slice_fusion.4
  54.9 2.2 bitcast_dynamic-update-slice_fusion.4
  57.7 2.2 bitcast_dynamic-update-slice_fusion.4
  60.5 2.2 bitcast_dynamic-update-slice_fusion.4
  63.2 2.2 bitcast_dynamic-update-slice_fusion.4
  66.0 2.2 bitcast_dynamic-update-slice_fusion.4
  68.8 2.2 bitcast_dynamic-update-slice_fusion.4
  71.6 2.2 bitcast_dynamic-update-slice_fusion.4
  73.8 4.0 fusion.159
  77.8 1.8 fusion.162
  79.6 2.1 add_convert_fusion.3
  81.7 2.0 subtract_convert_fusion.3
  86.8 1.6 convolution_subtract_fusion.3
  88.7 4.0 multiply_convert_fusion.6
  103.6 5.8 %fusion.34 = (f32[256,256]{1,0:T(8,128)}, f32[256,256]{1,0:T(8,128)}, f32[256,256]{1,0:T(8,128)}, bf16[12,1,256,256]{3,2,0,1:T(8,128)(2,1)S(1)}, bf16[12,1,256,256]{3,2,0,1:T(8,128)(2,1)S(1)}) fusion(f32[12,256,256]{2,1,0:T(8,128)S(1)} %convolution_add_fusion.2, f32[12]{0:T(128)S(1)} %copy-done.21, bf16[12,2,256,256]{3,2,0,1:T(8,128)(2,1)S(1)} %copy-done.8, ...), kind=kOutput, calls=%fused_computation.51 | convolution fusion | flops 425787392 | bytes 15466544 | tf_op jit(solution)/shard_map/nab,bc->nac/dot_general | solution.py:55
  109.4 3.2 fusion.432
  112.6 6.7 %fusion.77 = f32[2,768,640]{1,2,0:T(8,128)S(1)} fusion(s32[12,256]{1,0:T(8,128)S(1)} %copy-done.16, bf16[12,2,256,640]{2,3,0,1:T(8,128)(2,1)S(1)} %fusion.432), kind=kOutput, calls=%fused_computation.98 | convolution fusion | flops 6042157056 | bytes 11808768 | tf_op jit(solution)/shard_map/far,fcas->crs/dot_general | solution.py:129
  119.4 1.9 collective-permute-start.2
  121.5 8.8 %collective-permute-done.2 = bf16[2,768,256]{1,2,0:T(8,128)(2,1)S(1)} collective-permute-done((bf16[2,768,256]{1,2,0:T(8,128)(2,1)S(1)}, bf16[2,768,256]{1,2,0:T(8,128)(2,1)S(1)}, u32[]{:S(2)}, u32[]{:S(2)}) %collective-permute-start.2) | collective-permute-done | bytes 786464 | tf_op jit(solution)/shard_map/ppermute | solution.py:18
  131.9 4.3 collective-permute-start.3
  136.7 1.8 add_reduce_fusion.1
  145.7 5.6 collective-permute-done.4
  152.2 1.9 collective-permute-start.5
  154.8 146.1 %all-reduce.7.cloned.1.call-done = (f32[2,256,256]{2,1,0:T(8,128)}, f32[256,256]{1,0:T(8,128)}) async-done(((f32[2,256,256]{2,1,0:T(8,128)}, f32[256,256]{1,0:T(8,128)}), (f32[2,256,256]{2,1,0:T(8,128)}, f32[256,256]{1,0:T(8,128)})) %all-reduce.7.cloned.1.call-update) | async-done | bytes 786448 | tf_op jit(solution)/shard_map/psum | solution.py:160
  303.1 2.6 pad_maximum_fusion.1
  305.7 2.0 broadcast.239.clone
  307.6 47.8 %while.7 = (s32[]{:T(128)}, bf16[2,768,640]{1,2,0:T(8,128)(2,1)}, s32[12,3]{0,1:T(4,128)S(1)}, bf16[12,2,256,256]{3,2,0,1:T(8,128)(2,1)}, s32[]{:T(128)}) while((s32[]{:T(128)}, bf16[2,768,640]{1,2,0:T(8,128)(2,1)}, s32[12,3]{0,1:T(4,128)S(1)}, bf16[12,2,256,256]{3,2,0,1:T(8,128)(2,1)}, s32[]{:T(128)}) %tuple.82), condition=%wide.while_cond.5, body=%wide.while_body.5.sunk | while | flops 2 | bytes 1573489 | solution.py:146
  308.6 2.5 constant_dynamic-slice_fusion.8
  312.6 2.5 constant_dynamic-slice_fusion.8
  316.5 2.5 constant_dynamic-slice_fusion.8
  320.5 2.5 constant_dynamic-slice_fusion.8
  324.4 2.5 constant_dynamic-slice_fusion.8
  328.3 2.5 constant_dynamic-slice_fusion.8
  332.3 2.5 constant_dynamic-slice_fusion.8
  336.3 2.5 constant_dynamic-slice_fusion.8
  340.2 2.5 constant_dynamic-slice_fusion.8
  344.2 2.5 constant_dynamic-slice_fusion.8
  348.1 2.5 constant_dynamic-slice_fusion.8
  352.1 2.5 constant_dynamic-slice_fusion.8
  355.4 3.8 fusion.147
  359.3 1.8 fusion.150
  361.1 2.1 add_convert_fusion.1
  363.2 2.1 subtract_convert_fusion.1
  368.4 1.6 convolution_subtract_fusion.1
  370.3 3.8 multiply_convert_fusion.2
  385.0 5.7 %fusion.47 = (f32[256,256]{1,0:T(8,128)S(1)}, f32[256,256]{1,0:T(8,128)S(1)}, f32[256,256]{1,0:T(8,128)}, bf16[12,1,256,256]{3,2,0,1:T(8,128)(2,1)S(1)}, bf16[12,1,256,256]{3,2,0,1:T(8,128)(2,1)S(1)}) fusion(f32[12,256,256]{2,1,0:T(8,128)S(1)} %convolution_add_fusion, f32[12]{0:T(128)S(1)} %compare_convert_fusion, ...), kind=kOutput, calls=%fused_computation.64 | convolution fusion | flops 425787392 | bytes 15466544 | tf_op jit(solution)/shard_map/nab,bc->nac/dot_general | solution.py:55
  390.6 3.2 fusion.428
  393.8 6.7 %fusion.68 = f32[2,768,640]{1,2,0:T(8,128)S(1)} fusion(s32[12,256]{1,0:T(8,128)S(1)} %copy-done.14, bf16[12,2,256,640]{2,3,0,1:T(8,128)(2,1)S(1)} %fusion.428), kind=kOutput, calls=%fused_computation.97 | convolution fusion | flops 6042157056 | bytes 11808768 | tf_op jit(solution)/shard_map/far,fcas->crs/dot_general | solution.py:129
  400.6 1.9 copy-done.2
  402.5 4.0 collective-permute-start.6
  408.7 7.0 %collective-permute-done.6 = bf16[2,768,256]{1,2,0:T(8,128)(2,1)} collective-permute-done((bf16[2,768,256]{1,2,0:T(8,128)(2,1)S(1)}, bf16[2,768,256]{1,2,0:T(8,128)(2,1)}, u32[]{:S(2)}, u32[]{:S(2)}) %collective-permute-start.6) | collective-permute-done | bytes 786464 | tf_op jit(solution)/shard_map/ppermute | solution.py:18
  415.6 1.8 fusion.90
  420.2 131.4 %all-reduce.5.cloned.1.call-done = (f32[2,256,256]{2,1,0:T(8,128)}, f32[256,256]{1,0:T(8,128)}) async-done(((f32[2,256,256]{2,1,0:T(8,128)}, f32[256,256]{1,0:T(8,128)}), (f32[2,256,256]{2,1,0:T(8,128)}, f32[256,256]{1,0:T(8,128)})) %all-reduce.5.cloned.1.call-update) | async-done | bytes 786448 | tf_op jit(solution)/shard_map/psum | solution.py:160
  552.7 1.9 divide_subtract_fusion
  555.3 1.6 copy.43
  (180 shorter events, 82.1 us)
Async XLA Ops:
  7.2 30.1 %copy-start = (f32[2,512,384]{2,1,0:T(8,128)S(1)}, f32[2,512,384]{2,1,0:T(8,128)}, u32[]{:S(2)}) copy-start(f32[2,512,384]{2,1,0:T(8,128)} %param.13) | copy-start | bytes 4718596
  7.2 20.4 %copy-start.18 = (s32[2,2,12]{2,1,0:T(2,128)S(1)}, s32[2,2,12]{2,1,0:T(2,128)}, u32[]{:S(2)}) copy-start(s32[2,2,12]{2,1,0:T(2,128)} %param.16) | copy-start | bytes 580
  7.2 21.1 %copy-start.5 = (f32[2,256,256]{2,1,0:T(8,128)S(1)}, f32[2,256,256]{2,1,0:T(8,128)}, u32[]{:S(2)}) copy-start(f32[2,256,256]{2,1,0:T(8,128)} %param.14) | copy-start | bytes 1572868
  7.2 293.7 %all-reduce.7.cloned.1.call-start = ((), (), s32[]{:S(2)}) async-start(), calls=%async_computation.1 | async-start | bytes 1572864 | tf_op jit(solution)/shard_map/psum | solution.py:160
  8.6 13.2 %collective-permute-start = (bf16[2,256,384]{2,1,0:T(8,128)(2,1)S(1)}, bf16[2,256,384]{2,1,0:T(8,128)(2,1)S(1)}, u32[]{:S(2)}, u32[]{:S(2)}) collective-permute-start(bf16[2,256,384]{2,1,0:T(8,128)(2,1)S(1)} %slice.389), channel_id=1, source_target_pairs={{8,0},{16,8},{24,16},{32,24},{40,32},{48,40},{56,48},{64,56},{72,6... | collective-permute-start | bytes 1179656 | tf_op jit(solution)/shard_map/ppermute | solution.py:18
  21.8 7.3 %copy-start.9 = (bf16[2,256,384]{2,1,0:T(8,128)(2,1)}, bf16[2,256,384]{2,1,0:T(8,128)(2,1)S(1)}, u32[]{:S(2)}) copy-start(bf16[2,256,384]{2,1,0:T(8,128)(2,1)S(1)} %collective-permute-done) | copy-start | bytes 1179652
  23.2 14.0 %collective-permute-start.1 = (bf16[2,768,256]{2,1,0:T(8,128)(2,1)S(1)}, bf16[2,768,256]{2,1,0:T(8,128)(2,1)S(1)}, u32[]{:S(2)}, u32[]{:S(2)}) collective-permute-start(bf16[2,768,256]{2,1,0:T(8,128)(2,1)S(1)} %fusion.93), channel_id=1, source_target_pairs={{1,0},{2,1},{3,2},{4,3},{5,4},{6,5},{7,6},{9,8},{10,9},{11,10},{12... | collective-permute-start | bytes 2359304 | tf_op jit(solution)/shard_map/ppermute | solution.py:18
  73.8 4.0 copy-start.8
  73.8 4.0 copy-start.10
  73.8 4.0 copy-start.11
  86.8 1.9 copy-start.19
  102.0 1.6 copy-start.21
  103.6 5.8 %copy-start.17 = (s32[12,256]{1,0:T(8,128)S(1)}, s32[12,256]{1,0:T(8,128)}, u32[]{:S(2)}) copy-start(s32[12,256]{1,0:T(8,128)} %get-tuple-element.133) | copy-start | bytes 36868
  109.4 3.2 copy-start.16
  119.4 10.8 %collective-permute-start.2 = (bf16[2,768,256]{1,2,0:T(8,128)(2,1)S(1)}, bf16[2,768,256]{1,2,0:T(8,128)(2,1)S(1)}, u32[]{:S(2)}, u32[]{:S(2)}) collective-permute-start(bf16[2,768,256]{1,2,0:T(8,128)(2,1)S(1)} %slice.385), channel_id=1, source_target_pairs={{0,1},{1,2},{2,3},{3,4},{4,5},{5,6},{6,7},{8,9},{9,10},{10,11},{11... | collective-permute-start | bytes 2359304 | tf_op jit(solution)/shard_map/ppermute | solution.py:18
  130.5 1.4 copy-start.1
  131.9 8.8 %collective-permute-start.3 = (bf16[2,256,384]{1,2,0:T(8,128)(2,1)S(1)}, bf16[2,256,384]{1,2,0:T(8,128)(2,1)}, u32[]{:S(2)}, u32[]{:S(2)}) collective-permute-start(bf16[2,256,384]{1,2,0:T(8,128)(2,1)S(1)} %slice.388), channel_id=1, source_target_pairs={{0,8},{8,16},{16,24},{24,32},{32,40},{40,48},{48,56},{56,64},{64,7... | collective-permute-start | bytes 1179656 | tf_op jit(solution)/shard_map/ppermute | solution.py:18
  142.1 1.9 copy-start.12
  142.1 1.9 copy-start.13
  142.5 159.3 %copy-start.6 = (f32[2,256,256]{2,1,0:T(8,128)S(1)}, f32[2,256,256]{2,1,0:T(8,128)}, u32[]{:S(2)}) copy-start(f32[2,256,256]{2,1,0:T(8,128)} %param.14) | copy-start | bytes 1572868
  142.6 8.7 %collective-permute-start.4 = (bf16[2,256,384]{1,2,0:T(8,128)(2,1)S(1)}, bf16[2,256,384]{1,2,0:T(8,128)(2,1)S(1)}, u32[]{:S(2)}, u32[]{:S(2)}) collective-permute-start(bf16[2,256,384]{1,2,0:T(8,128)(2,1)S(1)} %slice.387), channel_id=1, source_target_pairs={{8,0},{16,8},{24,16},{32,24},{40,32},{48,40},{56,48},{64,56},{72,6... | collective-permute-start | bytes 1179656 | tf_op jit(solution)/shard_map/ppermute | solution.py:18
  144.9 406.6 %all-reduce.5.cloned.1.call-start = ((), (), s32[]{:S(2)}) async-start(), calls=%async_computation | async-start | bytes 1572864 | tf_op jit(solution)/shard_map/psum | solution.py:160
  152.2 150.8 %collective-permute-start.5 = (bf16[2,768,256]{1,2,0:T(8,128)(2,1)}, bf16[2,768,256]{1,2,0:T(8,128)(2,1)}, u32[]{:S(2)}, u32[]{:S(2)}) collective-permute-start(bf16[2,768,256]{1,2,0:T(8,128)(2,1)} %fusion.91), channel_id=1, source_target_pairs={{1,0},{2,1},{3,2},{4,3},{5,4},{6,5},{7,6},{9,8},{10,9},{11,10},{12... | collective-permute-start | bytes 2359304 | tf_op jit(solution)/shard_map/ppermute | solution.py:18
  355.4 3.8 copy-start.7
  368.4 1.9 copy-start.20
  385.0 5.7 %copy-start.15 = (s32[12,256]{1,0:T(8,128)S(1)}, s32[12,256]{1,0:T(8,128)}, u32[]{:S(2)}) copy-start(s32[12,256]{1,0:T(8,128)} %get-tuple-element.131) | copy-start | bytes 36868
  390.6 3.2 copy-start.14
  400.6 1.9 copy-start.2
  402.5 13.1 %collective-permute-start.6 = (bf16[2,768,256]{1,2,0:T(8,128)(2,1)S(1)}, bf16[2,768,256]{1,2,0:T(8,128)(2,1)}, u32[]{:S(2)}, u32[]{:S(2)}) collective-permute-start(bf16[2,768,256]{1,2,0:T(8,128)(2,1)S(1)} %slice.384), channel_id=1, source_target_pairs={{0,1},{1,2},{2,3},{3,4},{4,5},{5,6},{6,7},{8,9},{9,10},{10,11},{11... | collective-permute-start | bytes 2359304 | tf_op jit(solution)/shard_map/ppermute | solution.py:18
  408.7 7.0 %slice-start = ((f32[2,768,640]{1,2,0:T(8,128)}), f32[2,768,384]{1,2,0:T(8,128)S(1)}, s32[]{:S(2)}) async-start(f32[2,768,640]{1,2,0:T(8,128)} %copy-done.2), calls=%async_computation.2 | async-start | bytes 4718592 | tf_op jit(solution)/shard_map/slice | solution.py:107
  417.4 1.4 copy-start.3
  418.9 135.9 %collective-permute-start.7 = (bf16[2,256,384]{1,2,0:T(8,128)(2,1)S(1)}, bf16[2,256,384]{1,2,0:T(8,128)(2,1)S(1)}, u32[]{:S(2)}, u32[]{:S(2)}) collective-permute-start(bf16[2,256,384]{1,2,0:T(8,128)(2,1)S(1)} %slice.386), channel_id=1, source_target_pairs={{0,8},{8,16},{16,24},{24,32},{32,40},{40,48},{48,56},{56,64},{64,7... | collective-permute-start | bytes 1179656 | tf_op jit(solution)/shard_map/ppermute | solution.py:18
  551.6 3.0 copy-start.4
Sparse Core Ops, SparseCore 0:
  145.0 155.7 all-reduce.6
  407.5 144.0 all-reduce.4
where the time goes:
time: 575 us; the launch traced here: 564 us
  waiting for transfers between devices  317 us (55%)
  local copies, waits for them, and re-layouts  97.7 us (17%)
  matrix products  89.8 us (16%)
  other arithmetic  23.6 us (4%)
  starting transfers between devices  19.4 us (3%)
  between operations  16.4 us (3%)
    psum x2, waiting for transfers between devices, local(): lax.psum((probe_terms, weight_terms), ('row', 'col'))  277 us
    gather x96, local copies, waits for them, and re-layouts  80.6 us
    ppermute x8, waiting for transfers between devices, passed_along(): lax.ppermute(value, axis, [(source, source + steps) for source in range(f...  39.2 us
    dot_general x16, matrix products, product(): jnp.einsum('nab,bc->nac', part, table, preferred_element_type=jnp.float32)  37.9 us
    dot_general x16, matrix products, product(): jnp.einsum('ab,nbc->nac', table, part, preferred_element_type=jnp.float32)  32.1 us
    ppermute x8, starting transfers between devices, passed_along(): lax.ppermute(value, axis, [(source, source + steps) for source in range(f...  19.3 us
    dot_general x2, matrix products, place_patches(): jnp.einsum('far,fcas->crs', row_select, widened, preferred_element_type=j...  13.5 us
  transfers between devices with their start and end apart: 10, of which 7 were waited for; matrix products, arithmetic and copies ran while one was open for 4% of the time, Pallas kernels for 0%

commit v1 on v0

v1 whole, which is shorter than its diff:
```python
import functools

import jax
import jax.numpy as jnp
import ml_dtypes
import numpy as np
from jax import lax
from jax.experimental import pallas as pl
from jax.experimental.pallas import tpu as pltpu
from jax.sharding import Mesh, PartitionSpec as P

ITERS = 2
FLOOR = 0.3
ALPHA = 0.5
LANES = 128
CHUNK = 32
N_X, N_Z, N_Y, N_CORE = 4, 4, 4, 2
N_ROW, N_COL = N_X * N_Z, N_Y * N_CORE
ROW, COL = ("x", "z"), ("y", "core")
BF, F32 = jnp.bfloat16, jnp.float32


def chirp_blocks(size):
    offset = np.arange(size, dtype=np.int64)
    units = (offset[:, None] - offset[None, :]) ** 2 % (2 * size)
    phase = np.float32(np.pi) * units.astype(np.float32) / np.float32(size)
    scale = np.float32(1.0 / np.sqrt(size))
    real = (np.cos(phase) * scale).astype(ml_dtypes.bfloat16)
    imag = (np.sin(phase) * scale).astype(ml_dtypes.bfloat16)
    forward = np.block([[real, -imag], [imag, real]])
    return forward, np.ascontiguousarray(forward.T)


def frames_kernel(
    place, counts, pos,
    obj, below, right, corner, probe, amps, table_a, table_b,
    own_out, below_out, right_out, corner_out, keep_out, send_out, step_out,
    ext, acc, sums, wave, mis, patch,
):
    rows, cols = obj.shape[1], obj.shape[2]
    size = probe.shape[1]
    row_chunks = size // CHUNK
    inner_tiles, all_tiles = cols // LANES, (cols + size) // LANES
    for j in range(all_tiles):
        upper, lower = (obj, below) if j < inner_tiles else (right, corner)
        at = (j if j < inner_tiles else j - inner_tiles) * LANES
        ext[:, j, :rows, :] = upper[:, :, at : at + LANES].astype(BF).astype(F32)
        ext[:, j, rows:, :] = lower[:, :, at : at + LANES].astype(F32)
    acc[...] = jnp.zeros_like(acc)
    sums[...] = jnp.zeros_like(sums)
    peak = jnp.max(probe[0] * probe[0] + probe[1] * probe[1])
    step_out[0, 0] = ALPHA / (peak + 1e-6)
    lane = lax.broadcasted_iota(jnp.int32, (CHUNK, LANES), 1)

    def frame(index, carry):
        top, left = pos[0, index], pos[1, index]
        base = left // LANES
        shift = left - base * LANES
        back_shift = lax.rem(LANES - shift, LANES)
        whole = lane < LANES - shift
        fresh = lane >= shift
        for k in range(row_chunks):
            span = slice(k * CHUNK, (k + 1) * CHUNK)
            parts = []
            for c in range(2):
                tiles = [
                    pltpu.roll(ext[c, base + j, pl.ds(top + k * CHUNK, CHUNK), :], back_shift, 1)
                    for j in range(3)
                ]
                cut = jnp.concatenate(
                    [jnp.where(whole, tiles[0], tiles[1]), jnp.where(whole, tiles[1], tiles[2])], axis=1
                )
                patch[c, span, :] = cut
                parts.append(cut)
            re, im = parts
            pr, pi = probe[0, span, :], probe[1, span, :]
            wave[span, :] = (pr * re - pi * im).astype(BF)
            wave[size + k * CHUNK : size + (k + 1) * CHUNK, :] = (pr * im + pi * re).astype(BF)
            sums[2, span, :] += re * re + im * im
        near = jnp.dot(table_a[...], wave[...], preferred_element_type=F32).astype(BF)
        near = jnp.concatenate([near[:size], near[size:]], axis=1)
        far = jnp.dot(near, table_b[...], preferred_element_type=F32)
        fr, fi = far[:, :size], far[:, size:]
        scale = lax.rsqrt(jnp.maximum(fr * fr + fi * fi, FLOOR * FLOOR))
        factor = 1.0 - amps[0, index].astype(F32) * scale
        mis[:size, :] = (fr * factor).astype(BF)
        mis[size:, :] = (fi * factor).astype(BF)
        back = jnp.dot(table_b[...], mis[...], preferred_element_type=F32).astype(BF)
        back = jnp.concatenate([back[:size], back[size:]], axis=1)
        update = jnp.dot(back, table_a[...], preferred_element_type=F32)
        for k in range(row_chunks):
            span = slice(k * CHUNK, (k + 1) * CHUNK)
            ur, ui = update[span, :size], update[span, size:]
            pr, pi = probe[0, span, :], probe[1, span, :]
            re, im = patch[0, span, :], patch[1, span, :]
            sums[0, span, :] += re * ur + im * ui
            sums[1, span, :] += re * ui - im * ur
            grads = (pr * ur + pi * ui, pr * ui - pi * ur)
            for c in range(2):
                grad = grads[c].astype(BF).astype(F32)
                first = pltpu.roll(grad[:, :LANES], shift, 1)
                second = pltpu.roll(grad[:, LANES:], shift, 1)
                pieces = (
                    jnp.where(fresh, first, 0.0),
                    jnp.where(fresh, second, first),
                    jnp.where(fresh, 0.0, second),
                )
                for j, piece in enumerate(pieces):
                    acc[c, base + j, pl.ds(top + k * CHUNK, CHUNK), :] += piece
        return carry

    lax.fori_loop(0, counts[0], frame, 0)
    for j in range(all_tiles):
        upper, lower = (own_out, below_out) if j < inner_tiles else (right_out, corner_out)
        at = (j if j < inner_tiles else j - inner_tiles) * LANES
        upper[:, :, at : at + LANES] = acc[:, j, :rows, :].astype(upper.dtype)
        lower[:, :, at : at + LANES] = acc[:, j, rows:, :].astype(BF)
    core, y = place[0], place[1]
    half, quarter = size // N_CORE, size // (N_CORE * N_Y)
    for j in range(N_Y):
        inner = lax.rem(y + j, N_Y) * quarter
        keep_at = pl.multiple_of(core * half + inner, quarter)
        send_at = pl.multiple_of((1 - core) * half + inner, quarter)
        keep_out[j] = sums[:, pl.ds(keep_at, quarter), :]
        send_out[j] = sums[:, pl.ds(send_at, quarter), :]


def run_frames(place, counts, pos, obj, halos, probe, amps, tables, iteration):
    rows, cols = obj.shape[1], obj.shape[2]
    size = probe.shape[1]
    slots = amps.shape[1]
    vmem = pl.BlockSpec(memory_space=pltpu.VMEM)
    smem = pl.BlockSpec(memory_space=pltpu.SMEM)
    quarter = size // (N_CORE * N_Y)
    shapes = [
        jax.ShapeDtypeStruct((2, rows, cols), F32),
        jax.ShapeDtypeStruct((2, size, cols), BF),
        jax.ShapeDtypeStruct((2, rows, size), BF),
        jax.ShapeDtypeStruct((2, size, size), BF),
        jax.ShapeDtypeStruct((N_Y, 3, quarter, size), F32),
        jax.ShapeDtypeStruct((N_Y, 3, quarter, size), F32),
        jax.ShapeDtypeStruct((1, 1), F32),
    ]
    amp_spec = pl.BlockSpec((1, slots, size, size), lambda i: (iteration, 0, 0, 0))
    return pl.pallas_call(
        frames_kernel,
        grid=(1,),
        out_shape=shapes,
        in_specs=[smem] * 3 + [vmem] * 5 + [amp_spec] + [vmem] * 2,
        out_specs=[vmem] * 6 + [smem],
        scratch_shapes=[
            pltpu.VMEM((2, (cols + size) // LANES, rows + size, LANES), F32),
            pltpu.VMEM((2, (cols + size) // LANES, rows + size, LANES), F32),
            pltpu.VMEM((3, size, size), F32),
            pltpu.VMEM((2 * size, size), BF),
            pltpu.VMEM((2 * size, size), BF),
            pltpu.VMEM((2, size, size), F32),
        ],
        compiler_params=pltpu.CompilerParams(vmem_limit_bytes=48 << 20),
        cost_estimate=pl.CostEstimate(flops=6_000_000_000, bytes_accessed=8_000_000, transcendentals=0),
        name="frames",
    )(place, counts, pos, obj, *halos, probe, amps, *tables)


def update_kernel(obj, own, above, left, diag, step, obj_out, below_out, right_out):
    size = left.shape[2]
    rows = obj.shape[1]
    alpha = step[0, 0]
    rest_cols = obj.shape[2] - size
    a, l, d = above[...].astype(F32), left[...].astype(F32), diag[...].astype(F32)
    obj_out[:, :size, :size] = obj[:, :size, :size] - alpha * (
        own[:, :size, :size] + l[:, :size] + a[:, :, :size] + d
    )
    obj_out[:, :size, size:] = obj[:, :size, size:] - alpha * (own[:, :size, size:] + a[:, :, size:])
    obj_out[:, size:, :size] = obj[:, size:, :size] - alpha * (own[:, size:, :size] + l[:, size:])
    obj_out[:, size:, size:] = obj[:, size:, size:] - alpha * own[:, size:, size:]
    below_out[...] = obj_out[:, :size, :].astype(BF)
    right_out[...] = obj_out[:, :, :size].astype(BF)


def run_update(obj, own, above, left, diag, step):
    rows, cols = obj.shape[1], obj.shape[2]
    size = left.shape[2]
    vmem = pl.BlockSpec(memory_space=pltpu.VMEM)
    smem = pl.BlockSpec(memory_space=pltpu.SMEM)
    return pl.pallas_call(
        update_kernel,
        out_shape=[
            jax.ShapeDtypeStruct((2, rows, cols), F32),
            jax.ShapeDtypeStruct((2, size, cols), BF),
            jax.ShapeDtypeStruct((2, rows, size), BF),
        ],
        in_specs=[vmem] * 5 + [smem],
        out_specs=[vmem] * 3,
        compiler_params=pltpu.CompilerParams(vmem_limit_bytes=32 << 20),
        cost_estimate=pl.CostEstimate(flops=2_000_000, bytes_accessed=8_000_000, transcendentals=0),
        name="object_update",
    )(obj, own, above, left, diag, step)


def moved(value, axis, count, steps):
    first, last = max(0, -steps), min(count, count - steps)
    return lax.ppermute(value, axis, [(s, s + steps) for s in range(first, last)])


def moved_both(value, steps):
    pairs = []
    for r in range(N_ROW):
        for c in range(N_COL):
            to_r, to_c = r + steps, c + steps
            if 0 <= to_r < N_ROW and 0 <= to_c < N_COL:
                pairs.append((r * N_COL + c, to_r * N_COL + to_c))
    return lax.ppermute(value, ROW + COL, pairs)


def turned(value, axis, steps):
    return lax.ppermute(value, axis, [(s, (s + steps) % 4) for s in range(4)])


def swapped(value):
    return lax.ppermute(value, "core", [(0, 1), (1, 0)])


def halo(below, right, size):
    return (
        moved(below, ROW, N_ROW, -1),
        moved(right, COL, N_COL, -1),
        moved_both(below[:, :, :size], -1),
    )


def new_probe(keep, send, probe, place):
    size = probe.shape[1]
    half, quarter = size // N_CORE, size // (N_CORE * N_Y)
    core, y = place[0], place[1]
    part = keep + swapped(send)
    total = part[0]
    for j in range(1, N_Y):
        total = total + turned(part[j], "y", j)
    for axis in ("z", "x"):
        total = total + turned(total, axis, 1) + turned(total, axis, 2) + turned(total, axis, 3)
    mine = lax.dynamic_slice(probe, (0, core * half + y * quarter, 0), (2, quarter, size))
    fresh = mine - total[:2] / (total[2] + 1.0)
    chunks = [fresh] + [turned(fresh, "y", j) for j in range(1, N_Y)]
    mine_half = jnp.concatenate(chunks[::-1] + chunks[::-1], axis=1)
    at = lax.rem(N_Y - 1 - y + N_Y, N_Y) * quarter
    mine_half = lax.dynamic_slice(mine_half, (0, at, 0), (2, half, size))
    other = swapped(mine_half)
    first = jnp.where(core == 0, mine_half, other)
    second = jnp.where(core == 0, other, mine_half)
    return jnp.concatenate([first, second], axis=1)


def local(tables, obj, probe, amps, positions, counts):
    size = probe.shape[-1]
    place = jnp.stack([lax.axis_index("core"), lax.axis_index("y")]).astype(jnp.int32)
    below, right = obj[:, :size, :].astype(BF), obj[:, :, :size].astype(BF)
    for iteration in range(ITERS):
        halos = halo(below, right, size)
        own, down, across, both, keep, send, step = run_frames(
            place, counts[iteration, 0], positions[iteration], obj, halos, probe, amps, tables, iteration
        )
        diag = moved_both(both, 1)
        left = moved(across, COL, N_COL, 1)
        above = moved(down, ROW, N_ROW, 1)
        probe = new_probe(keep, send, probe, place)
        obj, below, right = run_update(obj, own, above, left, diag, step)
    return (obj, probe)


def solution(mesh):
    fine = Mesh(mesh.devices.reshape(N_X, N_Z, N_Y, N_CORE), ("x", "z", "y", "core"))
    placed = (
        P(None, ROW, COL),
        P(),
        P(None, ROW + COL, None, None),
        P(None, None, ROW + COL),
        P(None, COL, ROW),
    )
    blocks = tuple(jnp.asarray(block) for block in chirp_blocks(256))
    return jax.shard_map(
        functools.partial(local, blocks),
        mesh=fine, in_specs=placed, out_specs=(P(None, ROW, COL), P()), check_vma=False,
    )
```

time: 575 us -> 216 us (0.38); the launches traced: 564 us -> 217 us
  waiting for transfers between devices: 317 us -> 76 us
  local copies, waits for them, and re-layouts: 97.7 us -> 7.16 us
  matrix products: 89.8 us -> 0 us
  starting transfers between devices: 19.4 us -> 108 us
  Pallas kernels: 0 us -> 17.4 us
  other arithmetic: 23.6 us -> 7.02 us
  between operations: 16.4 us -> 1.21 us
    psum x2 -> x0, waiting for transfers between devices: 277 us -> none  [local(): lax.psum((probe_terms, weight_terms), ('row', 'col'))]
    dot_general x36 -> x0, matrix products: 89.8 us -> none  [the longest x16 37.9 us: product(): jnp.einsum('nab,bc->nac', part, table, preferred_element_type=jnp.float32)]
    ppermute x8 -> x40, starting transfers between devices: 19.3 us -> 108 us  [the longest x24 67.6 us: turned(): return lax.ppermute(value, axis, [(s, (s + steps) % 4) for s in range(4)])]
    gather x96 -> x0, local copies, waits for them, and re-layouts: 80.6 us -> none
    ppermute x8 -> x40, waiting for transfers between devices: 39.2 us -> 76 us  [the longest x24 46.7 us: turned(): return lax.ppermute(value, axis, [(s, (s + steps) % 4) for s in range(4)])]
    pallas_call x0 -> x4, Pallas kernels: none -> 17.4 us  [the longest x2 12.8 us: run_frames(): pl.pallas_call(frames_kernel, grid=(1,), out_shape=shapes, in_specs=[smem...]
    unnamed x48 -> x44, local copies, waits for them, and re-layouts: 11.4 us -> 3.92 us
  transfers between devices with their start and end apart: 10 -> 40, of which waited for: 7 -> 23; matrix products, arithmetic and copies ran while one was open for 4% -> 3% of each run, Pallas kernels for 0% -> 2%
where the time goes in v1:
time: 216 us; the launch traced here: 217 us
  starting transfers between devices  108 us (50%)
  waiting for transfers between devices  76 us (35%)
  Pallas kernels  17.4 us (8%)
  local copies, waits for them, and re-layouts  7.16 us (3%)
  other arithmetic  7.02 us (3%)
    ppermute x24, starting transfers between devices, turned(): return lax.ppermute(value, axis, [(s, (s + steps) % 4) for s in range(4)])  67.6 us
    ppermute x24, waiting for transfers between devices, turned(): return lax.ppermute(value, axis, [(s, (s + steps) % 4) for s in range(4)])  46.7 us
    ppermute x8, starting transfers between devices, moved(): lax.ppermute(value, axis, [(s, s + steps) for s in range(first, last)])  19.9 us
    ppermute x4, waiting for transfers between devices, moved_both(): return lax.ppermute(value, ROW + COL, pairs)  16.3 us
    ppermute x4, starting transfers between devices, swapped(): return lax.ppermute(value, 'core', [(0, 1), (1, 0)])  13 us
    pallas_call x2, Pallas kernels, run_frames(): pl.pallas_call(frames_kernel, grid=(1,), out_shape=shapes, in_specs=[smem...  12.8 us
    ppermute x8, waiting for transfers between devices, moved(): lax.ppermute(value, axis, [(s, s + steps) for s in range(first, last)])  9.99 us
    ppermute x4, starting transfers between devices, moved_both(): return lax.ppermute(value, ROW + COL, pairs)  7.97 us
  transfers between devices with their start and end apart: 40, of which 23 were waited for; matrix products, arithmetic and copies ran while one was open for 3% of the time, Pallas kernels for 2%

profile of v1, /device:TPU:1, one launch (start us, length us, event | category | flops | bytes accessed | tf_op | source)
XLA Modules:
  0.0 217.3 jit_solution(3482136506496687363)
XLA Ops:
  0.6 1.5 convert.4
  2.2 3.5 %collective-permute-start.1 = (bf16[2,512,256]{2,1,0:T(8,128)(2,1)S(1)}, bf16[2,512,256]{2,1,0:T(8,128)(2,1)S(1)}, u32[]{:S(2)}, u32[]{:S(2)}) collective-permute-start(bf16[2,512,256]{2,1,0:T(8,128)(2,1)S(1)} %slice.84), channel_id=1, source_target_pairs={{1,0},{2,1},{3,2},{4,3},{5,4},{6,5},{7,6},{9,8},{10,9},{11,10},{12... | collective-permute-start | bytes 1572872 | tf_op jit(solution)/shard_map/ppermute | solution.py:203
  5.7 1.3 collective-permute-start.2
  7.8 1.3 collective-permute-start
  9.9 8.2 %collective-permute-done.2.corner = bf16[2,256,256]{2,1,0:T(8,128)(2,1)S(1)} collective-permute-done((bf16[2,256,256]{2,1,0:T(8,128)(2,1)S(1)}, bf16[2,256,256]{2,1,0:T(8,128)(2,1)S(1)}, u32[]{:S(2)}, u32[]{:S(2)}) %collective-permute-start.2) | collective-permute-done | bytes 262176 | tf_op jit(solution)/shard_map/ppermute | solution.py:213
  18.1 6.3 %collective-permute-done.below = bf16[2,256,384]{2,1,0:T(8,128)(2,1)S(1)} collective-permute-done((bf16[2,256,384]{2,1,0:T(8,128)(2,1)}, bf16[2,256,384]{2,1,0:T(8,128)(2,1)S(1)}, u32[]{:S(2)}, u32[]{:S(2)}) %collective-permute-start) | collective-permute-done | bytes 393248 | tf_op jit(solution)/shard_map/ppermute | solution.py:203
  24.4 6.3 %frames.2 = (f32[2,512,384]{2,1,0:T(8,128)}, bf16[2,256,384]{2,1,0:T(8,128)(2,1)S(1)}, bf16[2,512,256]{2,1,0:T(8,128)(2,1)S(1)}, bf16[2,256,256]{2,1,0:T(8,128)(...) custom-call(s32[2]{0:T(128)S(1)} %pad_add_fusion.place, s32[1]{0:T(128)} %bitcast.2.counts, ...), custom_call_target="tpu_custom_call" | custom-call | flops 6000000000 | bytes 8000000 | tf_op jit(solution)/shard_map/frames/pallas_call | solution.py:145
  30.8 1.7 collective-permute-done.9
  32.6 5.5 %collective-permute-start.10 = (f32[3,32,256]{2,1,0:T(8,128)S(1)}, f32[3,32,256]{2,1,0:T(8,128)S(1)}, u32[]{:S(2)}, u32[]{:S(2)}) collective-permute-start(f32[3,32,256]{2,1,0:T(8,128)S(1)} %get-tuple-element.45), channel_id=1, source_target_pairs={{0,2},{2,4},{4,6},{6,0},{1,3},{3,5},{5,7},{7,1},{8,10},{10,12},{12... | collective-permute-start | bytes 294920 | tf_op jit(solution)/shard_map/ppermute | solution.py:217
  38.1 15.2 %collective-permute-start.12 = (f32[3,32,256]{2,1,0:T(8,128)S(1)}, f32[3,32,256]{2,1,0:T(8,128)S(1)}, u32[]{:S(2)}, u32[]{:S(2)}) collective-permute-start(f32[3,32,256]{2,1,0:T(8,128)S(1)} %get-tuple-element.46), channel_id=1, source_target_pairs={{0,6},{2,0},{4,2},{6,4},{1,7},{3,1},{5,3},{7,5},{8,14},{10,8},{12,... | collective-permute-start | bytes 294920 | tf_op jit(solution)/shard_map/ppermute | solution.py:217
  53.3 1.2 collective-permute-start.11
  54.5 1.6 collective-permute-done.10
  56.1 2.8 %collective-permute-done.11 = f32[3,32,256]{2,1,0:T(8,128)S(1)} collective-permute-done((f32[3,32,256]{2,1,0:T(8,128)S(1)}, f32[3,32,256]{2,1,0:T(8,128)S(1)}, u32[]{:S(2)}, u32[]{:S(2)}) %collective-permute-start.11) | collective-permute-done | bytes 98336 | tf_op jit(solution)/shard_map/ppermute | solution.py:217
  59.1 1.4 collective-permute-start.13
  60.4 2.0 collective-permute-done.15
  62.4 1.6 collective-permute-done.14
  64.1 1.7 collective-permute-done.13
  67.0 10.2 %collective-permute-start.17 = (f32[3,32,256]{2,1,0:T(8,128)}, f32[3,32,256]{2,1,0:T(8,128)}, u32[]{:S(2)}, u32[]{:S(2)}) collective-permute-start(f32[3,32,256]{2,1,0:T(8,128)} %add_add_fusion.3), channel_id=1, source_target_pairs={{0,64},{32,96},{64,0},{96,32},{1,65},{33,97},{65,1},{97,33},{2,66}... | collective-permute-start | bytes 294920 | tf_op jit(solution)/shard_map/ppermute | solution.py:217
  77.2 0.9 collective-permute-start.16
  78.1 1.5 collective-permute-done.17
  79.6 3.4 %collective-permute-done.16 = f32[3,32,256]{2,1,0:T(8,128)} collective-permute-done((f32[3,32,256]{2,1,0:T(8,128)}, f32[3,32,256]{2,1,0:T(8,128)}, u32[]{:S(2)}, u32[]{:S(2)}) %collective-permute-start.16) | collective-permute-done | bytes 98336 | tf_op jit(solution)/shard_map/ppermute | solution.py:217
  83.0 1.1 add_add_fusion.2
  84.1 1.5 fusion.8
  85.6 1.7 collective-permute-start.19
  87.3 2.9 %collective-permute-start.5 = (bf16[2,256,256]{2,1,0:T(8,128)(2,1)}, bf16[2,256,256]{2,1,0:T(8,128)(2,1)S(1)}, u32[]{:S(2)}, u32[]{:S(2)}) collective-permute-start(bf16[2,256,256]{2,1,0:T(8,128)(2,1)} %copy-done.7), channel_id=1, source_target_pairs={{0,9},{1,10},{2,11},{3,12},{4,13},{5,14},{6,15},{8,17},{9,18},{10,... | collective-permute-start | bytes 786440 | tf_op jit(solution)/shard_map/ppermute | solution.py:213
  90.3 3.5 %collective-permute-start.3 = (bf16[2,256,384]{2,1,0:T(8,128)(2,1)S(1)}, bf16[2,256,384]{2,1,0:T(8,128)(2,1)S(1)}, u32[]{:S(2)}, u32[]{:S(2)}) collective-permute-start(bf16[2,256,384]{2,1,0:T(8,128)(2,1)S(1)} %get-tuple-element.21), channel_id=1, source_target_pairs={{0,8},{8,16},{16,24},{24,32},{32,40},{40,48},{48,56},{56,64},{64,7... | collective-permute-start | bytes 1179656 | tf_op jit(solution)/shard_map/ppermute | solution.py:203
  93.8 1.9 collective-permute-start.4
  95.7 1.2 collective-permute-start.21
  96.9 1.7 collective-permute-start.20
  98.6 0.8 constant_dynamic-update-slice_fusion.7
  99.4 8.5 %collective-permute-done.20 = f32[2,32,256]{2,1,0:T(8,128)S(1)} collective-permute-done((f32[2,32,256]{2,1,0:T(8,128)}, f32[2,32,256]{2,1,0:T(8,128)S(1)}, u32[]{:S(2)}, u32[]{:S(2)}) %collective-permute-start.20) | collective-permute-done | bytes 65568 | tf_op jit(solution)/shard_map/ppermute | solution.py:217
  108.0 0.8 constant_dynamic-update-slice_fusion.4
  108.9 0.8 constant_dynamic-update-slice_fusion.3
  109.7 0.8 constant_dynamic-update-slice_fusion
  110.6 0.8 constant_dynamic-slice_fusion.1
  111.5 2.1 object_update.2
  113.6 1.1 copy-done.1
  114.8 2.4 %collective-permute-start.7 = (bf16[2,512,256]{2,1,0:T(8,128)(2,1)}, bf16[2,512,256]{2,1,0:T(8,128)(2,1)S(1)}, u32[]{:S(2)}, u32[]{:S(2)}) collective-permute-start(bf16[2,512,256]{2,1,0:T(8,128)(2,1)} %get-tuple-element.27), channel_id=1, source_target_pairs={{1,0},{2,1},{3,2},{4,3},{5,4},{6,5},{7,6},{9,8},{10,9},{11,10},{12... | collective-permute-start | bytes 1572872 | tf_op jit(solution)/shard_map/ppermute | solution.py:203
  117.2 1.3 collective-permute-start.6
  118.6 1.3 collective-permute-start.8
  119.9 1.1 broadcast_select_fusion.3
  121.0 8.0 %collective-permute-done.8.corner = bf16[2,256,256]{2,1,0:T(8,128)(2,1)S(1)} collective-permute-done((bf16[2,256,256]{2,1,0:T(8,128)(2,1)S(1)}, bf16[2,256,256]{2,1,0:T(8,128)(2,1)S(1)}, u32[]{:S(2)}, u32[]{:S(2)}) %collective-permute-start.8) | collective-permute-done | bytes 262176 | tf_op jit(solution)/shard_map/ppermute | solution.py:213
  129.0 3.7 %collective-permute-done.6.below = bf16[2,256,384]{2,1,0:T(8,128)(2,1)S(1)} collective-permute-done((bf16[2,256,384]{2,1,0:T(8,128)(2,1)S(1)}, bf16[2,256,384]{2,1,0:T(8,128)(2,1)S(1)}, u32[]{:S(2)}, u32[]{:S(2)}) %collective-permute-start.6) | collective-permute-done | bytes 393248 | tf_op jit(solution)/shard_map/ppermute | solution.py:203
  132.8 6.5 %frames.3 = (f32[2,512,384]{2,1,0:T(8,128)}, bf16[2,256,384]{2,1,0:T(8,128)(2,1)S(1)}, bf16[2,512,256]{2,1,0:T(8,128)(2,1)S(1)}, bf16[2,256,256]{2,1,0:T(8,128)(...) custom-call(s32[2]{0:T(128)S(1)} %pad_add_fusion.place, s32[1]{0:T(128)} %bitcast.4.counts, ...), custom_call_target="tpu_custom_call" | custom-call | flops 6000000000 | bytes 8000000 | tf_op jit(solution)/shard_map/frames/pallas_call | solution.py:145
  139.2 12.9 %collective-permute-start.26 = (f32[4,3,32,256]{3,2,1,0:T(8,128)S(1)}, f32[4,3,32,256]{3,2,1,0:T(8,128)S(1)}, u32[]{:S(2)}, u32[]{:S(2)}) collective-permute-start(f32[4,3,32,256]{3,2,1,0:T(8,128)S(1)} %get-tuple-element.37), channel_id=1, source_target_pairs={{0,1},{1,0},{2,3},{3,2},{4,5},{5,4},{6,7},{7,6},{8,9},{9,8},{10,11... | collective-permute-start | bytes 1179656 | tf_op jit(solution)/shard_map/ppermute | solution.py:221
  152.1 1.3 collective-permute-done.26
  153.6 2.7 %collective-permute-start.29 = (f32[3,32,256]{2,1,0:T(8,128)S(1)}, f32[3,32,256]{2,1,0:T(8,128)S(1)}, u32[]{:S(2)}, u32[]{:S(2)}) collective-permute-start(f32[3,32,256]{2,1,0:T(8,128)S(1)} %get-tuple-element.43), channel_id=1, source_target_pairs={{0,6},{2,0},{4,2},{6,4},{1,7},{3,1},{5,3},{7,5},{8,14},{10,8},{12,... | collective-permute-start | bytes 294920 | tf_op jit(solution)/shard_map/ppermute | solution.py:217
  156.3 2.5 %collective-permute-done.27 = f32[3,32,256]{2,1,0:T(8,128)S(1)} collective-permute-done((f32[3,32,256]{2,1,0:T(8,128)S(1)}, f32[3,32,256]{2,1,0:T(8,128)S(1)}, u32[]{:S(2)}, u32[]{:S(2)}) %collective-permute-start.27) | collective-permute-done | bytes 98336 | tf_op jit(solution)/shard_map/ppermute | solution.py:217
  158.8 1.3 collective-permute-done.29
  160.1 1.1 collective-permute-done.28
  161.4 14.0 %collective-permute-start.31 = (f32[3,32,256]{2,1,0:T(8,128)S(1)}, f32[3,32,256]{2,1,0:T(8,128)S(1)}, u32[]{:S(2)}, u32[]{:S(2)}) collective-permute-start(f32[3,32,256]{2,1,0:T(8,128)S(1)} %fusion.2), channel_id=1, source_target_pairs={{0,16},{8,24},{16,0},{24,8},{1,17},{9,25},{17,1},{25,9},{2,18},{10... | collective-permute-start | bytes 294920 | tf_op jit(solution)/shard_map/ppermute | solution.py:217
  176.1 1.2 collective-permute-done.31
  177.4 3.5 %collective-permute-done.30 = f32[3,32,256]{2,1,0:T(8,128)S(1)} collective-permute-done((f32[3,32,256]{2,1,0:T(8,128)S(1)}, f32[3,32,256]{2,1,0:T(8,128)S(1)}, u32[]{:S(2)}, u32[]{:S(2)}) %collective-permute-start.30) | collective-permute-done | bytes 98336 | tf_op jit(solution)/shard_map/ppermute | solution.py:217
  180.9 4.5 %collective-permute-start.34 = (f32[3,32,256]{2,1,0:T(8,128)S(1)}, f32[3,32,256]{2,1,0:T(8,128)S(1)}, u32[]{:S(2)}, u32[]{:S(2)}) collective-permute-start(f32[3,32,256]{2,1,0:T(8,128)S(1)} %add_add_fusion.1), channel_id=1, source_target_pairs={{0,64},{32,96},{64,0},{96,32},{1,65},{33,97},{65,1},{97,33},{2,66}... | collective-permute-start | bytes 294920 | tf_op jit(solution)/shard_map/ppermute | solution.py:217
  185.7 1.8 collective-permute-done.34
  187.4 2.7 %collective-permute-done.33 = f32[3,32,256]{2,1,0:T(8,128)S(1)} collective-permute-done((f32[3,32,256]{2,1,0:T(8,128)S(1)}, f32[3,32,256]{2,1,0:T(8,128)S(1)}, u32[]{:S(2)}, u32[]{:S(2)}) %collective-permute-start.33) | collective-permute-done | bytes 98336 | tf_op jit(solution)/shard_map/ppermute | solution.py:217
  190.2 4.4 %collective-permute-start.36 = (f32[2,32,256]{2,1,0:T(8,128)S(1)}, f32[2,32,256]{2,1,0:T(8,128)S(1)}, u32[]{:S(2)}, u32[]{:S(2)}) collective-permute-start(f32[2,32,256]{2,1,0:T(8,128)S(1)} %fusion.7), channel_id=1, source_target_pairs={{0,6},{2,0},{4,2},{6,4},{1,7},{3,1},{5,3},{7,5},{8,14},{10,8},{12,... | collective-permute-start | bytes 196616 | tf_op jit(solution)/shard_map/ppermute | solution.py:217
  194.6 2.5 %collective-permute-start.25 = (bf16[2,256,256]{2,1,0:T(8,128)(2,1)S(1)}, bf16[2,256,256]{2,1,0:T(8,128)(2,1)S(1)}, u32[]{:S(2)}, u32[]{:S(2)}) collective-permute-start(bf16[2,256,256]{2,1,0:T(8,128)(2,1)S(1)} %get-tuple-element.33), channel_id=1, source_target_pairs={{0,9},{1,10},{2,11},{3,12},{4,13},{5,14},{6,15},{8,17},{9,18},{10,... | collective-permute-start | bytes 786440 | tf_op jit(solution)/shard_map/ppermute | solution.py:213
  197.1 4.0 %collective-permute-start.23 = (bf16[2,256,384]{2,1,0:T(8,128)(2,1)S(1)}, bf16[2,256,384]{2,1,0:T(8,128)(2,1)S(1)}, u32[]{:S(2)}, u32[]{:S(2)}) collective-permute-start(bf16[2,256,384]{2,1,0:T(8,128)(2,1)S(1)} %get-tuple-element.31), channel_id=1, source_target_pairs={{0,8},{8,16},{16,24},{24,32},{32,40},{40,48},{48,56},{56,64},{64,7... | collective-permute-start | bytes 1179656 | tf_op jit(solution)/shard_map/ppermute | solution.py:203
  201.1 1.9 collective-permute-start.24
  203.1 1.3 collective-permute-start.37
  204.5 9.2 %collective-permute-done.37 = f32[2,32,256]{2,1,0:T(8,128)S(1)} collective-permute-done((f32[2,32,256]{2,1,0:T(8,128)S(1)}, f32[2,32,256]{2,1,0:T(8,128)S(1)}, u32[]{:S(2)}, u32[]{:S(2)}) %collective-permute-start.37) | collective-permute-done | bytes 65568 | tf_op jit(solution)/shard_map/ppermute | solution.py:217
  213.9 2.5 %object_update.3 = (f32[2,512,384]{2,1,0:T(8,128)}, bf16[2,256,384]{2,1,0:T(8,128)(2,1)}, bf16[2,512,256]{2,1,0:T(8,128)(2,1)}) custom-call(f32[2,512,384]{2,1,0:T(8,128)S(1)} %copy-done.2, f32[2,512,384]{2,1,0:T(8,128)S(1)} %copy-done.4, bf16[2,256,384]{2,1,0:T(8,128)(2,1)S(1)} %collective-permute-done.23.above, ...), custom_call_target="tpu_custom_call" | custom-call | flops 2000000 | bytes 8000000 | tf_op jit(solution)/shard_map/object_update/pallas_call | solution.py:186
  216.4 0.8 pad_maximum_fusion.1
  (94 shorter events, 5.1 us)
Async XLA Ops:
  2.1 7.0 %copy-start.14 = (s32[2,1,1]{0,2,1:T(1,128)S(1)}, s32[2,1,1]{0,2,1:T(1,128)}, u32[]{:S(2)}) copy-start(s32[2,1,1]{0,2,1:T(1,128)} %param.11) | copy-start | bytes 28
  2.1 7.7 %copy-start.13 = (s32[2,2,12]{2,1,0:T(2,128)S(1)}, s32[2,2,12]{2,1,0:T(2,128)}, u32[]{:S(2)}) copy-start(s32[2,2,12]{2,1,0:T(2,128)} %param.10) | copy-start | bytes 580
  2.2 22.2 %copy-start.5 = (f32[2,256,256]{2,1,0:T(8,128)S(1)}, f32[2,256,256]{2,1,0:T(8,128)}, u32[]{:S(2)}) copy-start(f32[2,256,256]{2,1,0:T(8,128)} %probe.1) | copy-start | bytes 1572868
  2.2 22.2 %copy-start.8 = (bf16[512,512]{1,0:T(8,128)(2,1)S(1)}, bf16[512,512]{1,0:T(8,128)(2,1)}, u32[]{:S(2)}) copy-start(bf16[512,512]{1,0:T(8,128)(2,1)} %constant.30.clone.table_b) | copy-start | bytes 1572868
  2.2 22.2 %copy-start.10 = (bf16[512,512]{1,0:T(8,128)(2,1)S(1)}, bf16[512,512]{1,0:T(8,128)(2,1)}, u32[]{:S(2)}) copy-start(bf16[512,512]{1,0:T(8,128)(2,1)} %constant.29.clone.table_a) | copy-start | bytes 1572868
  2.2 22.1 %collective-permute-start.1 = (bf16[2,512,256]{2,1,0:T(8,128)(2,1)S(1)}, bf16[2,512,256]{2,1,0:T(8,128)(2,1)S(1)}, u32[]{:S(2)}, u32[]{:S(2)}) collective-permute-start(bf16[2,512,256]{2,1,0:T(8,128)(2,1)S(1)} %slice.84), channel_id=1, source_target_pairs={{1,0},{2,1},{3,2},{4,3},{5,4},{6,5},{7,6},{9,8},{10,9},{11,10},{12... | collective-permute-start | bytes 1572872 | tf_op jit(solution)/shard_map/ppermute | solution.py:203
  5.7 12.4 %collective-permute-start.2 = (bf16[2,256,256]{2,1,0:T(8,128)(2,1)S(1)}, bf16[2,256,256]{2,1,0:T(8,128)(2,1)S(1)}, u32[]{:S(2)}, u32[]{:S(2)}) collective-permute-start(bf16[2,256,256]{2,1,0:T(8,128)(2,1)S(1)} %slice.85), channel_id=1, source_target_pairs={{9,0},{10,1},{11,2},{12,3},{13,4},{14,5},{15,6},{17,8},{18,9},{19,... | collective-permute-start | bytes 786440 | tf_op jit(solution)/shard_map/ppermute | solution.py:213
  7.8 16.5 %collective-permute-start = (bf16[2,256,384]{2,1,0:T(8,128)(2,1)}, bf16[2,256,384]{2,1,0:T(8,128)(2,1)S(1)}, u32[]{:S(2)}, u32[]{:S(2)}) collective-permute-start(bf16[2,256,384]{2,1,0:T(8,128)(2,1)} %slice.83), channel_id=1, source_target_pairs={{8,0},{16,8},{24,16},{32,24},{40,32},{48,40},{56,48},{64,56},{72,6... | collective-permute-start | bytes 1179656 | tf_op jit(solution)/shard_map/ppermute | solution.py:203
  30.7 22.6 %copy-start.6 = (bf16[2,512,256]{2,1,0:T(8,128)(2,1)}, bf16[2,512,256]{2,1,0:T(8,128)(2,1)S(1)}, u32[]{:S(2)}) copy-start(bf16[2,512,256]{2,1,0:T(8,128)(2,1)S(1)} %get-tuple-element.22) | copy-start | bytes 1572868
  30.7 22.6 %copy-start.7 = (bf16[2,256,256]{2,1,0:T(8,128)(2,1)}, bf16[2,256,256]{2,1,0:T(8,128)(2,1)S(1)}, u32[]{:S(2)}) copy-start(bf16[2,256,256]{2,1,0:T(8,128)(2,1)S(1)} %get-tuple-element.23) | copy-start | bytes 786436
  30.7 1.8 collective-permute-start.9
  32.6 23.5 %collective-permute-start.10 = (f32[3,32,256]{2,1,0:T(8,128)S(1)}, f32[3,32,256]{2,1,0:T(8,128)S(1)}, u32[]{:S(2)}, u32[]{:S(2)}) collective-permute-start(f32[3,32,256]{2,1,0:T(8,128)S(1)} %get-tuple-element.45), channel_id=1, source_target_pairs={{0,2},{2,4},{4,6},{6,0},{1,3},{3,5},{5,7},{7,1},{8,10},{10,12},{12... | collective-permute-start | bytes 294920 | tf_op jit(solution)/shard_map/ppermute | solution.py:217
  38.1 18.0 %collective-permute-start.12 = (f32[3,32,256]{2,1,0:T(8,128)S(1)}, f32[3,32,256]{2,1,0:T(8,128)S(1)}, u32[]{:S(2)}, u32[]{:S(2)}) collective-permute-start(f32[3,32,256]{2,1,0:T(8,128)S(1)} %get-tuple-element.46), channel_id=1, source_target_pairs={{0,6},{2,0},{4,2},{6,4},{1,7},{3,1},{5,3},{7,5},{8,14},{10,8},{12,... | collective-permute-start | bytes 294920 | tf_op jit(solution)/shard_map/ppermute | solution.py:217
  53.3 58.2 %copy-start = (f32[2,512,384]{2,1,0:T(8,128)S(1)}, f32[2,512,384]{2,1,0:T(8,128)}, u32[]{:S(2)}) copy-start(f32[2,512,384]{2,1,0:T(8,128)} %obj.3) | copy-start | bytes 4718596
  53.3 58.2 %copy-start.3 = (f32[2,512,384]{2,1,0:T(8,128)S(1)}, f32[2,512,384]{2,1,0:T(8,128)}, u32[]{:S(2)}) copy-start(f32[2,512,384]{2,1,0:T(8,128)} %get-tuple-element.20.own) | copy-start | bytes 4718596
  53.3 5.6 %collective-permute-start.11 = (f32[3,32,256]{2,1,0:T(8,128)S(1)}, f32[3,32,256]{2,1,0:T(8,128)S(1)}, u32[]{:S(2)}, u32[]{:S(2)}) collective-permute-start(f32[3,32,256]{2,1,0:T(8,128)S(1)} %get-tuple-element.47), channel_id=1, source_target_pairs={{0,4},{2,6},{4,0},{6,2},{1,5},{3,7},{5,1},{7,3},{8,12},{10,14},{12... | collective-permute-start | bytes 294920 | tf_op jit(solution)/shard_map/ppermute | solution.py:217
  58.9 3.5 %collective-permute-start.15 = (f32[3,32,256]{2,1,0:T(8,128)S(1)}, f32[3,32,256]{2,1,0:T(8,128)S(1)}, u32[]{:S(2)}, u32[]{:S(2)}) collective-permute-start(f32[3,32,256]{2,1,0:T(8,128)S(1)} %fusion.5), channel_id=1, source_target_pairs={{0,24},{8,0},{16,8},{24,16},{1,25},{9,1},{17,9},{25,17},{2,26},{10... | collective-permute-start | bytes 294920 | tf_op jit(solution)/shard_map/ppermute | solution.py:217
  59.0 5.1 %collective-permute-start.14 = (f32[3,32,256]{2,1,0:T(8,128)S(1)}, f32[3,32,256]{2,1,0:T(8,128)S(1)}, u32[]{:S(2)}, u32[]{:S(2)}) collective-permute-start(f32[3,32,256]{2,1,0:T(8,128)S(1)} %fusion.5), channel_id=1, source_target_pairs={{0,16},{8,24},{16,0},{24,8},{1,17},{9,25},{17,1},{25,9},{2,18},{10... | collective-permute-start | bytes 294920 | tf_op jit(solution)/shard_map/ppermute | solution.py:217
  59.1 6.7 %collective-permute-start.13 = (f32[3,32,256]{2,1,0:T(8,128)S(1)}, f32[3,32,256]{2,1,0:T(8,128)S(1)}, u32[]{:S(2)}, u32[]{:S(2)}) collective-permute-start(f32[3,32,256]{2,1,0:T(8,128)S(1)} %fusion.5), channel_id=1, source_target_pairs={{0,8},{8,16},{16,24},{24,0},{1,9},{9,17},{17,25},{25,1},{2,10},{10... | collective-permute-start | bytes 294920 | tf_op jit(solution)/shard_map/ppermute | solution.py:217
  66.4 11.6 %collective-permute-start.18 = (f32[3,32,256]{2,1,0:T(8,128)}, f32[3,32,256]{2,1,0:T(8,128)}, u32[]{:S(2)}, u32[]{:S(2)}) collective-permute-start(f32[3,32,256]{2,1,0:T(8,128)} %add_add_fusion.3), channel_id=1, source_target_pairs={{0,96},{32,0},{64,32},{96,64},{1,97},{33,1},{65,33},{97,65},{2,98}... | collective-permute-start | bytes 294920 | tf_op jit(solution)/shard_map/ppermute | solution.py:217
  67.0 12.6 %collective-permute-start.17 = (f32[3,32,256]{2,1,0:T(8,128)}, f32[3,32,256]{2,1,0:T(8,128)}, u32[]{:S(2)}, u32[]{:S(2)}) collective-permute-start(f32[3,32,256]{2,1,0:T(8,128)} %add_add_fusion.3), channel_id=1, source_target_pairs={{0,64},{32,96},{64,0},{96,32},{1,65},{33,97},{65,1},{97,33},{2,66}... | collective-permute-start | bytes 294920 | tf_op jit(solution)/shard_map/ppermute | solution.py:217
  77.2 5.8 %collective-permute-start.16 = (f32[3,32,256]{2,1,0:T(8,128)}, f32[3,32,256]{2,1,0:T(8,128)}, u32[]{:S(2)}, u32[]{:S(2)}) collective-permute-start(f32[3,32,256]{2,1,0:T(8,128)} %add_add_fusion.3), channel_id=1, source_target_pairs={{0,32},{32,64},{64,96},{96,0},{1,33},{33,65},{65,97},{97,1},{2,34}... | collective-permute-start | bytes 294920 | tf_op jit(solution)/shard_map/ppermute | solution.py:217
  85.6 11.3 %collective-permute-start.19 = (f32[2,32,256]{2,1,0:T(8,128)}, f32[2,32,256]{2,1,0:T(8,128)}, u32[]{:S(2)}, u32[]{:S(2)}) collective-permute-start(f32[2,32,256]{2,1,0:T(8,128)} %fusion.8), channel_id=1, source_target_pairs={{0,6},{2,0},{4,2},{6,4},{1,7},{3,1},{5,3},{7,5},{8,14},{10,8},{12,... | collective-permute-start | bytes 196616 | tf_op jit(solution)/shard_map/ppermute | solution.py:217
  87.3 24.0 %collective-permute-start.5 = (bf16[2,256,256]{2,1,0:T(8,128)(2,1)}, bf16[2,256,256]{2,1,0:T(8,128)(2,1)S(1)}, u32[]{:S(2)}, u32[]{:S(2)}) collective-permute-start(bf16[2,256,256]{2,1,0:T(8,128)(2,1)} %copy-done.7), channel_id=1, source_target_pairs={{0,9},{1,10},{2,11},{3,12},{4,13},{5,14},{6,15},{8,17},{9,18},{10,... | collective-permute-start | bytes 786440 | tf_op jit(solution)/shard_map/ppermute | solution.py:213
  90.3 21.1 %collective-permute-start.3 = (bf16[2,256,384]{2,1,0:T(8,128)(2,1)S(1)}, bf16[2,256,384]{2,1,0:T(8,128)(2,1)S(1)}, u32[]{:S(2)}, u32[]{:S(2)}) collective-permute-start(bf16[2,256,384]{2,1,0:T(8,128)(2,1)S(1)} %get-tuple-element.21), channel_id=1, source_target_pairs={{0,8},{8,16},{16,24},{24,32},{32,40},{40,48},{48,56},{56,64},{64,7... | collective-permute-start | bytes 1179656 | tf_op jit(solution)/shard_map/ppermute | solution.py:203
  93.8 17.6 %collective-permute-start.4 = (bf16[2,512,256]{2,1,0:T(8,128)(2,1)}, bf16[2,512,256]{2,1,0:T(8,128)(2,1)S(1)}, u32[]{:S(2)}, u32[]{:S(2)}) collective-permute-start(bf16[2,512,256]{2,1,0:T(8,128)(2,1)} %copy-done.6), channel_id=1, source_target_pairs={{0,1},{1,2},{2,3},{3,4},{4,5},{5,6},{6,7},{8,9},{9,10},{10,11},{11... | collective-permute-start | bytes 1572872 | tf_op jit(solution)/shard_map/ppermute | solution.py:203
  95.7 12.3 %collective-permute-start.21 = (f32[2,32,256]{2,1,0:T(8,128)}, f32[2,32,256]{2,1,0:T(8,128)S(1)}, u32[]{:S(2)}, u32[]{:S(2)}) collective-permute-start(f32[2,32,256]{2,1,0:T(8,128)} %fusion.8), channel_id=1, source_target_pairs={{0,2},{2,4},{4,6},{6,0},{1,3},{3,5},{5,7},{7,1},{8,10},{10,12},{12... | collective-permute-start | bytes 196616 | tf_op jit(solution)/shard_map/ppermute | solution.py:217
  96.9 11.0 %collective-permute-start.20 = (f32[2,32,256]{2,1,0:T(8,128)}, f32[2,32,256]{2,1,0:T(8,128)S(1)}, u32[]{:S(2)}, u32[]{:S(2)}) collective-permute-start(f32[2,32,256]{2,1,0:T(8,128)} %fusion.8), channel_id=1, source_target_pairs={{0,4},{2,6},{4,0},{6,2},{1,5},{3,7},{5,1},{7,3},{8,12},{10,14},{12... | collective-permute-start | bytes 196616 | tf_op jit(solution)/shard_map/ppermute | solution.py:217
  110.6 0.9 copy-start.12
  111.4 8.5 %collective-permute-start.22 = (f32[2,128,256]{2,1,0:T(8,128)}, f32[2,128,256]{2,1,0:T(8,128)}, u32[]{:S(2)}, u32[]{:S(2)}) collective-permute-start(f32[2,128,256]{2,1,0:T(8,128)} %constant_dynamic-slice_fusion.1), channel_id=1, source_target_pairs={{0,1},{1,0},{2,3},{3,2},{4,5},{5,4},{6,7},{7,6},{8,9},{9,8},{10,11... | collective-permute-start | bytes 786440 | tf_op jit(solution)/shard_map/ppermute | solution.py:221
  113.6 1.1 copy-start.1
  114.8 18.0 %copy-start.9 = (bf16[512,512]{1,0:T(8,128)(2,1)S(1)}, bf16[512,512]{1,0:T(8,128)(2,1)}, u32[]{:S(2)}) copy-start(bf16[512,512]{1,0:T(8,128)(2,1)} %constant.30.clone.table_b) | copy-start | bytes 1572868
  114.8 18.0 %copy-start.11 = (bf16[512,512]{1,0:T(8,128)(2,1)S(1)}, bf16[512,512]{1,0:T(8,128)(2,1)}, u32[]{:S(2)}) copy-start(bf16[512,512]{1,0:T(8,128)(2,1)} %constant.29.clone.table_a) | copy-start | bytes 1572868
  114.8 18.0 %collective-permute-start.7 = (bf16[2,512,256]{2,1,0:T(8,128)(2,1)}, bf16[2,512,256]{2,1,0:T(8,128)(2,1)S(1)}, u32[]{:S(2)}, u32[]{:S(2)}) collective-permute-start(bf16[2,512,256]{2,1,0:T(8,128)(2,1)} %get-tuple-element.27), channel_id=1, source_target_pairs={{1,0},{2,1},{3,2},{4,3},{5,4},{6,5},{7,6},{9,8},{10,9},{11,10},{12... | collective-permute-start | bytes 1572872 | tf_op jit(solution)/shard_map/ppermute | solution.py:203
  117.2 15.5 %collective-permute-start.6 = (bf16[2,256,384]{2,1,0:T(8,128)(2,1)S(1)}, bf16[2,256,384]{2,1,0:T(8,128)(2,1)S(1)}, u32[]{:S(2)}, u32[]{:S(2)}) collective-permute-start(bf16[2,256,384]{2,1,0:T(8,128)(2,1)S(1)} %get-tuple-element.26), channel_id=1, source_target_pairs={{8,0},{16,8},{24,16},{32,24},{40,32},{48,40},{56,48},{64,56},{72,6... | collective-permute-start | bytes 1179656 | tf_op jit(solution)/shard_map/ppermute | solution.py:203
  118.6 10.5 %collective-permute-start.8 = (bf16[2,256,256]{2,1,0:T(8,128)(2,1)S(1)}, bf16[2,256,256]{2,1,0:T(8,128)(2,1)S(1)}, u32[]{:S(2)}, u32[]{:S(2)}) collective-permute-start(bf16[2,256,256]{2,1,0:T(8,128)(2,1)S(1)} %slice.70), channel_id=1, source_target_pairs={{9,0},{10,1},{11,2},{12,3},{13,4},{14,5},{15,6},{17,8},{18,9},{19,... | collective-permute-start | bytes 786440 | tf_op jit(solution)/shard_map/ppermute | solution.py:213
  139.2 14.2 %collective-permute-start.26 = (f32[4,3,32,256]{3,2,1,0:T(8,128)S(1)}, f32[4,3,32,256]{3,2,1,0:T(8,128)S(1)}, u32[]{:S(2)}, u32[]{:S(2)}) collective-permute-start(f32[4,3,32,256]{3,2,1,0:T(8,128)S(1)} %get-tuple-element.37), channel_id=1, source_target_pairs={{0,1},{1,0},{2,3},{3,2},{4,5},{5,4},{6,7},{7,6},{8,9},{9,8},{10,11... | collective-permute-start | bytes 1179656 | tf_op jit(solution)/shard_map/ppermute | solution.py:221
  153.5 5.3 %collective-permute-start.27 = (f32[3,32,256]{2,1,0:T(8,128)S(1)}, f32[3,32,256]{2,1,0:T(8,128)S(1)}, u32[]{:S(2)}, u32[]{:S(2)}) collective-permute-start(f32[3,32,256]{2,1,0:T(8,128)S(1)} %get-tuple-element.42), channel_id=1, source_target_pairs={{0,2},{2,4},{4,6},{6,0},{1,3},{3,5},{5,7},{7,1},{8,10},{10,12},{12... | collective-permute-start | bytes 294920 | tf_op jit(solution)/shard_map/ppermute | solution.py:217
  153.6 6.5 %collective-permute-start.29 = (f32[3,32,256]{2,1,0:T(8,128)S(1)}, f32[3,32,256]{2,1,0:T(8,128)S(1)}, u32[]{:S(2)}, u32[]{:S(2)}) collective-permute-start(f32[3,32,256]{2,1,0:T(8,128)S(1)} %get-tuple-element.43), channel_id=1, source_target_pairs={{0,6},{2,0},{4,2},{6,4},{1,7},{3,1},{5,3},{7,5},{8,14},{10,8},{12,... | collective-permute-start | bytes 294920 | tf_op jit(solution)/shard_map/ppermute | solution.py:217
  156.3 5.0 %collective-permute-start.28 = (f32[3,32,256]{2,1,0:T(8,128)S(1)}, f32[3,32,256]{2,1,0:T(8,128)S(1)}, u32[]{:S(2)}, u32[]{:S(2)}) collective-permute-start(f32[3,32,256]{2,1,0:T(8,128)S(1)} %get-tuple-element.44), channel_id=1, source_target_pairs={{0,4},{2,6},{4,0},{6,2},{1,5},{3,7},{5,1},{7,3},{8,12},{10,14},{12... | collective-permute-start | bytes 294920 | tf_op jit(solution)/shard_map/ppermute | solution.py:217
  161.3 52.7 %copy-start.2 = (f32[2,512,384]{2,1,0:T(8,128)S(1)}, f32[2,512,384]{2,1,0:T(8,128)}, u32[]{:S(2)}) copy-start(f32[2,512,384]{2,1,0:T(8,128)} %copy-done.1) | copy-start | bytes 4718596
  161.3 52.7 %copy-start.4 = (f32[2,512,384]{2,1,0:T(8,128)S(1)}, f32[2,512,384]{2,1,0:T(8,128)}, u32[]{:S(2)}) copy-start(f32[2,512,384]{2,1,0:T(8,128)} %get-tuple-element.30.own) | copy-start | bytes 4718596
  161.3 14.8 %collective-permute-start.32 = (f32[3,32,256]{2,1,0:T(8,128)S(1)}, f32[3,32,256]{2,1,0:T(8,128)S(1)}, u32[]{:S(2)}, u32[]{:S(2)}) collective-permute-start(f32[3,32,256]{2,1,0:T(8,128)S(1)} %fusion.2), channel_id=1, source_target_pairs={{0,24},{8,0},{16,8},{24,16},{1,25},{9,1},{17,9},{25,17},{2,26},{10... | collective-permute-start | bytes 294920 | tf_op jit(solution)/shard_map/ppermute | solution.py:217
  161.4 16.0 %collective-permute-start.31 = (f32[3,32,256]{2,1,0:T(8,128)S(1)}, f32[3,32,256]{2,1,0:T(8,128)S(1)}, u32[]{:S(2)}, u32[]{:S(2)}) collective-permute-start(f32[3,32,256]{2,1,0:T(8,128)S(1)} %fusion.2), channel_id=1, source_target_pairs={{0,16},{8,24},{16,0},{24,8},{1,17},{9,25},{17,1},{25,9},{2,18},{10... | collective-permute-start | bytes 294920 | tf_op jit(solution)/shard_map/ppermute | solution.py:217
  175.4 5.5 %collective-permute-start.30 = (f32[3,32,256]{2,1,0:T(8,128)S(1)}, f32[3,32,256]{2,1,0:T(8,128)S(1)}, u32[]{:S(2)}, u32[]{:S(2)}) collective-permute-start(f32[3,32,256]{2,1,0:T(8,128)S(1)} %fusion.2), channel_id=1, source_target_pairs={{0,8},{8,16},{16,24},{24,0},{1,9},{9,17},{17,25},{25,1},{2,10},{10... | collective-permute-start | bytes 294920 | tf_op jit(solution)/shard_map/ppermute | solution.py:217
  180.9 4.8 %collective-permute-start.35 = (f32[3,32,256]{2,1,0:T(8,128)S(1)}, f32[3,32,256]{2,1,0:T(8,128)S(1)}, u32[]{:S(2)}, u32[]{:S(2)}) collective-permute-start(f32[3,32,256]{2,1,0:T(8,128)S(1)} %add_add_fusion.1), channel_id=1, source_target_pairs={{0,96},{32,0},{64,32},{96,64},{1,97},{33,1},{65,33},{97,65},{2,98}... | collective-permute-start | bytes 294920 | tf_op jit(solution)/shard_map/ppermute | solution.py:217
  180.9 6.5 %collective-permute-start.34 = (f32[3,32,256]{2,1,0:T(8,128)S(1)}, f32[3,32,256]{2,1,0:T(8,128)S(1)}, u32[]{:S(2)}, u32[]{:S(2)}) collective-permute-start(f32[3,32,256]{2,1,0:T(8,128)S(1)} %add_add_fusion.1), channel_id=1, source_target_pairs={{0,64},{32,96},{64,0},{96,32},{1,65},{33,97},{65,1},{97,33},{2,66}... | collective-permute-start | bytes 294920 | tf_op jit(solution)/shard_map/ppermute | solution.py:217
  185.4 4.7 %collective-permute-start.33 = (f32[3,32,256]{2,1,0:T(8,128)S(1)}, f32[3,32,256]{2,1,0:T(8,128)S(1)}, u32[]{:S(2)}, u32[]{:S(2)}) collective-permute-start(f32[3,32,256]{2,1,0:T(8,128)S(1)} %add_add_fusion.1), channel_id=1, source_target_pairs={{0,32},{32,64},{64,96},{96,0},{1,33},{33,65},{65,97},{97,1},{2,34}... | collective-permute-start | bytes 294920 | tf_op jit(solution)/shard_map/ppermute | solution.py:217
  190.2 12.9 %collective-permute-start.36 = (f32[2,32,256]{2,1,0:T(8,128)S(1)}, f32[2,32,256]{2,1,0:T(8,128)S(1)}, u32[]{:S(2)}, u32[]{:S(2)}) collective-permute-start(f32[2,32,256]{2,1,0:T(8,128)S(1)} %fusion.7), channel_id=1, source_target_pairs={{0,6},{2,0},{4,2},{6,4},{1,7},{3,1},{5,3},{7,5},{8,14},{10,8},{12,... | collective-permute-start | bytes 196616 | tf_op jit(solution)/shard_map/ppermute | solution.py:217
  194.6 19.3 %collective-permute-start.25 = (bf16[2,256,256]{2,1,0:T(8,128)(2,1)S(1)}, bf16[2,256,256]{2,1,0:T(8,128)(2,1)S(1)}, u32[]{:S(2)}, u32[]{:S(2)}) collective-permute-start(bf16[2,256,256]{2,1,0:T(8,128)(2,1)S(1)} %get-tuple-element.33), channel_id=1, source_target_pairs={{0,9},{1,10},{2,11},{3,12},{4,13},{5,14},{6,15},{8,17},{9,18},{10,... | collective-permute-start | bytes 786440 | tf_op jit(solution)/shard_map/ppermute | solution.py:213
  197.1 16.8 %collective-permute-start.23 = (bf16[2,256,384]{2,1,0:T(8,128)(2,1)S(1)}, bf16[2,256,384]{2,1,0:T(8,128)(2,1)S(1)}, u32[]{:S(2)}, u32[]{:S(2)}) collective-permute-start(bf16[2,256,384]{2,1,0:T(8,128)(2,1)S(1)} %get-tuple-element.31), channel_id=1, source_target_pairs={{0,8},{8,16},{16,24},{24,32},{32,40},{40,48},{48,56},{56,64},{64,7... | collective-permute-start | bytes 1179656 | tf_op jit(solution)/shard_map/ppermute | solution.py:203
  201.1 12.8 %collective-permute-start.24 = (bf16[2,512,256]{2,1,0:T(8,128)(2,1)S(1)}, bf16[2,512,256]{2,1,0:T(8,128)(2,1)S(1)}, u32[]{:S(2)}, u32[]{:S(2)}) collective-permute-start(bf16[2,512,256]{2,1,0:T(8,128)(2,1)S(1)} %get-tuple-element.32), channel_id=1, source_target_pairs={{0,1},{1,2},{2,3},{3,4},{4,5},{5,6},{6,7},{8,9},{9,10},{10,11},{11... | collective-permute-start | bytes 1572872 | tf_op jit(solution)/shard_map/ppermute | solution.py:203
  203.0 10.6 %collective-permute-start.38 = (f32[2,32,256]{2,1,0:T(8,128)S(1)}, f32[2,32,256]{2,1,0:T(8,128)S(1)}, u32[]{:S(2)}, u32[]{:S(2)}) collective-permute-start(f32[2,32,256]{2,1,0:T(8,128)S(1)} %fusion.7), channel_id=1, source_target_pairs={{0,2},{2,4},{4,6},{6,0},{1,3},{3,5},{5,7},{7,1},{8,10},{10,12},{12... | collective-permute-start | bytes 196616 | tf_op jit(solution)/shard_map/ppermute | solution.py:217
  203.1 10.5 %collective-permute-start.37 = (f32[2,32,256]{2,1,0:T(8,128)S(1)}, f32[2,32,256]{2,1,0:T(8,128)S(1)}, u32[]{:S(2)}, u32[]{:S(2)}) collective-permute-start(f32[2,32,256]{2,1,0:T(8,128)S(1)} %fusion.7), channel_id=1, source_target_pairs={{0,4},{2,6},{4,0},{6,2},{1,5},{3,7},{5,1},{7,3},{8,12},{10,14},{12... | collective-permute-start | bytes 196616 | tf_op jit(solution)/shard_map/ppermute | solution.py:217
  213.8 2.6 %collective-permute-start.39 = (f32[2,128,256]{2,1,0:T(8,128)S(1)}, f32[2,128,256]{2,1,0:T(8,128)S(1)}, u32[]{:S(2)}, u32[]{:S(2)}) collective-permute-start(f32[2,128,256]{2,1,0:T(8,128)S(1)} %constant_dynamic-slice_fusion), channel_id=1, source_target_pairs={{0,1},{1,0},{2,3},{3,2},{4,5},{5,4},{6,7},{7,6},{8,9},{9,8},{10,11... | collective-permute-start | bytes 786440 | tf_op jit(solution)/shard_map/ppermute | solution.py:221

commit v2 on v1

v2 whole, which is shorter than its diff:
```python
import functools

import jax
import jax.numpy as jnp
import ml_dtypes
import numpy as np
from jax import lax
from jax.experimental import pallas as pl
from jax.experimental.pallas import tpu as pltpu
from jax.sharding import Mesh, PartitionSpec as P

ITERS = 2
FLOOR = 0.3
ALPHA = 0.5
LANES = 128
CHUNK = 32
GROUPS = (4, 2, 1)
N_X, N_Z, N_Y, N_CORE = 4, 4, 4, 2
N_ROW, N_COL = N_X * N_Z, N_Y * N_CORE
ROW, COL = ("x", "z"), ("y", "core")
BF, F32 = jnp.bfloat16, jnp.float32


def chirp_blocks(size):
    offset = np.arange(size, dtype=np.int64)
    units = (offset[:, None] - offset[None, :]) ** 2 % (2 * size)
    phase = np.float32(np.pi) * units.astype(np.float32) / np.float32(size)
    scale = np.float32(1.0 / np.sqrt(size))
    real = (np.cos(phase) * scale).astype(ml_dtypes.bfloat16)
    imag = (np.sin(phase) * scale).astype(ml_dtypes.bfloat16)
    forward = np.block([[real, -imag], [imag, real]])
    return forward, np.ascontiguousarray(forward.T)


def frames_kernel(
    iteration, n_pieces,
    place, counts, pos, obj, below_left, below_right, right, corner, *rest,
):
    pieces, (amps, table_a, table_b), rest = rest[:n_pieces], rest[n_pieces : n_pieces + 3], rest[n_pieces + 3 :]
    own_out, low_left, low_right, right_out, corner_out, keep_out, send_out, step_out = rest[:8]
    ext, acc, sums, wave, mis, patch, levels, arrived, *probe_scratch = rest[8:]
    count = counts[0]

    def fetch(index):
        return pltpu.make_async_copy(amps.at[iteration, index], levels.at[index], arrived.at[index])

    def begin(index, carry):
        fetch(index).start()
        return carry

    lax.fori_loop(0, count, begin, 0)
    rows, cols = obj.shape[1], obj.shape[2]
    size = corner.shape[1]
    core, y = place[0], place[1]
    half, quarter = size // N_CORE, size // (N_CORE * N_Y)
    if n_pieces == 1:
        (probe,) = pieces
    else:
        (probe,) = probe_scratch
        for piece, side in ((pieces[0], core), (pieces[1], 1 - core)):
            for j in range(N_Y):
                at = pl.multiple_of(side * half + lax.rem(y - j + N_Y, N_Y) * quarter, quarter)
                probe[:, pl.ds(at, quarter), :] = piece[j]
    row_chunks = size // CHUNK
    inner_tiles, all_tiles, left_tiles = cols // LANES, (cols + size) // LANES, size // LANES
    for j in range(all_tiles):
        inside = j < inner_tiles
        at = (j if inside else j - inner_tiles) * LANES
        upper = obj if inside else right
        ext[:, j, :rows, :] = upper[:, :, at : at + LANES].astype(BF).astype(F32)
        lower = (below_left if j < left_tiles else below_right) if inside else corner
        at = at if j < left_tiles or not inside else at - size
        ext[:, j, rows:, :] = lower[:, :, at : at + LANES].astype(F32)
    acc[...] = jnp.zeros_like(acc)
    sums[...] = jnp.zeros_like(sums)
    peak = jnp.max(probe[0] * probe[0] + probe[1] * probe[1])
    step_out[0, 0] = ALPHA / (peak + 1e-6)
    lane = lax.broadcasted_iota(jnp.int32, (CHUNK, LANES), 1)

    def frames(indices):
        work = []
        for slot, index in enumerate(indices):
            top, left = pos[0, index], pos[1, index]
            base = left // LANES
            shift = left - base * LANES
            back_shift = lax.rem(LANES - shift, LANES)
            whole = lane < LANES - shift
            for k in range(row_chunks):
                span = slice(k * CHUNK, (k + 1) * CHUNK)
                parts = []
                for c in range(2):
                    tiles = [
                        pltpu.roll(ext[c, base + j, pl.ds(top + k * CHUNK, CHUNK), :], back_shift, 1)
                        for j in range(3)
                    ]
                    cut = jnp.concatenate(
                        [jnp.where(whole, tiles[0], tiles[1]), jnp.where(whole, tiles[1], tiles[2])], axis=1
                    )
                    patch[slot, c, span, :] = cut
                    parts.append(cut)
                re, im = parts
                pr, pi = probe[0, span, :], probe[1, span, :]
                wave[slot, span, :] = (pr * re - pi * im).astype(BF)
                wave[slot, size + k * CHUNK : size + (k + 1) * CHUNK, :] = (pr * im + pi * re).astype(BF)
                sums[2, span, :] += re * re + im * im
            work.append((index, top, base, shift))
        for slot, (index, top, base, shift) in enumerate(work):
            near = jnp.dot(table_a[...], wave[slot], preferred_element_type=F32).astype(BF)
            near = jnp.concatenate([near[:size], near[size:]], axis=1)
            far = jnp.dot(near, table_b[...], preferred_element_type=F32)
            fr, fi = far[:, :size], far[:, size:]
            scale = lax.rsqrt(jnp.maximum(fr * fr + fi * fi, FLOOR * FLOOR))
            fetch(index).wait()
            factor = 1.0 - levels[index].astype(F32) * scale
            mis[slot, :size, :] = (fr * factor).astype(BF)
            mis[slot, size:, :] = (fi * factor).astype(BF)
        updates = []
        for slot, _ in enumerate(work):
            back = jnp.dot(table_b[...], mis[slot], preferred_element_type=F32).astype(BF)
            back = jnp.concatenate([back[:size], back[size:]], axis=1)
            updates.append(jnp.dot(back, table_a[...], preferred_element_type=F32))
        for slot, (index, top, base, shift) in enumerate(work):
            update = updates[slot]
            fresh = lane >= shift
            for k in range(row_chunks):
                span = slice(k * CHUNK, (k + 1) * CHUNK)
                ur, ui = update[span, :size], update[span, size:]
                pr, pi = probe[0, span, :], probe[1, span, :]
                re, im = patch[slot, 0, span, :], patch[slot, 1, span, :]
                sums[0, span, :] += re * ur + im * ui
                sums[1, span, :] += re * ui - im * ur
                grads = (pr * ur + pi * ui, pr * ui - pi * ur)
                for c in range(2):
                    grad = grads[c].astype(BF).astype(F32)
                    first = pltpu.roll(grad[:, :LANES], shift, 1)
                    second = pltpu.roll(grad[:, LANES:], shift, 1)
                    pieces = (
                        jnp.where(fresh, first, 0.0),
                        jnp.where(fresh, second, first),
                        jnp.where(fresh, 0.0, second),
                    )
                    for j, piece in enumerate(pieces):
                        acc[c, base + j, pl.ds(top + k * CHUNK, CHUNK), :] += piece

    done = 0
    for group in GROUPS:
        times = (count - done) // group

        def several(index, carry, first=done, group=group):
            frames([first + index * group + i for i in range(group)])
            return carry

        lax.fori_loop(0, times, several, 0)
        done = done + times * group
    for j in range(all_tiles):
        inside = j < inner_tiles
        at = (j if inside else j - inner_tiles) * LANES
        upper = own_out if inside else right_out
        upper[:, :, at : at + LANES] = acc[:, j, :rows, :].astype(upper.dtype)
        lower = (low_left if j < left_tiles else low_right) if inside else corner_out
        at = at if j < left_tiles or not inside else at - size
        lower[:, :, at : at + LANES] = acc[:, j, rows:, :].astype(lower.dtype)
    for j in range(N_Y):
        inner = lax.rem(y + j, N_Y) * quarter
        keep_at = pl.multiple_of(core * half + inner, quarter)
        send_at = pl.multiple_of((1 - core) * half + inner, quarter)
        keep_out[j] = sums[:, pl.ds(keep_at, quarter), :]
        send_out[j] = sums[:, pl.ds(send_at, quarter), :]


def run_frames(place, counts, pos, obj, halos, pieces, amps, tables, iteration):
    rows, cols = obj.shape[1], obj.shape[2]
    slots, size = amps.shape[1], amps.shape[2]
    vmem = pl.BlockSpec(memory_space=pltpu.VMEM)
    smem = pl.BlockSpec(memory_space=pltpu.SMEM)
    quarter = size // (N_CORE * N_Y)
    shapes = [
        jax.ShapeDtypeStruct((2, rows, cols), F32),
        jax.ShapeDtypeStruct((2, size, size), F32),
        jax.ShapeDtypeStruct((2, size, cols - size), BF),
        jax.ShapeDtypeStruct((2, rows, size), BF),
        jax.ShapeDtypeStruct((2, size, size), BF),
        jax.ShapeDtypeStruct((N_Y, 3, quarter, size), F32),
        jax.ShapeDtypeStruct((N_Y, 3, quarter, size), F32),
        jax.ShapeDtypeStruct((1, 1), F32),
    ]
    scratch = [
        pltpu.VMEM((2, (cols + size) // LANES, rows + size, LANES), F32),
        pltpu.VMEM((2, (cols + size) // LANES, rows + size, LANES), F32),
        pltpu.VMEM((3, size, size), F32),
        pltpu.VMEM((GROUPS[0], 2 * size, size), BF),
        pltpu.VMEM((GROUPS[0], 2 * size, size), BF),
        pltpu.VMEM((GROUPS[0], 2, size, size), F32),
        pltpu.VMEM((slots, size, size), BF),
        pltpu.SemaphoreType.DMA((slots,)),
    ]
    if len(pieces) > 1:
        scratch.append(pltpu.VMEM((2, size, size), F32))
    return pl.pallas_call(
        functools.partial(frames_kernel, iteration, len(pieces)),
        out_shape=shapes,
        in_specs=[smem] * 3 + [vmem] * (5 + len(pieces)) + [pl.BlockSpec(memory_space=pl.ANY)] + [vmem] * 2,
        out_specs=[vmem] * 7 + [smem],
        scratch_shapes=scratch,
        compiler_params=pltpu.CompilerParams(vmem_limit_bytes=26 << 20),
        cost_estimate=pl.CostEstimate(flops=6_000_000_000, bytes_accessed=8_000_000, transcendentals=0),
        name="frames",
    )(place, counts, pos, obj, *halos, *pieces, amps, *tables)


def update_kernel(with_sum, obj, own, left, low_left, low_right, step, *rest):
    if with_sum:
        totals, (obj_out, halo_left, halo_right, right_out, total_out) = rest[:4], rest[4:]
        total_out[...] = totals[0][...] + totals[1][...] + totals[2][...] + totals[3][...]
    else:
        (obj_out,) = rest
    size = left.shape[2]
    alpha = step[0, 0]
    obj_out[:, :, :size] = obj[:, :, :size] - alpha * (own[:, :, :size] + left[...].astype(F32))
    obj_out[:, size:, size:] = obj[:, size:, size:] - alpha * own[:, size:, size:]
    obj_out[:, :size, :size] -= alpha * low_left[...].astype(F32)
    obj_out[:, :size, size:] = obj[:, :size, size:] - alpha * (own[:, :size, size:] + low_right[...].astype(F32))
    if with_sum:
        halo_left[...] = obj_out[:, :size, :size].astype(BF)
        halo_right[...] = obj_out[:, :size, size:].astype(BF)
        right_out[...] = obj_out[:, :, :size].astype(BF)


def run_update(obj, own, left, low_left, low_right, step, totals):
    rows, cols = obj.shape[1], obj.shape[2]
    size = left.shape[2]
    vmem = pl.BlockSpec(memory_space=pltpu.VMEM)
    smem = pl.BlockSpec(memory_space=pltpu.SMEM)
    shapes = [jax.ShapeDtypeStruct((2, rows, cols), F32)]
    if totals:
        shapes += [
            jax.ShapeDtypeStruct((2, size, size), BF),
            jax.ShapeDtypeStruct((2, size, cols - size), BF),
            jax.ShapeDtypeStruct((2, rows, size), BF),
            jax.ShapeDtypeStruct(totals[0].shape, F32),
        ]
    return pl.pallas_call(
        functools.partial(update_kernel, bool(totals)),
        out_shape=shapes,
        in_specs=[vmem] * 5 + [smem] + [vmem] * len(totals),
        out_specs=[vmem] * len(shapes),
        compiler_params=pltpu.CompilerParams(vmem_limit_bytes=16 << 20),
        cost_estimate=pl.CostEstimate(flops=2_000_000, bytes_accessed=8_000_000, transcendentals=0),
        name="object_update",
    )(obj, own, left, low_left, low_right, step, *totals)


def probe_kernel(place, mine, other, out):
    core, y = place[0], place[1]
    size = out.shape[1]
    half, quarter = size // N_CORE, size // (N_CORE * N_Y)
    for piece, side in ((mine, core), (other, 1 - core)):
        for j in range(N_Y):
            at = pl.multiple_of(side * half + lax.rem(y - j + N_Y, N_Y) * quarter, quarter)
            out[:, pl.ds(at, quarter), :] = piece[j]


def run_probe(place, mine, other):
    vmem = pl.BlockSpec(memory_space=pltpu.VMEM)
    size = mine.shape[-1]
    return pl.pallas_call(
        probe_kernel,
        out_shape=jax.ShapeDtypeStruct((2, size, size), F32),
        in_specs=[pl.BlockSpec(memory_space=pltpu.SMEM), vmem, vmem],
        out_specs=vmem,
        name="probe_whole",
    )(place, mine, other)


def moved(value, axis, count, steps):
    first, last = max(0, -steps), min(count, count - steps)
    return lax.ppermute(value, axis, [(s, s + steps) for s in range(first, last)])


def turned(value, axis, steps):
    return lax.ppermute(value, axis, [(s, (s + steps) % 4) for s in range(4)])


def swapped(value):
    return lax.ppermute(value, "core", [(0, 1), (1, 0)])


def halo(low_left, low_right, right):
    first = moved(low_left, ROW, N_ROW, -1)
    beside = moved(right, COL, N_COL, -1)
    second = moved(low_right, ROW, N_ROW, -1)
    corner = moved(first, COL, N_COL, -1)
    return (first, second, beside, corner)


def rims(low_left, low_right, right, corner):
    corner = moved(corner, COL, N_COL, 1)
    left = moved(right, COL, N_COL, 1)
    second = moved(low_right, ROW, N_ROW, 1)
    first = moved((low_left + corner.astype(F32)).astype(BF), ROW, N_ROW, 1)
    return (left, first, second)


def around(value, axis):
    return [value] + [turned(value, axis, j) for j in (1, 2, 3)]


def column_sum(keep, send):
    part = keep + swapped(send)
    return part[0] + turned(part[1], "y", 1) + turned(part[2], "y", 2) + turned(part[3], "y", 3)


def gathered(mine, total):
    fresh = mine - total[:2] / (total[2] + 1.0)
    half = jnp.stack(around(fresh, "y"))
    return (half, swapped(half))


def local(tables, obj, probe, amps, positions, counts):
    size = probe.shape[-1]
    half, quarter = size // N_CORE, size // (N_CORE * N_Y)
    core, y = lax.axis_index("core"), lax.axis_index("y")
    place = jnp.stack([core, y]).astype(jnp.int32)
    mine = lax.dynamic_slice(probe, (0, core * half + y * quarter, 0), (2, quarter, size))
    low_left, low_right = obj[:, :size, :size].astype(BF), obj[:, :size, size:].astype(BF)
    right = obj[:, :, :size].astype(BF)
    pieces = (probe,)
    for iteration in range(ITERS):
        halos = halo(low_left, low_right, right)
        own, low_left, low_right, right, corner, keep, send, step = run_frames(
            place, counts[iteration, 0], positions[iteration], obj, halos, pieces, amps, tables, iteration
        )
        left, above_left, above_right = rims(low_left, low_right, right, corner)
        totals = around(column_sum(keep, send), "z")
        if iteration < ITERS - 1:
            obj, low_left, low_right, right, total = run_update(
                obj, own, left, above_left, above_right, step, totals
            )
        else:
            (obj,) = run_update(obj, own, left, above_left, above_right, step, [])
            total = sum(totals[1:], totals[0])
        total = sum(around(total, "x")[1:], total)
        pieces = gathered(mine, total)
        mine = pieces[0][0]
    return (obj, run_probe(place, *pieces))


def solution(mesh):
    fine = Mesh(mesh.devices.reshape(N_X, N_Z, N_Y, N_CORE), ("x", "z", "y", "core"))
    placed = (
        P(None, ROW, COL),
        P(),
        P(None, ROW + COL, None, None),
        P(None, None, ROW + COL),
        P(None, COL, ROW),
    )
    blocks = tuple(jnp.asarray(block) for block in chirp_blocks(256))
    return jax.shard_map(
        functools.partial(local, blocks),
        mesh=fine, in_specs=placed, out_specs=(P(None, ROW, COL), P()), check_vma=False,
    )
```

time: 216 us -> 198 us (0.917)
  the two profiles are of different devices: /device:TPU:1 before, /device:TPU:6 now
where the time goes in v2:
time: 198 us; the launch traced here: 197 us
  starting transfers between devices  111 us (56%)
  waiting for transfers between devices  47.7 us (24%)
  local copies, waits for them, and re-layouts  18.4 us (9%)
  Pallas kernels  16.1 us (8%)
  other arithmetic  2.96 us (1%)
    ppermute x24, starting transfers between devices, turned(): return lax.ppermute(value, axis, [(s, (s + steps) % 4) for s in range(4)])  67.7 us
    ppermute x16, starting transfers between devices, moved(): lax.ppermute(value, axis, [(s, s + steps) for s in range(first, last)])  36.4 us
    ppermute x24, waiting for transfers between devices, turned(): return lax.ppermute(value, axis, [(s, (s + steps) % 4) for s in range(4)])  23.4 us
    ppermute x16, waiting for transfers between devices, moved(): lax.ppermute(value, axis, [(s, s + steps) for s in range(first, last)])  22.7 us
    unnamed x42, local copies, waits for them, and re-layouts  16.2 us
    pallas_call x2, Pallas kernels, run_frames(): pl.pallas_call(functools.partial(frames_kernel, iteration, len(pieces)),...  10.8 us
    ppermute x4, starting transfers between devices, swapped(): return lax.ppermute(value, 'core', [(0, 1), (1, 0)])  6.69 us
  transfers between devices with their start and end apart: 44, of which 21 were waited for; matrix products, arithmetic and copies ran while one was open for 2% of the time, Pallas kernels for 1%

profile of v2, /device:TPU:6, one launch (start us, length us, event | category | flops | bytes accessed | tf_op | source)
XLA Modules:
  0.0 197.0 jit_solution(8481917898020418781)
XLA Ops:
  0.7 1.6 convert.5
  2.3 6.2 %collective-permute-start = (bf16[2,256,256]{2,1,0:T(8,128)(2,1)S(1)}, bf16[2,256,256]{2,1,0:T(8,128)(2,1)S(1)}, u32[]{:S(2)}, u32[]{:S(2)}) collective-permute-start(bf16[2,256,256]{2,1,0:T(8,128)(2,1)S(1)} %slice.79), channel_id=1, source_target_pairs={{8,0},{16,8},{24,16},{32,24},{40,32},{48,40},{56,48},{64,56},{72,6... | collective-permute-start | bytes 786440 | tf_op jit(solution)/shard_map/ppermute | solution.py:277
  9.3 1.3 collective-permute-start.2
  11.3 2.3 %collective-permute-start.1 = (bf16[2,256,128]{2,1,0:T(8,128)(2,1)}, bf16[2,256,128]{2,1,0:T(8,128)(2,1)S(1)}, u32[]{:S(2)}, u32[]{:S(2)}) collective-permute-start(bf16[2,256,128]{2,1,0:T(8,128)(2,1)} %slice.80), channel_id=1, source_target_pairs={{8,0},{16,8},{24,16},{32,24},{40,32},{48,40},{56,48},{64,56},{72,6... | collective-permute-start | bytes 393224 | tf_op jit(solution)/shard_map/ppermute | solution.py:277
  14.1 1.3 collective-permute-start.3
  16.1 3.5 %collective-permute-done.1.below_right = bf16[2,256,128]{2,1,0:T(8,128)(2,1)S(1)} collective-permute-done((bf16[2,256,128]{2,1,0:T(8,128)(2,1)}, bf16[2,256,128]{2,1,0:T(8,128)(2,1)S(1)}, u32[]{:S(2)}, u32[]{:S(2)}) %collective-permute-start.1) | collective-permute-done | bytes 131104 | tf_op jit(solution)/shard_map/ppermute | solution.py:277
  21.8 1.0 copy-done.1
  22.8 1.9 copy-done.3
  24.7 1.0 copy-done.7
  25.7 0.9 copy-done.9
  26.7 0.9 copy-done.12
  27.6 1.0 copy-done.13
  28.6 1.0 copy-done.15
  29.7 5.9 %frames.2 = (f32[2,512,384]{2,1,0:T(8,128)S(1)}, f32[2,256,256]{2,1,0:T(8,128)S(1)}, bf16[2,256,128]{2,1,0:T(8,128)(2,1)S(1)}, bf16[2,512,256]{2,1,0:T(8,128)(2,...) custom-call(s32[2]{0:T(128)S(1)} %pad_add_fusion.place, ...), custom_call_target="tpu_custom_call" | custom-call | flops 6000000000 | bytes 8000000 | tf_op jit(solution)/shard_map/frames/pallas_call | solution.py:199
  35.6 2.6 %collective-permute-start.8 = (f32[4,3,32,256]{3,2,1,0:T(8,128)S(1)}, f32[4,3,32,256]{3,2,1,0:T(8,128)S(1)}, u32[]{:S(2)}, u32[]{:S(2)}) collective-permute-start(f32[4,3,32,256]{3,2,1,0:T(8,128)S(1)} %get-tuple-element.30), channel_id=1, source_target_pairs={{0,1},{1,0},{2,3},{3,2},{4,5},{5,4},{6,7},{7,6},{8,9},{9,8},{10,11... | collective-permute-start | bytes 1179656 | tf_op jit(solution)/shard_map/ppermute | solution.py:285
  38.2 1.9 collective-permute-start.5
  40.1 4.9 %collective-permute-start.7 = (bf16[2,256,128]{2,1,0:T(8,128)(2,1)S(1)}, bf16[2,256,128]{2,1,0:T(8,128)(2,1)S(1)}, u32[]{:S(2)}, u32[]{:S(2)}) collective-permute-start(bf16[2,256,128]{2,1,0:T(8,128)(2,1)S(1)} %get-tuple-element.27), channel_id=1, source_target_pairs={{0,8},{8,16},{16,24},{24,32},{32,40},{40,48},{48,56},{56,64},{64,7... | collective-permute-start | bytes 393224 | tf_op jit(solution)/shard_map/ppermute | solution.py:277
  45.0 1.7 collective-permute-start.4
  46.8 16.0 %collective-permute-start.9 = (f32[3,32,256]{2,1,0:T(8,128)S(1)}, f32[3,32,256]{2,1,0:T(8,128)S(1)}, u32[]{:S(2)}, u32[]{:S(2)}) collective-permute-start(f32[3,32,256]{2,1,0:T(8,128)S(1)} %get-tuple-element.47), channel_id=1, source_target_pairs={{0,2},{2,4},{4,6},{6,0},{1,3},{3,5},{5,7},{7,1},{8,10},{10,12},{12... | collective-permute-start | bytes 294920 | tf_op jit(solution)/shard_map/ppermute | solution.py:281
  62.8 2.3 %collective-permute-start.10 = (f32[3,32,256]{2,1,0:T(8,128)S(1)}, f32[3,32,256]{2,1,0:T(8,128)S(1)}, u32[]{:S(2)}, u32[]{:S(2)}) collective-permute-start(f32[3,32,256]{2,1,0:T(8,128)S(1)} %get-tuple-element.49), channel_id=1, source_target_pairs={{0,4},{2,6},{4,0},{6,2},{1,5},{3,7},{5,1},{7,3},{8,12},{10,14},{12... | collective-permute-start | bytes 294920 | tf_op jit(solution)/shard_map/ppermute | solution.py:281
  65.6 1.9 collective-permute-start.6
  67.5 1.0 collective-permute-done.11
  68.5 1.6 collective-permute-done.10
  70.4 2.3 %collective-permute-start.13 = (f32[3,32,256]{2,1,0:T(8,128)S(1)}, f32[3,32,256]{2,1,0:T(8,128)S(1)}, u32[]{:S(2)}, u32[]{:S(2)}) collective-permute-start(f32[3,32,256]{2,1,0:T(8,128)S(1)} %fusion.5.rest_0_), channel_id=1, source_target_pairs={{0,16},{8,24},{16,0},{24,8},{1,17},{9,25},{17,1},{25,9},{2,18},{10... | collective-permute-start | bytes 294920 | tf_op jit(solution)/shard_map/ppermute | solution.py:281
  72.9 5.0 %collective-permute-done.6.low_left = bf16[2,256,256]{2,1,0:T(8,128)(2,1)S(1)} collective-permute-done((bf16[2,256,256]{2,1,0:T(8,128)(2,1)S(1)}, bf16[2,256,256]{2,1,0:T(8,128)(2,1)S(1)}, u32[]{:S(2)}, u32[]{:S(2)}) %collective-permute-start.6) | collective-permute-done | bytes 262176 | tf_op jit(solution)/shard_map/ppermute | solution.py:277
  78.2 2.5 %collective-permute-done.12.rest_1_ = f32[3,32,256]{2,1,0:T(8,128)S(1)} collective-permute-done((f32[3,32,256]{2,1,0:T(8,128)S(1)}, f32[3,32,256]{2,1,0:T(8,128)S(1)}, u32[]{:S(2)}, u32[]{:S(2)}) %collective-permute-start.12) | collective-permute-done | bytes 98336 | tf_op jit(solution)/shard_map/ppermute | solution.py:281
  80.7 1.2 object_update.2
  83.7 3.4 %collective-permute-start.20 = (f32[3,32,256]{2,1,0:T(8,128)S(1)}, f32[3,32,256]{2,1,0:T(8,128)S(1)}, u32[]{:S(2)}, u32[]{:S(2)}) collective-permute-start(f32[3,32,256]{2,1,0:T(8,128)S(1)} %get-tuple-element.35), channel_id=1, source_target_pairs={{0,64},{32,96},{64,0},{96,32},{1,65},{33,97},{65,1},{97,33},{2,66}... | collective-permute-start | bytes 294920 | tf_op jit(solution)/shard_map/ppermute | solution.py:281
  87.2 2.6 %collective-permute-start.19 = (f32[3,32,256]{2,1,0:T(8,128)S(1)}, f32[3,32,256]{2,1,0:T(8,128)S(1)}, u32[]{:S(2)}, u32[]{:S(2)}) collective-permute-start(f32[3,32,256]{2,1,0:T(8,128)S(1)} %get-tuple-element.35), channel_id=1, source_target_pairs={{0,32},{32,64},{64,96},{96,0},{1,33},{33,65},{65,97},{97,1},{2,34}... | collective-permute-start | bytes 294920 | tf_op jit(solution)/shard_map/ppermute | solution.py:281
  89.8 1.9 collective-permute-start.15
  91.7 1.3 collective-permute-start.17
  93.9 3.8 %collective-permute-start.24 = (f32[2,32,256]{2,1,0:T(8,128)S(1)}, f32[2,32,256]{2,1,0:T(8,128)S(1)}, u32[]{:S(2)}, u32[]{:S(2)}) collective-permute-start(f32[2,32,256]{2,1,0:T(8,128)S(1)} %fusion.7), channel_id=1, source_target_pairs={{0,6},{2,0},{4,2},{6,4},{1,7},{3,1},{5,3},{7,5},{8,14},{10,8},{12,... | collective-permute-start | bytes 196616 | tf_op jit(solution)/shard_map/ppermute | solution.py:281
  97.7 1.9 collective-permute-start.23
  99.6 4.9 %collective-permute-done.24 = f32[2,32,256]{2,1,0:T(8,128)S(1)} collective-permute-done((f32[2,32,256]{2,1,0:T(8,128)S(1)}, f32[2,32,256]{2,1,0:T(8,128)S(1)}, u32[]{:S(2)}, u32[]{:S(2)}) %collective-permute-start.24) | collective-permute-done | bytes 65568 | tf_op jit(solution)/shard_map/ppermute | solution.py:281
  105.2 1.3 collective-permute-start.18
  106.5 2.0 %collective-permute-start.16 = (bf16[2,256,128]{2,1,0:T(8,128)(2,1)}, bf16[2,256,128]{2,1,0:T(8,128)(2,1)S(1)}, u32[]{:S(2)}, u32[]{:S(2)}) collective-permute-start(bf16[2,256,128]{2,1,0:T(8,128)(2,1)} %copy-done.10), channel_id=1, source_target_pairs={{8,0},{16,8},{24,16},{32,24},{40,32},{48,40},{56,48},{64,56},{72,6... | collective-permute-start | bytes 393224 | tf_op jit(solution)/shard_map/ppermute | solution.py:277
  108.6 6.3 %collective-permute-done.16.below_right = bf16[2,256,128]{2,1,0:T(8,128)(2,1)S(1)} collective-permute-done((bf16[2,256,128]{2,1,0:T(8,128)(2,1)}, bf16[2,256,128]{2,1,0:T(8,128)(2,1)S(1)}, u32[]{:S(2)}, u32[]{:S(2)}) %collective-permute-start.16) | collective-permute-done | bytes 131104 | tf_op jit(solution)/shard_map/ppermute | solution.py:277
  114.9 1.9 copy-done.4
  116.7 1.0 copy-done.14
  117.8 1.0 copy-done.16
  118.8 4.9 %frames.3 = (f32[2,512,384]{2,1,0:T(8,128)S(1)}, f32[2,256,256]{2,1,0:T(8,128)S(1)}, bf16[2,256,128]{2,1,0:T(8,128)(2,1)S(1)}, bf16[2,512,256]{2,1,0:T(8,128)(2,...) custom-call(s32[2]{0:T(128)S(1)} %pad_add_fusion.place, ...), custom_call_target="tpu_custom_call" | custom-call | flops 6000000000 | bytes 8000000 | tf_op jit(solution)/shard_map/frames/pallas_call | solution.py:199
  123.9 1.6 collective-permute-done.30
  125.6 10.3 %collective-permute-start.31 = (f32[3,32,256]{2,1,0:T(8,128)S(1)}, f32[3,32,256]{2,1,0:T(8,128)S(1)}, u32[]{:S(2)}, u32[]{:S(2)}) collective-permute-start(f32[3,32,256]{2,1,0:T(8,128)S(1)} %get-tuple-element.44), channel_id=1, source_target_pairs={{0,2},{2,4},{4,6},{6,0},{1,3},{3,5},{5,7},{7,1},{8,10},{10,12},{12... | collective-permute-start | bytes 294920 | tf_op jit(solution)/shard_map/ppermute | solution.py:281
  136.0 2.1 %collective-permute-start.32 = (f32[3,32,256]{2,1,0:T(8,128)S(1)}, f32[3,32,256]{2,1,0:T(8,128)S(1)}, u32[]{:S(2)}, u32[]{:S(2)}) collective-permute-start(f32[3,32,256]{2,1,0:T(8,128)S(1)} %get-tuple-element.46), channel_id=1, source_target_pairs={{0,4},{2,6},{4,0},{6,2},{1,5},{3,7},{5,1},{7,3},{8,12},{10,14},{12... | collective-permute-start | bytes 294920 | tf_op jit(solution)/shard_map/ppermute | solution.py:281
  138.5 3.0 %collective-permute-done.33 = f32[3,32,256]{2,1,0:T(8,128)S(1)} collective-permute-done((f32[3,32,256]{2,1,0:T(8,128)S(1)}, f32[3,32,256]{2,1,0:T(8,128)S(1)}, u32[]{:S(2)}, u32[]{:S(2)}) %collective-permute-start.33) | collective-permute-done | bytes 98336 | tf_op jit(solution)/shard_map/ppermute | solution.py:281
  142.1 8.1 %collective-permute-start.36 = (f32[3,32,256]{2,1,0:T(8,128)S(1)}, f32[3,32,256]{2,1,0:T(8,128)S(1)}, u32[]{:S(2)}, u32[]{:S(2)}) collective-permute-start(f32[3,32,256]{2,1,0:T(8,128)S(1)} %fusion.2), channel_id=1, source_target_pairs={{0,24},{8,0},{16,8},{24,16},{1,25},{9,1},{17,9},{25,17},{2,26},{10... | collective-permute-start | bytes 294920 | tf_op jit(solution)/shard_map/ppermute | solution.py:281
  150.2 0.9 collective-permute-start.34
  151.1 2.6 %collective-permute-done.36 = f32[3,32,256]{2,1,0:T(8,128)S(1)} collective-permute-done((f32[3,32,256]{2,1,0:T(8,128)S(1)}, f32[3,32,256]{2,1,0:T(8,128)S(1)}, u32[]{:S(2)}, u32[]{:S(2)}) %collective-permute-start.36) | collective-permute-done | bytes 98336 | tf_op jit(solution)/shard_map/ppermute | solution.py:281
  153.8 2.7 %collective-permute-done.35 = f32[3,32,256]{2,1,0:T(8,128)S(1)} collective-permute-done((f32[3,32,256]{2,1,0:T(8,128)S(1)}, f32[3,32,256]{2,1,0:T(8,128)S(1)}, u32[]{:S(2)}, u32[]{:S(2)}) %collective-permute-start.35) | collective-permute-done | bytes 98336 | tf_op jit(solution)/shard_map/ppermute | solution.py:281
  157.2 4.5 %collective-permute-start.39 = (f32[3,32,256]{2,1,0:T(8,128)S(1)}, f32[3,32,256]{2,1,0:T(8,128)S(1)}, u32[]{:S(2)}, u32[]{:S(2)}) collective-permute-start(f32[3,32,256]{2,1,0:T(8,128)S(1)} %add_add_fusion.1), channel_id=1, source_target_pairs={{0,96},{32,0},{64,32},{96,64},{1,97},{33,1},{65,33},{97,65},{2,98}... | collective-permute-start | bytes 294920 | tf_op jit(solution)/shard_map/ppermute | solution.py:281
  161.6 1.4 collective-permute-start.38
  163.0 2.5 %collective-permute-start.37 = (f32[3,32,256]{2,1,0:T(8,128)S(1)}, f32[3,32,256]{2,1,0:T(8,128)S(1)}, u32[]{:S(2)}, u32[]{:S(2)}) collective-permute-start(f32[3,32,256]{2,1,0:T(8,128)S(1)} %add_add_fusion.1), channel_id=1, source_target_pairs={{0,32},{32,64},{64,96},{96,0},{1,33},{33,65},{65,97},{97,1},{2,34}... | collective-permute-start | bytes 294920 | tf_op jit(solution)/shard_map/ppermute | solution.py:281
  165.6 1.3 collective-permute-start.27
  166.9 3.1 %collective-permute-start.26 = (bf16[2,512,256]{2,1,0:T(8,128)(2,1)S(1)}, bf16[2,512,256]{2,1,0:T(8,128)(2,1)S(1)}, u32[]{:S(2)}, u32[]{:S(2)}) collective-permute-start(bf16[2,512,256]{2,1,0:T(8,128)(2,1)S(1)} %get-tuple-element.37), channel_id=1, source_target_pairs={{0,1},{1,2},{2,3},{3,4},{4,5},{5,6},{6,7},{8,9},{9,10},{10,11},{11... | collective-permute-start | bytes 1572872 | tf_op jit(solution)/shard_map/ppermute | solution.py:277
  170.1 1.6 collective-permute-start.42
  171.7 1.6 collective-permute-start.41
  173.3 1.3 collective-permute-start.40
  174.7 2.0 %collective-permute-start.28 = (bf16[2,256,256]{2,1,0:T(8,128)(2,1)S(1)}, bf16[2,256,256]{2,1,0:T(8,128)(2,1)S(1)}, u32[]{:S(2)}, u32[]{:S(2)}) collective-permute-start(bf16[2,256,256]{2,1,0:T(8,128)(2,1)S(1)} %add_convert_fusion), channel_id=1, source_target_pairs={{0,8},{8,16},{16,24},{24,32},{32,40},{40,48},{48,56},{56,64},{64,7... | collective-permute-start | bytes 786440 | tf_op jit(solution)/shard_map/ppermute | solution.py:277
  176.8 1.4 collective-permute-done.41
  179.0 3.8 %collective-permute-start.43 = (f32[4,2,32,256]{3,2,1,0:T(8,128)S(1)}, f32[4,2,32,256]{3,2,1,0:T(8,128)S(1)}, u32[]{:S(2)}, u32[]{:S(2)}) collective-permute-start(f32[4,2,32,256]{3,2,1,0:T(8,128)S(1)} %pad_maximum_fusion.1.mine), channel_id=1, source_target_pairs={{0,1},{1,0},{2,3},{3,2},{4,5},{5,4},{6,7},{7,6},{8,9},{9,8},{10,11... | collective-permute-start | bytes 786440 | tf_op jit(solution)/shard_map/ppermute | solution.py:285
  182.7 1.9 collective-permute-start.29
  184.7 7.5 %collective-permute-done.29.low_right = bf16[2,256,128]{2,1,0:T(8,128)(2,1)S(1)} collective-permute-done((bf16[2,256,128]{2,1,0:T(8,128)(2,1)S(1)}, bf16[2,256,128]{2,1,0:T(8,128)(2,1)S(1)}, u32[]{:S(2)}, u32[]{:S(2)}) %collective-permute-start.29) | collective-permute-done | bytes 131104 | tf_op jit(solution)/shard_map/ppermute | solution.py:277
  192.2 2.3 %object_update.3 = f32[2,512,384]{2,1,0:T(8,128)} custom-call(f32[2,512,384]{2,1,0:T(8,128)S(1)} %get-tuple-element.31.obj, f32[2,512,384]{2,1,0:T(8,128)S(1)} %get-tuple-element.36.own, bf16[2,512,256]{2,1,0:T(8,128)(2,1)S(1)} %collective-permute-done.26.left, bf16[2,256,256]{2,1,0:T(8,128)(2,1)S(1)} %collective-permute-done.28.low_left, ...), custom_call_target="tpu_custom_call" | custom-call | flops 2000000 | bytes 8000000 | tf_op jit(solution)/shard_map/object_update/pallas_call | solution.py:242
  195.1 1.9 probe_whole.1
  (95 shorter events, 13.0 us)
Async XLA Ops:
  0.6 21.1 %copy-start = (f32[2,512,384]{2,1,0:T(8,128)S(1)}, f32[2,512,384]{2,1,0:T(8,128)}, u32[]{:S(2)}) copy-start(f32[2,512,384]{2,1,0:T(8,128)} %obj.3) | copy-start | bytes 4718596
  0.6 14.7 %copy-start.19 = (s32[2,2,12]{2,1,0:T(2,128)S(1)}, s32[2,2,12]{2,1,0:T(2,128)}, u32[]{:S(2)}) copy-start(s32[2,2,12]{2,1,0:T(2,128)} %param.10) | copy-start | bytes 580
  0.6 14.8 %copy-start.20 = (s32[2,1,1]{0,2,1:T(1,128)S(1)}, s32[2,1,1]{0,2,1:T(1,128)}, u32[]{:S(2)}) copy-start(s32[2,1,1]{0,2,1:T(1,128)} %param.11) | copy-start | bytes 28
  2.3 11.8 %collective-permute-start = (bf16[2,256,256]{2,1,0:T(8,128)(2,1)S(1)}, bf16[2,256,256]{2,1,0:T(8,128)(2,1)S(1)}, u32[]{:S(2)}, u32[]{:S(2)}) collective-permute-start(bf16[2,256,256]{2,1,0:T(8,128)(2,1)S(1)} %slice.79), channel_id=1, source_target_pairs={{8,0},{16,8},{24,16},{32,24},{40,32},{48,40},{56,48},{64,56},{72,6... | collective-permute-start | bytes 786440 | tf_op jit(solution)/shard_map/ppermute | solution.py:277
  9.3 11.6 %collective-permute-start.2 = (bf16[2,512,256]{2,1,0:T(8,128)(2,1)}, bf16[2,512,256]{2,1,0:T(8,128)(2,1)S(1)}, u32[]{:S(2)}, u32[]{:S(2)}) collective-permute-start(bf16[2,512,256]{2,1,0:T(8,128)(2,1)} %slice.81), channel_id=1, source_target_pairs={{1,0},{2,1},{3,2},{4,3},{5,4},{6,5},{7,6},{9,8},{10,9},{11,10},{12... | collective-permute-start | bytes 1572872 | tf_op jit(solution)/shard_map/ppermute | solution.py:277
  11.3 8.3 %collective-permute-start.1 = (bf16[2,256,128]{2,1,0:T(8,128)(2,1)}, bf16[2,256,128]{2,1,0:T(8,128)(2,1)S(1)}, u32[]{:S(2)}, u32[]{:S(2)}) collective-permute-start(bf16[2,256,128]{2,1,0:T(8,128)(2,1)} %slice.80), channel_id=1, source_target_pairs={{8,0},{16,8},{24,16},{32,24},{40,32},{48,40},{56,48},{64,56},{72,6... | collective-permute-start | bytes 393224 | tf_op jit(solution)/shard_map/ppermute | solution.py:277
  14.1 6.2 %collective-permute-start.3 = (bf16[2,256,256]{2,1,0:T(8,128)(2,1)S(1)}, bf16[2,256,256]{2,1,0:T(8,128)(2,1)S(1)}, u32[]{:S(2)}, u32[]{:S(2)}) collective-permute-start(bf16[2,256,256]{2,1,0:T(8,128)(2,1)S(1)} %collective-permute-done.below_left), channel_id=1, source_target_pairs={{1,0},{2,1},{3,2},{4,3},{5,4},{6,5},{7,6},{9,8},{10,9},{11,10},{12... | collective-permute-start | bytes 786440 | tf_op jit(solution)/shard_map/ppermute | solution.py:277
  15.5 99.4 %copy-start.2 = (s32[2]{0:T(128)}, s32[2]{0:T(128)S(1)}, u32[]{:S(2)}) copy-start(s32[2]{0:T(128)S(1)} %pad_add_fusion.place) | copy-start | bytes 28
  20.3 0.7 copy-start.8
  21.0 0.8 copy-start.6
  21.8 1.0 copy-start.1
  22.8 1.9 copy-start.3
  24.7 1.0 copy-start.7
  25.7 0.9 copy-start.9
  26.7 0.9 copy-start.12
  27.6 1.0 copy-start.13
  28.6 1.0 copy-start.15
  35.6 11.1 %collective-permute-start.8 = (f32[4,3,32,256]{3,2,1,0:T(8,128)S(1)}, f32[4,3,32,256]{3,2,1,0:T(8,128)S(1)}, u32[]{:S(2)}, u32[]{:S(2)}) collective-permute-start(f32[4,3,32,256]{3,2,1,0:T(8,128)S(1)} %get-tuple-element.30), channel_id=1, source_target_pairs={{0,1},{1,0},{2,3},{3,2},{4,5},{5,4},{6,7},{7,6},{8,9},{9,8},{10,11... | collective-permute-start | bytes 1179656 | tf_op jit(solution)/shard_map/ppermute | solution.py:285
  38.2 24.6 %collective-permute-start.5 = (bf16[2,256,256]{2,1,0:T(8,128)(2,1)S(1)}, bf16[2,256,256]{2,1,0:T(8,128)(2,1)S(1)}, u32[]{:S(2)}, u32[]{:S(2)}) collective-permute-start(bf16[2,256,256]{2,1,0:T(8,128)(2,1)S(1)} %get-tuple-element.26), channel_id=1, source_target_pairs={{0,1},{1,2},{2,3},{3,4},{4,5},{5,6},{6,7},{8,9},{9,10},{10,11},{11... | collective-permute-start | bytes 786440 | tf_op jit(solution)/shard_map/ppermute | solution.py:277
  40.1 32.6 %collective-permute-start.7 = (bf16[2,256,128]{2,1,0:T(8,128)(2,1)S(1)}, bf16[2,256,128]{2,1,0:T(8,128)(2,1)S(1)}, u32[]{:S(2)}, u32[]{:S(2)}) collective-permute-start(bf16[2,256,128]{2,1,0:T(8,128)(2,1)S(1)} %get-tuple-element.27), channel_id=1, source_target_pairs={{0,8},{8,16},{16,24},{24,32},{32,40},{40,48},{48,56},{56,64},{64,7... | collective-permute-start | bytes 393224 | tf_op jit(solution)/shard_map/ppermute | solution.py:277
  45.0 32.9 %collective-permute-start.4 = (bf16[2,512,256]{2,1,0:T(8,128)(2,1)S(1)}, bf16[2,512,256]{2,1,0:T(8,128)(2,1)S(1)}, u32[]{:S(2)}, u32[]{:S(2)}) collective-permute-start(bf16[2,512,256]{2,1,0:T(8,128)(2,1)S(1)} %get-tuple-element.24), channel_id=1, source_target_pairs={{0,1},{1,2},{2,3},{3,4},{4,5},{5,6},{6,7},{8,9},{9,10},{10,11},{11... | collective-permute-start | bytes 1572872 | tf_op jit(solution)/shard_map/ppermute | solution.py:277
  46.8 18.8 %collective-permute-start.9 = (f32[3,32,256]{2,1,0:T(8,128)S(1)}, f32[3,32,256]{2,1,0:T(8,128)S(1)}, u32[]{:S(2)}, u32[]{:S(2)}) collective-permute-start(f32[3,32,256]{2,1,0:T(8,128)S(1)} %get-tuple-element.47), channel_id=1, source_target_pairs={{0,2},{2,4},{4,6},{6,0},{1,3},{3,5},{5,7},{7,1},{8,10},{10,12},{12... | collective-permute-start | bytes 294920 | tf_op jit(solution)/shard_map/ppermute | solution.py:281
  62.8 5.7 %collective-permute-start.11 = (f32[3,32,256]{2,1,0:T(8,128)S(1)}, f32[3,32,256]{2,1,0:T(8,128)S(1)}, u32[]{:S(2)}, u32[]{:S(2)}) collective-permute-start(f32[3,32,256]{2,1,0:T(8,128)S(1)} %get-tuple-element.48), channel_id=1, source_target_pairs={{0,6},{2,0},{4,2},{6,4},{1,7},{3,1},{5,3},{7,5},{8,14},{10,8},{12,... | collective-permute-start | bytes 294920 | tf_op jit(solution)/shard_map/ppermute | solution.py:281
  62.8 7.2 %collective-permute-start.10 = (f32[3,32,256]{2,1,0:T(8,128)S(1)}, f32[3,32,256]{2,1,0:T(8,128)S(1)}, u32[]{:S(2)}, u32[]{:S(2)}) collective-permute-start(f32[3,32,256]{2,1,0:T(8,128)S(1)} %get-tuple-element.49), channel_id=1, source_target_pairs={{0,4},{2,6},{4,0},{6,2},{1,5},{3,7},{5,1},{7,3},{8,12},{10,14},{12... | collective-permute-start | bytes 294920 | tf_op jit(solution)/shard_map/ppermute | solution.py:281
  65.6 12.4 %collective-permute-start.6 = (bf16[2,256,256]{2,1,0:T(8,128)(2,1)S(1)}, bf16[2,256,256]{2,1,0:T(8,128)(2,1)S(1)}, u32[]{:S(2)}, u32[]{:S(2)}) collective-permute-start(bf16[2,256,256]{2,1,0:T(8,128)(2,1)S(1)} %add_convert_fusion.1), channel_id=1, source_target_pairs={{0,8},{8,16},{16,24},{24,32},{32,40},{40,48},{48,56},{56,64},{64,7... | collective-permute-start | bytes 786440 | tf_op jit(solution)/shard_map/ppermute | solution.py:277
  70.1 7.8 %collective-permute-start.14 = (f32[3,32,256]{2,1,0:T(8,128)S(1)}, f32[3,32,256]{2,1,0:T(8,128)S(1)}, u32[]{:S(2)}, u32[]{:S(2)}) collective-permute-start(f32[3,32,256]{2,1,0:T(8,128)S(1)} %fusion.5.rest_0_), channel_id=1, source_target_pairs={{0,24},{8,0},{16,8},{24,16},{1,25},{9,1},{17,9},{25,17},{2,26},{10... | collective-permute-start | bytes 294920 | tf_op jit(solution)/shard_map/ppermute | solution.py:281
  70.4 7.8 %collective-permute-start.13 = (f32[3,32,256]{2,1,0:T(8,128)S(1)}, f32[3,32,256]{2,1,0:T(8,128)S(1)}, u32[]{:S(2)}, u32[]{:S(2)}) collective-permute-start(f32[3,32,256]{2,1,0:T(8,128)S(1)} %fusion.5.rest_0_), channel_id=1, source_target_pairs={{0,16},{8,24},{16,0},{24,8},{1,17},{9,25},{17,1},{25,9},{2,18},{10... | collective-permute-start | bytes 294920 | tf_op jit(solution)/shard_map/ppermute | solution.py:281
  72.7 8.0 %collective-permute-start.12 = (f32[3,32,256]{2,1,0:T(8,128)S(1)}, f32[3,32,256]{2,1,0:T(8,128)S(1)}, u32[]{:S(2)}, u32[]{:S(2)}) collective-permute-start(f32[3,32,256]{2,1,0:T(8,128)S(1)} %fusion.5.rest_0_), channel_id=1, source_target_pairs={{0,8},{8,16},{16,24},{24,0},{1,9},{9,17},{17,25},{25,1},{2,10},{10... | collective-permute-start | bytes 294920 | tf_op jit(solution)/shard_map/ppermute | solution.py:281
  81.9 0.8 copy-start.5
  82.7 0.7 copy-start.10
  83.4 9.6 %collective-permute-start.21 = (f32[3,32,256]{2,1,0:T(8,128)S(1)}, f32[3,32,256]{2,1,0:T(8,128)S(1)}, u32[]{:S(2)}, u32[]{:S(2)}) collective-permute-start(f32[3,32,256]{2,1,0:T(8,128)S(1)} %get-tuple-element.35), channel_id=1, source_target_pairs={{0,96},{32,0},{64,32},{96,64},{1,97},{33,1},{65,33},{97,65},{2,98}... | collective-permute-start | bytes 294920 | tf_op jit(solution)/shard_map/ppermute | solution.py:281
  83.7 9.3 %collective-permute-start.20 = (f32[3,32,256]{2,1,0:T(8,128)S(1)}, f32[3,32,256]{2,1,0:T(8,128)S(1)}, u32[]{:S(2)}, u32[]{:S(2)}) collective-permute-start(f32[3,32,256]{2,1,0:T(8,128)S(1)} %get-tuple-element.35), channel_id=1, source_target_pairs={{0,64},{32,96},{64,0},{96,32},{1,65},{33,97},{65,1},{97,33},{2,66}... | collective-permute-start | bytes 294920 | tf_op jit(solution)/shard_map/ppermute | solution.py:281
  87.2 5.9 %collective-permute-start.19 = (f32[3,32,256]{2,1,0:T(8,128)S(1)}, f32[3,32,256]{2,1,0:T(8,128)S(1)}, u32[]{:S(2)}, u32[]{:S(2)}) collective-permute-start(f32[3,32,256]{2,1,0:T(8,128)S(1)} %get-tuple-element.35), channel_id=1, source_target_pairs={{0,32},{32,64},{64,96},{96,0},{1,33},{33,65},{65,97},{97,1},{2,34}... | collective-permute-start | bytes 294920 | tf_op jit(solution)/shard_map/ppermute | solution.py:281
  89.8 15.4 %collective-permute-start.15 = (bf16[2,256,256]{2,1,0:T(8,128)(2,1)S(1)}, bf16[2,256,256]{2,1,0:T(8,128)(2,1)S(1)}, u32[]{:S(2)}, u32[]{:S(2)}) collective-permute-start(bf16[2,256,256]{2,1,0:T(8,128)(2,1)S(1)} %get-tuple-element.32), channel_id=1, source_target_pairs={{8,0},{16,8},{24,16},{32,24},{40,32},{48,40},{56,48},{64,56},{72,6... | collective-permute-start | bytes 786440 | tf_op jit(solution)/shard_map/ppermute | solution.py:277
  91.7 23.1 %collective-permute-start.17 = (bf16[2,512,256]{2,1,0:T(8,128)(2,1)}, bf16[2,512,256]{2,1,0:T(8,128)(2,1)S(1)}, u32[]{:S(2)}, u32[]{:S(2)}) collective-permute-start(bf16[2,512,256]{2,1,0:T(8,128)(2,1)} %copy-done.5), channel_id=1, source_target_pairs={{1,0},{2,1},{3,2},{4,3},{5,4},{6,5},{7,6},{9,8},{10,9},{11,10},{12... | collective-permute-start | bytes 1572872 | tf_op jit(solution)/shard_map/ppermute | solution.py:277
  93.9 10.6 %collective-permute-start.24 = (f32[2,32,256]{2,1,0:T(8,128)S(1)}, f32[2,32,256]{2,1,0:T(8,128)S(1)}, u32[]{:S(2)}, u32[]{:S(2)}) collective-permute-start(f32[2,32,256]{2,1,0:T(8,128)S(1)} %fusion.7), channel_id=1, source_target_pairs={{0,6},{2,0},{4,2},{6,4},{1,7},{3,1},{5,3},{7,5},{8,14},{10,8},{12,... | collective-permute-start | bytes 196616 | tf_op jit(solution)/shard_map/ppermute | solution.py:281
  97.7 6.9 %collective-permute-start.23 = (f32[2,32,256]{2,1,0:T(8,128)S(1)}, f32[2,32,256]{2,1,0:T(8,128)S(1)}, u32[]{:S(2)}, u32[]{:S(2)}) collective-permute-start(f32[2,32,256]{2,1,0:T(8,128)S(1)} %fusion.7), channel_id=1, source_target_pairs={{0,4},{2,6},{4,0},{6,2},{1,5},{3,7},{5,1},{7,3},{8,12},{10,14},{12... | collective-permute-start | bytes 196616 | tf_op jit(solution)/shard_map/ppermute | solution.py:281
  99.6 5.5 %collective-permute-start.22 = (f32[2,32,256]{2,1,0:T(8,128)S(1)}, f32[2,32,256]{2,1,0:T(8,128)S(1)}, u32[]{:S(2)}, u32[]{:S(2)}) collective-permute-start(f32[2,32,256]{2,1,0:T(8,128)S(1)} %fusion.7), channel_id=1, source_target_pairs={{0,2},{2,4},{4,6},{6,0},{1,3},{3,5},{5,7},{7,1},{8,10},{10,12},{12... | collective-permute-start | bytes 196616 | tf_op jit(solution)/shard_map/ppermute | solution.py:281
  105.1 9.7 %collective-permute-start.25 = (f32[4,2,32,256]{3,2,1,0:T(8,128)S(1)}, f32[4,2,32,256]{3,2,1,0:T(8,128)S(1)}, u32[]{:S(2)}, u32[]{:S(2)}) collective-permute-start(f32[4,2,32,256]{3,2,1,0:T(8,128)S(1)} %pad_maximum_fusion.rest_0_), channel_id=1, source_target_pairs={{0,1},{1,0},{2,3},{3,2},{4,5},{5,4},{6,7},{7,6},{8,9},{9,8},{10,11... | collective-permute-start | bytes 786440 | tf_op jit(solution)/shard_map/ppermute | solution.py:285
  105.2 9.6 %collective-permute-start.18 = (bf16[2,256,256]{2,1,0:T(8,128)(2,1)S(1)}, bf16[2,256,256]{2,1,0:T(8,128)(2,1)S(1)}, u32[]{:S(2)}, u32[]{:S(2)}) collective-permute-start(bf16[2,256,256]{2,1,0:T(8,128)(2,1)S(1)} %collective-permute-done.15.below_left), channel_id=1, source_target_pairs={{1,0},{2,1},{3,2},{4,3},{5,4},{6,5},{7,6},{9,8},{10,9},{11,10},{12... | collective-permute-start | bytes 786440 | tf_op jit(solution)/shard_map/ppermute | solution.py:277
  106.5 8.3 %collective-permute-start.16 = (bf16[2,256,128]{2,1,0:T(8,128)(2,1)}, bf16[2,256,128]{2,1,0:T(8,128)(2,1)S(1)}, u32[]{:S(2)}, u32[]{:S(2)}) collective-permute-start(bf16[2,256,128]{2,1,0:T(8,128)(2,1)} %copy-done.10), channel_id=1, source_target_pairs={{8,0},{16,8},{24,16},{32,24},{40,32},{48,40},{56,48},{64,56},{72,6... | collective-permute-start | bytes 393224 | tf_op jit(solution)/shard_map/ppermute | solution.py:277
  114.8 1.9 copy-start.4
  116.7 1.0 copy-start.14
  117.8 1.0 copy-start.16
  123.7 1.8 collective-permute-start.30
  125.6 12.9 %collective-permute-start.31 = (f32[3,32,256]{2,1,0:T(8,128)S(1)}, f32[3,32,256]{2,1,0:T(8,128)S(1)}, u32[]{:S(2)}, u32[]{:S(2)}) collective-permute-start(f32[3,32,256]{2,1,0:T(8,128)S(1)} %get-tuple-element.44), channel_id=1, source_target_pairs={{0,2},{2,4},{4,6},{6,0},{1,3},{3,5},{5,7},{7,1},{8,10},{10,12},{12... | collective-permute-start | bytes 294920 | tf_op jit(solution)/shard_map/ppermute | solution.py:281
  135.9 5.6 %collective-permute-start.33 = (f32[3,32,256]{2,1,0:T(8,128)S(1)}, f32[3,32,256]{2,1,0:T(8,128)S(1)}, u32[]{:S(2)}, u32[]{:S(2)}) collective-permute-start(f32[3,32,256]{2,1,0:T(8,128)S(1)} %get-tuple-element.45), channel_id=1, source_target_pairs={{0,6},{2,0},{4,2},{6,4},{1,7},{3,1},{5,3},{7,5},{8,14},{10,8},{12,... | collective-permute-start | bytes 294920 | tf_op jit(solution)/shard_map/ppermute | solution.py:281
  136.0 6.1 %collective-permute-start.32 = (f32[3,32,256]{2,1,0:T(8,128)S(1)}, f32[3,32,256]{2,1,0:T(8,128)S(1)}, u32[]{:S(2)}, u32[]{:S(2)}) collective-permute-start(f32[3,32,256]{2,1,0:T(8,128)S(1)} %get-tuple-element.46), channel_id=1, source_target_pairs={{0,4},{2,6},{4,0},{6,2},{1,5},{3,7},{5,1},{7,3},{8,12},{10,14},{12... | collective-permute-start | bytes 294920 | tf_op jit(solution)/shard_map/ppermute | solution.py:281
  142.1 11.6 %collective-permute-start.36 = (f32[3,32,256]{2,1,0:T(8,128)S(1)}, f32[3,32,256]{2,1,0:T(8,128)S(1)}, u32[]{:S(2)}, u32[]{:S(2)}) collective-permute-start(f32[3,32,256]{2,1,0:T(8,128)S(1)} %fusion.2), channel_id=1, source_target_pairs={{0,24},{8,0},{16,8},{24,16},{1,25},{9,1},{17,9},{25,17},{2,26},{10... | collective-permute-start | bytes 294920 | tf_op jit(solution)/shard_map/ppermute | solution.py:281
  150.2 6.3 %collective-permute-start.35 = (f32[3,32,256]{2,1,0:T(8,128)S(1)}, f32[3,32,256]{2,1,0:T(8,128)S(1)}, u32[]{:S(2)}, u32[]{:S(2)}) collective-permute-start(f32[3,32,256]{2,1,0:T(8,128)S(1)} %fusion.2), channel_id=1, source_target_pairs={{0,16},{8,24},{16,0},{24,8},{1,17},{9,25},{17,1},{25,9},{2,18},{10... | collective-permute-start | bytes 294920 | tf_op jit(solution)/shard_map/ppermute | solution.py:281
  150.2 7.0 %collective-permute-start.34 = (f32[3,32,256]{2,1,0:T(8,128)S(1)}, f32[3,32,256]{2,1,0:T(8,128)S(1)}, u32[]{:S(2)}, u32[]{:S(2)}) collective-permute-start(f32[3,32,256]{2,1,0:T(8,128)S(1)} %fusion.2), channel_id=1, source_target_pairs={{0,8},{8,16},{16,24},{24,0},{1,9},{9,17},{17,25},{25,1},{2,10},{10... | collective-permute-start | bytes 294920 | tf_op jit(solution)/shard_map/ppermute | solution.py:281
  157.2 12.8 %collective-permute-start.39 = (f32[3,32,256]{2,1,0:T(8,128)S(1)}, f32[3,32,256]{2,1,0:T(8,128)S(1)}, u32[]{:S(2)}, u32[]{:S(2)}) collective-permute-start(f32[3,32,256]{2,1,0:T(8,128)S(1)} %add_add_fusion.1), channel_id=1, source_target_pairs={{0,96},{32,0},{64,32},{96,64},{1,97},{33,1},{65,33},{97,65},{2,98}... | collective-permute-start | bytes 294920 | tf_op jit(solution)/shard_map/ppermute | solution.py:281
  161.6 8.4 %collective-permute-start.38 = (f32[3,32,256]{2,1,0:T(8,128)S(1)}, f32[3,32,256]{2,1,0:T(8,128)S(1)}, u32[]{:S(2)}, u32[]{:S(2)}) collective-permute-start(f32[3,32,256]{2,1,0:T(8,128)S(1)} %add_add_fusion.1), channel_id=1, source_target_pairs={{0,64},{32,96},{64,0},{96,32},{1,65},{33,97},{65,1},{97,33},{2,66}... | collective-permute-start | bytes 294920 | tf_op jit(solution)/shard_map/ppermute | solution.py:281
  163.0 7.0 %collective-permute-start.37 = (f32[3,32,256]{2,1,0:T(8,128)S(1)}, f32[3,32,256]{2,1,0:T(8,128)S(1)}, u32[]{:S(2)}, u32[]{:S(2)}) collective-permute-start(f32[3,32,256]{2,1,0:T(8,128)S(1)} %add_add_fusion.1), channel_id=1, source_target_pairs={{0,32},{32,64},{64,96},{96,0},{1,33},{33,65},{65,97},{97,1},{2,34}... | collective-permute-start | bytes 294920 | tf_op jit(solution)/shard_map/ppermute | solution.py:281
  165.6 9.1 %collective-permute-start.27 = (bf16[2,256,256]{2,1,0:T(8,128)(2,1)S(1)}, bf16[2,256,256]{2,1,0:T(8,128)(2,1)S(1)}, u32[]{:S(2)}, u32[]{:S(2)}) collective-permute-start(bf16[2,256,256]{2,1,0:T(8,128)(2,1)S(1)} %get-tuple-element.39), channel_id=1, source_target_pairs={{0,1},{1,2},{2,3},{3,4},{4,5},{5,6},{6,7},{8,9},{9,10},{10,11},{11... | collective-permute-start | bytes 786440 | tf_op jit(solution)/shard_map/ppermute | solution.py:277
  166.9 25.3 %collective-permute-start.26 = (bf16[2,512,256]{2,1,0:T(8,128)(2,1)S(1)}, bf16[2,512,256]{2,1,0:T(8,128)(2,1)S(1)}, u32[]{:S(2)}, u32[]{:S(2)}) collective-permute-start(bf16[2,512,256]{2,1,0:T(8,128)(2,1)S(1)} %get-tuple-element.37), channel_id=1, source_target_pairs={{0,1},{1,2},{2,3},{3,4},{4,5},{5,6},{6,7},{8,9},{9,10},{10,11},{11... | collective-permute-start | bytes 1572872 | tf_op jit(solution)/shard_map/ppermute | solution.py:277
  170.1 6.7 %collective-permute-start.42 = (f32[2,32,256]{2,1,0:T(8,128)S(1)}, f32[2,32,256]{2,1,0:T(8,128)S(1)}, u32[]{:S(2)}, u32[]{:S(2)}) collective-permute-start(f32[2,32,256]{2,1,0:T(8,128)S(1)} %fusion.6), channel_id=1, source_target_pairs={{0,6},{2,0},{4,2},{6,4},{1,7},{3,1},{5,3},{7,5},{8,14},{10,8},{12,... | collective-permute-start | bytes 196616 | tf_op jit(solution)/shard_map/ppermute | solution.py:281
  171.7 6.5 %collective-permute-start.41 = (f32[2,32,256]{2,1,0:T(8,128)S(1)}, f32[2,32,256]{2,1,0:T(8,128)S(1)}, u32[]{:S(2)}, u32[]{:S(2)}) collective-permute-start(f32[2,32,256]{2,1,0:T(8,128)S(1)} %fusion.6), channel_id=1, source_target_pairs={{0,4},{2,6},{4,0},{6,2},{1,5},{3,7},{5,1},{7,3},{8,12},{10,14},{12... | collective-permute-start | bytes 196616 | tf_op jit(solution)/shard_map/ppermute | solution.py:281
  173.3 5.6 %collective-permute-start.40 = (f32[2,32,256]{2,1,0:T(8,128)S(1)}, f32[2,32,256]{2,1,0:T(8,128)S(1)}, u32[]{:S(2)}, u32[]{:S(2)}) collective-permute-start(f32[2,32,256]{2,1,0:T(8,128)S(1)} %fusion.6), channel_id=1, source_target_pairs={{0,2},{2,4},{4,6},{6,0},{1,3},{3,5},{5,7},{7,1},{8,10},{10,12},{12... | collective-permute-start | bytes 196616 | tf_op jit(solution)/shard_map/ppermute | solution.py:281
  174.7 17.4 %collective-permute-start.28 = (bf16[2,256,256]{2,1,0:T(8,128)(2,1)S(1)}, bf16[2,256,256]{2,1,0:T(8,128)(2,1)S(1)}, u32[]{:S(2)}, u32[]{:S(2)}) collective-permute-start(bf16[2,256,256]{2,1,0:T(8,128)(2,1)S(1)} %add_convert_fusion), channel_id=1, source_target_pairs={{0,8},{8,16},{16,24},{24,32},{32,40},{40,48},{48,56},{56,64},{64,7... | collective-permute-start | bytes 786440 | tf_op jit(solution)/shard_map/ppermute | solution.py:277
  179.0 15.5 %copy-start.17 = (f32[4,2,32,256]{3,2,1,0:T(8,128)}, f32[4,2,32,256]{3,2,1,0:T(8,128)S(1)}, u32[]{:S(2)}) copy-start(f32[4,2,32,256]{3,2,1,0:T(8,128)S(1)} %pad_maximum_fusion.1.mine) | copy-start | bytes 786436
  179.0 15.4 %collective-permute-start.43 = (f32[4,2,32,256]{3,2,1,0:T(8,128)S(1)}, f32[4,2,32,256]{3,2,1,0:T(8,128)S(1)}, u32[]{:S(2)}, u32[]{:S(2)}) collective-permute-start(f32[4,2,32,256]{3,2,1,0:T(8,128)S(1)} %pad_maximum_fusion.1.mine), channel_id=1, source_target_pairs={{0,1},{1,0},{2,3},{3,2},{4,5},{5,4},{6,7},{7,6},{8,9},{9,8},{10,11... | collective-permute-start | bytes 786440 | tf_op jit(solution)/shard_map/ppermute | solution.py:285
  182.7 9.4 %collective-permute-start.29 = (bf16[2,256,128]{2,1,0:T(8,128)(2,1)S(1)}, bf16[2,256,128]{2,1,0:T(8,128)(2,1)S(1)}, u32[]{:S(2)}, u32[]{:S(2)}) collective-permute-start(bf16[2,256,128]{2,1,0:T(8,128)(2,1)S(1)} %get-tuple-element.40), channel_id=1, source_target_pairs={{0,8},{8,16},{16,24},{24,32},{32,40},{40,48},{48,56},{56,64},{64,7... | collective-permute-start | bytes 393224 | tf_op jit(solution)/shard_map/ppermute | solution.py:277
  194.4 0.7 copy-start.18
  (1 other events, 0.7 us)

commit v3 on v2

--- a/solution.py
+++ b/solution.py
@@ -36,10 +36,21 @@
     iteration, n_pieces,
     place, counts, pos, obj, below_left, below_right, right, corner, *rest,
 ):
-    pieces, (amps, table_a, table_b), rest = rest[:n_pieces], rest[n_pieces : n_pieces + 3], rest[n_pieces + 3 :]
+    pieces, (amps, tab_a, tab_b), rest = rest[:n_pieces], rest[n_pieces : n_pieces + 3], rest[n_pieces + 3 :]
     own_out, low_left, low_right, right_out, corner_out, keep_out, send_out, step_out = rest[:8]
-    ext, acc, sums, wave, mis, patch, levels, arrived, *probe_scratch = rest[8:]
+    ext, acc, sums, wave, mis, patch, levels, arrived, here, *rest = rest[8:]
+    landing, probe_scratch = rest[: 7 + n_pieces], rest[7 + n_pieces :]
     count = counts[0]
+    copies = [
+        pltpu.make_async_copy(source, target, here.at[i])
+        for i, (source, target) in enumerate(
+            zip((obj, below_left, below_right, right, corner, *pieces, tab_a, tab_b), landing)
+        )
+    ]
+    for copy in copies:
+        copy.start()
+    obj, below_left, below_right, right, corner = landing[:5]
+    pieces, (table_a, table_b) = landing[5 : 5 + n_pieces], landing[5 + n_pieces :]
 
     def fetch(index):
         return pltpu.make_async_copy(amps.at[iteration, index], levels.at[index], arrived.at[index])
@@ -51,6 +62,23 @@
     lax.fori_loop(0, count, begin, 0)
     rows, cols = obj.shape[1], obj.shape[2]
     size = corner.shape[1]
+    row_chunks = size // CHUNK
+    inner_tiles, all_tiles, left_tiles = cols // LANES, (cols + size) // LANES, size // LANES
+    acc[...] = jnp.zeros_like(acc)
+    sums[...] = jnp.zeros_like(sums)
+    copies[0].wait()
+    for copy in copies[1:5]:
+        copy.wait()
+    for j in range(all_tiles):
+        inside = j < inner_tiles
+        at = (j if inside else j - inner_tiles) * LANES
+        upper = obj if inside else right
+        ext[:, j, :rows, :] = upper[:, :, at : at + LANES].astype(BF).astype(F32)
+        lower = (below_left if j < left_tiles else below_right) if inside else corner
+        at = at if j < left_tiles or not inside else at - size
+        ext[:, j, rows:, :] = lower[:, :, at : at + LANES].astype(F32)
+    for copy in copies[5:]:
+        copy.wait()
     core, y = place[0], place[1]
     half, quarter = size // N_CORE, size // (N_CORE * N_Y)
     if n_pieces == 1:
@@ -61,24 +89,14 @@
             for j in range(N_Y):
                 at = pl.multiple_of(side * half + lax.rem(y - j + N_Y, N_Y) * quarter, quarter)
                 probe[:, pl.ds(at, quarter), :] = piece[j]
-    row_chunks = size // CHUNK
-    inner_tiles, all_tiles, left_tiles = cols // LANES, (cols + size) // LANES, size // LANES
-    for j in range(all_tiles):
-        inside = j < inner_tiles
-        at = (j if inside else j - inner_tiles) * LANES
-        upper = obj if inside else right
-        ext[:, j, :rows, :] = upper[:, :, at : at + LANES].astype(BF).astype(F32)
-        lower = (below_left if j < left_tiles else below_right) if inside else corner
-        at = at if j < left_tiles or not inside else at - size
-        ext[:, j, rows:, :] = lower[:, :, at : at + LANES].astype(F32)
-    acc[...] = jnp.zeros_like(acc)
-    sums[...] = jnp.zeros_like(sums)
     peak = jnp.max(probe[0] * probe[0] + probe[1] * probe[1])
     step_out[0, 0] = ALPHA / (peak + 1e-6)
     lane = lax.broadcasted_iota(jnp.int32, (CHUNK, LANES), 1)
 
     def frames(indices):
         work = []
+        for index in indices:
+            fetch(index).wait()
         for slot, index in enumerate(indices):
             top, left = pos[0, index], pos[1, index]
             base = left // LANES
@@ -110,7 +128,6 @@
             far = jnp.dot(near, table_b[...], preferred_element_type=F32)
             fr, fi = far[:, :size], far[:, size:]
             scale = lax.rsqrt(jnp.maximum(fr * fr + fi * fi, FLOOR * FLOOR))
-            fetch(index).wait()
             factor = 1.0 - levels[index].astype(F32) * scale
             mis[slot, :size, :] = (fr * factor).astype(BF)
             mis[slot, size:, :] = (fi * factor).astype(BF)
@@ -194,15 +211,18 @@
         pltpu.VMEM((slots, size, size), BF),
         pltpu.SemaphoreType.DMA((slots,)),
     ]
+    loaded = (obj, *halos, *pieces, *tables)
+    scratch.append(pltpu.SemaphoreType.DMA((len(loaded),)))
+    scratch += [pltpu.VMEM(value.shape, value.dtype) for value in loaded]
     if len(pieces) > 1:
         scratch.append(pltpu.VMEM((2, size, size), F32))
     return pl.pallas_call(
         functools.partial(frames_kernel, iteration, len(pieces)),
         out_shape=shapes,
-        in_specs=[smem] * 3 + [vmem] * (5 + len(pieces)) + [pl.BlockSpec(memory_space=pl.ANY)] + [vmem] * 2,
+        in_specs=[smem] * 3 + [pl.BlockSpec(memory_space=pltpu.HBM)] * (8 + len(pieces)),
         out_specs=[vmem] * 7 + [smem],
         scratch_shapes=scratch,
-        compiler_params=pltpu.CompilerParams(vmem_limit_bytes=26 << 20),
+        compiler_params=pltpu.CompilerParams(vmem_limit_bytes=48 << 20),
         cost_estimate=pl.CostEstimate(flops=6_000_000_000, bytes_accessed=8_000_000, transcendentals=0),
         name="frames",
     )(place, counts, pos, obj, *halos, *pieces, amps, *tables)

time: 198 us -> 172 us (0.87)
  local copies, waits for them, and re-layouts: 18.4 us -> 2.61 us
  starting transfers between devices: 111 us -> 101 us
  Pallas kernels: 16.1 us -> 19 us
  waiting for transfers between devices: 47.7 us -> 45 us
    ppermute x24, starting transfers between devices: 67.7 us -> 40.6 us  [turned(): return lax.ppermute(value, axis, [(s, (s + steps) % 4) for s in range(4)])]
    unnamed x42 -> x26, local copies, waits for them, and re-layouts: 16.2 us -> 1.91 us
    ppermute x4, starting transfers between devices: 6.69 us -> 16.2 us  [swapped(): return lax.ppermute(value, 'core', [(0, 1), (1, 0)])]
    ppermute x16, starting transfers between devices: 36.4 us -> 44.4 us  [moved(): lax.ppermute(value, axis, [(s, s + steps) for s in range(first, last)])]
    ppermute x16, waiting for transfers between devices: 22.7 us -> 19.2 us  [moved(): lax.ppermute(value, axis, [(s, s + steps) for s in range(first, last)])]
    pallas_call x2, Pallas kernels: 10.8 us -> 13.7 us  [run_frames(): pl.pallas_call(functools.partial(frames_kernel, iteration, len(pieces)),...]
  transfers between devices with their start and end apart: 44 -> 44, of which waited for: 21 -> 20; matrix products, arithmetic and copies ran while one was open for 2% -> 1% of each run, Pallas kernels for 1% -> 1%
where the time goes in v3:
time: 172 us; the launch traced here: 171 us
  starting transfers between devices  101 us (59%)
  waiting for transfers between devices  45 us (26%)
  Pallas kernels  19 us (11%)
  local copies, waits for them, and re-layouts  2.61 us (2%)
  other arithmetic  2.15 us (1%)
    ppermute x16, starting transfers between devices, moved(): lax.ppermute(value, axis, [(s, s + steps) for s in range(first, last)])  44.4 us
    ppermute x24, starting transfers between devices, turned(): return lax.ppermute(value, axis, [(s, (s + steps) % 4) for s in range(4)])  40.6 us
    ppermute x24, waiting for transfers between devices, turned(): return lax.ppermute(value, axis, [(s, (s + steps) % 4) for s in range(4)])  24.4 us
    ppermute x16, waiting for transfers between devices, moved(): lax.ppermute(value, axis, [(s, s + steps) for s in range(first, last)])  19.2 us
    ppermute x4, starting transfers between devices, swapped(): return lax.ppermute(value, 'core', [(0, 1), (1, 0)])  16.2 us
    pallas_call x2, Pallas kernels, run_frames(): pl.pallas_call(functools.partial(frames_kernel, iteration, len(pieces)),...  13.7 us
  transfers between devices with their start and end apart: 44, of which 20 were waited for; matrix products, arithmetic and copies ran while one was open for 1% of the time, Pallas kernels for 1%

profile of v3, /device:TPU:6, one launch (start us, length us, event | category | flops | bytes accessed | tf_op | source)
XLA Modules:
  0.0 171.1 jit_solution(16533796649753845814)
XLA Ops:
  0.7 1.6 convert.5
  2.3 6.2 %collective-permute-start = (bf16[2,256,256]{2,1,0:T(8,128)(2,1)S(1)}, bf16[2,256,256]{2,1,0:T(8,128)(2,1)S(1)}, u32[]{:S(2)}, u32[]{:S(2)}) collective-permute-start(bf16[2,256,256]{2,1,0:T(8,128)(2,1)S(1)} %slice.79), channel_id=1, source_target_pairs={{8,0},{16,8},{24,16},{32,24},{40,32},{48,40},{56,48},{64,56},{72,6... | collective-permute-start | bytes 786440 | tf_op jit(solution)/shard_map/ppermute | solution.py:297
  8.6 1.3 collective-permute-start.2
  9.9 2.3 %collective-permute-start.1 = (bf16[2,256,128]{2,1,0:T(8,128)(2,1)S(1)}, bf16[2,256,128]{2,1,0:T(8,128)(2,1)S(1)}, u32[]{:S(2)}, u32[]{:S(2)}) collective-permute-start(bf16[2,256,128]{2,1,0:T(8,128)(2,1)S(1)} %slice.80), channel_id=1, source_target_pairs={{8,0},{16,8},{24,16},{32,24},{40,32},{48,40},{56,48},{64,56},{72,6... | collective-permute-start | bytes 393224 | tf_op jit(solution)/shard_map/ppermute | solution.py:297
  12.2 2.4 %collective-permute-done.below_left = bf16[2,256,256]{2,1,0:T(8,128)(2,1)S(1)} collective-permute-done((bf16[2,256,256]{2,1,0:T(8,128)(2,1)S(1)}, bf16[2,256,256]{2,1,0:T(8,128)(2,1)S(1)}, u32[]{:S(2)}, u32[]{:S(2)}) %collective-permute-start) | collective-permute-done | bytes 262176 | tf_op jit(solution)/shard_map/ppermute | solution.py:297
  14.7 1.3 collective-permute-start.3
  16.0 0.1 pad_add_fusion.place
  16.1 0.6 fusion.10
  16.6 1.4 collective-permute-done.1.below_right
  18.1 6.8 %frames.2 = (f32[2,512,384]{2,1,0:T(8,128)}, f32[2,256,256]{2,1,0:T(8,128)S(1)}, bf16[2,256,128]{2,1,0:T(8,128)(2,1)S(1)}, bf16[2,512,256]{2,1,0:T(8,128)(2,1)S(...) custom-call(s32[2]{0:T(128)S(1)} %pad_add_fusion.place, ...), custom_call_target="tpu_custom_call" | custom-call | flops 6000000000 | bytes 8000000 | tf_op jit(solution)/shard_map/frames/pallas_call | solution.py:219
  24.9 3.8 %collective-permute-start.8 = (f32[4,3,32,256]{3,2,1,0:T(8,128)S(1)}, f32[4,3,32,256]{3,2,1,0:T(8,128)S(1)}, u32[]{:S(2)}, u32[]{:S(2)}) collective-permute-start(f32[4,3,32,256]{3,2,1,0:T(8,128)S(1)} %get-tuple-element.30), channel_id=1, source_target_pairs={{0,1},{1,0},{2,3},{3,2},{4,5},{5,4},{6,7},{7,6},{8,9},{9,8},{10,11... | collective-permute-start | bytes 1179656 | tf_op jit(solution)/shard_map/ppermute | solution.py:305
  28.8 1.9 %collective-permute-start.5 = (bf16[2,256,256]{2,1,0:T(8,128)(2,1)S(1)}, bf16[2,256,256]{2,1,0:T(8,128)(2,1)S(1)}, u32[]{:S(2)}, u32[]{:S(2)}) collective-permute-start(bf16[2,256,256]{2,1,0:T(8,128)(2,1)S(1)} %get-tuple-element.26), channel_id=1, source_target_pairs={{0,1},{1,2},{2,3},{3,4},{4,5},{5,6},{6,7},{8,9},{9,10},{10,11},{11... | collective-permute-start | bytes 786440 | tf_op jit(solution)/shard_map/ppermute | solution.py:297
  30.7 8.0 %collective-permute-start.7 = (bf16[2,256,128]{2,1,0:T(8,128)(2,1)S(1)}, bf16[2,256,128]{2,1,0:T(8,128)(2,1)S(1)}, u32[]{:S(2)}, u32[]{:S(2)}) collective-permute-start(bf16[2,256,128]{2,1,0:T(8,128)(2,1)S(1)} %get-tuple-element.27), channel_id=1, source_target_pairs={{0,8},{8,16},{16,24},{24,32},{32,40},{40,48},{48,56},{56,64},{64,7... | collective-permute-start | bytes 393224 | tf_op jit(solution)/shard_map/ppermute | solution.py:297
  38.7 1.7 collective-permute-start.4
  40.5 6.5 %collective-permute-start.9 = (f32[3,32,256]{2,1,0:T(8,128)S(1)}, f32[3,32,256]{2,1,0:T(8,128)S(1)}, u32[]{:S(2)}, u32[]{:S(2)}) collective-permute-start(f32[3,32,256]{2,1,0:T(8,128)S(1)} %get-tuple-element.47), channel_id=1, source_target_pairs={{0,2},{2,4},{4,6},{6,0},{1,3},{3,5},{5,7},{7,1},{8,10},{10,12},{12... | collective-permute-start | bytes 294920 | tf_op jit(solution)/shard_map/ppermute | solution.py:301
  47.0 2.3 %collective-permute-start.10 = (f32[3,32,256]{2,1,0:T(8,128)S(1)}, f32[3,32,256]{2,1,0:T(8,128)S(1)}, u32[]{:S(2)}, u32[]{:S(2)}) collective-permute-start(f32[3,32,256]{2,1,0:T(8,128)S(1)} %get-tuple-element.49), channel_id=1, source_target_pairs={{0,4},{2,6},{4,0},{6,2},{1,5},{3,7},{5,1},{7,3},{8,12},{10,14},{12... | collective-permute-start | bytes 294920 | tf_op jit(solution)/shard_map/ppermute | solution.py:301
  49.3 0.4 collective-permute-done.9
  49.7 3.9 %collective-permute-start.6 = (bf16[2,256,256]{2,1,0:T(8,128)(2,1)S(1)}, bf16[2,256,256]{2,1,0:T(8,128)(2,1)S(1)}, u32[]{:S(2)}, u32[]{:S(2)}) collective-permute-start(bf16[2,256,256]{2,1,0:T(8,128)(2,1)S(1)} %add_convert_fusion.1), channel_id=1, source_target_pairs={{0,8},{8,16},{16,24},{24,32},{32,40},{40,48},{48,56},{56,64},{64,7... | collective-permute-start | bytes 786440 | tf_op jit(solution)/shard_map/ppermute | solution.py:297
  53.6 0.6 collective-permute-done.10
  54.3 4.1 %collective-permute-start.13 = (f32[3,32,256]{2,1,0:T(8,128)S(1)}, f32[3,32,256]{2,1,0:T(8,128)S(1)}, u32[]{:S(2)}, u32[]{:S(2)}) collective-permute-start(f32[3,32,256]{2,1,0:T(8,128)S(1)} %fusion.5.rest_0_), channel_id=1, source_target_pairs={{0,16},{8,24},{16,0},{24,8},{1,17},{9,25},{17,1},{25,9},{2,18},{10... | collective-permute-start | bytes 294920 | tf_op jit(solution)/shard_map/ppermute | solution.py:301
  58.4 3.4 %collective-permute-done.6.low_left = bf16[2,256,256]{2,1,0:T(8,128)(2,1)S(1)} collective-permute-done((bf16[2,256,256]{2,1,0:T(8,128)(2,1)S(1)}, bf16[2,256,256]{2,1,0:T(8,128)(2,1)S(1)}, u32[]{:S(2)}, u32[]{:S(2)}) %collective-permute-start.6) | collective-permute-done | bytes 262176 | tf_op jit(solution)/shard_map/ppermute | solution.py:297
  61.8 0.5 collective-permute-done.13.rest_2_
  62.3 3.4 %collective-permute-done.12.rest_1_ = f32[3,32,256]{2,1,0:T(8,128)S(1)} collective-permute-done((f32[3,32,256]{2,1,0:T(8,128)S(1)}, f32[3,32,256]{2,1,0:T(8,128)S(1)}, u32[]{:S(2)}, u32[]{:S(2)}) %collective-permute-start.12) | collective-permute-done | bytes 98336 | tf_op jit(solution)/shard_map/ppermute | solution.py:301
  65.7 1.2 object_update.2
  66.8 1.1 copy-done.2
  68.0 2.7 %collective-permute-start.21 = (f32[3,32,256]{2,1,0:T(8,128)S(1)}, f32[3,32,256]{2,1,0:T(8,128)S(1)}, u32[]{:S(2)}, u32[]{:S(2)}) collective-permute-start(f32[3,32,256]{2,1,0:T(8,128)S(1)} %get-tuple-element.35), channel_id=1, source_target_pairs={{0,96},{32,0},{64,32},{96,64},{1,97},{33,1},{65,33},{97,65},{2,98}... | collective-permute-start | bytes 294920 | tf_op jit(solution)/shard_map/ppermute | solution.py:301
  70.7 2.7 %collective-permute-start.19 = (f32[3,32,256]{2,1,0:T(8,128)S(1)}, f32[3,32,256]{2,1,0:T(8,128)S(1)}, u32[]{:S(2)}, u32[]{:S(2)}) collective-permute-start(f32[3,32,256]{2,1,0:T(8,128)S(1)} %get-tuple-element.35), channel_id=1, source_target_pairs={{0,32},{32,64},{64,96},{96,0},{1,33},{33,65},{65,97},{97,1},{2,34}... | collective-permute-start | bytes 294920 | tf_op jit(solution)/shard_map/ppermute | solution.py:301
  73.3 2.2 %collective-permute-start.15 = (bf16[2,256,256]{2,1,0:T(8,128)(2,1)S(1)}, bf16[2,256,256]{2,1,0:T(8,128)(2,1)S(1)}, u32[]{:S(2)}, u32[]{:S(2)}) collective-permute-start(bf16[2,256,256]{2,1,0:T(8,128)(2,1)S(1)} %get-tuple-element.32), channel_id=1, source_target_pairs={{8,0},{16,8},{24,16},{32,24},{40,32},{48,40},{56,48},{64,56},{72,6... | collective-permute-start | bytes 786440 | tf_op jit(solution)/shard_map/ppermute | solution.py:297
  75.5 1.3 collective-permute-start.17
  76.9 3.6 %collective-permute-start.24 = (f32[2,32,256]{2,1,0:T(8,128)S(1)}, f32[2,32,256]{2,1,0:T(8,128)S(1)}, u32[]{:S(2)}, u32[]{:S(2)}) collective-permute-start(f32[2,32,256]{2,1,0:T(8,128)S(1)} %fusion.7), channel_id=1, source_target_pairs={{0,6},{2,0},{4,2},{6,4},{1,7},{3,1},{5,3},{7,5},{8,14},{10,8},{12,... | collective-permute-start | bytes 196616 | tf_op jit(solution)/shard_map/ppermute | solution.py:301
  80.5 2.0 %collective-permute-start.23 = (f32[2,32,256]{2,1,0:T(8,128)S(1)}, f32[2,32,256]{2,1,0:T(8,128)S(1)}, u32[]{:S(2)}, u32[]{:S(2)}) collective-permute-start(f32[2,32,256]{2,1,0:T(8,128)S(1)} %fusion.7), channel_id=1, source_target_pairs={{0,4},{2,6},{4,0},{6,2},{1,5},{3,7},{5,1},{7,3},{8,12},{10,14},{12... | collective-permute-start | bytes 196616 | tf_op jit(solution)/shard_map/ppermute | solution.py:301
  82.5 6.0 %collective-permute-done.24 = f32[2,32,256]{2,1,0:T(8,128)S(1)} collective-permute-done((f32[2,32,256]{2,1,0:T(8,128)S(1)}, f32[2,32,256]{2,1,0:T(8,128)S(1)}, u32[]{:S(2)}, u32[]{:S(2)}) %collective-permute-start.24) | collective-permute-done | bytes 65568 | tf_op jit(solution)/shard_map/ppermute | solution.py:301
  88.5 0.1 collective-permute-start.25
  88.6 1.3 collective-permute-start.18
  89.9 3.5 %collective-permute-start.16 = (bf16[2,256,128]{2,1,0:T(8,128)(2,1)S(1)}, bf16[2,256,128]{2,1,0:T(8,128)(2,1)S(1)}, u32[]{:S(2)}, u32[]{:S(2)}) collective-permute-start(bf16[2,256,128]{2,1,0:T(8,128)(2,1)S(1)} %get-tuple-element.33), channel_id=1, source_target_pairs={{8,0},{16,8},{24,16},{32,24},{40,32},{48,40},{56,48},{64,56},{72,6... | collective-permute-start | bytes 393224 | tf_op jit(solution)/shard_map/ppermute | solution.py:297
  93.5 4.4 %collective-permute-done.16.below_right = bf16[2,256,128]{2,1,0:T(8,128)(2,1)S(1)} collective-permute-done((bf16[2,256,128]{2,1,0:T(8,128)(2,1)S(1)}, bf16[2,256,128]{2,1,0:T(8,128)(2,1)S(1)}, u32[]{:S(2)}, u32[]{:S(2)}) %collective-permute-start.16) | collective-permute-done | bytes 131104 | tf_op jit(solution)/shard_map/ppermute | solution.py:297
  97.9 6.9 %frames.3 = (f32[2,512,384]{2,1,0:T(8,128)}, f32[2,256,256]{2,1,0:T(8,128)S(1)}, bf16[2,256,128]{2,1,0:T(8,128)(2,1)S(1)}, bf16[2,512,256]{2,1,0:T(8,128)(2,1)S(...) custom-call(s32[2]{0:T(128)S(1)} %pad_add_fusion.place, ...), custom_call_target="tpu_custom_call" | custom-call | flops 6000000000 | bytes 8000000 | tf_op jit(solution)/shard_map/frames/pallas_call | solution.py:219
  104.8 8.8 %collective-permute-start.30 = (f32[4,3,32,256]{3,2,1,0:T(8,128)S(1)}, f32[4,3,32,256]{3,2,1,0:T(8,128)S(1)}, u32[]{:S(2)}, u32[]{:S(2)}) collective-permute-start(f32[4,3,32,256]{3,2,1,0:T(8,128)S(1)} %get-tuple-element.43), channel_id=1, source_target_pairs={{0,1},{1,0},{2,3},{3,2},{4,5},{5,4},{6,7},{7,6},{8,9},{9,8},{10,11... | collective-permute-start | bytes 1179656 | tf_op jit(solution)/shard_map/ppermute | solution.py:305
  113.6 1.3 collective-permute-done.30
  115.1 0.3 collective-permute-start.31
  115.4 3.2 %collective-permute-start.33 = (f32[3,32,256]{2,1,0:T(8,128)S(1)}, f32[3,32,256]{2,1,0:T(8,128)S(1)}, u32[]{:S(2)}, u32[]{:S(2)}) collective-permute-start(f32[3,32,256]{2,1,0:T(8,128)S(1)} %get-tuple-element.45), channel_id=1, source_target_pairs={{0,6},{2,0},{4,2},{6,4},{1,7},{3,1},{5,3},{7,5},{8,14},{10,8},{12,... | collective-permute-start | bytes 294920 | tf_op jit(solution)/shard_map/ppermute | solution.py:301
  118.6 3.0 %collective-permute-done.31 = f32[3,32,256]{2,1,0:T(8,128)S(1)} collective-permute-done((f32[3,32,256]{2,1,0:T(8,128)S(1)}, f32[3,32,256]{2,1,0:T(8,128)S(1)}, u32[]{:S(2)}, u32[]{:S(2)}) %collective-permute-start.31) | collective-permute-done | bytes 98336 | tf_op jit(solution)/shard_map/ppermute | solution.py:301
  121.6 1.4 collective-permute-done.33
  123.0 1.7 %collective-permute-done.32 = f32[3,32,256]{2,1,0:T(8,128)S(1)} collective-permute-done((f32[3,32,256]{2,1,0:T(8,128)S(1)}, f32[3,32,256]{2,1,0:T(8,128)S(1)}, u32[]{:S(2)}, u32[]{:S(2)}) %collective-permute-start.32) | collective-permute-done | bytes 98336 | tf_op jit(solution)/shard_map/ppermute | solution.py:301
  124.8 2.4 %collective-permute-start.35 = (f32[3,32,256]{2,1,0:T(8,128)S(1)}, f32[3,32,256]{2,1,0:T(8,128)S(1)}, u32[]{:S(2)}, u32[]{:S(2)}) collective-permute-start(f32[3,32,256]{2,1,0:T(8,128)S(1)} %fusion.2), channel_id=1, source_target_pairs={{0,16},{8,24},{16,0},{24,8},{1,17},{9,25},{17,1},{25,9},{2,18},{10... | collective-permute-start | bytes 294920 | tf_op jit(solution)/shard_map/ppermute | solution.py:301
  127.2 1.3 collective-permute-start.34
  128.5 1.9 %collective-permute-done.36 = f32[3,32,256]{2,1,0:T(8,128)S(1)} collective-permute-done((f32[3,32,256]{2,1,0:T(8,128)S(1)}, f32[3,32,256]{2,1,0:T(8,128)S(1)}, u32[]{:S(2)}, u32[]{:S(2)}) %collective-permute-start.36) | collective-permute-done | bytes 98336 | tf_op jit(solution)/shard_map/ppermute | solution.py:301
  130.4 1.4 collective-permute-done.35
  131.8 1.5 collective-permute-done.34
  133.4 5.4 %collective-permute-start.38 = (f32[3,32,256]{2,1,0:T(8,128)S(1)}, f32[3,32,256]{2,1,0:T(8,128)S(1)}, u32[]{:S(2)}, u32[]{:S(2)}) collective-permute-start(f32[3,32,256]{2,1,0:T(8,128)S(1)} %add_add_fusion.1), channel_id=1, source_target_pairs={{0,64},{32,96},{64,0},{96,32},{1,65},{33,97},{65,1},{97,33},{2,66}... | collective-permute-start | bytes 294920 | tf_op jit(solution)/shard_map/ppermute | solution.py:301
  138.8 1.3 collective-permute-start.27
  140.1 4.5 %collective-permute-start.26 = (bf16[2,512,256]{2,1,0:T(8,128)(2,1)S(1)}, bf16[2,512,256]{2,1,0:T(8,128)(2,1)S(1)}, u32[]{:S(2)}, u32[]{:S(2)}) collective-permute-start(bf16[2,512,256]{2,1,0:T(8,128)(2,1)S(1)} %get-tuple-element.37), channel_id=1, source_target_pairs={{0,1},{1,2},{2,3},{3,4},{4,5},{5,6},{6,7},{8,9},{9,10},{10,11},{11... | collective-permute-start | bytes 1572872 | tf_op jit(solution)/shard_map/ppermute | solution.py:297
  144.7 1.7 %collective-permute-start.42 = (f32[2,32,256]{2,1,0:T(8,128)S(1)}, f32[2,32,256]{2,1,0:T(8,128)S(1)}, u32[]{:S(2)}, u32[]{:S(2)}) collective-permute-start(f32[2,32,256]{2,1,0:T(8,128)S(1)} %fusion.6), channel_id=1, source_target_pairs={{0,6},{2,0},{4,2},{6,4},{1,7},{3,1},{5,3},{7,5},{8,14},{10,8},{12,... | collective-permute-start | bytes 196616 | tf_op jit(solution)/shard_map/ppermute | solution.py:301
  146.5 1.0 collective-permute-start.41
  147.5 1.2 collective-permute-start.40
  148.8 1.9 %collective-permute-start.28 = (bf16[2,256,256]{2,1,0:T(8,128)(2,1)S(1)}, bf16[2,256,256]{2,1,0:T(8,128)(2,1)S(1)}, u32[]{:S(2)}, u32[]{:S(2)}) collective-permute-start(bf16[2,256,256]{2,1,0:T(8,128)(2,1)S(1)} %add_convert_fusion), channel_id=1, source_target_pairs={{0,8},{8,16},{16,24},{24,32},{32,40},{40,48},{48,56},{56,64},{64,7... | collective-permute-start | bytes 786440 | tf_op jit(solution)/shard_map/ppermute | solution.py:297
  150.7 2.3 %collective-permute-done.41 = f32[2,32,256]{2,1,0:T(8,128)S(1)} collective-permute-done((f32[2,32,256]{2,1,0:T(8,128)S(1)}, f32[2,32,256]{2,1,0:T(8,128)S(1)}, u32[]{:S(2)}, u32[]{:S(2)}) %collective-permute-start.41) | collective-permute-done | bytes 65568 | tf_op jit(solution)/shard_map/ppermute | solution.py:301
  153.0 0.3 collective-permute-done.40
  153.4 3.4 %collective-permute-start.43 = (f32[4,2,32,256]{3,2,1,0:T(8,128)S(1)}, f32[4,2,32,256]{3,2,1,0:T(8,128)S(1)}, u32[]{:S(2)}, u32[]{:S(2)}) collective-permute-start(f32[4,2,32,256]{3,2,1,0:T(8,128)S(1)} %pad_maximum_fusion.1.mine), channel_id=1, source_target_pairs={{0,1},{1,0},{2,3},{3,2},{4,5},{5,4},{6,7},{7,6},{8,9},{9,8},{10,11... | collective-permute-start | bytes 786440 | tf_op jit(solution)/shard_map/ppermute | solution.py:305
  156.8 1.9 %collective-permute-start.29 = (bf16[2,256,128]{2,1,0:T(8,128)(2,1)S(1)}, bf16[2,256,128]{2,1,0:T(8,128)(2,1)S(1)}, u32[]{:S(2)}, u32[]{:S(2)}) collective-permute-start(bf16[2,256,128]{2,1,0:T(8,128)(2,1)S(1)} %get-tuple-element.40), channel_id=1, source_target_pairs={{0,8},{8,16},{16,24},{24,32},{32,40},{40,48},{48,56},{56,64},{64,7... | collective-permute-start | bytes 393224 | tf_op jit(solution)/shard_map/ppermute | solution.py:297
  158.7 7.5 %collective-permute-done.29.low_right = bf16[2,256,128]{2,1,0:T(8,128)(2,1)S(1)} collective-permute-done((bf16[2,256,128]{2,1,0:T(8,128)(2,1)S(1)}, bf16[2,256,128]{2,1,0:T(8,128)(2,1)S(1)}, u32[]{:S(2)}, u32[]{:S(2)}) %collective-permute-start.29) | collective-permute-done | bytes 131104 | tf_op jit(solution)/shard_map/ppermute | solution.py:297
  166.2 2.3 %object_update.3 = f32[2,512,384]{2,1,0:T(8,128)} custom-call(f32[2,512,384]{2,1,0:T(8,128)S(1)} %copy-done.3, f32[2,512,384]{2,1,0:T(8,128)S(1)} %copy-done.4, bf16[2,512,256]{2,1,0:T(8,128)(2,1)S(1)} %collective-permute-done.26.left, bf16[2,256,256]{2,1,0:T(8,128)(2,1)S(1)} %collective-permute-done.28.low_left, ...), custom_call_target="tpu_custom_call" | custom-call | flops 2000000 | bytes 8000000 | tf_op jit(solution)/shard_map/object_update/pallas_call | solution.py:262
  168.5 0.7 copy-done.10
  169.2 1.9 %probe_whole.1 = f32[2,256,256]{2,1,0:T(8,128)} custom-call(s32[2]{0:T(128)} %copy-done.6, f32[4,2,32,256]{3,2,1,0:T(8,128)} %copy-done.9, f32[4,2,32,256]{3,2,1,0:T(8,128)} %copy-done.10), custom_call_target="tpu_custom_call" | custom-call | tf_op jit(solution)/shard_map/probe_whole/pallas_call | solution.py:286
  (79 shorter events, 1.0 us)
Async XLA Ops:
  0.6 17.5 %copy-start.7 = (bf16[512,512]{1,0:T(8,128)(2,1)S(1)}, bf16[512,512]{1,0:T(8,128)(2,1)}, u32[]{:S(2)}) copy-start(bf16[512,512]{1,0:T(8,128)(2,1)} %constant.23.clone.rest_3_.rest_4_) | copy-start | bytes 1572868
  0.6 17.4 %copy-start.8 = (bf16[512,512]{1,0:T(8,128)(2,1)S(1)}, bf16[512,512]{1,0:T(8,128)(2,1)}, u32[]{:S(2)}) copy-start(bf16[512,512]{1,0:T(8,128)(2,1)} %constant.22.clone.rest_2_.rest_3_) | copy-start | bytes 1572868
  0.7 15.3 %copy-start.11 = (s32[2,2,12]{2,1,0:T(2,128)S(1)}, s32[2,2,12]{2,1,0:T(2,128)}, u32[]{:S(2)}) copy-start(s32[2,2,12]{2,1,0:T(2,128)} %param.10) | copy-start | bytes 580
  0.7 15.4 %copy-start.12 = (s32[2,1,1]{0,2,1:T(1,128)S(1)}, s32[2,1,1]{0,2,1:T(1,128)}, u32[]{:S(2)}) copy-start(s32[2,1,1]{0,2,1:T(1,128)} %param.11) | copy-start | bytes 28
  0.7 17.4 %copy-start.5 = (f32[2,256,256]{2,1,0:T(8,128)S(1)}, f32[2,256,256]{2,1,0:T(8,128)}, u32[]{:S(2)}) copy-start(f32[2,256,256]{2,1,0:T(8,128)} %rest_0_.1) | copy-start | bytes 1572868
  2.3 12.3 %collective-permute-start = (bf16[2,256,256]{2,1,0:T(8,128)(2,1)S(1)}, bf16[2,256,256]{2,1,0:T(8,128)(2,1)S(1)}, u32[]{:S(2)}, u32[]{:S(2)}) collective-permute-start(bf16[2,256,256]{2,1,0:T(8,128)(2,1)S(1)} %slice.79), channel_id=1, source_target_pairs={{8,0},{16,8},{24,16},{32,24},{40,32},{48,40},{56,48},{64,56},{72,6... | collective-permute-start | bytes 786440 | tf_op jit(solution)/shard_map/ppermute | solution.py:297
  8.6 9.5 %collective-permute-start.2 = (bf16[2,512,256]{2,1,0:T(8,128)(2,1)S(1)}, bf16[2,512,256]{2,1,0:T(8,128)(2,1)S(1)}, u32[]{:S(2)}, u32[]{:S(2)}) collective-permute-start(bf16[2,512,256]{2,1,0:T(8,128)(2,1)S(1)} %slice.81), channel_id=1, source_target_pairs={{1,0},{2,1},{3,2},{4,3},{5,4},{6,5},{7,6},{9,8},{10,9},{11,10},{12... | collective-permute-start | bytes 1572872 | tf_op jit(solution)/shard_map/ppermute | solution.py:297
  9.9 8.1 %collective-permute-start.1 = (bf16[2,256,128]{2,1,0:T(8,128)(2,1)S(1)}, bf16[2,256,128]{2,1,0:T(8,128)(2,1)S(1)}, u32[]{:S(2)}, u32[]{:S(2)}) collective-permute-start(bf16[2,256,128]{2,1,0:T(8,128)(2,1)S(1)} %slice.80), channel_id=1, source_target_pairs={{8,0},{16,8},{24,16},{32,24},{40,32},{48,40},{56,48},{64,56},{72,6... | collective-permute-start | bytes 393224 | tf_op jit(solution)/shard_map/ppermute | solution.py:297
  14.7 3.4 %collective-permute-start.3 = (bf16[2,256,256]{2,1,0:T(8,128)(2,1)S(1)}, bf16[2,256,256]{2,1,0:T(8,128)(2,1)S(1)}, u32[]{:S(2)}, u32[]{:S(2)}) collective-permute-start(bf16[2,256,256]{2,1,0:T(8,128)(2,1)S(1)} %collective-permute-done.below_left), channel_id=1, source_target_pairs={{1,0},{2,1},{3,2},{4,3},{5,4},{6,5},{7,6},{9,8},{10,9},{11,10},{12... | collective-permute-start | bytes 786440 | tf_op jit(solution)/shard_map/ppermute | solution.py:297
  16.1 81.8 %copy-start.6 = (s32[2]{0:T(128)}, s32[2]{0:T(128)S(1)}, u32[]{:S(2)}) copy-start(s32[2]{0:T(128)S(1)} %pad_add_fusion.place) | copy-start | bytes 28
  24.9 15.4 %collective-permute-start.8 = (f32[4,3,32,256]{3,2,1,0:T(8,128)S(1)}, f32[4,3,32,256]{3,2,1,0:T(8,128)S(1)}, u32[]{:S(2)}, u32[]{:S(2)}) collective-permute-start(f32[4,3,32,256]{3,2,1,0:T(8,128)S(1)} %get-tuple-element.30), channel_id=1, source_target_pairs={{0,1},{1,0},{2,3},{3,2},{4,5},{5,4},{6,7},{7,6},{8,9},{9,8},{10,11... | collective-permute-start | bytes 1179656 | tf_op jit(solution)/shard_map/ppermute | solution.py:305
  28.8 18.2 %collective-permute-start.5 = (bf16[2,256,256]{2,1,0:T(8,128)(2,1)S(1)}, bf16[2,256,256]{2,1,0:T(8,128)(2,1)S(1)}, u32[]{:S(2)}, u32[]{:S(2)}) collective-permute-start(bf16[2,256,256]{2,1,0:T(8,128)(2,1)S(1)} %get-tuple-element.26), channel_id=1, source_target_pairs={{0,1},{1,2},{2,3},{3,4},{4,5},{5,6},{6,7},{8,9},{9,10},{10,11},{11... | collective-permute-start | bytes 786440 | tf_op jit(solution)/shard_map/ppermute | solution.py:297
  30.7 27.7 %collective-permute-start.7 = (bf16[2,256,128]{2,1,0:T(8,128)(2,1)S(1)}, bf16[2,256,128]{2,1,0:T(8,128)(2,1)S(1)}, u32[]{:S(2)}, u32[]{:S(2)}) collective-permute-start(bf16[2,256,128]{2,1,0:T(8,128)(2,1)S(1)} %get-tuple-element.27), channel_id=1, source_target_pairs={{0,8},{8,16},{16,24},{24,32},{32,40},{40,48},{48,56},{56,64},{64,7... | collective-permute-start | bytes 393224 | tf_op jit(solution)/shard_map/ppermute | solution.py:297
  38.7 23.1 %collective-permute-start.4 = (bf16[2,512,256]{2,1,0:T(8,128)(2,1)S(1)}, bf16[2,512,256]{2,1,0:T(8,128)(2,1)S(1)}, u32[]{:S(2)}, u32[]{:S(2)}) collective-permute-start(bf16[2,512,256]{2,1,0:T(8,128)(2,1)S(1)} %get-tuple-element.24), channel_id=1, source_target_pairs={{0,1},{1,2},{2,3},{3,4},{4,5},{5,6},{6,7},{8,9},{9,10},{10,11},{11... | collective-permute-start | bytes 1572872 | tf_op jit(solution)/shard_map/ppermute | solution.py:297
  40.4 25.3 %copy-start = (f32[2,512,384]{2,1,0:T(8,128)S(1)}, f32[2,512,384]{2,1,0:T(8,128)}, u32[]{:S(2)}) copy-start(f32[2,512,384]{2,1,0:T(8,128)} %obj.3) | copy-start | bytes 4718596
  40.4 25.3 %copy-start.1 = (f32[2,512,384]{2,1,0:T(8,128)S(1)}, f32[2,512,384]{2,1,0:T(8,128)}, u32[]{:S(2)}) copy-start(f32[2,512,384]{2,1,0:T(8,128)} %get-tuple-element.23.own) | copy-start | bytes 4718596
  40.5 9.2 %collective-permute-start.9 = (f32[3,32,256]{2,1,0:T(8,128)S(1)}, f32[3,32,256]{2,1,0:T(8,128)S(1)}, u32[]{:S(2)}, u32[]{:S(2)}) collective-permute-start(f32[3,32,256]{2,1,0:T(8,128)S(1)} %get-tuple-element.47), channel_id=1, source_target_pairs={{0,2},{2,4},{4,6},{6,0},{1,3},{3,5},{5,7},{7,1},{8,10},{10,12},{12... | collective-permute-start | bytes 294920 | tf_op jit(solution)/shard_map/ppermute | solution.py:301
  47.0 6.6 %collective-permute-start.11 = (f32[3,32,256]{2,1,0:T(8,128)S(1)}, f32[3,32,256]{2,1,0:T(8,128)S(1)}, u32[]{:S(2)}, u32[]{:S(2)}) collective-permute-start(f32[3,32,256]{2,1,0:T(8,128)S(1)} %get-tuple-element.48), channel_id=1, source_target_pairs={{0,6},{2,0},{4,2},{6,4},{1,7},{3,1},{5,3},{7,5},{8,14},{10,8},{12,... | collective-permute-start | bytes 294920 | tf_op jit(solution)/shard_map/ppermute | solution.py:301
  47.0 7.2 %collective-permute-start.10 = (f32[3,32,256]{2,1,0:T(8,128)S(1)}, f32[3,32,256]{2,1,0:T(8,128)S(1)}, u32[]{:S(2)}, u32[]{:S(2)}) collective-permute-start(f32[3,32,256]{2,1,0:T(8,128)S(1)} %get-tuple-element.49), channel_id=1, source_target_pairs={{0,4},{2,6},{4,0},{6,2},{1,5},{3,7},{5,1},{7,3},{8,12},{10,14},{12... | collective-permute-start | bytes 294920 | tf_op jit(solution)/shard_map/ppermute | solution.py:301
  49.7 12.1 %collective-permute-start.6 = (bf16[2,256,256]{2,1,0:T(8,128)(2,1)S(1)}, bf16[2,256,256]{2,1,0:T(8,128)(2,1)S(1)}, u32[]{:S(2)}, u32[]{:S(2)}) collective-permute-start(bf16[2,256,256]{2,1,0:T(8,128)(2,1)S(1)} %add_convert_fusion.1), channel_id=1, source_target_pairs={{0,8},{8,16},{16,24},{24,32},{32,40},{40,48},{48,56},{56,64},{64,7... | collective-permute-start | bytes 786440 | tf_op jit(solution)/shard_map/ppermute | solution.py:297
  54.2 7.6 %collective-permute-start.14 = (f32[3,32,256]{2,1,0:T(8,128)S(1)}, f32[3,32,256]{2,1,0:T(8,128)S(1)}, u32[]{:S(2)}, u32[]{:S(2)}) collective-permute-start(f32[3,32,256]{2,1,0:T(8,128)S(1)} %fusion.5.rest_0_), channel_id=1, source_target_pairs={{0,24},{8,0},{16,8},{24,16},{1,25},{9,1},{17,9},{25,17},{2,26},{10... | collective-permute-start | bytes 294920 | tf_op jit(solution)/shard_map/ppermute | solution.py:301
  54.3 7.9 %collective-permute-start.13 = (f32[3,32,256]{2,1,0:T(8,128)S(1)}, f32[3,32,256]{2,1,0:T(8,128)S(1)}, u32[]{:S(2)}, u32[]{:S(2)}) collective-permute-start(f32[3,32,256]{2,1,0:T(8,128)S(1)} %fusion.5.rest_0_), channel_id=1, source_target_pairs={{0,16},{8,24},{16,0},{24,8},{1,17},{9,25},{17,1},{25,9},{2,18},{10... | collective-permute-start | bytes 294920 | tf_op jit(solution)/shard_map/ppermute | solution.py:301
  58.4 7.3 %collective-permute-start.12 = (f32[3,32,256]{2,1,0:T(8,128)S(1)}, f32[3,32,256]{2,1,0:T(8,128)S(1)}, u32[]{:S(2)}, u32[]{:S(2)}) collective-permute-start(f32[3,32,256]{2,1,0:T(8,128)S(1)} %fusion.5.rest_0_), channel_id=1, source_target_pairs={{0,8},{8,16},{16,24},{24,0},{1,9},{9,17},{17,25},{25,1},{2,10},{10... | collective-permute-start | bytes 294920 | tf_op jit(solution)/shard_map/ppermute | solution.py:301
  66.8 1.1 copy-start.2
  68.0 8.9 %collective-permute-start.21 = (f32[3,32,256]{2,1,0:T(8,128)S(1)}, f32[3,32,256]{2,1,0:T(8,128)S(1)}, u32[]{:S(2)}, u32[]{:S(2)}) collective-permute-start(f32[3,32,256]{2,1,0:T(8,128)S(1)} %get-tuple-element.35), channel_id=1, source_target_pairs={{0,96},{32,0},{64,32},{96,64},{1,97},{33,1},{65,33},{97,65},{2,98}... | collective-permute-start | bytes 294920 | tf_op jit(solution)/shard_map/ppermute | solution.py:301
  70.7 6.2 %collective-permute-start.20 = (f32[3,32,256]{2,1,0:T(8,128)S(1)}, f32[3,32,256]{2,1,0:T(8,128)S(1)}, u32[]{:S(2)}, u32[]{:S(2)}) collective-permute-start(f32[3,32,256]{2,1,0:T(8,128)S(1)} %get-tuple-element.35), channel_id=1, source_target_pairs={{0,64},{32,96},{64,0},{96,32},{1,65},{33,97},{65,1},{97,33},{2,66}... | collective-permute-start | bytes 294920 | tf_op jit(solution)/shard_map/ppermute | solution.py:301
  70.7 6.2 %collective-permute-start.19 = (f32[3,32,256]{2,1,0:T(8,128)S(1)}, f32[3,32,256]{2,1,0:T(8,128)S(1)}, u32[]{:S(2)}, u32[]{:S(2)}) collective-permute-start(f32[3,32,256]{2,1,0:T(8,128)S(1)} %get-tuple-element.35), channel_id=1, source_target_pairs={{0,32},{32,64},{64,96},{96,0},{1,33},{33,65},{65,97},{97,1},{2,34}... | collective-permute-start | bytes 294920 | tf_op jit(solution)/shard_map/ppermute | solution.py:301
  73.3 15.3 %collective-permute-start.15 = (bf16[2,256,256]{2,1,0:T(8,128)(2,1)S(1)}, bf16[2,256,256]{2,1,0:T(8,128)(2,1)S(1)}, u32[]{:S(2)}, u32[]{:S(2)}) collective-permute-start(bf16[2,256,256]{2,1,0:T(8,128)(2,1)S(1)} %get-tuple-element.32), channel_id=1, source_target_pairs={{8,0},{16,8},{24,16},{32,24},{40,32},{48,40},{56,48},{64,56},{72,6... | collective-permute-start | bytes 786440 | tf_op jit(solution)/shard_map/ppermute | solution.py:297
  75.5 22.3 %collective-permute-start.17 = (bf16[2,512,256]{2,1,0:T(8,128)(2,1)S(1)}, bf16[2,512,256]{2,1,0:T(8,128)(2,1)S(1)}, u32[]{:S(2)}, u32[]{:S(2)}) collective-permute-start(bf16[2,512,256]{2,1,0:T(8,128)(2,1)S(1)} %get-tuple-element.34), channel_id=1, source_target_pairs={{1,0},{2,1},{3,2},{4,3},{5,4},{6,5},{7,6},{9,8},{10,9},{11,10},{12... | collective-permute-start | bytes 1572872 | tf_op jit(solution)/shard_map/ppermute | solution.py:297
  76.9 11.6 %collective-permute-start.24 = (f32[2,32,256]{2,1,0:T(8,128)S(1)}, f32[2,32,256]{2,1,0:T(8,128)S(1)}, u32[]{:S(2)}, u32[]{:S(2)}) collective-permute-start(f32[2,32,256]{2,1,0:T(8,128)S(1)} %fusion.7), channel_id=1, source_target_pairs={{0,6},{2,0},{4,2},{6,4},{1,7},{3,1},{5,3},{7,5},{8,14},{10,8},{12,... | collective-permute-start | bytes 196616 | tf_op jit(solution)/shard_map/ppermute | solution.py:301
  80.5 8.0 %collective-permute-start.23 = (f32[2,32,256]{2,1,0:T(8,128)S(1)}, f32[2,32,256]{2,1,0:T(8,128)S(1)}, u32[]{:S(2)}, u32[]{:S(2)}) collective-permute-start(f32[2,32,256]{2,1,0:T(8,128)S(1)} %fusion.7), channel_id=1, source_target_pairs={{0,4},{2,6},{4,0},{6,2},{1,5},{3,7},{5,1},{7,3},{8,12},{10,14},{12... | collective-permute-start | bytes 196616 | tf_op jit(solution)/shard_map/ppermute | solution.py:301
  82.5 6.0 %collective-permute-start.22 = (f32[2,32,256]{2,1,0:T(8,128)S(1)}, f32[2,32,256]{2,1,0:T(8,128)S(1)}, u32[]{:S(2)}, u32[]{:S(2)}) collective-permute-start(f32[2,32,256]{2,1,0:T(8,128)S(1)} %fusion.7), channel_id=1, source_target_pairs={{0,2},{2,4},{4,6},{6,0},{1,3},{3,5},{5,7},{7,1},{8,10},{10,12},{12... | collective-permute-start | bytes 196616 | tf_op jit(solution)/shard_map/ppermute | solution.py:301
  88.5 9.3 %collective-permute-start.25 = (f32[4,2,32,256]{3,2,1,0:T(8,128)S(1)}, f32[4,2,32,256]{3,2,1,0:T(8,128)S(1)}, u32[]{:S(2)}, u32[]{:S(2)}) collective-permute-start(f32[4,2,32,256]{3,2,1,0:T(8,128)S(1)} %pad_maximum_fusion.rest_0_), channel_id=1, source_target_pairs={{0,1},{1,0},{2,3},{3,2},{4,5},{5,4},{6,7},{7,6},{8,9},{9,8},{10,11... | collective-permute-start | bytes 786440 | tf_op jit(solution)/shard_map/ppermute | solution.py:305
  88.6 9.2 %collective-permute-start.18 = (bf16[2,256,256]{2,1,0:T(8,128)(2,1)S(1)}, bf16[2,256,256]{2,1,0:T(8,128)(2,1)S(1)}, u32[]{:S(2)}, u32[]{:S(2)}) collective-permute-start(bf16[2,256,256]{2,1,0:T(8,128)(2,1)S(1)} %collective-permute-done.15.below_left), channel_id=1, source_target_pairs={{1,0},{2,1},{3,2},{4,3},{5,4},{6,5},{7,6},{9,8},{10,9},{11,10},{12... | collective-permute-start | bytes 786440 | tf_op jit(solution)/shard_map/ppermute | solution.py:297
  89.9 7.9 %collective-permute-start.16 = (bf16[2,256,128]{2,1,0:T(8,128)(2,1)S(1)}, bf16[2,256,128]{2,1,0:T(8,128)(2,1)S(1)}, u32[]{:S(2)}, u32[]{:S(2)}) collective-permute-start(bf16[2,256,128]{2,1,0:T(8,128)(2,1)S(1)} %get-tuple-element.33), channel_id=1, source_target_pairs={{8,0},{16,8},{24,16},{32,24},{40,32},{48,40},{56,48},{64,56},{72,6... | collective-permute-start | bytes 393224 | tf_op jit(solution)/shard_map/ppermute | solution.py:297
  104.8 10.2 %collective-permute-start.30 = (f32[4,3,32,256]{3,2,1,0:T(8,128)S(1)}, f32[4,3,32,256]{3,2,1,0:T(8,128)S(1)}, u32[]{:S(2)}, u32[]{:S(2)}) collective-permute-start(f32[4,3,32,256]{3,2,1,0:T(8,128)S(1)} %get-tuple-element.43), channel_id=1, source_target_pairs={{0,1},{1,0},{2,3},{3,2},{4,5},{5,4},{6,7},{7,6},{8,9},{9,8},{10,11... | collective-permute-start | bytes 1179656 | tf_op jit(solution)/shard_map/ppermute | solution.py:305
  115.1 6.6 %collective-permute-start.31 = (f32[3,32,256]{2,1,0:T(8,128)S(1)}, f32[3,32,256]{2,1,0:T(8,128)S(1)}, u32[]{:S(2)}, u32[]{:S(2)}) collective-permute-start(f32[3,32,256]{2,1,0:T(8,128)S(1)} %get-tuple-element.44), channel_id=1, source_target_pairs={{0,2},{2,4},{4,6},{6,0},{1,3},{3,5},{5,7},{7,1},{8,10},{10,12},{12... | collective-permute-start | bytes 294920 | tf_op jit(solution)/shard_map/ppermute | solution.py:301
  115.4 7.6 %collective-permute-start.33 = (f32[3,32,256]{2,1,0:T(8,128)S(1)}, f32[3,32,256]{2,1,0:T(8,128)S(1)}, u32[]{:S(2)}, u32[]{:S(2)}) collective-permute-start(f32[3,32,256]{2,1,0:T(8,128)S(1)} %get-tuple-element.45), channel_id=1, source_target_pairs={{0,6},{2,0},{4,2},{6,4},{1,7},{3,1},{5,3},{7,5},{8,14},{10,8},{12,... | collective-permute-start | bytes 294920 | tf_op jit(solution)/shard_map/ppermute | solution.py:301
  118.6 47.6 %copy-start.3 = (f32[2,512,384]{2,1,0:T(8,128)S(1)}, f32[2,512,384]{2,1,0:T(8,128)}, u32[]{:S(2)}) copy-start(f32[2,512,384]{2,1,0:T(8,128)} %copy-done.2) | copy-start | bytes 4718596
  118.6 47.6 %copy-start.4 = (f32[2,512,384]{2,1,0:T(8,128)S(1)}, f32[2,512,384]{2,1,0:T(8,128)}, u32[]{:S(2)}) copy-start(f32[2,512,384]{2,1,0:T(8,128)} %get-tuple-element.36.own) | copy-start | bytes 4718596
  118.6 6.1 %collective-permute-start.32 = (f32[3,32,256]{2,1,0:T(8,128)S(1)}, f32[3,32,256]{2,1,0:T(8,128)S(1)}, u32[]{:S(2)}, u32[]{:S(2)}) collective-permute-start(f32[3,32,256]{2,1,0:T(8,128)S(1)} %get-tuple-element.46), channel_id=1, source_target_pairs={{0,4},{2,6},{4,0},{6,2},{1,5},{3,7},{5,1},{7,3},{8,12},{10,14},{12... | collective-permute-start | bytes 294920 | tf_op jit(solution)/shard_map/ppermute | solution.py:301
  124.7 5.7 %collective-permute-start.36 = (f32[3,32,256]{2,1,0:T(8,128)S(1)}, f32[3,32,256]{2,1,0:T(8,128)S(1)}, u32[]{:S(2)}, u32[]{:S(2)}) collective-permute-start(f32[3,32,256]{2,1,0:T(8,128)S(1)} %fusion.2), channel_id=1, source_target_pairs={{0,24},{8,0},{16,8},{24,16},{1,25},{9,1},{17,9},{25,17},{2,26},{10... | collective-permute-start | bytes 294920 | tf_op jit(solution)/shard_map/ppermute | solution.py:301
  124.8 7.0 %collective-permute-start.35 = (f32[3,32,256]{2,1,0:T(8,128)S(1)}, f32[3,32,256]{2,1,0:T(8,128)S(1)}, u32[]{:S(2)}, u32[]{:S(2)}) collective-permute-start(f32[3,32,256]{2,1,0:T(8,128)S(1)} %fusion.2), channel_id=1, source_target_pairs={{0,16},{8,24},{16,0},{24,8},{1,17},{9,25},{17,1},{25,9},{2,18},{10... | collective-permute-start | bytes 294920 | tf_op jit(solution)/shard_map/ppermute | solution.py:301
  127.2 6.1 %collective-permute-start.34 = (f32[3,32,256]{2,1,0:T(8,128)S(1)}, f32[3,32,256]{2,1,0:T(8,128)S(1)}, u32[]{:S(2)}, u32[]{:S(2)}) collective-permute-start(f32[3,32,256]{2,1,0:T(8,128)S(1)} %fusion.2), channel_id=1, source_target_pairs={{0,8},{8,16},{16,24},{24,0},{1,9},{9,17},{17,25},{25,1},{2,10},{10... | collective-permute-start | bytes 294920 | tf_op jit(solution)/shard_map/ppermute | solution.py:301
  133.3 11.3 %collective-permute-start.39 = (f32[3,32,256]{2,1,0:T(8,128)S(1)}, f32[3,32,256]{2,1,0:T(8,128)S(1)}, u32[]{:S(2)}, u32[]{:S(2)}) collective-permute-start(f32[3,32,256]{2,1,0:T(8,128)S(1)} %add_add_fusion.1), channel_id=1, source_target_pairs={{0,96},{32,0},{64,32},{96,64},{1,97},{33,1},{65,33},{97,65},{2,98}... | collective-permute-start | bytes 294920 | tf_op jit(solution)/shard_map/ppermute | solution.py:301
  133.4 11.2 %collective-permute-start.38 = (f32[3,32,256]{2,1,0:T(8,128)S(1)}, f32[3,32,256]{2,1,0:T(8,128)S(1)}, u32[]{:S(2)}, u32[]{:S(2)}) collective-permute-start(f32[3,32,256]{2,1,0:T(8,128)S(1)} %add_add_fusion.1), channel_id=1, source_target_pairs={{0,64},{32,96},{64,0},{96,32},{1,65},{33,97},{65,1},{97,33},{2,66}... | collective-permute-start | bytes 294920 | tf_op jit(solution)/shard_map/ppermute | solution.py:301
  138.8 5.8 %collective-permute-start.37 = (f32[3,32,256]{2,1,0:T(8,128)S(1)}, f32[3,32,256]{2,1,0:T(8,128)S(1)}, u32[]{:S(2)}, u32[]{:S(2)}) collective-permute-start(f32[3,32,256]{2,1,0:T(8,128)S(1)} %add_add_fusion.1), channel_id=1, source_target_pairs={{0,32},{32,64},{64,96},{96,0},{1,33},{33,65},{65,97},{97,1},{2,34}... | collective-permute-start | bytes 294920 | tf_op jit(solution)/shard_map/ppermute | solution.py:301
  138.8 9.9 %collective-permute-start.27 = (bf16[2,256,256]{2,1,0:T(8,128)(2,1)S(1)}, bf16[2,256,256]{2,1,0:T(8,128)(2,1)S(1)}, u32[]{:S(2)}, u32[]{:S(2)}) collective-permute-start(bf16[2,256,256]{2,1,0:T(8,128)(2,1)S(1)} %get-tuple-element.39), channel_id=1, source_target_pairs={{0,1},{1,2},{2,3},{3,4},{4,5},{5,6},{6,7},{8,9},{9,10},{10,11},{11... | collective-permute-start | bytes 786440 | tf_op jit(solution)/shard_map/ppermute | solution.py:297
  140.1 26.1 %collective-permute-start.26 = (bf16[2,512,256]{2,1,0:T(8,128)(2,1)S(1)}, bf16[2,512,256]{2,1,0:T(8,128)(2,1)S(1)}, u32[]{:S(2)}, u32[]{:S(2)}) collective-permute-start(bf16[2,512,256]{2,1,0:T(8,128)(2,1)S(1)} %get-tuple-element.37), channel_id=1, source_target_pairs={{0,1},{1,2},{2,3},{3,4},{4,5},{5,6},{6,7},{8,9},{9,10},{10,11},{11... | collective-permute-start | bytes 1572872 | tf_op jit(solution)/shard_map/ppermute | solution.py:297
  144.7 6.0 %collective-permute-start.42 = (f32[2,32,256]{2,1,0:T(8,128)S(1)}, f32[2,32,256]{2,1,0:T(8,128)S(1)}, u32[]{:S(2)}, u32[]{:S(2)}) collective-permute-start(f32[2,32,256]{2,1,0:T(8,128)S(1)} %fusion.6), channel_id=1, source_target_pairs={{0,6},{2,0},{4,2},{6,4},{1,7},{3,1},{5,3},{7,5},{8,14},{10,8},{12,... | collective-permute-start | bytes 196616 | tf_op jit(solution)/shard_map/ppermute | solution.py:301
  146.5 6.5 %collective-permute-start.41 = (f32[2,32,256]{2,1,0:T(8,128)S(1)}, f32[2,32,256]{2,1,0:T(8,128)S(1)}, u32[]{:S(2)}, u32[]{:S(2)}) collective-permute-start(f32[2,32,256]{2,1,0:T(8,128)S(1)} %fusion.6), channel_id=1, source_target_pairs={{0,4},{2,6},{4,0},{6,2},{1,5},{3,7},{5,1},{7,3},{8,12},{10,14},{12... | collective-permute-start | bytes 196616 | tf_op jit(solution)/shard_map/ppermute | solution.py:301
  147.5 5.9 %collective-permute-start.40 = (f32[2,32,256]{2,1,0:T(8,128)S(1)}, f32[2,32,256]{2,1,0:T(8,128)S(1)}, u32[]{:S(2)}, u32[]{:S(2)}) collective-permute-start(f32[2,32,256]{2,1,0:T(8,128)S(1)} %fusion.6), channel_id=1, source_target_pairs={{0,2},{2,4},{4,6},{6,0},{1,3},{3,5},{5,7},{7,1},{8,10},{10,12},{12... | collective-permute-start | bytes 196616 | tf_op jit(solution)/shard_map/ppermute | solution.py:301
  148.8 17.4 %collective-permute-start.28 = (bf16[2,256,256]{2,1,0:T(8,128)(2,1)S(1)}, bf16[2,256,256]{2,1,0:T(8,128)(2,1)S(1)}, u32[]{:S(2)}, u32[]{:S(2)}) collective-permute-start(bf16[2,256,256]{2,1,0:T(8,128)(2,1)S(1)} %add_convert_fusion), channel_id=1, source_target_pairs={{0,8},{8,16},{16,24},{24,32},{32,40},{40,48},{48,56},{56,64},{64,7... | collective-permute-start | bytes 786440 | tf_op jit(solution)/shard_map/ppermute | solution.py:297
  153.3 15.1 %copy-start.9 = (f32[4,2,32,256]{3,2,1,0:T(8,128)}, f32[4,2,32,256]{3,2,1,0:T(8,128)S(1)}, u32[]{:S(2)}) copy-start(f32[4,2,32,256]{3,2,1,0:T(8,128)S(1)} %pad_maximum_fusion.1.mine) | copy-start | bytes 786436
  153.4 15.1 %collective-permute-start.43 = (f32[4,2,32,256]{3,2,1,0:T(8,128)S(1)}, f32[4,2,32,256]{3,2,1,0:T(8,128)S(1)}, u32[]{:S(2)}, u32[]{:S(2)}) collective-permute-start(f32[4,2,32,256]{3,2,1,0:T(8,128)S(1)} %pad_maximum_fusion.1.mine), channel_id=1, source_target_pairs={{0,1},{1,0},{2,3},{3,2},{4,5},{5,4},{6,7},{7,6},{8,9},{9,8},{10,11... | collective-permute-start | bytes 786440 | tf_op jit(solution)/shard_map/ppermute | solution.py:305
  156.8 9.4 %collective-permute-start.29 = (bf16[2,256,128]{2,1,0:T(8,128)(2,1)S(1)}, bf16[2,256,128]{2,1,0:T(8,128)(2,1)S(1)}, u32[]{:S(2)}, u32[]{:S(2)}) collective-permute-start(bf16[2,256,128]{2,1,0:T(8,128)(2,1)S(1)} %get-tuple-element.40), channel_id=1, source_target_pairs={{0,8},{8,16},{16,24},{24,32},{32,40},{40,48},{48,56},{56,64},{64,7... | collective-permute-start | bytes 393224 | tf_op jit(solution)/shard_map/ppermute | solution.py:297
  168.5 0.7 copy-start.10

commit v4 on v3

--- a/solution.py
+++ b/solution.py
@@ -34,23 +34,23 @@
 
 def frames_kernel(
     iteration, n_pieces,
-    place, counts, pos, obj, below_left, below_right, right, corner, *rest,
+    place, counts, pos, obj, below, right, corner, *rest,
 ):
     pieces, (amps, tab_a, tab_b), rest = rest[:n_pieces], rest[n_pieces : n_pieces + 3], rest[n_pieces + 3 :]
     own_out, low_left, low_right, right_out, corner_out, keep_out, send_out, step_out = rest[:8]
     ext, acc, sums, wave, mis, patch, levels, arrived, here, *rest = rest[8:]
-    landing, probe_scratch = rest[: 7 + n_pieces], rest[7 + n_pieces :]
+    landing, probe_scratch = rest[: 6 + n_pieces], rest[6 + n_pieces :]
     count = counts[0]
     copies = [
         pltpu.make_async_copy(source, target, here.at[i])
         for i, (source, target) in enumerate(
-            zip((obj, below_left, below_right, right, corner, *pieces, tab_a, tab_b), landing)
+            zip((obj, below, right, corner, *pieces, tab_a, tab_b), landing)
         )
     ]
     for copy in copies:
         copy.start()
-    obj, below_left, below_right, right, corner = landing[:5]
-    pieces, (table_a, table_b) = landing[5 : 5 + n_pieces], landing[5 + n_pieces :]
+    obj, below, right, corner = landing[:4]
+    pieces, (table_a, table_b) = landing[4 : 4 + n_pieces], landing[4 + n_pieces :]
 
     def fetch(index):
         return pltpu.make_async_copy(amps.at[iteration, index], levels.at[index], arrived.at[index])
@@ -67,17 +67,16 @@
     acc[...] = jnp.zeros_like(acc)
     sums[...] = jnp.zeros_like(sums)
     copies[0].wait()
-    for copy in copies[1:5]:
+    for copy in copies[1:4]:
         copy.wait()
     for j in range(all_tiles):
         inside = j < inner_tiles
         at = (j if inside else j - inner_tiles) * LANES
         upper = obj if inside else right
         ext[:, j, :rows, :] = upper[:, :, at : at + LANES].astype(BF).astype(F32)
-        lower = (below_left if j < left_tiles else below_right) if inside else corner
-        at = at if j < left_tiles or not inside else at - size
+        lower = below if inside else corner
         ext[:, j, rows:, :] = lower[:, :, at : at + LANES].astype(F32)
-    for copy in copies[5:]:
+    for copy in copies[4:]:
         copy.wait()
     core, y = place[0], place[1]
     half, quarter = size // N_CORE, size // (N_CORE * N_Y)
@@ -219,7 +218,7 @@
     return pl.pallas_call(
         functools.partial(frames_kernel, iteration, len(pieces)),
         out_shape=shapes,
-        in_specs=[smem] * 3 + [pl.BlockSpec(memory_space=pltpu.HBM)] * (8 + len(pieces)),
+        in_specs=[smem] * 3 + [pl.BlockSpec(memory_space=pltpu.HBM)] * (7 + len(pieces)),
         out_specs=[vmem] * 7 + [smem],
         scratch_shapes=scratch,
         compiler_params=pltpu.CompilerParams(vmem_limit_bytes=48 << 20),
@@ -228,46 +227,58 @@
     )(place, counts, pos, obj, *halos, *pieces, amps, *tables)
 
 
-def update_kernel(with_sum, obj, own, left, low_left, low_right, step, *rest):
-    if with_sum:
-        totals, (obj_out, halo_left, halo_right, right_out, total_out) = rest[:4], rest[4:]
-        total_out[...] = totals[0][...] + totals[1][...] + totals[2][...] + totals[3][...]
-    else:
-        (obj_out,) = rest
+def spec(space):
+    return pl.BlockSpec(memory_space=space)
+
+
+def small_call(body, shapes, operands, name, limit=16):
+    spaces = [pltpu.SMEM if v.size <= 2 else pltpu.VMEM for v in operands[0]] + [pl.ANY] * len(operands[1])
+    return pl.pallas_call(
+        body,
+        out_shape=shapes,
+        in_specs=[spec(space) for space in spaces],
+        out_specs=[spec(pltpu.VMEM)] * len(shapes),
+        compiler_params=pltpu.CompilerParams(vmem_limit_bytes=limit << 20),
+        cost_estimate=pl.CostEstimate(flops=2_000_000, bytes_accessed=4_000_000, transcendentals=0),
+        name=name,
+    )(*operands[0], *operands[1])
+
+
+def y_kernel(a, b, c, d, low_left, low_right, corner, total, down):
+    size = low_left.shape[2]
+    total[...] = a[0] + b[...] + c[...] + d[...]
+    down[:, :, :size] = (low_left[...] + corner[...].astype(F32)).astype(BF)
+    down[:, :, size:] = low_right[...]
+
+
+def z_kernel(a, b, c, d, waited, total):
+    total[...] = a[...] + b[...] + c[...] + d[...]
+
+
+def probe_step(a, b, c, d, mine, fresh):
+    total = a[...] + b[...] + c[...] + d[...]
+    fresh[...] = mine[...] - total[:2] / (total[2:] + 1.0)
+
+
+def x_kernel(a, b, c, d, mine, waited, fresh):
+    probe_step(a, b, c, d, mine, fresh)
+
+
+def object_step(obj, own, left, down, step, obj_out):
     size = left.shape[2]
     alpha = step[0, 0]
     obj_out[:, :, :size] = obj[:, :, :size] - alpha * (own[:, :, :size] + left[...].astype(F32))
+    obj_out[:, :size, :size] -= alpha * down[:, :, :size].astype(F32)
+    obj_out[:, :size, size:] = obj[:, :size, size:] - alpha * (own[:, :size, size:] + down[:, :, size:].astype(F32))
     obj_out[:, size:, size:] = obj[:, size:, size:] - alpha * own[:, size:, size:]
-    obj_out[:, :size, :size] -= alpha * low_left[...].astype(F32)
-    obj_out[:, :size, size:] = obj[:, :size, size:] - alpha * (own[:, :size, size:] + low_right[...].astype(F32))
-    if with_sum:
-        halo_left[...] = obj_out[:, :size, :size].astype(BF)
-        halo_right[...] = obj_out[:, :size, size:].astype(BF)
-        right_out[...] = obj_out[:, :, :size].astype(BF)
-
-
-def run_update(obj, own, left, low_left, low_right, step, totals):
-    rows, cols = obj.shape[1], obj.shape[2]
+
+
+def both_kernel(a, b, c, d, mine, obj, own, left, down, step, fresh, obj_out, below, right):
+    probe_step(a, b, c, d, mine, fresh)
+    object_step(obj, own, left, down, step, obj_out)
     size = left.shape[2]
-    vmem = pl.BlockSpec(memory_space=pltpu.VMEM)
-    smem = pl.BlockSpec(memory_space=pltpu.SMEM)
-    shapes = [jax.ShapeDtypeStruct((2, rows, cols), F32)]
-    if totals:
-        shapes += [
-            jax.ShapeDtypeStruct((2, size, size), BF),
-            jax.ShapeDtypeStruct((2, size, cols - size), BF),
-            jax.ShapeDtypeStruct((2, rows, size), BF),
-            jax.ShapeDtypeStruct(totals[0].shape, F32),
-        ]
-    return pl.pallas_call(
-        functools.partial(update_kernel, bool(totals)),
-        out_shape=shapes,
-        in_specs=[vmem] * 5 + [smem] + [vmem] * len(totals),
-        out_specs=[vmem] * len(shapes),
-        compiler_params=pltpu.CompilerParams(vmem_limit_bytes=16 << 20),
-        cost_estimate=pl.CostEstimate(flops=2_000_000, bytes_accessed=8_000_000, transcendentals=0),
-        name="object_update",
-    )(obj, own, left, low_left, low_right, step, *totals)
+    below[...] = obj_out[:, :size, :].astype(BF)
+    right[...] = obj_out[:, :, :size].astype(BF)
 
 
 def probe_kernel(place, mine, other, out):
@@ -305,63 +316,54 @@
     return lax.ppermute(value, "core", [(0, 1), (1, 0)])
 
 
-def halo(low_left, low_right, right):
-    first = moved(low_left, ROW, N_ROW, -1)
-    beside = moved(right, COL, N_COL, -1)
-    second = moved(low_right, ROW, N_ROW, -1)
-    corner = moved(first, COL, N_COL, -1)
-    return (first, second, beside, corner)
-
-
-def rims(low_left, low_right, right, corner):
-    corner = moved(corner, COL, N_COL, 1)
-    left = moved(right, COL, N_COL, 1)
-    second = moved(low_right, ROW, N_ROW, 1)
-    first = moved((low_left + corner.astype(F32)).astype(BF), ROW, N_ROW, 1)
-    return (left, first, second)
+def halo(below, right):
+    size = below.shape[1]
+    below = moved(below, ROW, N_ROW, -1)
+    right = moved(right, COL, N_COL, -1)
+    corner = moved(below[:, :, :size], COL, N_COL, -1)
+    return (below, right, corner)
 
 
 def around(value, axis):
     return [value] + [turned(value, axis, j) for j in (1, 2, 3)]
 
 
-def column_sum(keep, send):
-    part = keep + swapped(send)
-    return part[0] + turned(part[1], "y", 1) + turned(part[2], "y", 2) + turned(part[3], "y", 3)
-
-
-def gathered(mine, total):
-    fresh = mine - total[:2] / (total[2] + 1.0)
-    half = jnp.stack(around(fresh, "y"))
-    return (half, swapped(half))
-
-
 def local(tables, obj, probe, amps, positions, counts):
+    rows, cols = obj.shape[1], obj.shape[2]
     size = probe.shape[-1]
     half, quarter = size // N_CORE, size // (N_CORE * N_Y)
     core, y = lax.axis_index("core"), lax.axis_index("y")
     place = jnp.stack([core, y]).astype(jnp.int32)
     mine = lax.dynamic_slice(probe, (0, core * half + y * quarter, 0), (2, quarter, size))
-    low_left, low_right = obj[:, :size, :size].astype(BF), obj[:, :size, size:].astype(BF)
-    right = obj[:, :, :size].astype(BF)
+    whole = jax.ShapeDtypeStruct(obj.shape, F32)
+    flat = jax.ShapeDtypeStruct((2, size, cols), BF)
+    tall = jax.ShapeDtypeStruct((2, rows, size), BF)
+    share = jax.ShapeDtypeStruct((3, quarter, size), F32)
+    part = jax.ShapeDtypeStruct(mine.shape, F32)
+    below, right = obj[:, :size, :].astype(BF), obj[:, :, :size].astype(BF)
     pieces = (probe,)
     for iteration in range(ITERS):
-        halos = halo(low_left, low_right, right)
+        halos = halo(below, right)
         own, low_left, low_right, right, corner, keep, send, step = run_frames(
             place, counts[iteration, 0], positions[iteration], obj, halos, pieces, amps, tables, iteration
         )
-        left, above_left, above_right = rims(low_left, low_right, right, corner)
-        totals = around(column_sum(keep, send), "z")
+        corner = moved(corner, COL, N_COL, 1)
+        left = moved(right, COL, N_COL, 1)
+        sums = keep + swapped(send)
+        sums = [sums[:1]] + [turned(sums[j], "y", j) for j in (1, 2, 3)]
+        total, down = small_call(y_kernel, [share, flat], ([*sums, low_left, low_right, corner], []), "y_sum")
+        down = moved(down, ROW, N_ROW, 1)
+        (total,) = small_call(z_kernel, [share], (around(total, "z"), [left]), "z_sum")
+        sums = around(total, "x") + [mine]
         if iteration < ITERS - 1:
-            obj, low_left, low_right, right, total = run_update(
-                obj, own, left, above_left, above_right, step, totals
+            mine, obj, below, right = small_call(
+                both_kernel, [part, whole, flat, tall], ([*sums, obj, own, left, down, step], []), "x_sum_object"
             )
         else:
-            (obj,) = run_update(obj, own, left, above_left, above_right, step, [])
-            total = sum(totals[1:], totals[0])
-        total = sum(around(total, "x")[1:], total)
-        pieces = gathered(mine, total)
-        mine = pieces[0][0]
+            (mine,) = small_call(x_kernel, [part], (sums, [down]), "x_sum")
+            (obj,) = small_call(object_step, [whole], ([obj, own, left, down, step], []), "object_update")
+        stack = jnp.stack(around(mine, "y"))
+        pieces = (stack, swapped(stack))
     return (obj, run_probe(place, *pieces))
 
 

time: 172 us -> 185 us (1.076)
  the two profiles are of different devices: /device:TPU:6 before, /device:TPU:1 now
where the time goes in v4:
time: 185 us; the launch traced here: 184 us
  waiting for transfers between devices  77.6 us (42%)
  starting transfers between devices  76.7 us (41%)
  Pallas kernels  21.2 us (11%)
  local copies, waits for them, and re-layouts  5.63 us (3%)
    ppermute x24, waiting for transfers between devices, turned(): return lax.ppermute(value, axis, [(s, (s + steps) % 4) for s in range(4)])  59.4 us
    ppermute x24, starting transfers between devices, turned(): return lax.ppermute(value, axis, [(s, (s + steps) % 4) for s in range(4)])  36 us
    ppermute x12, starting transfers between devices, moved(): lax.ppermute(value, axis, [(s, s + steps) for s in range(first, last)])  34.8 us
    ppermute x12, waiting for transfers between devices, moved(): lax.ppermute(value, axis, [(s, s + steps) for s in range(first, last)])  18.2 us
    pallas_call x2, Pallas kernels, run_frames(): pl.pallas_call(functools.partial(frames_kernel, iteration, len(pieces)),...  14.7 us
    ppermute x4, starting transfers between devices, swapped(): return lax.ppermute(value, 'core', [(0, 1), (1, 0)])  5.93 us
    pallas_call x7, Pallas kernels, small_call(): pl.pallas_call(body, out_shape=shapes, in_specs=[spec(space) for space in...  4.62 us
  transfers between devices with their start and end apart: 40, of which 22 were waited for; matrix products, arithmetic and copies ran while one was open for 1% of the time, Pallas kernels for 2%

profile of v4, /device:TPU:1, one launch (start us, length us, event | category | flops | bytes accessed | tf_op | source)
XLA Modules:
  0.0 183.9 jit_solution(11187022575927510257)
XLA Ops:
  0.6 1.5 convert.4
  2.2 0.8 slice.66
  3.0 1.3 collective-permute-start
  4.3 0.8 slice.67
  5.1 3.3 %collective-permute-start.1 = (bf16[2,512,256]{2,1,0:T(8,128)(2,1)}, bf16[2,512,256]{2,1,0:T(8,128)(2,1)S(1)}, u32[]{:S(2)}, u32[]{:S(2)}) collective-permute-start(bf16[2,512,256]{2,1,0:T(8,128)(2,1)} %slice.67), channel_id=1, source_target_pairs={{1,0},{2,1},{3,2},{4,3},{5,4},{6,5},{7,6},{9,8},{10,9},{11,10},{12... | collective-permute-start | bytes 1572872 | tf_op jit(solution)/shard_map/ppermute | solution.py:308
  8.4 0.6 fusion
  9.0 7.3 %collective-permute-done.below = bf16[2,256,384]{2,1,0:T(8,128)(2,1)S(1)} collective-permute-done((bf16[2,256,384]{2,1,0:T(8,128)(2,1)}, bf16[2,256,384]{2,1,0:T(8,128)(2,1)S(1)}, u32[]{:S(2)}, u32[]{:S(2)}) %collective-permute-start) | collective-permute-done | bytes 393248 | tf_op jit(solution)/shard_map/ppermute | solution.py:308
  16.4 3.2 %collective-permute-start.2 = (bf16[2,256,256]{2,1,0:T(8,128)(2,1)S(1)}, bf16[2,256,256]{2,1,0:T(8,128)(2,1)S(1)}, u32[]{:S(2)}, u32[]{:S(2)}) collective-permute-start(bf16[2,256,256]{2,1,0:T(8,128)(2,1)S(1)} %slice.68), channel_id=1, source_target_pairs={{1,0},{2,1},{3,2},{4,3},{5,4},{6,5},{7,6},{9,8},{10,9},{11,10},{12... | collective-permute-start | bytes 786440 | tf_op jit(solution)/shard_map/ppermute | solution.py:308
  19.6 5.1 %collective-permute-done.2.corner = bf16[2,256,256]{2,1,0:T(8,128)(2,1)S(1)} collective-permute-done((bf16[2,256,256]{2,1,0:T(8,128)(2,1)S(1)}, bf16[2,256,256]{2,1,0:T(8,128)(2,1)S(1)}, u32[]{:S(2)}, u32[]{:S(2)}) %collective-permute-start.2) | collective-permute-done | bytes 262176 | tf_op jit(solution)/shard_map/ppermute | solution.py:308
  24.8 6.5 %frames.2 = (f32[2,512,384]{2,1,0:T(8,128)}, f32[2,256,256]{2,1,0:T(8,128)S(1)}, bf16[2,256,128]{2,1,0:T(8,128)(2,1)S(1)}, bf16[2,512,256]{2,1,0:T(8,128)(2,1)},...) custom-call(s32[2]{0:T(128)S(1)} %pad_add_fusion.place, ...), custom_call_target="tpu_custom_call" | custom-call | flops 6000000000 | bytes 8000000 | tf_op jit(solution)/shard_map/frames/pallas_call | solution.py:218
  31.4 5.8 %collective-permute-start.7 = (bf16[2,256,256]{2,1,0:T(8,128)(2,1)S(1)}, bf16[2,256,256]{2,1,0:T(8,128)(2,1)S(1)}, u32[]{:S(2)}, u32[]{:S(2)}) collective-permute-start(bf16[2,256,256]{2,1,0:T(8,128)(2,1)S(1)} %get-tuple-element.30), channel_id=1, source_target_pairs={{0,1},{1,2},{2,3},{3,4},{4,5},{5,6},{6,7},{8,9},{9,10},{10,11},{11... | collective-permute-start | bytes 786440 | tf_op jit(solution)/shard_map/ppermute | solution.py:308
  37.2 1.9 %collective-permute-start.11 = (bf16[2,512,256]{2,1,0:T(8,128)(2,1)}, bf16[2,512,256]{2,1,0:T(8,128)(2,1)S(1)}, u32[]{:S(2)}, u32[]{:S(2)}) collective-permute-start(bf16[2,512,256]{2,1,0:T(8,128)(2,1)} %get-tuple-element.32), channel_id=1, source_target_pairs={{0,1},{1,2},{2,3},{3,4},{4,5},{5,6},{6,7},{8,9},{9,10},{10,11},{11... | collective-permute-start | bytes 1572872 | tf_op jit(solution)/shard_map/ppermute | solution.py:308
  39.4 2.8 %collective-permute-start.5 = (f32[3,32,256]{2,1,0:T(8,128)S(1)}, f32[3,32,256]{2,1,0:T(8,128)S(1)}, u32[]{:S(2)}, u32[]{:S(2)}) collective-permute-start(f32[3,32,256]{2,1,0:T(8,128)S(1)} %get-tuple-element.55), channel_id=1, source_target_pairs={{0,4},{2,6},{4,0},{6,2},{1,5},{3,7},{5,1},{7,3},{8,12},{10,14},{12... | collective-permute-start | bytes 294920 | tf_op jit(solution)/shard_map/ppermute | solution.py:312
  42.1 1.1 collective-permute-done.6.d
  43.2 7.5 %collective-permute-done.5.c = f32[3,32,256]{2,1,0:T(8,128)S(1)} collective-permute-done((f32[3,32,256]{2,1,0:T(8,128)S(1)}, f32[3,32,256]{2,1,0:T(8,128)S(1)}, u32[]{:S(2)}, u32[]{:S(2)}) %collective-permute-start.5) | collective-permute-done | bytes 98336 | tf_op jit(solution)/shard_map/ppermute | solution.py:312
  50.7 0.8 y_sum.2
  51.5 3.6 %collective-permute-start.15 = (bf16[2,256,384]{2,1,0:T(8,128)(2,1)}, bf16[2,256,384]{2,1,0:T(8,128)(2,1)S(1)}, u32[]{:S(2)}, u32[]{:S(2)}) collective-permute-start(bf16[2,256,384]{2,1,0:T(8,128)(2,1)} %get-tuple-element.34), channel_id=1, source_target_pairs={{0,8},{8,16},{16,24},{24,32},{32,40},{40,48},{48,56},{56,64},{64,7... | collective-permute-start | bytes 1179656 | tf_op jit(solution)/shard_map/ppermute | solution.py:308
  55.1 5.1 %collective-permute-start.10 = (f32[3,32,256]{2,1,0:T(8,128)S(1)}, f32[3,32,256]{2,1,0:T(8,128)S(1)}, u32[]{:S(2)}, u32[]{:S(2)}) collective-permute-start(f32[3,32,256]{2,1,0:T(8,128)S(1)} %get-tuple-element.31.a), channel_id=1, source_target_pairs={{0,24},{8,0},{16,8},{24,16},{1,25},{9,1},{17,9},{25,17},{2,26},{10... | collective-permute-start | bytes 294920 | tf_op jit(solution)/shard_map/ppermute | solution.py:312
  60.5 0.8 collective-permute-start.8
  61.3 2.6 %collective-permute-done.10.d = f32[3,32,256]{2,1,0:T(8,128)S(1)} collective-permute-done((f32[3,32,256]{2,1,0:T(8,128)S(1)}, f32[3,32,256]{2,1,0:T(8,128)S(1)}, u32[]{:S(2)}, u32[]{:S(2)}) %collective-permute-start.10) | collective-permute-done | bytes 98336 | tf_op jit(solution)/shard_map/ppermute | solution.py:312
  63.9 7.9 %collective-permute-done.9.c = f32[3,32,256]{2,1,0:T(8,128)S(1)} collective-permute-done((f32[3,32,256]{2,1,0:T(8,128)S(1)}, f32[3,32,256]{2,1,0:T(8,128)S(1)}, u32[]{:S(2)}, u32[]{:S(2)}) %collective-permute-start.9) | collective-permute-done | bytes 98336 | tf_op jit(solution)/shard_map/ppermute | solution.py:312
  71.8 5.9 %collective-permute-start.14 = (f32[3,32,256]{2,1,0:T(8,128)S(1)}, f32[3,32,256]{2,1,0:T(8,128)S(1)}, u32[]{:S(2)}, u32[]{:S(2)}) collective-permute-start(f32[3,32,256]{2,1,0:T(8,128)S(1)} %z_sum.2.a), channel_id=1, source_target_pairs={{0,96},{32,0},{64,32},{96,64},{1,97},{33,1},{65,33},{97,65},{2,98}... | collective-permute-start | bytes 294920 | tf_op jit(solution)/shard_map/ppermute | solution.py:312
  77.8 1.6 collective-permute-start.13
  79.3 0.4 collective-permute-start.12
  79.7 3.0 %collective-permute-done.13.c = f32[3,32,256]{2,1,0:T(8,128)S(1)} collective-permute-done((f32[3,32,256]{2,1,0:T(8,128)S(1)}, f32[3,32,256]{2,1,0:T(8,128)S(1)}, u32[]{:S(2)}, u32[]{:S(2)}) %collective-permute-start.13) | collective-permute-done | bytes 98336 | tf_op jit(solution)/shard_map/ppermute | solution.py:312
  82.7 3.2 %collective-permute-done.12.b = f32[3,32,256]{2,1,0:T(8,128)S(1)} collective-permute-done((f32[3,32,256]{2,1,0:T(8,128)S(1)}, f32[3,32,256]{2,1,0:T(8,128)S(1)}, u32[]{:S(2)}, u32[]{:S(2)}) %collective-permute-start.12) | collective-permute-done | bytes 98336 | tf_op jit(solution)/shard_map/ppermute | solution.py:312
  85.9 1.4 copy-done.1
  87.3 1.3 x_sum_object.1
  88.7 1.1 copy-done.2
  89.8 1.3 collective-permute-start.16
  91.1 2.8 %collective-permute-start.17 = (bf16[2,512,256]{2,1,0:T(8,128)(2,1)S(1)}, bf16[2,512,256]{2,1,0:T(8,128)(2,1)S(1)}, u32[]{:S(2)}, u32[]{:S(2)}) collective-permute-start(bf16[2,512,256]{2,1,0:T(8,128)(2,1)S(1)} %get-tuple-element.38), channel_id=1, source_target_pairs={{1,0},{2,1},{3,2},{4,3},{5,4},{6,5},{7,6},{9,8},{10,9},{11,10},{12... | collective-permute-start | bytes 1572872 | tf_op jit(solution)/shard_map/ppermute | solution.py:308
  93.8 1.2 collective-permute-start.21
  95.0 0.7 collective-permute-start.19
  95.7 2.2 %collective-permute-done.21 = f32[2,32,256]{2,1,0:T(8,128)S(1)} collective-permute-done((f32[2,32,256]{2,1,0:T(8,128)S(1)}, f32[2,32,256]{2,1,0:T(8,128)S(1)}, u32[]{:S(2)}, u32[]{:S(2)}) %collective-permute-start.21) | collective-permute-done | bytes 65568 | tf_op jit(solution)/shard_map/ppermute | solution.py:312
  97.9 1.8 collective-permute-done.20
  99.7 1.3 collective-permute-done.19
  101.1 3.4 %collective-permute-start.22 = (f32[4,2,32,256]{3,2,1,0:T(8,128)S(1)}, f32[4,2,32,256]{3,2,1,0:T(8,128)S(1)}, u32[]{:S(2)}, u32[]{:S(2)}) collective-permute-start(f32[4,2,32,256]{3,2,1,0:T(8,128)S(1)} %pad_maximum_fusion.rest_0_), channel_id=1, source_target_pairs={{0,1},{1,0},{2,3},{3,2},{4,5},{5,4},{6,7},{7,6},{8,9},{9,8},{10,11... | collective-permute-start | bytes 786440 | tf_op jit(solution)/shard_map/ppermute | solution.py:316
  104.5 1.9 %collective-permute-start.18 = (bf16[2,256,256]{2,1,0:T(8,128)(2,1)S(1)}, bf16[2,256,256]{2,1,0:T(8,128)(2,1)S(1)}, u32[]{:S(2)}, u32[]{:S(2)}) collective-permute-start(bf16[2,256,256]{2,1,0:T(8,128)(2,1)S(1)} %slice.73), channel_id=1, source_target_pairs={{1,0},{2,1},{3,2},{4,3},{5,4},{6,5},{7,6},{9,8},{10,9},{11,10},{12... | collective-permute-start | bytes 786440 | tf_op jit(solution)/shard_map/ppermute | solution.py:308
  106.5 5.7 %collective-permute-done.18.corner = bf16[2,256,256]{2,1,0:T(8,128)(2,1)S(1)} collective-permute-done((bf16[2,256,256]{2,1,0:T(8,128)(2,1)S(1)}, bf16[2,256,256]{2,1,0:T(8,128)(2,1)S(1)}, u32[]{:S(2)}, u32[]{:S(2)}) %collective-permute-start.18) | collective-permute-done | bytes 262176 | tf_op jit(solution)/shard_map/ppermute | solution.py:308
  112.2 8.2 %frames.3 = (f32[2,512,384]{2,1,0:T(8,128)}, f32[2,256,256]{2,1,0:T(8,128)S(1)}, bf16[2,256,128]{2,1,0:T(8,128)(2,1)S(1)}, bf16[2,512,256]{2,1,0:T(8,128)(2,1)S(...) custom-call(s32[2]{0:T(128)S(1)} %pad_add_fusion.place, ...), custom_call_target="tpu_custom_call" | custom-call | flops 6000000000 | bytes 8000000 | tf_op jit(solution)/shard_map/frames/pallas_call | solution.py:218
  120.5 5.8 %collective-permute-start.28 = (bf16[2,256,256]{2,1,0:T(8,128)(2,1)S(1)}, bf16[2,256,256]{2,1,0:T(8,128)(2,1)S(1)}, u32[]{:S(2)}, u32[]{:S(2)}) collective-permute-start(bf16[2,256,256]{2,1,0:T(8,128)(2,1)S(1)} %get-tuple-element.46), channel_id=1, source_target_pairs={{0,1},{1,2},{2,3},{3,4},{4,5},{5,6},{6,7},{8,9},{9,10},{10,11},{11... | collective-permute-start | bytes 786440 | tf_op jit(solution)/shard_map/ppermute | solution.py:308
  126.4 1.9 %collective-permute-start.23 = (bf16[2,512,256]{2,1,0:T(8,128)(2,1)S(1)}, bf16[2,512,256]{2,1,0:T(8,128)(2,1)S(1)}, u32[]{:S(2)}, u32[]{:S(2)}) collective-permute-start(bf16[2,512,256]{2,1,0:T(8,128)(2,1)S(1)} %get-tuple-element.41), channel_id=1, source_target_pairs={{0,1},{1,2},{2,3},{3,4},{4,5},{5,6},{6,7},{8,9},{9,10},{10,11},{11... | collective-permute-start | bytes 1572872 | tf_op jit(solution)/shard_map/ppermute | solution.py:308
  128.5 1.4 collective-permute-start.26
  130.0 2.4 %collective-permute-done.27.d = f32[3,32,256]{2,1,0:T(8,128)S(1)} collective-permute-done((f32[3,32,256]{2,1,0:T(8,128)S(1)}, f32[3,32,256]{2,1,0:T(8,128)S(1)}, u32[]{:S(2)}, u32[]{:S(2)}) %collective-permute-start.27) | collective-permute-done | bytes 98336 | tf_op jit(solution)/shard_map/ppermute | solution.py:312
  132.3 6.3 %collective-permute-done.26.c = f32[3,32,256]{2,1,0:T(8,128)S(1)} collective-permute-done((f32[3,32,256]{2,1,0:T(8,128)S(1)}, f32[3,32,256]{2,1,0:T(8,128)S(1)}, u32[]{:S(2)}, u32[]{:S(2)}) %collective-permute-start.26) | collective-permute-done | bytes 98336 | tf_op jit(solution)/shard_map/ppermute | solution.py:312
  138.7 0.8 collective-permute-done.25.b
  139.6 2.0 %collective-permute-start.29 = (bf16[2,256,384]{2,1,0:T(8,128)(2,1)S(1)}, bf16[2,256,384]{2,1,0:T(8,128)(2,1)S(1)}, u32[]{:S(2)}, u32[]{:S(2)}) collective-permute-start(bf16[2,256,384]{2,1,0:T(8,128)(2,1)S(1)} %get-tuple-element.47), channel_id=1, source_target_pairs={{0,8},{8,16},{16,24},{24,32},{32,40},{40,48},{48,56},{56,64},{64,7... | collective-permute-start | bytes 1179656 | tf_op jit(solution)/shard_map/ppermute | solution.py:308
  141.6 3.5 %collective-permute-start.32 = (f32[3,32,256]{2,1,0:T(8,128)S(1)}, f32[3,32,256]{2,1,0:T(8,128)S(1)}, u32[]{:S(2)}, u32[]{:S(2)}) collective-permute-start(f32[3,32,256]{2,1,0:T(8,128)S(1)} %get-tuple-element.49.a), channel_id=1, source_target_pairs={{0,24},{8,0},{16,8},{24,16},{1,25},{9,1},{17,9},{25,17},{2,26},{10... | collective-permute-start | bytes 294920 | tf_op jit(solution)/shard_map/ppermute | solution.py:312
  145.2 0.7 collective-permute-start.30
  145.8 2.4 %collective-permute-done.32.d = f32[3,32,256]{2,1,0:T(8,128)S(1)} collective-permute-done((f32[3,32,256]{2,1,0:T(8,128)S(1)}, f32[3,32,256]{2,1,0:T(8,128)S(1)}, u32[]{:S(2)}, u32[]{:S(2)}) %collective-permute-start.32) | collective-permute-done | bytes 98336 | tf_op jit(solution)/shard_map/ppermute | solution.py:312
  148.3 6.0 %collective-permute-done.31.c = f32[3,32,256]{2,1,0:T(8,128)S(1)} collective-permute-done((f32[3,32,256]{2,1,0:T(8,128)S(1)}, f32[3,32,256]{2,1,0:T(8,128)S(1)}, u32[]{:S(2)}, u32[]{:S(2)}) %collective-permute-start.31) | collective-permute-done | bytes 98336 | tf_op jit(solution)/shard_map/ppermute | solution.py:312
  154.3 6.2 %collective-permute-start.35 = (f32[3,32,256]{2,1,0:T(8,128)S(1)}, f32[3,32,256]{2,1,0:T(8,128)S(1)}, u32[]{:S(2)}, u32[]{:S(2)}) collective-permute-start(f32[3,32,256]{2,1,0:T(8,128)S(1)} %z_sum.3.a), channel_id=1, source_target_pairs={{0,96},{32,0},{64,32},{96,64},{1,97},{33,1},{65,33},{97,65},{2,98}... | collective-permute-start | bytes 294920 | tf_op jit(solution)/shard_map/ppermute | solution.py:312
  160.4 1.0 collective-permute-start.34
  161.5 0.8 collective-permute-start.33
  162.2 2.5 %collective-permute-done.35.d = f32[3,32,256]{2,1,0:T(8,128)S(1)} collective-permute-done((f32[3,32,256]{2,1,0:T(8,128)S(1)}, f32[3,32,256]{2,1,0:T(8,128)S(1)}, u32[]{:S(2)}, u32[]{:S(2)}) %collective-permute-start.35) | collective-permute-done | bytes 98336 | tf_op jit(solution)/shard_map/ppermute | solution.py:312
  164.7 1.7 collective-permute-done.34.c
  166.5 2.2 %collective-permute-done.33.b = f32[3,32,256]{2,1,0:T(8,128)S(1)} collective-permute-done((f32[3,32,256]{2,1,0:T(8,128)S(1)}, f32[3,32,256]{2,1,0:T(8,128)S(1)}, u32[]{:S(2)}, u32[]{:S(2)}) %collective-permute-start.33) | collective-permute-done | bytes 98336 | tf_op jit(solution)/shard_map/ppermute | solution.py:312
  168.8 3.5 %collective-permute-start.37 = (f32[2,32,256]{2,1,0:T(8,128)S(1)}, f32[2,32,256]{2,1,0:T(8,128)S(1)}, u32[]{:S(2)}, u32[]{:S(2)}) collective-permute-start(f32[2,32,256]{2,1,0:T(8,128)S(1)} %x_sum.1), channel_id=1, source_target_pairs={{0,4},{2,6},{4,0},{6,2},{1,5},{3,7},{5,1},{7,3},{8,12},{10,14},{12... | collective-permute-start | bytes 196616 | tf_op jit(solution)/shard_map/ppermute | solution.py:312
  172.3 1.6 collective-permute-done.37
  173.9 2.7 %collective-permute-done.36 = f32[2,32,256]{2,1,0:T(8,128)S(1)} collective-permute-done((f32[2,32,256]{2,1,0:T(8,128)S(1)}, f32[2,32,256]{2,1,0:T(8,128)S(1)}, u32[]{:S(2)}, u32[]{:S(2)}) %collective-permute-start.36) | collective-permute-done | bytes 65568 | tf_op jit(solution)/shard_map/ppermute | solution.py:312
  176.6 2.4 %collective-permute-start.39 = (f32[4,2,32,256]{3,2,1,0:T(8,128)S(1)}, f32[4,2,32,256]{3,2,1,0:T(8,128)S(1)}, u32[]{:S(2)}, u32[]{:S(2)}) collective-permute-start(f32[4,2,32,256]{3,2,1,0:T(8,128)S(1)} %pad_maximum_fusion.1.mine), channel_id=1, source_target_pairs={{0,1},{1,0},{2,3},{3,2},{4,5},{5,4},{6,7},{7,6},{8,9},{9,8},{10,11... | collective-permute-start | bytes 786440 | tf_op jit(solution)/shard_map/ppermute | solution.py:316
  179.0 2.3 %object_update.1 = f32[2,512,384]{2,1,0:T(8,128)} custom-call(f32[2,512,384]{2,1,0:T(8,128)S(1)} %copy-done.3, f32[2,512,384]{2,1,0:T(8,128)S(1)} %copy-done.4, bf16[2,512,256]{2,1,0:T(8,128)(2,1)S(1)} %collective-permute-done.23.left.waited, bf16[2,256,384]{2,1,0:T(8,128)(2,1)S(1)} %collective-permute-done.29.down.waited, f32[1,1]{1,0:T(1,128)} %get-tuple-element.48.step), custom_call_target="tpu_custom_call" | custom-call | flops 2000000 | bytes 4000000 | tf_op jit(solution)/shard_map/object_update/pallas_call | solution.py:236
  181.3 0.7 copy-done.12
  182.1 1.9 %probe_whole.1 = f32[2,256,256]{2,1,0:T(8,128)} custom-call(s32[2]{0:T(128)} %copy-done.6, f32[4,2,32,256]{3,2,1,0:T(8,128)} %copy-done.11, f32[4,2,32,256]{3,2,1,0:T(8,128)} %copy-done.12), custom_call_target="tpu_custom_call" | custom-call | tf_op jit(solution)/shard_map/probe_whole/pallas_call | solution.py:297
  (71 shorter events, 1.3 us)
Async XLA Ops:
  0.6 7.8 %copy-start.14 = (s32[2,1,1]{0,2,1:T(1,128)S(1)}, s32[2,1,1]{0,2,1:T(1,128)}, u32[]{:S(2)}) copy-start(s32[2,1,1]{0,2,1:T(1,128)} %param.11) | copy-start | bytes 28
  2.1 17.5 %copy-start.13 = (s32[2,2,12]{2,1,0:T(2,128)S(1)}, s32[2,2,12]{2,1,0:T(2,128)}, u32[]{:S(2)}) copy-start(s32[2,2,12]{2,1,0:T(2,128)} %param.10) | copy-start | bytes 580
  2.2 22.6 %copy-start.5 = (f32[2,256,256]{2,1,0:T(8,128)S(1)}, f32[2,256,256]{2,1,0:T(8,128)}, u32[]{:S(2)}) copy-start(f32[2,256,256]{2,1,0:T(8,128)} %rest_0_.1) | copy-start | bytes 1572868
  2.2 22.6 %copy-start.7 = (bf16[512,512]{1,0:T(8,128)(2,1)S(1)}, bf16[512,512]{1,0:T(8,128)(2,1)}, u32[]{:S(2)}) copy-start(bf16[512,512]{1,0:T(8,128)(2,1)} %constant.21.clone.rest_3_.rest_4_) | copy-start | bytes 1572868
  2.2 22.6 %copy-start.9 = (bf16[512,512]{1,0:T(8,128)(2,1)S(1)}, bf16[512,512]{1,0:T(8,128)(2,1)}, u32[]{:S(2)}) copy-start(bf16[512,512]{1,0:T(8,128)(2,1)} %constant.20.clone.rest_2_.rest_3_) | copy-start | bytes 1572868
  3.0 13.4 %collective-permute-start = (bf16[2,256,384]{2,1,0:T(8,128)(2,1)}, bf16[2,256,384]{2,1,0:T(8,128)(2,1)S(1)}, u32[]{:S(2)}, u32[]{:S(2)}) collective-permute-start(bf16[2,256,384]{2,1,0:T(8,128)(2,1)} %slice.66), channel_id=1, source_target_pairs={{8,0},{16,8},{24,16},{32,24},{40,32},{48,40},{56,48},{64,56},{72,6... | collective-permute-start | bytes 1179656 | tf_op jit(solution)/shard_map/ppermute | solution.py:308
  5.1 14.5 %collective-permute-start.1 = (bf16[2,512,256]{2,1,0:T(8,128)(2,1)}, bf16[2,512,256]{2,1,0:T(8,128)(2,1)S(1)}, u32[]{:S(2)}, u32[]{:S(2)}) collective-permute-start(bf16[2,512,256]{2,1,0:T(8,128)(2,1)} %slice.67), channel_id=1, source_target_pairs={{1,0},{2,1},{3,2},{4,3},{5,4},{6,5},{7,6},{9,8},{10,9},{11,10},{12... | collective-permute-start | bytes 1572872 | tf_op jit(solution)/shard_map/ppermute | solution.py:308
  16.4 8.4 %collective-permute-start.2 = (bf16[2,256,256]{2,1,0:T(8,128)(2,1)S(1)}, bf16[2,256,256]{2,1,0:T(8,128)(2,1)S(1)}, u32[]{:S(2)}, u32[]{:S(2)}) collective-permute-start(bf16[2,256,256]{2,1,0:T(8,128)(2,1)S(1)} %slice.68), channel_id=1, source_target_pairs={{1,0},{2,1},{3,2},{4,3},{5,4},{6,5},{7,6},{9,8},{10,9},{11,10},{12... | collective-permute-start | bytes 786440 | tf_op jit(solution)/shard_map/ppermute | solution.py:308
  19.6 92.6 %copy-start.6 = (s32[2]{0:T(128)}, s32[2]{0:T(128)S(1)}, u32[]{:S(2)}) copy-start(s32[2]{0:T(128)S(1)} %pad_add_fusion.place) | copy-start | bytes 28
  31.3 7.9 %collective-permute-start.3 = (f32[4,3,32,256]{3,2,1,0:T(8,128)S(1)}, f32[4,3,32,256]{3,2,1,0:T(8,128)S(1)}, u32[]{:S(2)}, u32[]{:S(2)}) collective-permute-start(f32[4,3,32,256]{3,2,1,0:T(8,128)S(1)} %get-tuple-element.27), channel_id=1, source_target_pairs={{0,1},{1,0},{2,3},{3,2},{4,5},{5,4},{6,7},{7,6},{8,9},{9,8},{10,11... | collective-permute-start | bytes 1179656 | tf_op jit(solution)/shard_map/ppermute | solution.py:316
  31.4 10.7 %collective-permute-start.7 = (bf16[2,256,256]{2,1,0:T(8,128)(2,1)S(1)}, bf16[2,256,256]{2,1,0:T(8,128)(2,1)S(1)}, u32[]{:S(2)}, u32[]{:S(2)}) collective-permute-start(bf16[2,256,256]{2,1,0:T(8,128)(2,1)S(1)} %get-tuple-element.30), channel_id=1, source_target_pairs={{0,1},{1,2},{2,3},{3,4},{4,5},{5,6},{6,7},{8,9},{9,10},{10,11},{11... | collective-permute-start | bytes 786440 | tf_op jit(solution)/shard_map/ppermute | solution.py:308
  37.2 24.0 %collective-permute-start.11 = (bf16[2,512,256]{2,1,0:T(8,128)(2,1)}, bf16[2,512,256]{2,1,0:T(8,128)(2,1)S(1)}, u32[]{:S(2)}, u32[]{:S(2)}) collective-permute-start(bf16[2,512,256]{2,1,0:T(8,128)(2,1)} %get-tuple-element.32), channel_id=1, source_target_pairs={{0,1},{1,2},{2,3},{3,4},{4,5},{5,6},{6,7},{8,9},{9,10},{10,11},{11... | collective-permute-start | bytes 1572872 | tf_op jit(solution)/shard_map/ppermute | solution.py:308
  39.2 46.7 %copy-start = (f32[2,512,384]{2,1,0:T(8,128)S(1)}, f32[2,512,384]{2,1,0:T(8,128)}, u32[]{:S(2)}) copy-start(f32[2,512,384]{2,1,0:T(8,128)} %obj.3) | copy-start | bytes 4718596
  39.3 3.9 %collective-permute-start.6 = (f32[3,32,256]{2,1,0:T(8,128)S(1)}, f32[3,32,256]{2,1,0:T(8,128)S(1)}, u32[]{:S(2)}, u32[]{:S(2)}) collective-permute-start(f32[3,32,256]{2,1,0:T(8,128)S(1)} %get-tuple-element.54), channel_id=1, source_target_pairs={{0,6},{2,0},{4,2},{6,4},{1,7},{3,1},{5,3},{7,5},{8,14},{10,8},{12,... | collective-permute-start | bytes 294920 | tf_op jit(solution)/shard_map/ppermute | solution.py:312
  39.4 11.3 %collective-permute-start.5 = (f32[3,32,256]{2,1,0:T(8,128)S(1)}, f32[3,32,256]{2,1,0:T(8,128)S(1)}, u32[]{:S(2)}, u32[]{:S(2)}) collective-permute-start(f32[3,32,256]{2,1,0:T(8,128)S(1)} %get-tuple-element.55), channel_id=1, source_target_pairs={{0,4},{2,6},{4,0},{6,2},{1,5},{3,7},{5,1},{7,3},{8,12},{10,14},{12... | collective-permute-start | bytes 294920 | tf_op jit(solution)/shard_map/ppermute | solution.py:312
  42.1 8.6 %collective-permute-start.4 = (f32[3,32,256]{2,1,0:T(8,128)S(1)}, f32[3,32,256]{2,1,0:T(8,128)S(1)}, u32[]{:S(2)}, u32[]{:S(2)}) collective-permute-start(f32[3,32,256]{2,1,0:T(8,128)S(1)} %get-tuple-element.56), channel_id=1, source_target_pairs={{0,2},{2,4},{4,6},{6,0},{1,3},{3,5},{5,7},{7,1},{8,10},{10,12},{12... | collective-permute-start | bytes 294920 | tf_op jit(solution)/shard_map/ppermute | solution.py:312
  51.5 34.4 %collective-permute-start.15 = (bf16[2,256,384]{2,1,0:T(8,128)(2,1)}, bf16[2,256,384]{2,1,0:T(8,128)(2,1)S(1)}, u32[]{:S(2)}, u32[]{:S(2)}) collective-permute-start(bf16[2,256,384]{2,1,0:T(8,128)(2,1)} %get-tuple-element.34), channel_id=1, source_target_pairs={{0,8},{8,16},{16,24},{24,32},{32,40},{40,48},{48,56},{56,64},{64,7... | collective-permute-start | bytes 1179656 | tf_op jit(solution)/shard_map/ppermute | solution.py:308
  55.1 8.8 %collective-permute-start.10 = (f32[3,32,256]{2,1,0:T(8,128)S(1)}, f32[3,32,256]{2,1,0:T(8,128)S(1)}, u32[]{:S(2)}, u32[]{:S(2)}) collective-permute-start(f32[3,32,256]{2,1,0:T(8,128)S(1)} %get-tuple-element.31.a), channel_id=1, source_target_pairs={{0,24},{8,0},{16,8},{24,16},{1,25},{9,1},{17,9},{25,17},{2,26},{10... | collective-permute-start | bytes 294920 | tf_op jit(solution)/shard_map/ppermute | solution.py:312
  60.2 11.6 %collective-permute-start.9 = (f32[3,32,256]{2,1,0:T(8,128)S(1)}, f32[3,32,256]{2,1,0:T(8,128)S(1)}, u32[]{:S(2)}, u32[]{:S(2)}) collective-permute-start(f32[3,32,256]{2,1,0:T(8,128)S(1)} %get-tuple-element.31.a), channel_id=1, source_target_pairs={{0,16},{8,24},{16,0},{24,8},{1,17},{9,25},{17,1},{25,9},{2,18},{10... | collective-permute-start | bytes 294920 | tf_op jit(solution)/shard_map/ppermute | solution.py:312
  60.5 11.3 %collective-permute-start.8 = (f32[3,32,256]{2,1,0:T(8,128)S(1)}, f32[3,32,256]{2,1,0:T(8,128)S(1)}, u32[]{:S(2)}, u32[]{:S(2)}) collective-permute-start(f32[3,32,256]{2,1,0:T(8,128)S(1)} %get-tuple-element.31.a), channel_id=1, source_target_pairs={{0,8},{8,16},{16,24},{24,0},{1,9},{9,17},{17,25},{25,1},{2,10},{10... | collective-permute-start | bytes 294920 | tf_op jit(solution)/shard_map/ppermute | solution.py:312
  71.8 7.8 %collective-permute-start.14 = (f32[3,32,256]{2,1,0:T(8,128)S(1)}, f32[3,32,256]{2,1,0:T(8,128)S(1)}, u32[]{:S(2)}, u32[]{:S(2)}) collective-permute-start(f32[3,32,256]{2,1,0:T(8,128)S(1)} %z_sum.2.a), channel_id=1, source_target_pairs={{0,96},{32,0},{64,32},{96,64},{1,97},{33,1},{65,33},{97,65},{2,98}... | collective-permute-start | bytes 294920 | tf_op jit(solution)/shard_map/ppermute | solution.py:312
  77.8 5.0 %collective-permute-start.13 = (f32[3,32,256]{2,1,0:T(8,128)S(1)}, f32[3,32,256]{2,1,0:T(8,128)S(1)}, u32[]{:S(2)}, u32[]{:S(2)}) collective-permute-start(f32[3,32,256]{2,1,0:T(8,128)S(1)} %z_sum.2.a), channel_id=1, source_target_pairs={{0,64},{32,96},{64,0},{96,32},{1,65},{33,97},{65,1},{97,33},{2,66}... | collective-permute-start | bytes 294920 | tf_op jit(solution)/shard_map/ppermute | solution.py:312
  79.3 6.6 %collective-permute-start.12 = (f32[3,32,256]{2,1,0:T(8,128)S(1)}, f32[3,32,256]{2,1,0:T(8,128)S(1)}, u32[]{:S(2)}, u32[]{:S(2)}) collective-permute-start(f32[3,32,256]{2,1,0:T(8,128)S(1)} %z_sum.2.a), channel_id=1, source_target_pairs={{0,32},{32,64},{64,96},{96,0},{1,33},{33,65},{65,97},{97,1},{2,34}... | collective-permute-start | bytes 294920 | tf_op jit(solution)/shard_map/ppermute | solution.py:312
  85.9 1.4 copy-start.1
  87.3 24.9 %copy-start.8 = (bf16[512,512]{1,0:T(8,128)(2,1)S(1)}, bf16[512,512]{1,0:T(8,128)(2,1)}, u32[]{:S(2)}) copy-start(bf16[512,512]{1,0:T(8,128)(2,1)} %constant.21.clone.rest_3_.rest_4_) | copy-start | bytes 1572868
  87.3 24.9 %copy-start.10 = (bf16[512,512]{1,0:T(8,128)(2,1)S(1)}, bf16[512,512]{1,0:T(8,128)(2,1)}, u32[]{:S(2)}) copy-start(bf16[512,512]{1,0:T(8,128)(2,1)} %constant.20.clone.rest_2_.rest_3_) | copy-start | bytes 1572868
  88.6 1.1 copy-start.2
  89.8 14.7 %collective-permute-start.16 = (bf16[2,256,384]{2,1,0:T(8,128)(2,1)S(1)}, bf16[2,256,384]{2,1,0:T(8,128)(2,1)S(1)}, u32[]{:S(2)}, u32[]{:S(2)}) collective-permute-start(bf16[2,256,384]{2,1,0:T(8,128)(2,1)S(1)} %get-tuple-element.37), channel_id=1, source_target_pairs={{8,0},{16,8},{24,16},{32,24},{40,32},{48,40},{56,48},{64,56},{72,6... | collective-permute-start | bytes 1179656 | tf_op jit(solution)/shard_map/ppermute | solution.py:308
  91.1 15.4 %collective-permute-start.17 = (bf16[2,512,256]{2,1,0:T(8,128)(2,1)S(1)}, bf16[2,512,256]{2,1,0:T(8,128)(2,1)S(1)}, u32[]{:S(2)}, u32[]{:S(2)}) collective-permute-start(bf16[2,512,256]{2,1,0:T(8,128)(2,1)S(1)} %get-tuple-element.38), channel_id=1, source_target_pairs={{1,0},{2,1},{3,2},{4,3},{5,4},{6,5},{7,6},{9,8},{10,9},{11,10},{12... | collective-permute-start | bytes 1572872 | tf_op jit(solution)/shard_map/ppermute | solution.py:308
  93.8 4.1 %collective-permute-start.21 = (f32[2,32,256]{2,1,0:T(8,128)S(1)}, f32[2,32,256]{2,1,0:T(8,128)S(1)}, u32[]{:S(2)}, u32[]{:S(2)}) collective-permute-start(f32[2,32,256]{2,1,0:T(8,128)S(1)} %get-tuple-element.39.mine), channel_id=1, source_target_pairs={{0,6},{2,0},{4,2},{6,4},{1,7},{3,1},{5,3},{7,5},{8,14},{10,8},{12,... | collective-permute-start | bytes 196616 | tf_op jit(solution)/shard_map/ppermute | solution.py:312
  95.0 4.7 %collective-permute-start.20 = (f32[2,32,256]{2,1,0:T(8,128)S(1)}, f32[2,32,256]{2,1,0:T(8,128)S(1)}, u32[]{:S(2)}, u32[]{:S(2)}) collective-permute-start(f32[2,32,256]{2,1,0:T(8,128)S(1)} %get-tuple-element.39.mine), channel_id=1, source_target_pairs={{0,4},{2,6},{4,0},{6,2},{1,5},{3,7},{5,1},{7,3},{8,12},{10,14},{12... | collective-permute-start | bytes 196616 | tf_op jit(solution)/shard_map/ppermute | solution.py:312
  95.0 6.1 %collective-permute-start.19 = (f32[2,32,256]{2,1,0:T(8,128)S(1)}, f32[2,32,256]{2,1,0:T(8,128)S(1)}, u32[]{:S(2)}, u32[]{:S(2)}) collective-permute-start(f32[2,32,256]{2,1,0:T(8,128)S(1)} %get-tuple-element.39.mine), channel_id=1, source_target_pairs={{0,2},{2,4},{4,6},{6,0},{1,3},{3,5},{5,7},{7,1},{8,10},{10,12},{12... | collective-permute-start | bytes 196616 | tf_op jit(solution)/shard_map/ppermute | solution.py:312
  101.1 5.3 %collective-permute-start.22 = (f32[4,2,32,256]{3,2,1,0:T(8,128)S(1)}, f32[4,2,32,256]{3,2,1,0:T(8,128)S(1)}, u32[]{:S(2)}, u32[]{:S(2)}) collective-permute-start(f32[4,2,32,256]{3,2,1,0:T(8,128)S(1)} %pad_maximum_fusion.rest_0_), channel_id=1, source_target_pairs={{0,1},{1,0},{2,3},{3,2},{4,5},{5,4},{6,7},{7,6},{8,9},{9,8},{10,11... | collective-permute-start | bytes 786440 | tf_op jit(solution)/shard_map/ppermute | solution.py:316
  104.5 7.7 %collective-permute-start.18 = (bf16[2,256,256]{2,1,0:T(8,128)(2,1)S(1)}, bf16[2,256,256]{2,1,0:T(8,128)(2,1)S(1)}, u32[]{:S(2)}, u32[]{:S(2)}) collective-permute-start(bf16[2,256,256]{2,1,0:T(8,128)(2,1)S(1)} %slice.73), channel_id=1, source_target_pairs={{1,0},{2,1},{3,2},{4,3},{5,4},{6,5},{7,6},{9,8},{10,9},{11,10},{12... | collective-permute-start | bytes 786440 | tf_op jit(solution)/shard_map/ppermute | solution.py:308
  120.4 7.9 %collective-permute-start.24 = (f32[4,3,32,256]{3,2,1,0:T(8,128)S(1)}, f32[4,3,32,256]{3,2,1,0:T(8,128)S(1)}, u32[]{:S(2)}, u32[]{:S(2)}) collective-permute-start(f32[4,3,32,256]{3,2,1,0:T(8,128)S(1)} %get-tuple-element.43), channel_id=1, source_target_pairs={{0,1},{1,0},{2,3},{3,2},{4,5},{5,4},{6,7},{7,6},{8,9},{9,8},{10,11... | collective-permute-start | bytes 1179656 | tf_op jit(solution)/shard_map/ppermute | solution.py:316
  120.5 9.4 %collective-permute-start.28 = (bf16[2,256,256]{2,1,0:T(8,128)(2,1)S(1)}, bf16[2,256,256]{2,1,0:T(8,128)(2,1)S(1)}, u32[]{:S(2)}, u32[]{:S(2)}) collective-permute-start(bf16[2,256,256]{2,1,0:T(8,128)(2,1)S(1)} %get-tuple-element.46), channel_id=1, source_target_pairs={{0,1},{1,2},{2,3},{3,4},{4,5},{5,6},{6,7},{8,9},{9,10},{10,11},{11... | collective-permute-start | bytes 786440 | tf_op jit(solution)/shard_map/ppermute | solution.py:308
  126.4 19.5 %collective-permute-start.23 = (bf16[2,512,256]{2,1,0:T(8,128)(2,1)S(1)}, bf16[2,512,256]{2,1,0:T(8,128)(2,1)S(1)}, u32[]{:S(2)}, u32[]{:S(2)}) collective-permute-start(bf16[2,512,256]{2,1,0:T(8,128)(2,1)S(1)} %get-tuple-element.41), channel_id=1, source_target_pairs={{0,1},{1,2},{2,3},{3,4},{4,5},{5,6},{6,7},{8,9},{9,10},{10,11},{11... | collective-permute-start | bytes 1572872 | tf_op jit(solution)/shard_map/ppermute | solution.py:308
  128.4 3.9 %collective-permute-start.27 = (f32[3,32,256]{2,1,0:T(8,128)S(1)}, f32[3,32,256]{2,1,0:T(8,128)S(1)}, u32[]{:S(2)}, u32[]{:S(2)}) collective-permute-start(f32[3,32,256]{2,1,0:T(8,128)S(1)} %get-tuple-element.50), channel_id=1, source_target_pairs={{0,6},{2,0},{4,2},{6,4},{1,7},{3,1},{5,3},{7,5},{8,14},{10,8},{12,... | collective-permute-start | bytes 294920 | tf_op jit(solution)/shard_map/ppermute | solution.py:312
  128.5 10.2 %collective-permute-start.26 = (f32[3,32,256]{2,1,0:T(8,128)S(1)}, f32[3,32,256]{2,1,0:T(8,128)S(1)}, u32[]{:S(2)}, u32[]{:S(2)}) collective-permute-start(f32[3,32,256]{2,1,0:T(8,128)S(1)} %get-tuple-element.51), channel_id=1, source_target_pairs={{0,4},{2,6},{4,0},{6,2},{1,5},{3,7},{5,1},{7,3},{8,12},{10,14},{12... | collective-permute-start | bytes 294920 | tf_op jit(solution)/shard_map/ppermute | solution.py:312
  129.9 9.6 %collective-permute-start.25 = (f32[3,32,256]{2,1,0:T(8,128)S(1)}, f32[3,32,256]{2,1,0:T(8,128)S(1)}, u32[]{:S(2)}, u32[]{:S(2)}) collective-permute-start(f32[3,32,256]{2,1,0:T(8,128)S(1)} %get-tuple-element.52), channel_id=1, source_target_pairs={{0,2},{2,4},{4,6},{6,0},{1,3},{3,5},{5,7},{7,1},{8,10},{10,12},{12... | collective-permute-start | bytes 294920 | tf_op jit(solution)/shard_map/ppermute | solution.py:312
  139.5 39.5 %copy-start.3 = (f32[2,512,384]{2,1,0:T(8,128)S(1)}, f32[2,512,384]{2,1,0:T(8,128)}, u32[]{:S(2)}) copy-start(f32[2,512,384]{2,1,0:T(8,128)} %copy-done.2) | copy-start | bytes 4718596
  139.5 39.5 %copy-start.4 = (f32[2,512,384]{2,1,0:T(8,128)S(1)}, f32[2,512,384]{2,1,0:T(8,128)}, u32[]{:S(2)}) copy-start(f32[2,512,384]{2,1,0:T(8,128)} %get-tuple-element.40.own) | copy-start | bytes 4718596
  139.6 29.1 %collective-permute-start.29 = (bf16[2,256,384]{2,1,0:T(8,128)(2,1)S(1)}, bf16[2,256,384]{2,1,0:T(8,128)(2,1)S(1)}, u32[]{:S(2)}, u32[]{:S(2)}) collective-permute-start(bf16[2,256,384]{2,1,0:T(8,128)(2,1)S(1)} %get-tuple-element.47), channel_id=1, source_target_pairs={{0,8},{8,16},{16,24},{24,32},{32,40},{40,48},{48,56},{56,64},{64,7... | collective-permute-start | bytes 1179656 | tf_op jit(solution)/shard_map/ppermute | solution.py:308
  141.6 6.6 %collective-permute-start.32 = (f32[3,32,256]{2,1,0:T(8,128)S(1)}, f32[3,32,256]{2,1,0:T(8,128)S(1)}, u32[]{:S(2)}, u32[]{:S(2)}) collective-permute-start(f32[3,32,256]{2,1,0:T(8,128)S(1)} %get-tuple-element.49.a), channel_id=1, source_target_pairs={{0,24},{8,0},{16,8},{24,16},{1,25},{9,1},{17,9},{25,17},{2,26},{10... | collective-permute-start | bytes 294920 | tf_op jit(solution)/shard_map/ppermute | solution.py:312
  145.2 9.1 %collective-permute-start.31 = (f32[3,32,256]{2,1,0:T(8,128)S(1)}, f32[3,32,256]{2,1,0:T(8,128)S(1)}, u32[]{:S(2)}, u32[]{:S(2)}) collective-permute-start(f32[3,32,256]{2,1,0:T(8,128)S(1)} %get-tuple-element.49.a), channel_id=1, source_target_pairs={{0,16},{8,24},{16,0},{24,8},{1,17},{9,25},{17,1},{25,9},{2,18},{10... | collective-permute-start | bytes 294920 | tf_op jit(solution)/shard_map/ppermute | solution.py:312
  145.2 9.1 %collective-permute-start.30 = (f32[3,32,256]{2,1,0:T(8,128)S(1)}, f32[3,32,256]{2,1,0:T(8,128)S(1)}, u32[]{:S(2)}, u32[]{:S(2)}) collective-permute-start(f32[3,32,256]{2,1,0:T(8,128)S(1)} %get-tuple-element.49.a), channel_id=1, source_target_pairs={{0,8},{8,16},{16,24},{24,0},{1,9},{9,17},{17,25},{25,1},{2,10},{10... | collective-permute-start | bytes 294920 | tf_op jit(solution)/shard_map/ppermute | solution.py:312
  154.3 10.5 %collective-permute-start.35 = (f32[3,32,256]{2,1,0:T(8,128)S(1)}, f32[3,32,256]{2,1,0:T(8,128)S(1)}, u32[]{:S(2)}, u32[]{:S(2)}) collective-permute-start(f32[3,32,256]{2,1,0:T(8,128)S(1)} %z_sum.3.a), channel_id=1, source_target_pairs={{0,96},{32,0},{64,32},{96,64},{1,97},{33,1},{65,33},{97,65},{2,98}... | collective-permute-start | bytes 294920 | tf_op jit(solution)/shard_map/ppermute | solution.py:312
  160.4 6.0 %collective-permute-start.34 = (f32[3,32,256]{2,1,0:T(8,128)S(1)}, f32[3,32,256]{2,1,0:T(8,128)S(1)}, u32[]{:S(2)}, u32[]{:S(2)}) collective-permute-start(f32[3,32,256]{2,1,0:T(8,128)S(1)} %z_sum.3.a), channel_id=1, source_target_pairs={{0,64},{32,96},{64,0},{96,32},{1,65},{33,97},{65,1},{97,33},{2,66}... | collective-permute-start | bytes 294920 | tf_op jit(solution)/shard_map/ppermute | solution.py:312
  161.5 7.2 %collective-permute-start.33 = (f32[3,32,256]{2,1,0:T(8,128)S(1)}, f32[3,32,256]{2,1,0:T(8,128)S(1)}, u32[]{:S(2)}, u32[]{:S(2)}) collective-permute-start(f32[3,32,256]{2,1,0:T(8,128)S(1)} %z_sum.3.a), channel_id=1, source_target_pairs={{0,32},{32,64},{64,96},{96,0},{1,33},{33,65},{65,97},{97,1},{2,34}... | collective-permute-start | bytes 294920 | tf_op jit(solution)/shard_map/ppermute | solution.py:312
  168.7 3.6 %collective-permute-start.38 = (f32[2,32,256]{2,1,0:T(8,128)S(1)}, f32[2,32,256]{2,1,0:T(8,128)S(1)}, u32[]{:S(2)}, u32[]{:S(2)}) collective-permute-start(f32[2,32,256]{2,1,0:T(8,128)S(1)} %x_sum.1), channel_id=1, source_target_pairs={{0,6},{2,0},{4,2},{6,4},{1,7},{3,1},{5,3},{7,5},{8,14},{10,8},{12,... | collective-permute-start | bytes 196616 | tf_op jit(solution)/shard_map/ppermute | solution.py:312
  168.8 5.1 %collective-permute-start.37 = (f32[2,32,256]{2,1,0:T(8,128)S(1)}, f32[2,32,256]{2,1,0:T(8,128)S(1)}, u32[]{:S(2)}, u32[]{:S(2)}) collective-permute-start(f32[2,32,256]{2,1,0:T(8,128)S(1)} %x_sum.1), channel_id=1, source_target_pairs={{0,4},{2,6},{4,0},{6,2},{1,5},{3,7},{5,1},{7,3},{8,12},{10,14},{12... | collective-permute-start | bytes 196616 | tf_op jit(solution)/shard_map/ppermute | solution.py:312
  172.3 4.3 %collective-permute-start.36 = (f32[2,32,256]{2,1,0:T(8,128)S(1)}, f32[2,32,256]{2,1,0:T(8,128)S(1)}, u32[]{:S(2)}, u32[]{:S(2)}) collective-permute-start(f32[2,32,256]{2,1,0:T(8,128)S(1)} %x_sum.1), channel_id=1, source_target_pairs={{0,2},{2,4},{4,6},{6,0},{1,3},{3,5},{5,7},{7,1},{8,10},{10,12},{12... | collective-permute-start | bytes 196616 | tf_op jit(solution)/shard_map/ppermute | solution.py:312
  176.6 4.7 %copy-start.11 = (f32[4,2,32,256]{3,2,1,0:T(8,128)}, f32[4,2,32,256]{3,2,1,0:T(8,128)S(1)}, u32[]{:S(2)}) copy-start(f32[4,2,32,256]{3,2,1,0:T(8,128)S(1)} %pad_maximum_fusion.1.mine) | copy-start | bytes 786436
  176.6 4.7 %collective-permute-start.39 = (f32[4,2,32,256]{3,2,1,0:T(8,128)S(1)}, f32[4,2,32,256]{3,2,1,0:T(8,128)S(1)}, u32[]{:S(2)}, u32[]{:S(2)}) collective-permute-start(f32[4,2,32,256]{3,2,1,0:T(8,128)S(1)} %pad_maximum_fusion.1.mine), channel_id=1, source_target_pairs={{0,1},{1,0},{2,3},{3,2},{4,5},{5,4},{6,7},{7,6},{8,9},{9,8},{10,11... | collective-permute-start | bytes 786440 | tf_op jit(solution)/shard_map/ppermute | solution.py:316
  181.3 0.7 copy-start.12

commit v5 on v4

--- a/solution.py
+++ b/solution.py
@@ -29,28 +29,34 @@
     real = (np.cos(phase) * scale).astype(ml_dtypes.bfloat16)
     imag = (np.sin(phase) * scale).astype(ml_dtypes.bfloat16)
     forward = np.block([[real, -imag], [imag, real]])
-    return forward, np.ascontiguousarray(forward.T)
+    return np.stack([forward, forward.T])
 
 
 def frames_kernel(
-    iteration, n_pieces,
-    place, counts, pos, obj, below, right, corner, *rest,
+    iteration, n_low, n_pieces,
+    place, counts, pos, obj, *rest,
 ):
-    pieces, (amps, tab_a, tab_b), rest = rest[:n_pieces], rest[n_pieces : n_pieces + 3], rest[n_pieces + 3 :]
+    lows, (right, corner), rest = rest[:n_low], rest[n_low : n_low + 2], rest[n_low + 2 :]
+    pieces, (amps, tables), rest = rest[:n_pieces], rest[n_pieces : n_pieces + 2], rest[n_pieces + 2 :]
     own_out, low_left, low_right, right_out, corner_out, keep_out, send_out, step_out = rest[:8]
     ext, acc, sums, wave, mis, patch, levels, arrived, here, *rest = rest[8:]
-    landing, probe_scratch = rest[: 6 + n_pieces], rest[6 + n_pieces :]
+    landing, probe_scratch = rest[: 5 + n_pieces], rest[5 + n_pieces :]
     count = counts[0]
+    low_parts, at = [], 0
+    for low in lows:
+        low_parts.append(landing[1].at[:, :, at : at + low.shape[2]])
+        at += low.shape[2]
+    sources = (obj, right, corner, *lows, *pieces, tables)
+    targets = (landing[0], *landing[2:4], *low_parts, *landing[4:])
     copies = [
         pltpu.make_async_copy(source, target, here.at[i])
-        for i, (source, target) in enumerate(
-            zip((obj, below, right, corner, *pieces, tab_a, tab_b), landing)
-        )
+        for i, (source, target) in enumerate(zip(sources, targets))
     ]
     for copy in copies:
         copy.start()
     obj, below, right, corner = landing[:4]
-    pieces, (table_a, table_b) = landing[4 : 4 + n_pieces], landing[4 + n_pieces :]
+    pieces, tables = landing[4 : 4 + n_pieces], landing[4 + n_pieces]
+    table_a, table_b = tables.at[0], tables.at[1]
 
     def fetch(index):
         return pltpu.make_async_copy(amps.at[iteration, index], levels.at[index], arrived.at[index])
@@ -67,7 +73,7 @@
     acc[...] = jnp.zeros_like(acc)
     sums[...] = jnp.zeros_like(sums)
     copies[0].wait()
-    for copy in copies[1:4]:
+    for copy in copies[1 : 3 + n_low]:
         copy.wait()
     for j in range(all_tiles):
         inside = j < inner_tiles
@@ -76,17 +82,17 @@
         ext[:, j, :rows, :] = upper[:, :, at : at + LANES].astype(BF).astype(F32)
         lower = below if inside else corner
         ext[:, j, rows:, :] = lower[:, :, at : at + LANES].astype(F32)
-    for copy in copies[4:]:
+    for copy in copies[3 + n_low :]:
         copy.wait()
-    core, y = place[0], place[1]
-    half, quarter = size // N_CORE, size // (N_CORE * N_Y)
+    core, x = place[0], place[1]
+    half, quarter = size // N_CORE, size // (N_CORE * N_X)
     if n_pieces == 1:
         (probe,) = pieces
     else:
         (probe,) = probe_scratch
         for piece, side in ((pieces[0], core), (pieces[1], 1 - core)):
-            for j in range(N_Y):
-                at = pl.multiple_of(side * half + lax.rem(y - j + N_Y, N_Y) * quarter, quarter)
+            for j in range(N_X):
+                at = pl.multiple_of(side * half + lax.rem(x - j + N_X, N_X) * quarter, quarter)
                 probe[:, pl.ds(at, quarter), :] = piece[j]
     peak = jnp.max(probe[0] * probe[0] + probe[1] * probe[1])
     step_out[0, 0] = ALPHA / (peak + 1e-6)
@@ -176,8 +182,8 @@
         lower = (low_left if j < left_tiles else low_right) if inside else corner_out
         at = at if j < left_tiles or not inside else at - size
         lower[:, :, at : at + LANES] = acc[:, j, rows:, :].astype(lower.dtype)
-    for j in range(N_Y):
-        inner = lax.rem(y + j, N_Y) * quarter
+    for j in range(N_X):
+        inner = lax.rem(x + j, N_X) * quarter
         keep_at = pl.multiple_of(core * half + inner, quarter)
         send_at = pl.multiple_of((1 - core) * half + inner, quarter)
         keep_out[j] = sums[:, pl.ds(keep_at, quarter), :]
@@ -189,15 +195,15 @@
     slots, size = amps.shape[1], amps.shape[2]
     vmem = pl.BlockSpec(memory_space=pltpu.VMEM)
     smem = pl.BlockSpec(memory_space=pltpu.SMEM)
-    quarter = size // (N_CORE * N_Y)
+    quarter = size // (N_CORE * N_X)
     shapes = [
         jax.ShapeDtypeStruct((2, rows, cols), F32),
         jax.ShapeDtypeStruct((2, size, size), F32),
         jax.ShapeDtypeStruct((2, size, cols - size), BF),
         jax.ShapeDtypeStruct((2, rows, size), BF),
         jax.ShapeDtypeStruct((2, size, size), BF),
-        jax.ShapeDtypeStruct((N_Y, 3, quarter, size), F32),
-        jax.ShapeDtypeStruct((N_Y, 3, quarter, size), F32),
+        jax.ShapeDtypeStruct((N_X, 3, quarter, size), F32),
+        jax.ShapeDtypeStruct((N_X, 3, quarter, size), F32),
         jax.ShapeDtypeStruct((1, 1), F32),
     ]
     scratch = [
@@ -210,21 +216,22 @@
         pltpu.VMEM((slots, size, size), BF),
         pltpu.SemaphoreType.DMA((slots,)),
     ]
-    loaded = (obj, *halos, *pieces, *tables)
-    scratch.append(pltpu.SemaphoreType.DMA((len(loaded),)))
-    scratch += [pltpu.VMEM(value.shape, value.dtype) for value in loaded]
+    lows, right, corner = halos
+    scratch.append(pltpu.SemaphoreType.DMA((4 + len(lows) + len(pieces),)))
+    scratch += [pltpu.VMEM(obj.shape, F32), pltpu.VMEM((2, size, cols), BF)]
+    scratch += [pltpu.VMEM(value.shape, value.dtype) for value in (right, corner, *pieces, tables)]
     if len(pieces) > 1:
         scratch.append(pltpu.VMEM((2, size, size), F32))
     return pl.pallas_call(
-        functools.partial(frames_kernel, iteration, len(pieces)),
+        functools.partial(frames_kernel, iteration, len(lows), len(pieces)),
         out_shape=shapes,
-        in_specs=[smem] * 3 + [pl.BlockSpec(memory_space=pltpu.HBM)] * (7 + len(pieces)),
+        in_specs=[smem] * 3 + [pl.BlockSpec(memory_space=pltpu.HBM)] * (5 + len(lows) + len(pieces)),
         out_specs=[vmem] * 7 + [smem],
         scratch_shapes=scratch,
-        compiler_params=pltpu.CompilerParams(vmem_limit_bytes=48 << 20),
+        compiler_params=pltpu.CompilerParams(vmem_limit_bytes=44 << 20),
         cost_estimate=pl.CostEstimate(flops=6_000_000_000, bytes_accessed=8_000_000, transcendentals=0),
         name="frames",
-    )(place, counts, pos, obj, *halos, *pieces, amps, *tables)
+    )(place, counts, pos, obj, *lows, right, corner, *pieces, amps, tables)
 
 
 def spec(space):
@@ -244,14 +251,14 @@
     )(*operands[0], *operands[1])
 
 
-def y_kernel(a, b, c, d, low_left, low_right, corner, total, down):
+def x_kernel(a, b, c, d, low_left, low_right, corner, total, down):
     size = low_left.shape[2]
     total[...] = a[0] + b[...] + c[...] + d[...]
     down[:, :, :size] = (low_left[...] + corner[...].astype(F32)).astype(BF)
     down[:, :, size:] = low_right[...]
 
 
-def z_kernel(a, b, c, d, waited, total):
+def y_kernel(a, b, c, d, waited, total):
     total[...] = a[...] + b[...] + c[...] + d[...]
 
 
@@ -260,7 +267,7 @@
     fresh[...] = mine[...] - total[:2] / (total[2:] + 1.0)
 
 
-def x_kernel(a, b, c, d, mine, waited, fresh):
+def z_kernel(a, b, c, d, mine, waited, fresh):
     probe_step(a, b, c, d, mine, fresh)
 
 
@@ -282,12 +289,12 @@
 
 
 def probe_kernel(place, mine, other, out):
-    core, y = place[0], place[1]
+    core, x = place[0], place[1]
     size = out.shape[1]
-    half, quarter = size // N_CORE, size // (N_CORE * N_Y)
+    half, quarter = size // N_CORE, size // (N_CORE * N_X)
     for piece, side in ((mine, core), (other, 1 - core)):
-        for j in range(N_Y):
-            at = pl.multiple_of(side * half + lax.rem(y - j + N_Y, N_Y) * quarter, quarter)
+        for j in range(N_X):
+            at = pl.multiple_of(side * half + lax.rem(x - j + N_X, N_X) * quarter, quarter)
             out[:, pl.ds(at, quarter), :] = piece[j]
 
 
@@ -316,12 +323,13 @@
     return lax.ppermute(value, "core", [(0, 1), (1, 0)])
 
 
-def halo(below, right):
-    size = below.shape[1]
-    below = moved(below, ROW, N_ROW, -1)
+def halo(lows, right):
+    size = right.shape[2]
+    first = moved(lows[0], ROW, N_ROW, -1)
     right = moved(right, COL, N_COL, -1)
-    corner = moved(below[:, :, :size], COL, N_COL, -1)
-    return (below, right, corner)
+    others = [moved(low, ROW, N_ROW, -1) for low in lows[1:]]
+    corner = moved(first[:, :, :size], COL, N_COL, -1)
+    return ((first, *others), right, corner)
 
 
 def around(value, axis):
@@ -331,38 +339,39 @@
 def local(tables, obj, probe, amps, positions, counts):
     rows, cols = obj.shape[1], obj.shape[2]
     size = probe.shape[-1]
-    half, quarter = size // N_CORE, size // (N_CORE * N_Y)
-    core, y = lax.axis_index("core"), lax.axis_index("y")
-    place = jnp.stack([core, y]).astype(jnp.int32)
-    mine = lax.dynamic_slice(probe, (0, core * half + y * quarter, 0), (2, quarter, size))
+    half, quarter = size // N_CORE, size // (N_CORE * N_X)
+    core, x = lax.axis_index("core"), lax.axis_index("x")
+    place = jnp.stack([core, x]).astype(jnp.int32)
+    mine = lax.dynamic_slice(probe, (0, core * half + x * quarter, 0), (2, quarter, size))
     whole = jax.ShapeDtypeStruct(obj.shape, F32)
     flat = jax.ShapeDtypeStruct((2, size, cols), BF)
     tall = jax.ShapeDtypeStruct((2, rows, size), BF)
     share = jax.ShapeDtypeStruct((3, quarter, size), F32)
     part = jax.ShapeDtypeStruct(mine.shape, F32)
-    below, right = obj[:, :size, :].astype(BF), obj[:, :, :size].astype(BF)
+    lows = [obj[:, :size, :size].astype(BF), obj[:, :size, size:].astype(BF)]
+    right = obj[:, :, :size].astype(BF)
     pieces = (probe,)
     for iteration in range(ITERS):
-        halos = halo(below, right)
+        halos = halo(lows, right)
         own, low_left, low_right, right, corner, keep, send, step = run_frames(
             place, counts[iteration, 0], positions[iteration], obj, halos, pieces, amps, tables, iteration
         )
         corner = moved(corner, COL, N_COL, 1)
         left = moved(right, COL, N_COL, 1)
         sums = keep + swapped(send)
-        sums = [sums[:1]] + [turned(sums[j], "y", j) for j in (1, 2, 3)]
-        total, down = small_call(y_kernel, [share, flat], ([*sums, low_left, low_right, corner], []), "y_sum")
+        sums = [sums[:1]] + [turned(sums[j], "x", j) for j in (1, 2, 3)]
+        total, down = small_call(x_kernel, [share, flat], ([*sums, low_left, low_right, corner], []), "x_sum")
         down = moved(down, ROW, N_ROW, 1)
-        (total,) = small_call(z_kernel, [share], (around(total, "z"), [left]), "z_sum")
-        sums = around(total, "x") + [mine]
+        (total,) = small_call(y_kernel, [share], (around(total, "y"), [left]), "y_sum")
+        sums = around(total, "z") + [mine]
         if iteration < ITERS - 1:
-            mine, obj, below, right = small_call(
-                both_kernel, [part, whole, flat, tall], ([*sums, obj, own, left, down, step], []), "x_sum_object"
+            mine, obj, *lows, right = small_call(
+                both_kernel, [part, whole, flat, tall], ([*sums, obj, own, left, down, step], []), "z_sum_object"
             )
         else:
-            (mine,) = small_call(x_kernel, [part], (sums, [down]), "x_sum")
+            (mine,) = small_call(z_kernel, [part], (sums, [down]), "z_sum")
             (obj,) = small_call(object_step, [whole], ([obj, own, left, down, step], []), "object_update")
-        stack = jnp.stack(around(mine, "y"))
+        stack = jnp.stack(around(mine, "x"))
         pieces = (stack, swapped(stack))
     return (obj, run_probe(place, *pieces))
 
@@ -376,7 +385,7 @@
         P(None, None, ROW + COL),
         P(None, COL, ROW),
     )
-    blocks = tuple(jnp.asarray(block) for block in chirp_blocks(256))
+    blocks = jnp.asarray(chirp_blocks(256))
     return jax.shard_map(
         functools.partial(local, blocks),
         mesh=fine, in_specs=placed, out_specs=(P(None, ROW, COL), P()), check_vma=False,

time: 185 us -> 163 us (0.88)
  waiting for transfers between devices: 77.6 us -> 56.9 us
    ppermute x24, waiting for transfers between devices: 59.4 us -> 43.2 us  [turned(): return lax.ppermute(value, axis, [(s, (s + steps) % 4) for s in range(4)])]
    ppermute x12 -> x13, waiting for transfers between devices: 18.2 us -> 13.7 us  [moved(): lax.ppermute(value, axis, [(s, s + steps) for s in range(first, last)])]
    ppermute x12 -> x13, starting transfers between devices: 34.8 us -> 35.3 us  [moved(): lax.ppermute(value, axis, [(s, s + steps) for s in range(first, last)])]
  transfers between devices with their start and end apart: 40 -> 41, of which waited for: 22 -> 26; matrix products, arithmetic and copies ran while one was open for 1% -> 1% of each run, Pallas kernels for 2% -> 2%
where the time goes in v5:
time: 163 us
  starting transfers between devices  76.8 us (47%)
  waiting for transfers between devices  56.9 us (35%)
  Pallas kernels  21.4 us (13%)
  local copies, waits for them, and re-layouts  4.97 us (3%)
  other arithmetic  1.87 us (1%)
    ppermute x24, waiting for transfers between devices, turned(): return lax.ppermute(value, axis, [(s, (s + steps) % 4) for s in range(4)])  43.2 us
    ppermute x13, starting transfers between devices, moved(): lax.ppermute(value, axis, [(s, s + steps) for s in range(first, last)])  35.3 us
    ppermute x24, starting transfers between devices, turned(): return lax.ppermute(value, axis, [(s, (s + steps) % 4) for s in range(4)])  35 us
    pallas_call x2, Pallas kernels, run_frames(): pl.pallas_call(functools.partial(frames_kernel, iteration, len(lows), len...  15 us
    ppermute x13, waiting for transfers between devices, moved(): lax.ppermute(value, axis, [(s, s + steps) for s in range(first, last)])  13.7 us
    ppermute x4, starting transfers between devices, swapped(): return lax.ppermute(value, 'core', [(0, 1), (1, 0)])  6.52 us
    pallas_call x7, Pallas kernels, small_call(): pl.pallas_call(body, out_shape=shapes, in_specs=[spec(space) for space in...  4.59 us
    unnamed x22, local copies, waits for them, and re-layouts  3.38 us
  transfers between devices with their start and end apart: 41, of which 26 were waited for; matrix products, arithmetic and copies ran while one was open for 1% of the time, Pallas kernels for 2%

profile of v5, /device:TPU:1, one launch (start us, length us, event | category | flops | bytes accessed | tf_op | source)
XLA Modules:
  0.0 163.0 jit_solution(6436676366789356263)
XLA Ops:
  0.7 1.6 %convert.5 = bf16[2,512,384]{2,1,0:T(8,128)(2,1)S(1)} convert(f32[2,512,384]{2,1,0:T(8,128)} %obj.3) | non-fusion elementwise | flops 393216 | bytes 2359296 | tf_op jit(solution)/shard_map/convert.2
  2.3 1.3 collective-permute-start
  3.6 0.8 slice.69
  4.5 3.3 %collective-permute-start.2 = (bf16[2,512,256]{2,1,0:T(8,128)(2,1)}, bf16[2,512,256]{2,1,0:T(8,128)(2,1)S(1)}, u32[]{:S(2)}, u32[]{:S(2)}) collective-permute-start(bf16[2,512,256]{2,1,0:T(8,128)(2,1)} %slice.69), channel_id=1, source_target_pairs={{1,0},{2,1},{3,2},{4,3},{5,4},{6,5},{7,6},{9,8},{10,9},{11,10},{12... | collective-permute-start | bytes 1572872 | tf_op jit(solution)/shard_map/ppermute | solution.py:315
  7.8 1.3 collective-permute-start.1
  9.1 3.6 %collective-permute-done.rest_0_ = bf16[2,256,256]{2,1,0:T(8,128)(2,1)S(1)} collective-permute-done((bf16[2,256,256]{2,1,0:T(8,128)(2,1)S(1)}, bf16[2,256,256]{2,1,0:T(8,128)(2,1)S(1)}, u32[]{:S(2)}, u32[]{:S(2)}) %collective-permute-start) | collective-permute-done | bytes 262176 | tf_op jit(solution)/shard_map/ppermute | solution.py:315
  12.7 3.3 %collective-permute-start.3 = (bf16[2,256,256]{2,1,0:T(8,128)(2,1)S(1)}, bf16[2,256,256]{2,1,0:T(8,128)(2,1)S(1)}, u32[]{:S(2)}, u32[]{:S(2)}) collective-permute-start(bf16[2,256,256]{2,1,0:T(8,128)(2,1)S(1)} %collective-permute-done.rest_0_), channel_id=1, source_target_pairs={{1,0},{2,1},{3,2},{4,3},{5,4},{6,5},{7,6},{9,8},{10,9},{11,10},{12... | collective-permute-start | bytes 786440 | tf_op jit(solution)/shard_map/ppermute | solution.py:315
  16.8 4.4 %collective-permute-done.3.rest_3_ = bf16[2,256,256]{2,1,0:T(8,128)(2,1)S(1)} collective-permute-done((bf16[2,256,256]{2,1,0:T(8,128)(2,1)S(1)}, bf16[2,256,256]{2,1,0:T(8,128)(2,1)S(1)}, u32[]{:S(2)}, u32[]{:S(2)}) %collective-permute-start.3) | collective-permute-done | bytes 262176 | tf_op jit(solution)/shard_map/ppermute | solution.py:315
  21.2 1.2 copy-done.5
  22.4 7.7 %frames.2 = (f32[2,512,384]{2,1,0:T(8,128)S(1)}, f32[2,256,256]{2,1,0:T(8,128)S(1)}, bf16[2,256,128]{2,1,0:T(8,128)(2,1)S(1)}, bf16[2,512,256]{2,1,0:T(8,128)(2,...) custom-call(s32[2]{0:T(128)S(1)} %pad_add_fusion.place, ...), custom_call_target="tpu_custom_call" | custom-call | flops 6000000000 | bytes 8000000 | tf_op jit(solution)/shard_map/frames/pallas_call | solution.py:225
  30.2 1.9 %collective-permute-start.8 = (bf16[2,256,256]{2,1,0:T(8,128)(2,1)S(1)}, bf16[2,256,256]{2,1,0:T(8,128)(2,1)S(1)}, u32[]{:S(2)}, u32[]{:S(2)}) collective-permute-start(bf16[2,256,256]{2,1,0:T(8,128)(2,1)S(1)} %get-tuple-element.30), channel_id=1, source_target_pairs={{0,1},{1,2},{2,3},{3,4},{4,5},{5,6},{6,7},{8,9},{9,10},{10,11},{11... | collective-permute-start | bytes 786440 | tf_op jit(solution)/shard_map/ppermute | solution.py:315
  32.1 1.9 %collective-permute-start.12 = (bf16[2,512,256]{2,1,0:T(8,128)(2,1)}, bf16[2,512,256]{2,1,0:T(8,128)(2,1)S(1)}, u32[]{:S(2)}, u32[]{:S(2)}) collective-permute-start(bf16[2,512,256]{2,1,0:T(8,128)(2,1)} %get-tuple-element.32), channel_id=1, source_target_pairs={{0,1},{1,2},{2,3},{3,4},{4,5},{5,6},{6,7},{8,9},{9,10},{10,11},{11... | collective-permute-start | bytes 1572872 | tf_op jit(solution)/shard_map/ppermute | solution.py:315
  34.2 12.5 %collective-permute-start.7 = (f32[3,32,256]{2,1,0:T(8,128)S(1)}, f32[3,32,256]{2,1,0:T(8,128)S(1)}, u32[]{:S(2)}, u32[]{:S(2)}) collective-permute-start(f32[3,32,256]{2,1,0:T(8,128)S(1)} %get-tuple-element.54), channel_id=1, source_target_pairs={{0,96},{32,0},{64,32},{96,64},{1,97},{33,1},{65,33},{97,65},{2,98}... | collective-permute-start | bytes 294920 | tf_op jit(solution)/shard_map/ppermute | solution.py:319
  46.7 0.7 collective-permute-start.5
  47.3 3.5 %collective-permute-done.7.d = f32[3,32,256]{2,1,0:T(8,128)S(1)} collective-permute-done((f32[3,32,256]{2,1,0:T(8,128)S(1)}, f32[3,32,256]{2,1,0:T(8,128)S(1)}, u32[]{:S(2)}, u32[]{:S(2)}) %collective-permute-start.7) | collective-permute-done | bytes 98336 | tf_op jit(solution)/shard_map/ppermute | solution.py:319
  50.8 1.4 collective-permute-done.6.c
  52.3 2.2 %collective-permute-done.5.b = f32[3,32,256]{2,1,0:T(8,128)S(1)} collective-permute-done((f32[3,32,256]{2,1,0:T(8,128)S(1)}, f32[3,32,256]{2,1,0:T(8,128)S(1)}, u32[]{:S(2)}, u32[]{:S(2)}) %collective-permute-start.5) | collective-permute-done | bytes 98336 | tf_op jit(solution)/shard_map/ppermute | solution.py:319
  54.4 0.8 x_sum.2
  55.3 1.5 collective-permute-start.16
  56.9 2.9 %collective-permute-start.10 = (f32[3,32,256]{2,1,0:T(8,128)S(1)}, f32[3,32,256]{2,1,0:T(8,128)S(1)}, u32[]{:S(2)}, u32[]{:S(2)}) collective-permute-start(f32[3,32,256]{2,1,0:T(8,128)S(1)} %get-tuple-element.31.a), channel_id=1, source_target_pairs={{0,4},{2,6},{4,0},{6,2},{1,5},{3,7},{5,1},{7,3},{8,12},{10,14},{12... | collective-permute-start | bytes 294920 | tf_op jit(solution)/shard_map/ppermute | solution.py:319
  60.3 1.6 collective-permute-done.10.c
  61.9 3.7 %collective-permute-done.9.b = f32[3,32,256]{2,1,0:T(8,128)S(1)} collective-permute-done((f32[3,32,256]{2,1,0:T(8,128)S(1)}, f32[3,32,256]{2,1,0:T(8,128)S(1)}, u32[]{:S(2)}, u32[]{:S(2)}) %collective-permute-start.9) | collective-permute-done | bytes 98336 | tf_op jit(solution)/shard_map/ppermute | solution.py:319
  65.6 2.0 %collective-permute-start.15 = (f32[3,32,256]{2,1,0:T(8,128)S(1)}, f32[3,32,256]{2,1,0:T(8,128)S(1)}, u32[]{:S(2)}, u32[]{:S(2)}) collective-permute-start(f32[3,32,256]{2,1,0:T(8,128)S(1)} %y_sum.2.a), channel_id=1, source_target_pairs={{0,24},{8,0},{16,8},{24,16},{1,25},{9,1},{17,9},{25,17},{2,26},{10... | collective-permute-start | bytes 294920 | tf_op jit(solution)/shard_map/ppermute | solution.py:319
  67.6 1.5 collective-permute-start.14
  69.7 2.9 %collective-permute-done.14.c = f32[3,32,256]{2,1,0:T(8,128)S(1)} collective-permute-done((f32[3,32,256]{2,1,0:T(8,128)S(1)}, f32[3,32,256]{2,1,0:T(8,128)S(1)}, u32[]{:S(2)}, u32[]{:S(2)}) %collective-permute-start.14) | collective-permute-done | bytes 98336 | tf_op jit(solution)/shard_map/ppermute | solution.py:319
  72.6 1.2 collective-permute-done.13.b
  73.7 1.4 copy-done.2
  75.2 1.3 z_sum_object.1
  76.5 1.3 collective-permute-start.17
  77.8 6.5 %collective-permute-start.18 = (bf16[2,512,256]{2,1,0:T(8,128)(2,1)S(1)}, bf16[2,512,256]{2,1,0:T(8,128)(2,1)S(1)}, u32[]{:S(2)}, u32[]{:S(2)}) collective-permute-start(bf16[2,512,256]{2,1,0:T(8,128)(2,1)S(1)} %get-tuple-element.38), channel_id=1, source_target_pairs={{1,0},{2,1},{3,2},{4,3},{5,4},{6,5},{7,6},{9,8},{10,9},{11,10},{12... | collective-permute-start | bytes 1572872 | tf_op jit(solution)/shard_map/ppermute | solution.py:315
  84.2 2.5 %collective-permute-start.22 = (f32[2,32,256]{2,1,0:T(8,128)S(1)}, f32[2,32,256]{2,1,0:T(8,128)S(1)}, u32[]{:S(2)}, u32[]{:S(2)}) collective-permute-start(f32[2,32,256]{2,1,0:T(8,128)S(1)} %get-tuple-element.39.mine), channel_id=1, source_target_pairs={{0,96},{32,0},{64,32},{96,64},{1,97},{33,1},{65,33},{97,65},{2,98}... | collective-permute-start | bytes 196616 | tf_op jit(solution)/shard_map/ppermute | solution.py:319
  86.7 1.8 %collective-permute-start.21 = (f32[2,32,256]{2,1,0:T(8,128)S(1)}, f32[2,32,256]{2,1,0:T(8,128)S(1)}, u32[]{:S(2)}, u32[]{:S(2)}) collective-permute-start(f32[2,32,256]{2,1,0:T(8,128)S(1)} %get-tuple-element.39.mine), channel_id=1, source_target_pairs={{0,64},{32,96},{64,0},{96,32},{1,65},{33,97},{65,1},{97,33},{2,66}... | collective-permute-start | bytes 196616 | tf_op jit(solution)/shard_map/ppermute | solution.py:319
  88.5 0.9 collective-permute-done.22
  89.4 2.8 %collective-permute-done.21 = f32[2,32,256]{2,1,0:T(8,128)S(1)} collective-permute-done((f32[2,32,256]{2,1,0:T(8,128)S(1)}, f32[2,32,256]{2,1,0:T(8,128)S(1)}, u32[]{:S(2)}, u32[]{:S(2)}) %collective-permute-start.21) | collective-permute-done | bytes 65568 | tf_op jit(solution)/shard_map/ppermute | solution.py:319
  92.2 1.3 collective-permute-done.20
  93.6 0.8 collective-permute-start.23
  94.4 1.9 %collective-permute-start.19 = (bf16[2,256,256]{2,1,0:T(8,128)(2,1)S(1)}, bf16[2,256,256]{2,1,0:T(8,128)(2,1)S(1)}, u32[]{:S(2)}, u32[]{:S(2)}) collective-permute-start(bf16[2,256,256]{2,1,0:T(8,128)(2,1)S(1)} %slice.74), channel_id=1, source_target_pairs={{1,0},{2,1},{3,2},{4,3},{5,4},{6,5},{7,6},{9,8},{10,9},{11,10},{12... | collective-permute-start | bytes 786440 | tf_op jit(solution)/shard_map/ppermute | solution.py:315
  96.3 5.7 %collective-permute-done.19.rest_2_ = bf16[2,256,256]{2,1,0:T(8,128)(2,1)S(1)} collective-permute-done((bf16[2,256,256]{2,1,0:T(8,128)(2,1)S(1)}, bf16[2,256,256]{2,1,0:T(8,128)(2,1)S(1)}, u32[]{:S(2)}, u32[]{:S(2)}) %collective-permute-start.19) | collective-permute-done | bytes 262176 | tf_op jit(solution)/shard_map/ppermute | solution.py:315
  102.0 7.3 %frames.3 = (f32[2,512,384]{2,1,0:T(8,128)S(1)}, f32[2,256,256]{2,1,0:T(8,128)S(1)}, bf16[2,256,128]{2,1,0:T(8,128)(2,1)S(1)}, bf16[2,512,256]{2,1,0:T(8,128)(2,...) custom-call(s32[2]{0:T(128)S(1)} %pad_add_fusion.place, ...), custom_call_target="tpu_custom_call" | custom-call | flops 6000000000 | bytes 8000000 | tf_op jit(solution)/shard_map/frames/pallas_call | solution.py:225
  109.5 2.2 %collective-permute-start.29 = (bf16[2,256,256]{2,1,0:T(8,128)(2,1)S(1)}, bf16[2,256,256]{2,1,0:T(8,128)(2,1)S(1)}, u32[]{:S(2)}, u32[]{:S(2)}) collective-permute-start(bf16[2,256,256]{2,1,0:T(8,128)(2,1)S(1)} %get-tuple-element.46), channel_id=1, source_target_pairs={{0,1},{1,2},{2,3},{3,4},{4,5},{5,6},{6,7},{8,9},{9,10},{10,11},{11... | collective-permute-start | bytes 786440 | tf_op jit(solution)/shard_map/ppermute | solution.py:315
  111.6 1.9 %collective-permute-start.24 = (bf16[2,512,256]{2,1,0:T(8,128)(2,1)S(1)}, bf16[2,512,256]{2,1,0:T(8,128)(2,1)S(1)}, u32[]{:S(2)}, u32[]{:S(2)}) collective-permute-start(bf16[2,512,256]{2,1,0:T(8,128)(2,1)S(1)} %get-tuple-element.41), channel_id=1, source_target_pairs={{0,1},{1,2},{2,3},{3,4},{4,5},{5,6},{6,7},{8,9},{9,10},{10,11},{11... | collective-permute-start | bytes 1572872 | tf_op jit(solution)/shard_map/ppermute | solution.py:315
  113.7 1.2 collective-permute-start.28
  114.9 0.9 collective-permute-start.27
  115.8 1.8 %collective-permute-done.28.d = f32[3,32,256]{2,1,0:T(8,128)S(1)} collective-permute-done((f32[3,32,256]{2,1,0:T(8,128)S(1)}, f32[3,32,256]{2,1,0:T(8,128)S(1)}, u32[]{:S(2)}, u32[]{:S(2)}) %collective-permute-start.28) | collective-permute-done | bytes 98336 | tf_op jit(solution)/shard_map/ppermute | solution.py:319
  117.6 2.4 %collective-permute-done.27.c = f32[3,32,256]{2,1,0:T(8,128)S(1)} collective-permute-done((f32[3,32,256]{2,1,0:T(8,128)S(1)}, f32[3,32,256]{2,1,0:T(8,128)S(1)}, u32[]{:S(2)}, u32[]{:S(2)}) %collective-permute-start.27) | collective-permute-done | bytes 98336 | tf_op jit(solution)/shard_map/ppermute | solution.py:319
  120.0 3.0 %collective-permute-done.26.b = f32[3,32,256]{2,1,0:T(8,128)S(1)} collective-permute-done((f32[3,32,256]{2,1,0:T(8,128)S(1)}, f32[3,32,256]{2,1,0:T(8,128)S(1)}, u32[]{:S(2)}, u32[]{:S(2)}) %collective-permute-start.26) | collective-permute-done | bytes 98336 | tf_op jit(solution)/shard_map/ppermute | solution.py:319
  123.0 6.9 %collective-permute-start.30 = (bf16[2,256,384]{2,1,0:T(8,128)(2,1)S(1)}, bf16[2,256,384]{2,1,0:T(8,128)(2,1)S(1)}, u32[]{:S(2)}, u32[]{:S(2)}) collective-permute-start(bf16[2,256,384]{2,1,0:T(8,128)(2,1)S(1)} %get-tuple-element.47), channel_id=1, source_target_pairs={{0,8},{8,16},{16,24},{24,32},{32,40},{40,48},{48,56},{56,64},{64,7... | collective-permute-start | bytes 1179656 | tf_op jit(solution)/shard_map/ppermute | solution.py:315
  130.0 1.6 collective-permute-start.32
  131.6 1.9 %collective-permute-done.33.d = f32[3,32,256]{2,1,0:T(8,128)S(1)} collective-permute-done((f32[3,32,256]{2,1,0:T(8,128)S(1)}, f32[3,32,256]{2,1,0:T(8,128)S(1)}, u32[]{:S(2)}, u32[]{:S(2)}) %collective-permute-start.33) | collective-permute-done | bytes 98336 | tf_op jit(solution)/shard_map/ppermute | solution.py:319
  133.5 1.6 collective-permute-done.32.c
  135.1 1.2 collective-permute-done.31.b
  136.3 3.7 %collective-permute-start.36 = (f32[3,32,256]{2,1,0:T(8,128)S(1)}, f32[3,32,256]{2,1,0:T(8,128)S(1)}, u32[]{:S(2)}, u32[]{:S(2)}) collective-permute-start(f32[3,32,256]{2,1,0:T(8,128)S(1)} %y_sum.3.a), channel_id=1, source_target_pairs={{0,24},{8,0},{16,8},{24,16},{1,25},{9,1},{17,9},{25,17},{2,26},{10... | collective-permute-start | bytes 294920 | tf_op jit(solution)/shard_map/ppermute | solution.py:319
  140.3 0.7 collective-permute-start.34
  141.0 1.6 collective-permute-done.36.d
  142.6 2.5 %collective-permute-done.35.c = f32[3,32,256]{2,1,0:T(8,128)S(1)} collective-permute-done((f32[3,32,256]{2,1,0:T(8,128)S(1)}, f32[3,32,256]{2,1,0:T(8,128)S(1)}, u32[]{:S(2)}, u32[]{:S(2)}) %collective-permute-start.35) | collective-permute-done | bytes 98336 | tf_op jit(solution)/shard_map/ppermute | solution.py:319
  145.0 0.9 collective-permute-done.34.b
  146.1 2.1 %collective-permute-start.38 = (f32[2,32,256]{2,1,0:T(8,128)S(1)}, f32[2,32,256]{2,1,0:T(8,128)S(1)}, u32[]{:S(2)}, u32[]{:S(2)}) collective-permute-start(f32[2,32,256]{2,1,0:T(8,128)S(1)} %z_sum.1), channel_id=1, source_target_pairs={{0,64},{32,96},{64,0},{96,32},{1,65},{33,97},{65,1},{97,33},{2,66}... | collective-permute-start | bytes 196616 | tf_op jit(solution)/shard_map/ppermute | solution.py:319
  148.2 1.0 collective-permute-done.39
  149.2 1.6 collective-permute-done.38
  150.8 1.7 %collective-permute-done.37 = f32[2,32,256]{2,1,0:T(8,128)S(1)} collective-permute-done((f32[2,32,256]{2,1,0:T(8,128)S(1)}, f32[2,32,256]{2,1,0:T(8,128)S(1)}, u32[]{:S(2)}, u32[]{:S(2)}) %collective-permute-start.37) | collective-permute-done | bytes 65568 | tf_op jit(solution)/shard_map/ppermute | solution.py:319
  152.5 5.6 %collective-permute-start.40 = (f32[4,2,32,256]{3,2,1,0:T(8,128)S(1)}, f32[4,2,32,256]{3,2,1,0:T(8,128)S(1)}, u32[]{:S(2)}, u32[]{:S(2)}) collective-permute-start(f32[4,2,32,256]{3,2,1,0:T(8,128)S(1)} %pad_maximum_fusion.1.mine), channel_id=1, source_target_pairs={{0,1},{1,0},{2,3},{3,2},{4,5},{5,4},{6,7},{7,6},{8,9},{9,8},{10,11... | collective-permute-start | bytes 786440 | tf_op jit(solution)/shard_map/ppermute | solution.py:323
  158.1 2.3 %object_update.1 = f32[2,512,384]{2,1,0:T(8,128)} custom-call(f32[2,512,384]{2,1,0:T(8,128)S(1)} %get-tuple-element.36.obj, f32[2,512,384]{2,1,0:T(8,128)S(1)} %get-tuple-element.40.own, bf16[2,512,256]{2,1,0:T(8,128)(2,1)S(1)} %collective-permute-done.24.left.waited, bf16[2,256,384]{2,1,0:T(8,128)(2,1)S(1)} %collective-permute-done.30.down.waited, ...), custom_call_target="tpu_custom_call" | custom-call | flops 2000000 | bytes 4000000 | tf_op jit(solution)/shard_map/object_update/pallas_call | solution.py:243
  160.4 0.7 copy-done.8
  161.2 1.9 %probe_whole.1 = f32[2,256,256]{2,1,0:T(8,128)} custom-call(s32[2]{0:T(128)} %copy-done.4, f32[4,2,32,256]{3,2,1,0:T(8,128)} %copy-done.7, f32[4,2,32,256]{3,2,1,0:T(8,128)} %copy-done.8), custom_call_target="tpu_custom_call" | custom-call | tf_op jit(solution)/shard_map/probe_whole/pallas_call | solution.py:304
  (65 shorter events, 3.1 us)
Async XLA Ops:
  0.6 20.6 %copy-start = (f32[2,512,384]{2,1,0:T(8,128)S(1)}, f32[2,512,384]{2,1,0:T(8,128)}, u32[]{:S(2)}) copy-start(f32[2,512,384]{2,1,0:T(8,128)} %obj.3) | copy-start | bytes 4718596
  0.6 15.4 %copy-start.9 = (s32[2,2,12]{2,1,0:T(2,128)S(1)}, s32[2,2,12]{2,1,0:T(2,128)}, u32[]{:S(2)}) copy-start(s32[2,2,12]{2,1,0:T(2,128)} %param.9) | copy-start | bytes 580
  0.7 15.5 %copy-start.10 = (s32[2,1,1]{0,2,1:T(1,128)S(1)}, s32[2,1,1]{0,2,1:T(1,128)}, u32[]{:S(2)}) copy-start(s32[2,1,1]{0,2,1:T(1,128)} %param.10) | copy-start | bytes 28
  0.7 20.5 %copy-start.3 = (f32[2,256,256]{2,1,0:T(8,128)S(1)}, f32[2,256,256]{2,1,0:T(8,128)}, u32[]{:S(2)}) copy-start(f32[2,256,256]{2,1,0:T(8,128)} %rest_4_.1) | copy-start | bytes 1572868
  2.3 10.4 %collective-permute-start = (bf16[2,256,256]{2,1,0:T(8,128)(2,1)S(1)}, bf16[2,256,256]{2,1,0:T(8,128)(2,1)S(1)}, u32[]{:S(2)}, u32[]{:S(2)}) collective-permute-start(bf16[2,256,256]{2,1,0:T(8,128)(2,1)S(1)} %slice.67), channel_id=1, source_target_pairs={{8,0},{16,8},{24,16},{32,24},{40,32},{48,40},{56,48},{64,56},{72,6... | collective-permute-start | bytes 786440 | tf_op jit(solution)/shard_map/ppermute | solution.py:315
  4.5 16.7 %collective-permute-start.2 = (bf16[2,512,256]{2,1,0:T(8,128)(2,1)}, bf16[2,512,256]{2,1,0:T(8,128)(2,1)S(1)}, u32[]{:S(2)}, u32[]{:S(2)}) collective-permute-start(bf16[2,512,256]{2,1,0:T(8,128)(2,1)} %slice.69), channel_id=1, source_target_pairs={{1,0},{2,1},{3,2},{4,3},{5,4},{6,5},{7,6},{9,8},{10,9},{11,10},{12... | collective-permute-start | bytes 1572872 | tf_op jit(solution)/shard_map/ppermute | solution.py:315
  7.8 9.0 %collective-permute-start.1 = (bf16[2,256,128]{2,1,0:T(8,128)(2,1)S(1)}, bf16[2,256,128]{2,1,0:T(8,128)(2,1)S(1)}, u32[]{:S(2)}, u32[]{:S(2)}) collective-permute-start(bf16[2,256,128]{2,1,0:T(8,128)(2,1)S(1)} %slice.68), channel_id=1, source_target_pairs={{8,0},{16,8},{24,16},{32,24},{40,32},{48,40},{56,48},{64,56},{72,6... | collective-permute-start | bytes 393224 | tf_op jit(solution)/shard_map/ppermute | solution.py:315
  12.7 8.5 %collective-permute-start.3 = (bf16[2,256,256]{2,1,0:T(8,128)(2,1)S(1)}, bf16[2,256,256]{2,1,0:T(8,128)(2,1)S(1)}, u32[]{:S(2)}, u32[]{:S(2)}) collective-permute-start(bf16[2,256,256]{2,1,0:T(8,128)(2,1)S(1)} %collective-permute-done.rest_0_), channel_id=1, source_target_pairs={{1,0},{2,1},{3,2},{4,3},{5,4},{6,5},{7,6},{9,8},{10,9},{11,10},{12... | collective-permute-start | bytes 786440 | tf_op jit(solution)/shard_map/ppermute | solution.py:315
  16.2 85.9 %copy-start.4 = (s32[2]{0:T(128)}, s32[2]{0:T(128)S(1)}, u32[]{:S(2)}) copy-start(s32[2]{0:T(128)S(1)} %pad_add_fusion.place) | copy-start | bytes 28
  21.2 1.2 copy-start.5
  30.1 25.2 %copy-start.1 = (f32[2,512,384]{2,1,0:T(8,128)}, f32[2,512,384]{2,1,0:T(8,128)S(1)}, u32[]{:S(2)}) copy-start(f32[2,512,384]{2,1,0:T(8,128)S(1)} %get-tuple-element.33.own) | copy-start | bytes 4718596
  30.1 4.0 %collective-permute-start.4 = (f32[4,3,32,256]{3,2,1,0:T(8,128)S(1)}, f32[4,3,32,256]{3,2,1,0:T(8,128)S(1)}, u32[]{:S(2)}, u32[]{:S(2)}) collective-permute-start(f32[4,3,32,256]{3,2,1,0:T(8,128)S(1)} %get-tuple-element.27), channel_id=1, source_target_pairs={{0,1},{1,0},{2,3},{3,2},{4,5},{5,4},{6,7},{7,6},{8,9},{9,8},{10,11... | collective-permute-start | bytes 1179656 | tf_op jit(solution)/shard_map/ppermute | solution.py:323
  30.2 17.1 %collective-permute-start.8 = (bf16[2,256,256]{2,1,0:T(8,128)(2,1)S(1)}, bf16[2,256,256]{2,1,0:T(8,128)(2,1)S(1)}, u32[]{:S(2)}, u32[]{:S(2)}) collective-permute-start(bf16[2,256,256]{2,1,0:T(8,128)(2,1)S(1)} %get-tuple-element.30), channel_id=1, source_target_pairs={{0,1},{1,2},{2,3},{3,4},{4,5},{5,6},{6,7},{8,9},{9,10},{10,11},{11... | collective-permute-start | bytes 786440 | tf_op jit(solution)/shard_map/ppermute | solution.py:315
  32.1 27.6 %collective-permute-start.12 = (bf16[2,512,256]{2,1,0:T(8,128)(2,1)}, bf16[2,512,256]{2,1,0:T(8,128)(2,1)S(1)}, u32[]{:S(2)}, u32[]{:S(2)}) collective-permute-start(bf16[2,512,256]{2,1,0:T(8,128)(2,1)} %get-tuple-element.32), channel_id=1, source_target_pairs={{0,1},{1,2},{2,3},{3,4},{4,5},{5,6},{6,7},{8,9},{9,10},{10,11},{11... | collective-permute-start | bytes 1572872 | tf_op jit(solution)/shard_map/ppermute | solution.py:315
  34.2 16.6 %collective-permute-start.7 = (f32[3,32,256]{2,1,0:T(8,128)S(1)}, f32[3,32,256]{2,1,0:T(8,128)S(1)}, u32[]{:S(2)}, u32[]{:S(2)}) collective-permute-start(f32[3,32,256]{2,1,0:T(8,128)S(1)} %get-tuple-element.54), channel_id=1, source_target_pairs={{0,96},{32,0},{64,32},{96,64},{1,97},{33,1},{65,33},{97,65},{2,98}... | collective-permute-start | bytes 294920 | tf_op jit(solution)/shard_map/ppermute | solution.py:319
  46.6 5.6 %collective-permute-start.6 = (f32[3,32,256]{2,1,0:T(8,128)S(1)}, f32[3,32,256]{2,1,0:T(8,128)S(1)}, u32[]{:S(2)}, u32[]{:S(2)}) collective-permute-start(f32[3,32,256]{2,1,0:T(8,128)S(1)} %get-tuple-element.55), channel_id=1, source_target_pairs={{0,64},{32,96},{64,0},{96,32},{1,65},{33,97},{65,1},{97,33},{2,66}... | collective-permute-start | bytes 294920 | tf_op jit(solution)/shard_map/ppermute | solution.py:319
  46.7 7.8 %collective-permute-start.5 = (f32[3,32,256]{2,1,0:T(8,128)S(1)}, f32[3,32,256]{2,1,0:T(8,128)S(1)}, u32[]{:S(2)}, u32[]{:S(2)}) collective-permute-start(f32[3,32,256]{2,1,0:T(8,128)S(1)} %get-tuple-element.56), channel_id=1, source_target_pairs={{0,32},{32,64},{64,96},{96,0},{1,33},{33,65},{65,97},{97,1},{2,34}... | collective-permute-start | bytes 294920 | tf_op jit(solution)/shard_map/ppermute | solution.py:319
  55.3 18.5 %collective-permute-start.16 = (bf16[2,256,384]{2,1,0:T(8,128)(2,1)}, bf16[2,256,384]{2,1,0:T(8,128)(2,1)S(1)}, u32[]{:S(2)}, u32[]{:S(2)}) collective-permute-start(bf16[2,256,384]{2,1,0:T(8,128)(2,1)} %get-tuple-element.34), channel_id=1, source_target_pairs={{0,8},{8,16},{16,24},{24,32},{32,40},{40,48},{48,56},{56,64},{64,7... | collective-permute-start | bytes 1179656 | tf_op jit(solution)/shard_map/ppermute | solution.py:315
  56.8 3.5 %collective-permute-start.11 = (f32[3,32,256]{2,1,0:T(8,128)S(1)}, f32[3,32,256]{2,1,0:T(8,128)S(1)}, u32[]{:S(2)}, u32[]{:S(2)}) collective-permute-start(f32[3,32,256]{2,1,0:T(8,128)S(1)} %get-tuple-element.31.a), channel_id=1, source_target_pairs={{0,6},{2,0},{4,2},{6,4},{1,7},{3,1},{5,3},{7,5},{8,14},{10,8},{12,... | collective-permute-start | bytes 294920 | tf_op jit(solution)/shard_map/ppermute | solution.py:319
  56.9 5.1 %collective-permute-start.10 = (f32[3,32,256]{2,1,0:T(8,128)S(1)}, f32[3,32,256]{2,1,0:T(8,128)S(1)}, u32[]{:S(2)}, u32[]{:S(2)}) collective-permute-start(f32[3,32,256]{2,1,0:T(8,128)S(1)} %get-tuple-element.31.a), channel_id=1, source_target_pairs={{0,4},{2,6},{4,0},{6,2},{1,5},{3,7},{5,1},{7,3},{8,12},{10,14},{12... | collective-permute-start | bytes 294920 | tf_op jit(solution)/shard_map/ppermute | solution.py:319
  59.8 5.8 %collective-permute-start.9 = (f32[3,32,256]{2,1,0:T(8,128)S(1)}, f32[3,32,256]{2,1,0:T(8,128)S(1)}, u32[]{:S(2)}, u32[]{:S(2)}) collective-permute-start(f32[3,32,256]{2,1,0:T(8,128)S(1)} %get-tuple-element.31.a), channel_id=1, source_target_pairs={{0,2},{2,4},{4,6},{6,0},{1,3},{3,5},{5,7},{7,1},{8,10},{10,12},{12... | collective-permute-start | bytes 294920 | tf_op jit(solution)/shard_map/ppermute | solution.py:319
  65.6 4.0 %collective-permute-start.15 = (f32[3,32,256]{2,1,0:T(8,128)S(1)}, f32[3,32,256]{2,1,0:T(8,128)S(1)}, u32[]{:S(2)}, u32[]{:S(2)}) collective-permute-start(f32[3,32,256]{2,1,0:T(8,128)S(1)} %y_sum.2.a), channel_id=1, source_target_pairs={{0,24},{8,0},{16,8},{24,16},{1,25},{9,1},{17,9},{25,17},{2,26},{10... | collective-permute-start | bytes 294920 | tf_op jit(solution)/shard_map/ppermute | solution.py:319
  67.6 5.0 %collective-permute-start.14 = (f32[3,32,256]{2,1,0:T(8,128)S(1)}, f32[3,32,256]{2,1,0:T(8,128)S(1)}, u32[]{:S(2)}, u32[]{:S(2)}) collective-permute-start(f32[3,32,256]{2,1,0:T(8,128)S(1)} %y_sum.2.a), channel_id=1, source_target_pairs={{0,16},{8,24},{16,0},{24,8},{1,17},{9,25},{17,1},{25,9},{2,18},{10... | collective-permute-start | bytes 294920 | tf_op jit(solution)/shard_map/ppermute | solution.py:319
  69.1 4.7 %collective-permute-start.13 = (f32[3,32,256]{2,1,0:T(8,128)S(1)}, f32[3,32,256]{2,1,0:T(8,128)S(1)}, u32[]{:S(2)}, u32[]{:S(2)}) collective-permute-start(f32[3,32,256]{2,1,0:T(8,128)S(1)} %y_sum.2.a), channel_id=1, source_target_pairs={{0,8},{8,16},{16,24},{24,0},{1,9},{9,17},{17,25},{25,1},{2,10},{10... | collective-permute-start | bytes 294920 | tf_op jit(solution)/shard_map/ppermute | solution.py:319
  73.7 1.4 copy-start.2
  75.2 26.9 %copy-start.6 = (bf16[2,512,512]{2,1,0:T(8,128)(2,1)S(1)}, bf16[2,512,512]{2,1,0:T(8,128)(2,1)}, u32[]{:S(2)}) copy-start(bf16[2,512,512]{2,1,0:T(8,128)(2,1)} %constant.20.clone.rest_6_) | copy-start | bytes 3145732
  76.5 17.9 %collective-permute-start.17 = (bf16[2,256,384]{2,1,0:T(8,128)(2,1)S(1)}, bf16[2,256,384]{2,1,0:T(8,128)(2,1)S(1)}, u32[]{:S(2)}, u32[]{:S(2)}) collective-permute-start(bf16[2,256,384]{2,1,0:T(8,128)(2,1)S(1)} %get-tuple-element.37), channel_id=1, source_target_pairs={{8,0},{16,8},{24,16},{32,24},{40,32},{48,40},{56,48},{64,56},{72,6... | collective-permute-start | bytes 1179656 | tf_op jit(solution)/shard_map/ppermute | solution.py:315
  77.8 18.6 %collective-permute-start.18 = (bf16[2,512,256]{2,1,0:T(8,128)(2,1)S(1)}, bf16[2,512,256]{2,1,0:T(8,128)(2,1)S(1)}, u32[]{:S(2)}, u32[]{:S(2)}) collective-permute-start(bf16[2,512,256]{2,1,0:T(8,128)(2,1)S(1)} %get-tuple-element.38), channel_id=1, source_target_pairs={{1,0},{2,1},{3,2},{4,3},{5,4},{6,5},{7,6},{9,8},{10,9},{11,10},{12... | collective-permute-start | bytes 1572872 | tf_op jit(solution)/shard_map/ppermute | solution.py:315
  84.2 5.2 %collective-permute-start.22 = (f32[2,32,256]{2,1,0:T(8,128)S(1)}, f32[2,32,256]{2,1,0:T(8,128)S(1)}, u32[]{:S(2)}, u32[]{:S(2)}) collective-permute-start(f32[2,32,256]{2,1,0:T(8,128)S(1)} %get-tuple-element.39.mine), channel_id=1, source_target_pairs={{0,96},{32,0},{64,32},{96,64},{1,97},{33,1},{65,33},{97,65},{2,98}... | collective-permute-start | bytes 196616 | tf_op jit(solution)/shard_map/ppermute | solution.py:319
  86.7 5.5 %collective-permute-start.21 = (f32[2,32,256]{2,1,0:T(8,128)S(1)}, f32[2,32,256]{2,1,0:T(8,128)S(1)}, u32[]{:S(2)}, u32[]{:S(2)}) collective-permute-start(f32[2,32,256]{2,1,0:T(8,128)S(1)} %get-tuple-element.39.mine), channel_id=1, source_target_pairs={{0,64},{32,96},{64,0},{96,32},{1,65},{33,97},{65,1},{97,33},{2,66}... | collective-permute-start | bytes 196616 | tf_op jit(solution)/shard_map/ppermute | solution.py:319
  88.5 5.1 %collective-permute-start.20 = (f32[2,32,256]{2,1,0:T(8,128)S(1)}, f32[2,32,256]{2,1,0:T(8,128)S(1)}, u32[]{:S(2)}, u32[]{:S(2)}) collective-permute-start(f32[2,32,256]{2,1,0:T(8,128)S(1)} %get-tuple-element.39.mine), channel_id=1, source_target_pairs={{0,32},{32,64},{64,96},{96,0},{1,33},{33,65},{65,97},{97,1},{2,34}... | collective-permute-start | bytes 196616 | tf_op jit(solution)/shard_map/ppermute | solution.py:319
  93.6 2.7 %collective-permute-start.23 = (f32[4,2,32,256]{3,2,1,0:T(8,128)S(1)}, f32[4,2,32,256]{3,2,1,0:T(8,128)S(1)}, u32[]{:S(2)}, u32[]{:S(2)}) collective-permute-start(f32[4,2,32,256]{3,2,1,0:T(8,128)S(1)} %pad_maximum_fusion.rest_3_), channel_id=1, source_target_pairs={{0,1},{1,0},{2,3},{3,2},{4,5},{5,4},{6,7},{7,6},{8,9},{9,8},{10,11... | collective-permute-start | bytes 786440 | tf_op jit(solution)/shard_map/ppermute | solution.py:323
  94.4 7.7 %collective-permute-start.19 = (bf16[2,256,256]{2,1,0:T(8,128)(2,1)S(1)}, bf16[2,256,256]{2,1,0:T(8,128)(2,1)S(1)}, u32[]{:S(2)}, u32[]{:S(2)}) collective-permute-start(bf16[2,256,256]{2,1,0:T(8,128)(2,1)S(1)} %slice.74), channel_id=1, source_target_pairs={{1,0},{2,1},{3,2},{4,3},{5,4},{6,5},{7,6},{9,8},{10,9},{11,10},{12... | collective-permute-start | bytes 786440 | tf_op jit(solution)/shard_map/ppermute | solution.py:315
  109.4 4.2 %collective-permute-start.25 = (f32[4,3,32,256]{3,2,1,0:T(8,128)S(1)}, f32[4,3,32,256]{3,2,1,0:T(8,128)S(1)}, u32[]{:S(2)}, u32[]{:S(2)}) collective-permute-start(f32[4,3,32,256]{3,2,1,0:T(8,128)S(1)} %get-tuple-element.43), channel_id=1, source_target_pairs={{0,1},{1,0},{2,3},{3,2},{4,5},{5,4},{6,7},{7,6},{8,9},{9,8},{10,11... | collective-permute-start | bytes 1179656 | tf_op jit(solution)/shard_map/ppermute | solution.py:323
  109.5 6.4 %collective-permute-start.29 = (bf16[2,256,256]{2,1,0:T(8,128)(2,1)S(1)}, bf16[2,256,256]{2,1,0:T(8,128)(2,1)S(1)}, u32[]{:S(2)}, u32[]{:S(2)}) collective-permute-start(bf16[2,256,256]{2,1,0:T(8,128)(2,1)S(1)} %get-tuple-element.46), channel_id=1, source_target_pairs={{0,1},{1,2},{2,3},{3,4},{4,5},{5,6},{6,7},{8,9},{9,10},{10,11},{11... | collective-permute-start | bytes 786440 | tf_op jit(solution)/shard_map/ppermute | solution.py:315
  111.6 20.0 %collective-permute-start.24 = (bf16[2,512,256]{2,1,0:T(8,128)(2,1)S(1)}, bf16[2,512,256]{2,1,0:T(8,128)(2,1)S(1)}, u32[]{:S(2)}, u32[]{:S(2)}) collective-permute-start(bf16[2,512,256]{2,1,0:T(8,128)(2,1)S(1)} %get-tuple-element.41), channel_id=1, source_target_pairs={{0,1},{1,2},{2,3},{3,4},{4,5},{5,6},{6,7},{8,9},{9,10},{10,11},{11... | collective-permute-start | bytes 1572872 | tf_op jit(solution)/shard_map/ppermute | solution.py:315
  113.7 3.9 %collective-permute-start.28 = (f32[3,32,256]{2,1,0:T(8,128)S(1)}, f32[3,32,256]{2,1,0:T(8,128)S(1)}, u32[]{:S(2)}, u32[]{:S(2)}) collective-permute-start(f32[3,32,256]{2,1,0:T(8,128)S(1)} %get-tuple-element.50), channel_id=1, source_target_pairs={{0,96},{32,0},{64,32},{96,64},{1,97},{33,1},{65,33},{97,65},{2,98}... | collective-permute-start | bytes 294920 | tf_op jit(solution)/shard_map/ppermute | solution.py:319
  114.9 5.0 %collective-permute-start.27 = (f32[3,32,256]{2,1,0:T(8,128)S(1)}, f32[3,32,256]{2,1,0:T(8,128)S(1)}, u32[]{:S(2)}, u32[]{:S(2)}) collective-permute-start(f32[3,32,256]{2,1,0:T(8,128)S(1)} %get-tuple-element.51), channel_id=1, source_target_pairs={{0,64},{32,96},{64,0},{96,32},{1,65},{33,97},{65,1},{97,33},{2,66}... | collective-permute-start | bytes 294920 | tf_op jit(solution)/shard_map/ppermute | solution.py:319
  115.8 7.1 %collective-permute-start.26 = (f32[3,32,256]{2,1,0:T(8,128)S(1)}, f32[3,32,256]{2,1,0:T(8,128)S(1)}, u32[]{:S(2)}, u32[]{:S(2)}) collective-permute-start(f32[3,32,256]{2,1,0:T(8,128)S(1)} %get-tuple-element.52), channel_id=1, source_target_pairs={{0,32},{32,64},{64,96},{96,0},{1,33},{33,65},{65,97},{97,1},{2,34}... | collective-permute-start | bytes 294920 | tf_op jit(solution)/shard_map/ppermute | solution.py:319
  123.0 23.0 %collective-permute-start.30 = (bf16[2,256,384]{2,1,0:T(8,128)(2,1)S(1)}, bf16[2,256,384]{2,1,0:T(8,128)(2,1)S(1)}, u32[]{:S(2)}, u32[]{:S(2)}) collective-permute-start(bf16[2,256,384]{2,1,0:T(8,128)(2,1)S(1)} %get-tuple-element.47), channel_id=1, source_target_pairs={{0,8},{8,16},{16,24},{24,32},{32,40},{40,48},{48,56},{56,64},{64,7... | collective-permute-start | bytes 1179656 | tf_op jit(solution)/shard_map/ppermute | solution.py:315
  129.9 3.5 %collective-permute-start.33 = (f32[3,32,256]{2,1,0:T(8,128)S(1)}, f32[3,32,256]{2,1,0:T(8,128)S(1)}, u32[]{:S(2)}, u32[]{:S(2)}) collective-permute-start(f32[3,32,256]{2,1,0:T(8,128)S(1)} %get-tuple-element.49.a), channel_id=1, source_target_pairs={{0,6},{2,0},{4,2},{6,4},{1,7},{3,1},{5,3},{7,5},{8,14},{10,8},{12,... | collective-permute-start | bytes 294920 | tf_op jit(solution)/shard_map/ppermute | solution.py:319
  130.0 5.1 %collective-permute-start.32 = (f32[3,32,256]{2,1,0:T(8,128)S(1)}, f32[3,32,256]{2,1,0:T(8,128)S(1)}, u32[]{:S(2)}, u32[]{:S(2)}) collective-permute-start(f32[3,32,256]{2,1,0:T(8,128)S(1)} %get-tuple-element.49.a), channel_id=1, source_target_pairs={{0,4},{2,6},{4,0},{6,2},{1,5},{3,7},{5,1},{7,3},{8,12},{10,14},{12... | collective-permute-start | bytes 294920 | tf_op jit(solution)/shard_map/ppermute | solution.py:319
  131.6 4.7 %collective-permute-start.31 = (f32[3,32,256]{2,1,0:T(8,128)S(1)}, f32[3,32,256]{2,1,0:T(8,128)S(1)}, u32[]{:S(2)}, u32[]{:S(2)}) collective-permute-start(f32[3,32,256]{2,1,0:T(8,128)S(1)} %get-tuple-element.49.a), channel_id=1, source_target_pairs={{0,2},{2,4},{4,6},{6,0},{1,3},{3,5},{5,7},{7,1},{8,10},{10,12},{12... | collective-permute-start | bytes 294920 | tf_op jit(solution)/shard_map/ppermute | solution.py:319
  136.3 6.3 %collective-permute-start.36 = (f32[3,32,256]{2,1,0:T(8,128)S(1)}, f32[3,32,256]{2,1,0:T(8,128)S(1)}, u32[]{:S(2)}, u32[]{:S(2)}) collective-permute-start(f32[3,32,256]{2,1,0:T(8,128)S(1)} %y_sum.3.a), channel_id=1, source_target_pairs={{0,24},{8,0},{16,8},{24,16},{1,25},{9,1},{17,9},{25,17},{2,26},{10... | collective-permute-start | bytes 294920 | tf_op jit(solution)/shard_map/ppermute | solution.py:319
  140.0 5.1 %collective-permute-start.35 = (f32[3,32,256]{2,1,0:T(8,128)S(1)}, f32[3,32,256]{2,1,0:T(8,128)S(1)}, u32[]{:S(2)}, u32[]{:S(2)}) collective-permute-start(f32[3,32,256]{2,1,0:T(8,128)S(1)} %y_sum.3.a), channel_id=1, source_target_pairs={{0,16},{8,24},{16,0},{24,8},{1,17},{9,25},{17,1},{25,9},{2,18},{10... | collective-permute-start | bytes 294920 | tf_op jit(solution)/shard_map/ppermute | solution.py:319
  140.3 5.7 %collective-permute-start.34 = (f32[3,32,256]{2,1,0:T(8,128)S(1)}, f32[3,32,256]{2,1,0:T(8,128)S(1)}, u32[]{:S(2)}, u32[]{:S(2)}) collective-permute-start(f32[3,32,256]{2,1,0:T(8,128)S(1)} %y_sum.3.a), channel_id=1, source_target_pairs={{0,8},{8,16},{16,24},{24,0},{1,9},{9,17},{17,25},{25,1},{2,10},{10... | collective-permute-start | bytes 294920 | tf_op jit(solution)/shard_map/ppermute | solution.py:319
  146.0 3.2 %collective-permute-start.39 = (f32[2,32,256]{2,1,0:T(8,128)S(1)}, f32[2,32,256]{2,1,0:T(8,128)S(1)}, u32[]{:S(2)}, u32[]{:S(2)}) collective-permute-start(f32[2,32,256]{2,1,0:T(8,128)S(1)} %z_sum.1), channel_id=1, source_target_pairs={{0,96},{32,0},{64,32},{96,64},{1,97},{33,1},{65,33},{97,65},{2,98}... | collective-permute-start | bytes 196616 | tf_op jit(solution)/shard_map/ppermute | solution.py:319
  146.1 4.7 %collective-permute-start.38 = (f32[2,32,256]{2,1,0:T(8,128)S(1)}, f32[2,32,256]{2,1,0:T(8,128)S(1)}, u32[]{:S(2)}, u32[]{:S(2)}) collective-permute-start(f32[2,32,256]{2,1,0:T(8,128)S(1)} %z_sum.1), channel_id=1, source_target_pairs={{0,64},{32,96},{64,0},{96,32},{1,65},{33,97},{65,1},{97,33},{2,66}... | collective-permute-start | bytes 196616 | tf_op jit(solution)/shard_map/ppermute | solution.py:319
  148.2 4.3 %collective-permute-start.37 = (f32[2,32,256]{2,1,0:T(8,128)S(1)}, f32[2,32,256]{2,1,0:T(8,128)S(1)}, u32[]{:S(2)}, u32[]{:S(2)}) collective-permute-start(f32[2,32,256]{2,1,0:T(8,128)S(1)} %z_sum.1), channel_id=1, source_target_pairs={{0,32},{32,64},{64,96},{96,0},{1,33},{33,65},{65,97},{97,1},{2,34}... | collective-permute-start | bytes 196616 | tf_op jit(solution)/shard_map/ppermute | solution.py:319
  152.5 7.9 %copy-start.7 = (f32[4,2,32,256]{3,2,1,0:T(8,128)}, f32[4,2,32,256]{3,2,1,0:T(8,128)S(1)}, u32[]{:S(2)}) copy-start(f32[4,2,32,256]{3,2,1,0:T(8,128)S(1)} %pad_maximum_fusion.1.mine) | copy-start | bytes 786436
  152.5 7.9 %collective-permute-start.40 = (f32[4,2,32,256]{3,2,1,0:T(8,128)S(1)}, f32[4,2,32,256]{3,2,1,0:T(8,128)S(1)}, u32[]{:S(2)}, u32[]{:S(2)}) collective-permute-start(f32[4,2,32,256]{3,2,1,0:T(8,128)S(1)} %pad_maximum_fusion.1.mine), channel_id=1, source_target_pairs={{0,1},{1,0},{2,3},{3,2},{4,5},{5,4},{6,7},{7,6},{8,9},{9,8},{10,11... | collective-permute-start | bytes 786440 | tf_op jit(solution)/shard_map/ppermute | solution.py:323
  160.4 0.7 copy-start.8

commit v6 on v5

--- a/solution.py
+++ b/solution.py
@@ -14,7 +14,7 @@
 ALPHA = 0.5
 LANES = 128
 CHUNK = 32
-GROUPS = (4, 2, 1)
+GROUPS = (6, 2, 1)
 N_X, N_Z, N_Y, N_CORE = 4, 4, 4, 2
 N_ROW, N_COL = N_X * N_Z, N_Y * N_CORE
 ROW, COL = ("x", "z"), ("y", "core")
@@ -38,8 +38,8 @@
 ):
     lows, (right, corner), rest = rest[:n_low], rest[n_low : n_low + 2], rest[n_low + 2 :]
     pieces, (amps, tables), rest = rest[:n_pieces], rest[n_pieces : n_pieces + 2], rest[n_pieces + 2 :]
-    own_out, low_left, low_right, right_out, corner_out, keep_out, send_out, step_out = rest[:8]
-    ext, acc, sums, wave, mis, patch, levels, arrived, here, *rest = rest[8:]
+    own_out, down_out, right_out, corner_out, keep_out, send_out, step_out = rest[:7]
+    ext, acc, sums, wave, mis, patch, levels, arrived, here, *rest = rest[7:]
     landing, probe_scratch = rest[: 5 + n_pieces], rest[5 + n_pieces :]
     count = counts[0]
     low_parts, at = [], 0
@@ -69,7 +69,7 @@
     rows, cols = obj.shape[1], obj.shape[2]
     size = corner.shape[1]
     row_chunks = size // CHUNK
-    inner_tiles, all_tiles, left_tiles = cols // LANES, (cols + size) // LANES, size // LANES
+    inner_tiles, all_tiles = cols // LANES, (cols + size) // LANES
     acc[...] = jnp.zeros_like(acc)
     sums[...] = jnp.zeros_like(sums)
     copies[0].wait()
@@ -179,8 +179,7 @@
         at = (j if inside else j - inner_tiles) * LANES
         upper = own_out if inside else right_out
         upper[:, :, at : at + LANES] = acc[:, j, :rows, :].astype(upper.dtype)
-        lower = (low_left if j < left_tiles else low_right) if inside else corner_out
-        at = at if j < left_tiles or not inside else at - size
+        lower = down_out if inside else corner_out
         lower[:, :, at : at + LANES] = acc[:, j, rows:, :].astype(lower.dtype)
     for j in range(N_X):
         inner = lax.rem(x + j, N_X) * quarter
@@ -198,8 +197,7 @@
     quarter = size // (N_CORE * N_X)
     shapes = [
         jax.ShapeDtypeStruct((2, rows, cols), F32),
-        jax.ShapeDtypeStruct((2, size, size), F32),
-        jax.ShapeDtypeStruct((2, size, cols - size), BF),
+        jax.ShapeDtypeStruct((2, size, cols), BF),
         jax.ShapeDtypeStruct((2, rows, size), BF),
         jax.ShapeDtypeStruct((2, size, size), BF),
         jax.ShapeDtypeStruct((N_X, 3, quarter, size), F32),
@@ -226,9 +224,9 @@
         functools.partial(frames_kernel, iteration, len(lows), len(pieces)),
         out_shape=shapes,
         in_specs=[smem] * 3 + [pl.BlockSpec(memory_space=pltpu.HBM)] * (5 + len(lows) + len(pieces)),
-        out_specs=[vmem] * 7 + [smem],
+        out_specs=[vmem] * 6 + [smem],
         scratch_shapes=scratch,
-        compiler_params=pltpu.CompilerParams(vmem_limit_bytes=44 << 20),
+        compiler_params=pltpu.CompilerParams(vmem_limit_bytes=48 << 20),
         cost_estimate=pl.CostEstimate(flops=6_000_000_000, bytes_accessed=8_000_000, transcendentals=0),
         name="frames",
     )(place, counts, pos, obj, *lows, right, corner, *pieces, amps, tables)
@@ -251,38 +249,39 @@
     )(*operands[0], *operands[1])
 
 
-def x_kernel(a, b, c, d, low_left, low_right, corner, total, down):
-    size = low_left.shape[2]
-    total[...] = a[0] + b[...] + c[...] + d[...]
-    down[:, :, :size] = (low_left[...] + corner[...].astype(F32)).astype(BF)
-    down[:, :, size:] = low_right[...]
-
-
-def y_kernel(a, b, c, d, waited, total):
-    total[...] = a[...] + b[...] + c[...] + d[...]
-
-
-def probe_step(a, b, c, d, mine, fresh):
+def sum_kernel(a, b, c, d, *rest):
+    total = rest[-1]
+    total[...] = a[...].reshape(total.shape) + b[...] + c[...] + d[...]
+
+
+def probe_step(a, b, c, d, mine, *rest):
+    fresh = rest[-1]
     total = a[...] + b[...] + c[...] + d[...]
     fresh[...] = mine[...] - total[:2] / (total[2:] + 1.0)
 
 
-def z_kernel(a, b, c, d, mine, waited, fresh):
-    probe_step(a, b, c, d, mine, fresh)
-
-
-def object_step(obj, own, left, down, step, obj_out):
+def stack_kernel(a, b, c, d, *rest):
+    for j, chunk in enumerate((a, b, c, d)):
+        rest[-1][j] = chunk[...]
+
+
+def object_step(obj, own, left, down, diag, step, obj_out):
     size = left.shape[2]
     alpha = step[0, 0]
     obj_out[:, :, :size] = obj[:, :, :size] - alpha * (own[:, :, :size] + left[...].astype(F32))
-    obj_out[:, :size, :size] -= alpha * down[:, :, :size].astype(F32)
+    obj_out[:, :size, :size] -= alpha * (down[:, :, :size].astype(F32) + diag[...].astype(F32))
     obj_out[:, :size, size:] = obj[:, :size, size:] - alpha * (own[:, :size, size:] + down[:, :, size:].astype(F32))
     obj_out[:, size:, size:] = obj[:, size:, size:] - alpha * own[:, size:, size:]
 
 
-def both_kernel(a, b, c, d, mine, obj, own, left, down, step, fresh, obj_out, below, right):
-    probe_step(a, b, c, d, mine, fresh)
-    object_step(obj, own, left, down, step, obj_out)
+def last_kernel(obj, own, left, down, diag, step, obj_out, done):
+    object_step(obj, own, left, down, diag, step, obj_out)
+    done[...] = obj_out[0, :8, :LANES]
+
+
+def both_kernel(a, b, c, d, obj, own, left, down, diag, step, total, obj_out, below, right):
+    sum_kernel(a, b, c, d, total)
+    object_step(obj, own, left, down, diag, step, obj_out)
     size = left.shape[2]
     below[...] = obj_out[:, :size, :].astype(BF)
     right[...] = obj_out[:, :, :size].astype(BF)
@@ -323,13 +322,13 @@
     return lax.ppermute(value, "core", [(0, 1), (1, 0)])
 
 
-def halo(lows, right):
-    size = right.shape[2]
-    first = moved(lows[0], ROW, N_ROW, -1)
-    right = moved(right, COL, N_COL, -1)
-    others = [moved(low, ROW, N_ROW, -1) for low in lows[1:]]
-    corner = moved(first[:, :, :size], COL, N_COL, -1)
-    return ((first, *others), right, corner)
+def moved_both(value, steps):
+    pairs = []
+    for r in range(N_ROW):
+        for c in range(N_COL):
+            if 0 <= r + steps < N_ROW and 0 <= c + steps < N_COL:
+                pairs.append((r * N_COL + c, (r + steps) * N_COL + c + steps))
+    return lax.ppermute(value, ROW + COL, pairs)
 
 
 def around(value, axis):
@@ -348,30 +347,36 @@
     tall = jax.ShapeDtypeStruct((2, rows, size), BF)
     share = jax.ShapeDtypeStruct((3, quarter, size), F32)
     part = jax.ShapeDtypeStruct(mine.shape, F32)
-    lows = [obj[:, :size, :size].astype(BF), obj[:, :size, size:].astype(BF)]
-    right = obj[:, :, :size].astype(BF)
+    row = jax.ShapeDtypeStruct((8, LANES), F32)
+    half_probe = jax.ShapeDtypeStruct((N_X, *mine.shape), F32)
+    first = moved(obj[:, :size, :size].astype(BF), ROW, N_ROW, -1)
+    beside = moved(obj[:, :, :size].astype(BF), COL, N_COL, -1)
+    second = moved(obj[:, :size, size:].astype(BF), ROW, N_ROW, -1)
+    halos = ((first, second), beside, moved(first, COL, N_COL, -1))
     pieces = (probe,)
     for iteration in range(ITERS):
-        halos = halo(lows, right)
-        own, low_left, low_right, right, corner, keep, send, step = run_frames(
+        own, down, right, corner, keep, send, step = run_frames(
             place, counts[iteration, 0], positions[iteration], obj, halos, pieces, amps, tables, iteration
         )
-        corner = moved(corner, COL, N_COL, 1)
-        left = moved(right, COL, N_COL, 1)
+        rims = [moved(right, COL, N_COL, 1), moved(down, ROW, N_ROW, 1), moved_both(corner, 1)]
         sums = keep + swapped(send)
         sums = [sums[:1]] + [turned(sums[j], "x", j) for j in (1, 2, 3)]
-        total, down = small_call(x_kernel, [share, flat], ([*sums, low_left, low_right, corner], []), "x_sum")
-        down = moved(down, ROW, N_ROW, 1)
-        (total,) = small_call(y_kernel, [share], (around(total, "y"), [left]), "y_sum")
-        sums = around(total, "z") + [mine]
+        (total,) = small_call(sum_kernel, [share], (sums, []), "x_sum")
+        sums = around(total, "y")
         if iteration < ITERS - 1:
-            mine, obj, *lows, right = small_call(
-                both_kernel, [part, whole, flat, tall], ([*sums, obj, own, left, down, step], []), "z_sum_object"
+            total, obj, below, right = small_call(
+                both_kernel, [share, whole, flat, tall], ([*sums, obj, own, *rims, step], []), "y_sum_object"
             )
+            below, right = moved(below, ROW, N_ROW, -1), moved(right, COL, N_COL, -1)
+            corner = moved(below[:, :, :size], COL, N_COL, -1)
+            halos, waited = ((below,), right, corner), [corner]
+            (mine,) = small_call(probe_step, [part], ([*around(total, "z"), mine], [below]), "z_sum")
         else:
-            (mine,) = small_call(z_kernel, [part], (sums, [down]), "z_sum")
-            (obj,) = small_call(object_step, [whole], ([obj, own, left, down, step], []), "object_update")
-        stack = jnp.stack(around(mine, "x"))
+            (total,) = small_call(sum_kernel, [share], (sums, rims), "y_sum")
+            obj, done = small_call(last_kernel, [whole, row], ([obj, own, *rims, step], []), "object_update")
+            (mine,) = small_call(probe_step, [part], ([*around(total, "z"), mine], []), "z_sum")
+            waited = [done]
+        (stack,) = small_call(stack_kernel, [half_probe], (around(mine, "x"), waited), "half_probe")
         pieces = (stack, swapped(stack))
     return (obj, run_probe(place, *pieces))
 

time: 163 us -> 180 us (1.10)
  starting transfers between devices: 76.8 us -> 97.4 us
  waiting for transfers between devices: 56.9 us -> 53.5 us
    ppermute x24, starting transfers between devices: 35 us -> 49.1 us  [turned(): return lax.ppermute(value, axis, [(s, (s + steps) % 4) for s in range(4)])]
    ppermute x0 -> x2, starting transfers between devices: none -> 13.4 us  [moved_both(): return lax.ppermute(value, ROW + COL, pairs)]
    ppermute x24, waiting for transfers between devices: 43.2 us -> 33.2 us  [turned(): return lax.ppermute(value, axis, [(s, (s + steps) % 4) for s in range(4)])]
    ppermute x13 -> x11, starting transfers between devices: 35.3 us -> 26.6 us  [moved(): lax.ppermute(value, axis, [(s, s + steps) for s in range(first, last)])]
    ppermute x13 -> x11, waiting for transfers between devices: 13.7 us -> 17.9 us  [moved(): lax.ppermute(value, axis, [(s, s + steps) for s in range(first, last)])]
    ppermute x4, waiting for transfers between devices: 0.01 us -> 2.33 us  [swapped(): return lax.ppermute(value, 'core', [(0, 1), (1, 0)])]
    pallas_call x7 -> x9, Pallas kernels: 4.59 us -> 3.88 us  [small_call(): pl.pallas_call(body, out_shape=shapes, in_specs=[spec(space) for space in...]
  transfers between devices with their start and end apart: 41 -> 41, of which waited for: 26 -> 24; matrix products, arithmetic and copies ran while one was open for 1% -> 1% of each run, Pallas kernels for 2% -> 1%
where the time goes in v6:
time: 180 us
  starting transfers between devices  97.4 us (54%)
  waiting for transfers between devices  53.5 us (30%)
  Pallas kernels  20.9 us (12%)
  local copies, waits for them, and re-layouts  5.54 us (3%)
  other arithmetic  1.82 us (1%)
    ppermute x24, starting transfers between devices, turned(): return lax.ppermute(value, axis, [(s, (s + steps) % 4) for s in range(4)])  49.1 us
    ppermute x24, waiting for transfers between devices, turned(): return lax.ppermute(value, axis, [(s, (s + steps) % 4) for s in range(4)])  33.2 us
    ppermute x11, starting transfers between devices, moved(): lax.ppermute(value, axis, [(s, s + steps) for s in range(first, last)])  26.6 us
    ppermute x11, waiting for transfers between devices, moved(): lax.ppermute(value, axis, [(s, s + steps) for s in range(first, last)])  17.9 us
    pallas_call x2, Pallas kernels, run_frames(): pl.pallas_call(functools.partial(frames_kernel, iteration, len(lows), len...  15.1 us
    ppermute x2, starting transfers between devices, moved_both(): return lax.ppermute(value, ROW + COL, pairs)  13.4 us
    ppermute x4, starting transfers between devices, swapped(): return lax.ppermute(value, 'core', [(0, 1), (1, 0)])  8.24 us
    pallas_call x9, Pallas kernels, small_call(): pl.pallas_call(body, out_shape=shapes, in_specs=[spec(space) for space in...  3.88 us
  transfers between devices with their start and end apart: 41, of which 24 were waited for; matrix products, arithmetic and copies ran while one was open for 1% of the time, Pallas kernels for 1%

profile of v6, /device:TPU:1, one launch (start us, length us, event | category | flops | bytes accessed | tf_op | source)
XLA Modules:
  0.0 180.1 jit_solution(6800668400563601368)
XLA Ops:
  0.7 1.6 convert.5
  2.3 1.3 collective-permute-start
  3.6 0.8 slice.69
  4.4 3.3 %collective-permute-start.2 = (bf16[2,512,256]{2,1,0:T(8,128)(2,1)}, bf16[2,512,256]{2,1,0:T(8,128)(2,1)S(1)}, u32[]{:S(2)}, u32[]{:S(2)}) collective-permute-start(bf16[2,512,256]{2,1,0:T(8,128)(2,1)} %slice.69), channel_id=1, source_target_pairs={{1,0},{2,1},{3,2},{4,3},{5,4},{6,5},{7,6},{9,8},{10,9},{11,10},{12... | collective-permute-start | bytes 1572872 | tf_op jit(solution)/shard_map/ppermute | solution.py:314
  7.8 1.3 collective-permute-start.1
  9.1 3.6 %collective-permute-done.rest_0_ = bf16[2,256,256]{2,1,0:T(8,128)(2,1)S(1)} collective-permute-done((bf16[2,256,256]{2,1,0:T(8,128)(2,1)S(1)}, bf16[2,256,256]{2,1,0:T(8,128)(2,1)S(1)}, u32[]{:S(2)}, u32[]{:S(2)}) %collective-permute-start) | collective-permute-done | bytes 262176 | tf_op jit(solution)/shard_map/ppermute | solution.py:314
  12.7 3.3 %collective-permute-start.3 = (bf16[2,256,256]{2,1,0:T(8,128)(2,1)S(1)}, bf16[2,256,256]{2,1,0:T(8,128)(2,1)S(1)}, u32[]{:S(2)}, u32[]{:S(2)}) collective-permute-start(bf16[2,256,256]{2,1,0:T(8,128)(2,1)S(1)} %collective-permute-done.rest_0_), channel_id=1, source_target_pairs={{1,0},{2,1},{3,2},{4,3},{5,4},{6,5},{7,6},{9,8},{10,9},{11,10},{12... | collective-permute-start | bytes 786440 | tf_op jit(solution)/shard_map/ppermute | solution.py:314
  16.1 0.6 fusion
  16.7 4.4 %collective-permute-done.3.rest_3_ = bf16[2,256,256]{2,1,0:T(8,128)(2,1)S(1)} collective-permute-done((bf16[2,256,256]{2,1,0:T(8,128)(2,1)S(1)}, bf16[2,256,256]{2,1,0:T(8,128)(2,1)S(1)}, u32[]{:S(2)}, u32[]{:S(2)}) %collective-permute-start.3) | collective-permute-done | bytes 262176 | tf_op jit(solution)/shard_map/ppermute | solution.py:314
  21.2 6.3 %frames.2 = (f32[2,512,384]{2,1,0:T(8,128)}, bf16[2,256,384]{2,1,0:T(8,128)(2,1)S(1)}, bf16[2,512,256]{2,1,0:T(8,128)(2,1)S(1)}, bf16[2,256,256]{2,1,0:T(8,128)(...) custom-call(s32[2]{0:T(128)S(1)} %pad_add_fusion.place, s32[1]{0:T(128)} %bitcast.2.counts, ...), custom_call_target="tpu_custom_call" | custom-call | flops 6000000000 | bytes 8000000 | tf_op jit(solution)/shard_map/frames/pallas_call | solution.py:223
  27.6 11.8 %collective-permute-start.13 = (bf16[2,256,256]{2,1,0:T(8,128)(2,1)S(1)}, bf16[2,256,256]{2,1,0:T(8,128)(2,1)S(1)}, u32[]{:S(2)}, u32[]{:S(2)}) collective-permute-start(bf16[2,256,256]{2,1,0:T(8,128)(2,1)S(1)} %get-tuple-element.27), channel_id=1, source_target_pairs={{0,9},{1,10},{2,11},{3,12},{4,13},{5,14},{6,15},{8,17},{9,18},{10,... | collective-permute-start | bytes 786440 | tf_op jit(solution)/shard_map/ppermute | solution.py:331
  39.5 1.3 collective-permute-start.12
  40.8 3.1 %collective-permute-start.11 = (bf16[2,512,256]{2,1,0:T(8,128)(2,1)S(1)}, bf16[2,512,256]{2,1,0:T(8,128)(2,1)S(1)}, u32[]{:S(2)}, u32[]{:S(2)}) collective-permute-start(bf16[2,512,256]{2,1,0:T(8,128)(2,1)S(1)} %get-tuple-element.25), channel_id=1, source_target_pairs={{0,1},{1,2},{2,3},{3,4},{4,5},{5,6},{6,7},{8,9},{9,10},{10,11},{11... | collective-permute-start | bytes 1572872 | tf_op jit(solution)/shard_map/ppermute | solution.py:314
  44.1 5.4 %collective-permute-start.6 = (f32[3,32,256]{2,1,0:T(8,128)S(1)}, f32[3,32,256]{2,1,0:T(8,128)S(1)}, u32[]{:S(2)}, u32[]{:S(2)}) collective-permute-start(f32[3,32,256]{2,1,0:T(8,128)S(1)} %get-tuple-element.47), channel_id=1, source_target_pairs={{0,64},{32,96},{64,0},{96,32},{1,65},{33,97},{65,1},{97,33},{2,66}... | collective-permute-start | bytes 294920 | tf_op jit(solution)/shard_map/ppermute | solution.py:318
  49.5 2.8 %collective-permute-start.5 = (f32[3,32,256]{2,1,0:T(8,128)S(1)}, f32[3,32,256]{2,1,0:T(8,128)S(1)}, u32[]{:S(2)}, u32[]{:S(2)}) collective-permute-start(f32[3,32,256]{2,1,0:T(8,128)S(1)} %get-tuple-element.48), channel_id=1, source_target_pairs={{0,32},{32,64},{64,96},{96,0},{1,33},{33,65},{65,97},{97,1},{2,34}... | collective-permute-start | bytes 294920 | tf_op jit(solution)/shard_map/ppermute | solution.py:318
  52.2 0.4 collective-permute-done.6.c
  52.7 1.5 collective-permute-done.5.b
  54.4 5.3 %collective-permute-start.9 = (f32[3,32,256]{2,1,0:T(8,128)S(1)}, f32[3,32,256]{2,1,0:T(8,128)S(1)}, u32[]{:S(2)}, u32[]{:S(2)}) collective-permute-start(f32[3,32,256]{2,1,0:T(8,128)S(1)} %x_sum.2.a), channel_id=1, source_target_pairs={{0,4},{2,6},{4,0},{6,2},{1,5},{3,7},{5,1},{7,3},{8,12},{10,14},{12... | collective-permute-start | bytes 294920 | tf_op jit(solution)/shard_map/ppermute | solution.py:318
  60.0 1.8 collective-permute-done.9.c
  61.8 3.4 %collective-permute-done.8.b = f32[3,32,256]{2,1,0:T(8,128)S(1)} collective-permute-done((f32[3,32,256]{2,1,0:T(8,128)S(1)}, f32[3,32,256]{2,1,0:T(8,128)S(1)}, u32[]{:S(2)}, u32[]{:S(2)}) %collective-permute-start.8) | collective-permute-done | bytes 98336 | tf_op jit(solution)/shard_map/ppermute | solution.py:318
  65.2 1.4 copy-done.1
  66.6 1.3 y_sum_object.1
  67.9 1.1 copy-done.2
  69.0 1.3 collective-permute-start.14
  70.3 9.8 %collective-permute-done.14.rest_0_ = bf16[2,256,384]{2,1,0:T(8,128)(2,1)S(1)} collective-permute-done((bf16[2,256,384]{2,1,0:T(8,128)(2,1)S(1)}, bf16[2,256,384]{2,1,0:T(8,128)(2,1)S(1)}, u32[]{:S(2)}, u32[]{:S(2)}) %collective-permute-start.14) | collective-permute-done | bytes 393248 | tf_op jit(solution)/shard_map/ppermute | solution.py:314
  80.2 0.7 slice.74
  80.9 5.0 %collective-permute-start.16 = (bf16[2,256,256]{2,1,0:T(8,128)(2,1)}, bf16[2,256,256]{2,1,0:T(8,128)(2,1)S(1)}, u32[]{:S(2)}, u32[]{:S(2)}) collective-permute-start(bf16[2,256,256]{2,1,0:T(8,128)(2,1)} %slice.74), channel_id=1, source_target_pairs={{1,0},{2,1},{3,2},{4,3},{5,4},{6,5},{7,6},{9,8},{10,9},{11,10},{12... | collective-permute-start | bytes 786440 | tf_op jit(solution)/shard_map/ppermute | solution.py:314
  85.9 1.9 %collective-permute-start.15 = (bf16[2,512,256]{2,1,0:T(8,128)(2,1)S(1)}, bf16[2,512,256]{2,1,0:T(8,128)(2,1)S(1)}, u32[]{:S(2)}, u32[]{:S(2)}) collective-permute-start(bf16[2,512,256]{2,1,0:T(8,128)(2,1)S(1)} %get-tuple-element.31), channel_id=1, source_target_pairs={{1,0},{2,1},{3,2},{4,3},{5,4},{6,5},{7,6},{9,8},{10,9},{11,10},{12... | collective-permute-start | bytes 1572872 | tf_op jit(solution)/shard_map/ppermute | solution.py:314
  87.9 7.0 %collective-permute-start.19 = (f32[3,32,256]{2,1,0:T(8,128)S(1)}, f32[3,32,256]{2,1,0:T(8,128)S(1)}, u32[]{:S(2)}, u32[]{:S(2)}) collective-permute-start(f32[3,32,256]{2,1,0:T(8,128)S(1)} %get-tuple-element.32.a), channel_id=1, source_target_pairs={{0,24},{8,0},{16,8},{24,16},{1,25},{9,1},{17,9},{25,17},{2,26},{10... | collective-permute-start | bytes 294920 | tf_op jit(solution)/shard_map/ppermute | solution.py:318
  94.8 0.7 collective-permute-start.17
  95.5 3.3 %collective-permute-done.19.d = f32[3,32,256]{2,1,0:T(8,128)S(1)} collective-permute-done((f32[3,32,256]{2,1,0:T(8,128)S(1)}, f32[3,32,256]{2,1,0:T(8,128)S(1)}, u32[]{:S(2)}, u32[]{:S(2)}) %collective-permute-start.19) | collective-permute-done | bytes 98336 | tf_op jit(solution)/shard_map/ppermute | solution.py:318
  98.8 2.1 %collective-permute-done.18.c = f32[3,32,256]{2,1,0:T(8,128)S(1)} collective-permute-done((f32[3,32,256]{2,1,0:T(8,128)S(1)}, f32[3,32,256]{2,1,0:T(8,128)S(1)}, u32[]{:S(2)}, u32[]{:S(2)}) %collective-permute-start.18) | collective-permute-done | bytes 98336 | tf_op jit(solution)/shard_map/ppermute | solution.py:318
  100.8 1.3 collective-permute-done.17.b
  102.4 1.4 collective-permute-start.20
  103.7 1.6 collective-permute-done.22.d
  105.4 1.6 collective-permute-done.21.c
  107.0 2.1 %collective-permute-done.20.b = f32[2,32,256]{2,1,0:T(8,128)S(1)} collective-permute-done((f32[2,32,256]{2,1,0:T(8,128)S(1)}, f32[2,32,256]{2,1,0:T(8,128)S(1)}, u32[]{:S(2)}, u32[]{:S(2)}) %collective-permute-start.20) | collective-permute-done | bytes 65568 | tf_op jit(solution)/shard_map/ppermute | solution.py:318
  109.1 0.9 collective-permute-start.23
  110.0 1.2 collective-permute-done.23.rest_4_
  111.1 8.8 %frames.3 = (f32[2,512,384]{2,1,0:T(8,128)}, bf16[2,256,384]{2,1,0:T(8,128)(2,1)S(1)}, bf16[2,512,256]{2,1,0:T(8,128)(2,1)S(1)}, bf16[2,256,256]{2,1,0:T(8,128)(...) custom-call(s32[2]{0:T(128)S(1)} %pad_add_fusion.place, s32[1]{0:T(128)} %bitcast.7.counts, ...), custom_call_target="tpu_custom_call" | custom-call | flops 6000000000 | bytes 8000000 | tf_op jit(solution)/shard_map/frames/pallas_call | solution.py:223
  120.0 1.6 collective-permute-start.26
  121.6 2.2 %collective-permute-start.25 = (bf16[2,256,384]{2,1,0:T(8,128)(2,1)S(1)}, bf16[2,256,384]{2,1,0:T(8,128)(2,1)S(1)}, u32[]{:S(2)}, u32[]{:S(2)}) collective-permute-start(bf16[2,256,384]{2,1,0:T(8,128)(2,1)S(1)} %get-tuple-element.35), channel_id=1, source_target_pairs={{0,8},{8,16},{16,24},{24,32},{32,40},{40,48},{48,56},{56,64},{64,7... | collective-permute-start | bytes 1179656 | tf_op jit(solution)/shard_map/ppermute | solution.py:314
  123.8 2.6 %collective-permute-start.24 = (bf16[2,512,256]{2,1,0:T(8,128)(2,1)S(1)}, bf16[2,512,256]{2,1,0:T(8,128)(2,1)S(1)}, u32[]{:S(2)}, u32[]{:S(2)}) collective-permute-start(bf16[2,512,256]{2,1,0:T(8,128)(2,1)S(1)} %get-tuple-element.34), channel_id=1, source_target_pairs={{0,1},{1,2},{2,3},{3,4},{4,5},{5,6},{6,7},{8,9},{9,10},{10,11},{11... | collective-permute-start | bytes 1572872 | tf_op jit(solution)/shard_map/ppermute | solution.py:314
  126.6 4.8 %collective-permute-start.30 = (f32[3,32,256]{2,1,0:T(8,128)S(1)}, f32[3,32,256]{2,1,0:T(8,128)S(1)}, u32[]{:S(2)}, u32[]{:S(2)}) collective-permute-start(f32[3,32,256]{2,1,0:T(8,128)S(1)} %get-tuple-element.42), channel_id=1, source_target_pairs={{0,96},{32,0},{64,32},{96,64},{1,97},{33,1},{65,33},{97,65},{2,98}... | collective-permute-start | bytes 294920 | tf_op jit(solution)/shard_map/ppermute | solution.py:318
  131.4 3.3 %collective-permute-start.29 = (f32[3,32,256]{2,1,0:T(8,128)S(1)}, f32[3,32,256]{2,1,0:T(8,128)S(1)}, u32[]{:S(2)}, u32[]{:S(2)}) collective-permute-start(f32[3,32,256]{2,1,0:T(8,128)S(1)} %get-tuple-element.43), channel_id=1, source_target_pairs={{0,64},{32,96},{64,0},{96,32},{1,65},{33,97},{65,1},{97,33},{2,66}... | collective-permute-start | bytes 294920 | tf_op jit(solution)/shard_map/ppermute | solution.py:318
  134.7 3.0 %collective-permute-start.28 = (f32[3,32,256]{2,1,0:T(8,128)S(1)}, f32[3,32,256]{2,1,0:T(8,128)S(1)}, u32[]{:S(2)}, u32[]{:S(2)}) collective-permute-start(f32[3,32,256]{2,1,0:T(8,128)S(1)} %get-tuple-element.44), channel_id=1, source_target_pairs={{0,32},{32,64},{64,96},{96,0},{1,33},{33,65},{65,97},{97,1},{2,34}... | collective-permute-start | bytes 294920 | tf_op jit(solution)/shard_map/ppermute | solution.py:318
  137.7 2.0 %collective-permute-done.28.b = f32[3,32,256]{2,1,0:T(8,128)S(1)} collective-permute-done((f32[3,32,256]{2,1,0:T(8,128)S(1)}, f32[3,32,256]{2,1,0:T(8,128)S(1)}, u32[]{:S(2)}, u32[]{:S(2)}) %collective-permute-start.28) | collective-permute-done | bytes 98336 | tf_op jit(solution)/shard_map/ppermute | solution.py:318
  139.8 4.4 %collective-permute-start.32 = (f32[3,32,256]{2,1,0:T(8,128)S(1)}, f32[3,32,256]{2,1,0:T(8,128)S(1)}, u32[]{:S(2)}, u32[]{:S(2)}) collective-permute-start(f32[3,32,256]{2,1,0:T(8,128)S(1)} %x_sum.3.a), channel_id=1, source_target_pairs={{0,4},{2,6},{4,0},{6,2},{1,5},{3,7},{5,1},{7,3},{8,12},{10,14},{12... | collective-permute-start | bytes 294920 | tf_op jit(solution)/shard_map/ppermute | solution.py:318
  144.5 1.8 collective-permute-done.32.c
  146.3 3.7 %collective-permute-done.31.b = f32[3,32,256]{2,1,0:T(8,128)S(1)} collective-permute-done((f32[3,32,256]{2,1,0:T(8,128)S(1)}, f32[3,32,256]{2,1,0:T(8,128)S(1)}, u32[]{:S(2)}, u32[]{:S(2)}) %collective-permute-start.31) | collective-permute-done | bytes 98336 | tf_op jit(solution)/shard_map/ppermute | solution.py:318
  150.0 5.0 %collective-permute-start.36 = (f32[3,32,256]{2,1,0:T(8,128)S(1)}, f32[3,32,256]{2,1,0:T(8,128)S(1)}, u32[]{:S(2)}, u32[]{:S(2)}) collective-permute-start(f32[3,32,256]{2,1,0:T(8,128)S(1)} %y_sum.1.a), channel_id=1, source_target_pairs={{0,24},{8,0},{16,8},{24,16},{1,25},{9,1},{17,9},{25,17},{2,26},{10... | collective-permute-start | bytes 294920 | tf_op jit(solution)/shard_map/ppermute | solution.py:318
  155.2 0.8 collective-permute-start.34
  155.9 1.0 collective-permute-done.36.d
  156.9 3.2 %collective-permute-done.35.c = f32[3,32,256]{2,1,0:T(8,128)S(1)} collective-permute-done((f32[3,32,256]{2,1,0:T(8,128)S(1)}, f32[3,32,256]{2,1,0:T(8,128)S(1)}, u32[]{:S(2)}, u32[]{:S(2)}) %collective-permute-start.35) | collective-permute-done | bytes 98336 | tf_op jit(solution)/shard_map/ppermute | solution.py:318
  160.1 0.8 collective-permute-done.34.b
  160.9 2.3 %collective-permute-start.39 = (f32[2,32,256]{2,1,0:T(8,128)S(1)}, f32[2,32,256]{2,1,0:T(8,128)S(1)}, u32[]{:S(2)}, u32[]{:S(2)}) collective-permute-start(f32[2,32,256]{2,1,0:T(8,128)S(1)} %z_sum.3.a), channel_id=1, source_target_pairs={{0,96},{32,0},{64,32},{96,64},{1,97},{33,1},{65,33},{97,65},{2,98}... | collective-permute-start | bytes 196616 | tf_op jit(solution)/shard_map/ppermute | solution.py:318
  163.2 1.6 collective-permute-start.38
  164.8 0.7 collective-permute-start.37
  165.5 2.4 %object_update.1 = (f32[2,512,384]{2,1,0:T(8,128)}, f32[8,128]{1,0:T(8,128)S(1)}) custom-call(f32[2,512,384]{2,1,0:T(8,128)S(1)} %copy-done.3, f32[2,512,384]{2,1,0:T(8,128)S(1)} %copy-done.4, bf16[2,512,256]{2,1,0:T(8,128)(2,1)S(1)} %collective-permute-done.24.left.rest_0_, bf16[2,256,384]{2,1,0:T(8,128)(2,1)S(1)} %collective-permute-done.25.down.rest_1_, ...), custom_call_target="tpu_custom_call" | custom-call | flops 2000000 | bytes 4000000 | tf_op jit(solution)/shard_map/object_update/pallas_call | solution.py:241
  167.9 1.2 collective-permute-done.37.b
  169.2 7.2 %collective-permute-start.40 = (f32[4,2,32,256]{3,2,1,0:T(8,128)S(1)}, f32[4,2,32,256]{3,2,1,0:T(8,128)S(1)}, u32[]{:S(2)}, u32[]{:S(2)}) collective-permute-start(f32[4,2,32,256]{3,2,1,0:T(8,128)S(1)} %half_probe.3.mine), channel_id=1, source_target_pairs={{0,1},{1,0},{2,3},{3,2},{4,5},{5,4},{6,7},{7,6},{8,9},{9,8},{10,11... | collective-permute-start | bytes 786440 | tf_op jit(solution)/shard_map/ppermute | solution.py:322
  176.4 1.2 collective-permute-done.40.other
  177.5 0.7 copy-done.9
  178.2 1.9 %probe_whole.1 = f32[2,256,256]{2,1,0:T(8,128)} custom-call(s32[2]{0:T(128)} %copy-done.7, f32[4,2,32,256]{3,2,1,0:T(8,128)} %copy-done.5, f32[4,2,32,256]{3,2,1,0:T(8,128)} %copy-done.9), custom_call_target="tpu_custom_call" | custom-call | tf_op jit(solution)/shard_map/probe_whole/pallas_call | solution.py:303
  (67 shorter events, 1.9 us)
Async XLA Ops:
  0.6 20.5 %copy-start.8 = (bf16[2,512,512]{2,1,0:T(8,128)(2,1)S(1)}, bf16[2,512,512]{2,1,0:T(8,128)(2,1)}, u32[]{:S(2)}) copy-start(bf16[2,512,512]{2,1,0:T(8,128)(2,1)} %constant.20.clone.rest_6_) | copy-start | bytes 3145732
  0.6 15.4 %copy-start.10 = (s32[2,2,12]{2,1,0:T(2,128)S(1)}, s32[2,2,12]{2,1,0:T(2,128)}, u32[]{:S(2)}) copy-start(s32[2,2,12]{2,1,0:T(2,128)} %param.9) | copy-start | bytes 580
  0.7 15.5 %copy-start.11 = (s32[2,1,1]{0,2,1:T(1,128)S(1)}, s32[2,1,1]{0,2,1:T(1,128)}, u32[]{:S(2)}) copy-start(s32[2,1,1]{0,2,1:T(1,128)} %param.10) | copy-start | bytes 28
  0.7 20.5 %copy-start.6 = (f32[2,256,256]{2,1,0:T(8,128)S(1)}, f32[2,256,256]{2,1,0:T(8,128)}, u32[]{:S(2)}) copy-start(f32[2,256,256]{2,1,0:T(8,128)} %rest_4_.1) | copy-start | bytes 1572868
  2.3 10.4 %collective-permute-start = (bf16[2,256,256]{2,1,0:T(8,128)(2,1)S(1)}, bf16[2,256,256]{2,1,0:T(8,128)(2,1)S(1)}, u32[]{:S(2)}, u32[]{:S(2)}) collective-permute-start(bf16[2,256,256]{2,1,0:T(8,128)(2,1)S(1)} %slice.67), channel_id=1, source_target_pairs={{8,0},{16,8},{24,16},{32,24},{40,32},{48,40},{56,48},{64,56},{72,6... | collective-permute-start | bytes 786440 | tf_op jit(solution)/shard_map/ppermute | solution.py:314
  4.4 16.7 %collective-permute-start.2 = (bf16[2,512,256]{2,1,0:T(8,128)(2,1)}, bf16[2,512,256]{2,1,0:T(8,128)(2,1)S(1)}, u32[]{:S(2)}, u32[]{:S(2)}) collective-permute-start(bf16[2,512,256]{2,1,0:T(8,128)(2,1)} %slice.69), channel_id=1, source_target_pairs={{1,0},{2,1},{3,2},{4,3},{5,4},{6,5},{7,6},{9,8},{10,9},{11,10},{12... | collective-permute-start | bytes 1572872 | tf_op jit(solution)/shard_map/ppermute | solution.py:314
  7.8 8.9 %collective-permute-start.1 = (bf16[2,256,128]{2,1,0:T(8,128)(2,1)S(1)}, bf16[2,256,128]{2,1,0:T(8,128)(2,1)S(1)}, u32[]{:S(2)}, u32[]{:S(2)}) collective-permute-start(bf16[2,256,128]{2,1,0:T(8,128)(2,1)S(1)} %slice.68), channel_id=1, source_target_pairs={{8,0},{16,8},{24,16},{32,24},{40,32},{48,40},{56,48},{64,56},{72,6... | collective-permute-start | bytes 393224 | tf_op jit(solution)/shard_map/ppermute | solution.py:314
  12.7 8.5 %collective-permute-start.3 = (bf16[2,256,256]{2,1,0:T(8,128)(2,1)S(1)}, bf16[2,256,256]{2,1,0:T(8,128)(2,1)S(1)}, u32[]{:S(2)}, u32[]{:S(2)}) collective-permute-start(bf16[2,256,256]{2,1,0:T(8,128)(2,1)S(1)} %collective-permute-done.rest_0_), channel_id=1, source_target_pairs={{1,0},{2,1},{3,2},{4,3},{5,4},{6,5},{7,6},{9,8},{10,9},{11,10},{12... | collective-permute-start | bytes 786440 | tf_op jit(solution)/shard_map/ppermute | solution.py:314
  16.1 95.0 %copy-start.7 = (s32[2]{0:T(128)}, s32[2]{0:T(128)S(1)}, u32[]{:S(2)}) copy-start(s32[2]{0:T(128)S(1)} %pad_add_fusion.place) | copy-start | bytes 28
  27.5 37.6 %copy-start = (f32[2,512,384]{2,1,0:T(8,128)S(1)}, f32[2,512,384]{2,1,0:T(8,128)}, u32[]{:S(2)}) copy-start(f32[2,512,384]{2,1,0:T(8,128)} %obj.3) | copy-start | bytes 4718596
  27.5 16.4 %collective-permute-start.4 = (f32[4,3,32,256]{3,2,1,0:T(8,128)S(1)}, f32[4,3,32,256]{3,2,1,0:T(8,128)S(1)}, u32[]{:S(2)}, u32[]{:S(2)}) collective-permute-start(f32[4,3,32,256]{3,2,1,0:T(8,128)S(1)} %get-tuple-element.23), channel_id=1, source_target_pairs={{0,1},{1,0},{2,3},{3,2},{4,5},{5,4},{6,7},{7,6},{8,9},{9,8},{10,11... | collective-permute-start | bytes 1179656 | tf_op jit(solution)/shard_map/ppermute | solution.py:322
  27.6 32.1 %collective-permute-start.13 = (bf16[2,256,256]{2,1,0:T(8,128)(2,1)S(1)}, bf16[2,256,256]{2,1,0:T(8,128)(2,1)S(1)}, u32[]{:S(2)}, u32[]{:S(2)}) collective-permute-start(bf16[2,256,256]{2,1,0:T(8,128)(2,1)S(1)} %get-tuple-element.27), channel_id=1, source_target_pairs={{0,9},{1,10},{2,11},{3,12},{4,13},{5,14},{6,15},{8,17},{9,18},{10,... | collective-permute-start | bytes 786440 | tf_op jit(solution)/shard_map/ppermute | solution.py:331
  39.5 20.3 %collective-permute-start.12 = (bf16[2,256,384]{2,1,0:T(8,128)(2,1)S(1)}, bf16[2,256,384]{2,1,0:T(8,128)(2,1)S(1)}, u32[]{:S(2)}, u32[]{:S(2)}) collective-permute-start(bf16[2,256,384]{2,1,0:T(8,128)(2,1)S(1)} %get-tuple-element.26), channel_id=1, source_target_pairs={{0,8},{8,16},{16,24},{24,32},{32,40},{40,48},{48,56},{56,64},{64,7... | collective-permute-start | bytes 1179656 | tf_op jit(solution)/shard_map/ppermute | solution.py:314
  40.8 19.0 %collective-permute-start.11 = (bf16[2,512,256]{2,1,0:T(8,128)(2,1)S(1)}, bf16[2,512,256]{2,1,0:T(8,128)(2,1)S(1)}, u32[]{:S(2)}, u32[]{:S(2)}) collective-permute-start(bf16[2,512,256]{2,1,0:T(8,128)(2,1)S(1)} %get-tuple-element.25), channel_id=1, source_target_pairs={{0,1},{1,2},{2,3},{3,4},{4,5},{5,6},{6,7},{8,9},{9,10},{10,11},{11... | collective-permute-start | bytes 1572872 | tf_op jit(solution)/shard_map/ppermute | solution.py:314
  44.0 5.4 %collective-permute-start.7 = (f32[3,32,256]{2,1,0:T(8,128)S(1)}, f32[3,32,256]{2,1,0:T(8,128)S(1)}, u32[]{:S(2)}, u32[]{:S(2)}) collective-permute-start(f32[3,32,256]{2,1,0:T(8,128)S(1)} %get-tuple-element.46), channel_id=1, source_target_pairs={{0,96},{32,0},{64,32},{96,64},{1,97},{33,1},{65,33},{97,65},{2,98}... | collective-permute-start | bytes 294920 | tf_op jit(solution)/shard_map/ppermute | solution.py:318
  44.1 8.5 %collective-permute-start.6 = (f32[3,32,256]{2,1,0:T(8,128)S(1)}, f32[3,32,256]{2,1,0:T(8,128)S(1)}, u32[]{:S(2)}, u32[]{:S(2)}) collective-permute-start(f32[3,32,256]{2,1,0:T(8,128)S(1)} %get-tuple-element.47), channel_id=1, source_target_pairs={{0,64},{32,96},{64,0},{96,32},{1,65},{33,97},{65,1},{97,33},{2,66}... | collective-permute-start | bytes 294920 | tf_op jit(solution)/shard_map/ppermute | solution.py:318
  49.5 4.7 %collective-permute-start.5 = (f32[3,32,256]{2,1,0:T(8,128)S(1)}, f32[3,32,256]{2,1,0:T(8,128)S(1)}, u32[]{:S(2)}, u32[]{:S(2)}) collective-permute-start(f32[3,32,256]{2,1,0:T(8,128)S(1)} %get-tuple-element.48), channel_id=1, source_target_pairs={{0,32},{32,64},{64,96},{96,0},{1,33},{33,65},{65,97},{97,1},{2,34}... | collective-permute-start | bytes 294920 | tf_op jit(solution)/shard_map/ppermute | solution.py:318
  54.2 5.8 %collective-permute-start.10 = (f32[3,32,256]{2,1,0:T(8,128)S(1)}, f32[3,32,256]{2,1,0:T(8,128)S(1)}, u32[]{:S(2)}, u32[]{:S(2)}) collective-permute-start(f32[3,32,256]{2,1,0:T(8,128)S(1)} %x_sum.2.a), channel_id=1, source_target_pairs={{0,6},{2,0},{4,2},{6,4},{1,7},{3,1},{5,3},{7,5},{8,14},{10,8},{12,... | collective-permute-start | bytes 294920 | tf_op jit(solution)/shard_map/ppermute | solution.py:318
  54.4 7.3 %collective-permute-start.9 = (f32[3,32,256]{2,1,0:T(8,128)S(1)}, f32[3,32,256]{2,1,0:T(8,128)S(1)}, u32[]{:S(2)}, u32[]{:S(2)}) collective-permute-start(f32[3,32,256]{2,1,0:T(8,128)S(1)} %x_sum.2.a), channel_id=1, source_target_pairs={{0,4},{2,6},{4,0},{6,2},{1,5},{3,7},{5,1},{7,3},{8,12},{10,14},{12... | collective-permute-start | bytes 294920 | tf_op jit(solution)/shard_map/ppermute | solution.py:318
  59.8 5.4 %collective-permute-start.8 = (f32[3,32,256]{2,1,0:T(8,128)S(1)}, f32[3,32,256]{2,1,0:T(8,128)S(1)}, u32[]{:S(2)}, u32[]{:S(2)}) collective-permute-start(f32[3,32,256]{2,1,0:T(8,128)S(1)} %x_sum.2.a), channel_id=1, source_target_pairs={{0,2},{2,4},{4,6},{6,0},{1,3},{3,5},{5,7},{7,1},{8,10},{10,12},{12... | collective-permute-start | bytes 294920 | tf_op jit(solution)/shard_map/ppermute | solution.py:318
  65.2 1.4 copy-start.1
  67.9 1.1 copy-start.2
  69.0 11.1 %collective-permute-start.14 = (bf16[2,256,384]{2,1,0:T(8,128)(2,1)S(1)}, bf16[2,256,384]{2,1,0:T(8,128)(2,1)S(1)}, u32[]{:S(2)}, u32[]{:S(2)}) collective-permute-start(bf16[2,256,384]{2,1,0:T(8,128)(2,1)S(1)} %get-tuple-element.30), channel_id=1, source_target_pairs={{8,0},{16,8},{24,16},{32,24},{40,32},{48,40},{56,48},{64,56},{72,6... | collective-permute-start | bytes 1179656 | tf_op jit(solution)/shard_map/ppermute | solution.py:314
  80.9 28.2 %collective-permute-start.16 = (bf16[2,256,256]{2,1,0:T(8,128)(2,1)}, bf16[2,256,256]{2,1,0:T(8,128)(2,1)S(1)}, u32[]{:S(2)}, u32[]{:S(2)}) collective-permute-start(bf16[2,256,256]{2,1,0:T(8,128)(2,1)} %slice.74), channel_id=1, source_target_pairs={{1,0},{2,1},{3,2},{4,3},{5,4},{6,5},{7,6},{9,8},{10,9},{11,10},{12... | collective-permute-start | bytes 786440 | tf_op jit(solution)/shard_map/ppermute | solution.py:314
  85.9 24.1 %collective-permute-start.15 = (bf16[2,512,256]{2,1,0:T(8,128)(2,1)S(1)}, bf16[2,512,256]{2,1,0:T(8,128)(2,1)S(1)}, u32[]{:S(2)}, u32[]{:S(2)}) collective-permute-start(bf16[2,512,256]{2,1,0:T(8,128)(2,1)S(1)} %get-tuple-element.31), channel_id=1, source_target_pairs={{1,0},{2,1},{3,2},{4,3},{5,4},{6,5},{7,6},{9,8},{10,9},{11,10},{12... | collective-permute-start | bytes 1572872 | tf_op jit(solution)/shard_map/ppermute | solution.py:314
  87.9 10.9 %collective-permute-start.19 = (f32[3,32,256]{2,1,0:T(8,128)S(1)}, f32[3,32,256]{2,1,0:T(8,128)S(1)}, u32[]{:S(2)}, u32[]{:S(2)}) collective-permute-start(f32[3,32,256]{2,1,0:T(8,128)S(1)} %get-tuple-element.32.a), channel_id=1, source_target_pairs={{0,24},{8,0},{16,8},{24,16},{1,25},{9,1},{17,9},{25,17},{2,26},{10... | collective-permute-start | bytes 294920 | tf_op jit(solution)/shard_map/ppermute | solution.py:318
  94.8 6.0 %collective-permute-start.18 = (f32[3,32,256]{2,1,0:T(8,128)S(1)}, f32[3,32,256]{2,1,0:T(8,128)S(1)}, u32[]{:S(2)}, u32[]{:S(2)}) collective-permute-start(f32[3,32,256]{2,1,0:T(8,128)S(1)} %get-tuple-element.32.a), channel_id=1, source_target_pairs={{0,16},{8,24},{16,0},{24,8},{1,17},{9,25},{17,1},{25,9},{2,18},{10... | collective-permute-start | bytes 294920 | tf_op jit(solution)/shard_map/ppermute | solution.py:318
  94.8 7.3 %collective-permute-start.17 = (f32[3,32,256]{2,1,0:T(8,128)S(1)}, f32[3,32,256]{2,1,0:T(8,128)S(1)}, u32[]{:S(2)}, u32[]{:S(2)}) collective-permute-start(f32[3,32,256]{2,1,0:T(8,128)S(1)} %get-tuple-element.32.a), channel_id=1, source_target_pairs={{0,8},{8,16},{16,24},{24,0},{1,9},{9,17},{17,25},{25,1},{2,10},{10... | collective-permute-start | bytes 294920 | tf_op jit(solution)/shard_map/ppermute | solution.py:318
  102.2 3.2 %collective-permute-start.22 = (f32[2,32,256]{2,1,0:T(8,128)S(1)}, f32[2,32,256]{2,1,0:T(8,128)S(1)}, u32[]{:S(2)}, u32[]{:S(2)}) collective-permute-start(f32[2,32,256]{2,1,0:T(8,128)S(1)} %z_sum.2.a.mine), channel_id=1, source_target_pairs={{0,96},{32,0},{64,32},{96,64},{1,97},{33,1},{65,33},{97,65},{2,98}... | collective-permute-start | bytes 196616 | tf_op jit(solution)/shard_map/ppermute | solution.py:318
  102.3 4.7 %collective-permute-start.21 = (f32[2,32,256]{2,1,0:T(8,128)S(1)}, f32[2,32,256]{2,1,0:T(8,128)S(1)}, u32[]{:S(2)}, u32[]{:S(2)}) collective-permute-start(f32[2,32,256]{2,1,0:T(8,128)S(1)} %z_sum.2.a.mine), channel_id=1, source_target_pairs={{0,64},{32,96},{64,0},{96,32},{1,65},{33,97},{65,1},{97,33},{2,66}... | collective-permute-start | bytes 196616 | tf_op jit(solution)/shard_map/ppermute | solution.py:318
  102.4 6.7 %collective-permute-start.20 = (f32[2,32,256]{2,1,0:T(8,128)S(1)}, f32[2,32,256]{2,1,0:T(8,128)S(1)}, u32[]{:S(2)}, u32[]{:S(2)}) collective-permute-start(f32[2,32,256]{2,1,0:T(8,128)S(1)} %z_sum.2.a.mine), channel_id=1, source_target_pairs={{0,32},{32,64},{64,96},{96,0},{1,33},{33,65},{65,97},{97,1},{2,34}... | collective-permute-start | bytes 196616 | tf_op jit(solution)/shard_map/ppermute | solution.py:318
  109.1 2.1 %collective-permute-start.23 = (f32[4,2,32,256]{3,2,1,0:T(8,128)S(1)}, f32[4,2,32,256]{3,2,1,0:T(8,128)S(1)}, u32[]{:S(2)}, u32[]{:S(2)}) collective-permute-start(f32[4,2,32,256]{3,2,1,0:T(8,128)S(1)} %half_probe.2.rest_3_), channel_id=1, source_target_pairs={{0,1},{1,0},{2,3},{3,2},{4,5},{5,4},{6,7},{7,6},{8,9},{9,8},{10,11... | collective-permute-start | bytes 786440 | tf_op jit(solution)/shard_map/ppermute | solution.py:322
  119.9 6.5 %collective-permute-start.27 = (f32[4,3,32,256]{3,2,1,0:T(8,128)S(1)}, f32[4,3,32,256]{3,2,1,0:T(8,128)S(1)}, u32[]{:S(2)}, u32[]{:S(2)}) collective-permute-start(f32[4,3,32,256]{3,2,1,0:T(8,128)S(1)} %get-tuple-element.40), channel_id=1, source_target_pairs={{0,1},{1,0},{2,3},{3,2},{4,5},{5,4},{6,7},{7,6},{8,9},{9,8},{10,11... | collective-permute-start | bytes 1179656 | tf_op jit(solution)/shard_map/ppermute | solution.py:322
  120.0 24.3 %collective-permute-start.26 = (bf16[2,256,256]{2,1,0:T(8,128)(2,1)S(1)}, bf16[2,256,256]{2,1,0:T(8,128)(2,1)S(1)}, u32[]{:S(2)}, u32[]{:S(2)}) collective-permute-start(bf16[2,256,256]{2,1,0:T(8,128)(2,1)S(1)} %get-tuple-element.36), channel_id=1, source_target_pairs={{0,9},{1,10},{2,11},{3,12},{4,13},{5,14},{6,15},{8,17},{9,18},{10,... | collective-permute-start | bytes 786440 | tf_op jit(solution)/shard_map/ppermute | solution.py:331
  121.6 22.7 %collective-permute-start.25 = (bf16[2,256,384]{2,1,0:T(8,128)(2,1)S(1)}, bf16[2,256,384]{2,1,0:T(8,128)(2,1)S(1)}, u32[]{:S(2)}, u32[]{:S(2)}) collective-permute-start(bf16[2,256,384]{2,1,0:T(8,128)(2,1)S(1)} %get-tuple-element.35), channel_id=1, source_target_pairs={{0,8},{8,16},{16,24},{24,32},{32,40},{40,48},{48,56},{56,64},{64,7... | collective-permute-start | bytes 1179656 | tf_op jit(solution)/shard_map/ppermute | solution.py:314
  123.8 20.5 %collective-permute-start.24 = (bf16[2,512,256]{2,1,0:T(8,128)(2,1)S(1)}, bf16[2,512,256]{2,1,0:T(8,128)(2,1)S(1)}, u32[]{:S(2)}, u32[]{:S(2)}) collective-permute-start(bf16[2,512,256]{2,1,0:T(8,128)(2,1)S(1)} %get-tuple-element.34), channel_id=1, source_target_pairs={{0,1},{1,2},{2,3},{3,4},{4,5},{5,6},{6,7},{8,9},{9,10},{10,11},{11... | collective-permute-start | bytes 1572872 | tf_op jit(solution)/shard_map/ppermute | solution.py:314
  126.5 39.0 %copy-start.3 = (f32[2,512,384]{2,1,0:T(8,128)S(1)}, f32[2,512,384]{2,1,0:T(8,128)}, u32[]{:S(2)}) copy-start(f32[2,512,384]{2,1,0:T(8,128)} %copy-done.2) | copy-start | bytes 4718596
  126.5 39.0 %copy-start.4 = (f32[2,512,384]{2,1,0:T(8,128)S(1)}, f32[2,512,384]{2,1,0:T(8,128)}, u32[]{:S(2)}) copy-start(f32[2,512,384]{2,1,0:T(8,128)} %get-tuple-element.33.own) | copy-start | bytes 4718596
  126.6 8.1 %collective-permute-start.30 = (f32[3,32,256]{2,1,0:T(8,128)S(1)}, f32[3,32,256]{2,1,0:T(8,128)S(1)}, u32[]{:S(2)}, u32[]{:S(2)}) collective-permute-start(f32[3,32,256]{2,1,0:T(8,128)S(1)} %get-tuple-element.42), channel_id=1, source_target_pairs={{0,96},{32,0},{64,32},{96,64},{1,97},{33,1},{65,33},{97,65},{2,98}... | collective-permute-start | bytes 294920 | tf_op jit(solution)/shard_map/ppermute | solution.py:318
  131.4 6.3 %collective-permute-start.29 = (f32[3,32,256]{2,1,0:T(8,128)S(1)}, f32[3,32,256]{2,1,0:T(8,128)S(1)}, u32[]{:S(2)}, u32[]{:S(2)}) collective-permute-start(f32[3,32,256]{2,1,0:T(8,128)S(1)} %get-tuple-element.43), channel_id=1, source_target_pairs={{0,64},{32,96},{64,0},{96,32},{1,65},{33,97},{65,1},{97,33},{2,66}... | collective-permute-start | bytes 294920 | tf_op jit(solution)/shard_map/ppermute | solution.py:318
  134.7 5.1 %collective-permute-start.28 = (f32[3,32,256]{2,1,0:T(8,128)S(1)}, f32[3,32,256]{2,1,0:T(8,128)S(1)}, u32[]{:S(2)}, u32[]{:S(2)}) collective-permute-start(f32[3,32,256]{2,1,0:T(8,128)S(1)} %get-tuple-element.44), channel_id=1, source_target_pairs={{0,32},{32,64},{64,96},{96,0},{1,33},{33,65},{65,97},{97,1},{2,34}... | collective-permute-start | bytes 294920 | tf_op jit(solution)/shard_map/ppermute | solution.py:318
  139.8 4.7 %collective-permute-start.33 = (f32[3,32,256]{2,1,0:T(8,128)S(1)}, f32[3,32,256]{2,1,0:T(8,128)S(1)}, u32[]{:S(2)}, u32[]{:S(2)}) collective-permute-start(f32[3,32,256]{2,1,0:T(8,128)S(1)} %x_sum.3.a), channel_id=1, source_target_pairs={{0,6},{2,0},{4,2},{6,4},{1,7},{3,1},{5,3},{7,5},{8,14},{10,8},{12,... | collective-permute-start | bytes 294920 | tf_op jit(solution)/shard_map/ppermute | solution.py:318
  139.8 6.4 %collective-permute-start.32 = (f32[3,32,256]{2,1,0:T(8,128)S(1)}, f32[3,32,256]{2,1,0:T(8,128)S(1)}, u32[]{:S(2)}, u32[]{:S(2)}) collective-permute-start(f32[3,32,256]{2,1,0:T(8,128)S(1)} %x_sum.3.a), channel_id=1, source_target_pairs={{0,4},{2,6},{4,0},{6,2},{1,5},{3,7},{5,1},{7,3},{8,12},{10,14},{12... | collective-permute-start | bytes 294920 | tf_op jit(solution)/shard_map/ppermute | solution.py:318
  144.3 5.7 %collective-permute-start.31 = (f32[3,32,256]{2,1,0:T(8,128)S(1)}, f32[3,32,256]{2,1,0:T(8,128)S(1)}, u32[]{:S(2)}, u32[]{:S(2)}) collective-permute-start(f32[3,32,256]{2,1,0:T(8,128)S(1)} %x_sum.3.a), channel_id=1, source_target_pairs={{0,2},{2,4},{4,6},{6,0},{1,3},{3,5},{5,7},{7,1},{8,10},{10,12},{12... | collective-permute-start | bytes 294920 | tf_op jit(solution)/shard_map/ppermute | solution.py:318
  150.0 6.9 %collective-permute-start.36 = (f32[3,32,256]{2,1,0:T(8,128)S(1)}, f32[3,32,256]{2,1,0:T(8,128)S(1)}, u32[]{:S(2)}, u32[]{:S(2)}) collective-permute-start(f32[3,32,256]{2,1,0:T(8,128)S(1)} %y_sum.1.a), channel_id=1, source_target_pairs={{0,24},{8,0},{16,8},{24,16},{1,25},{9,1},{17,9},{25,17},{2,26},{10... | collective-permute-start | bytes 294920 | tf_op jit(solution)/shard_map/ppermute | solution.py:318
  155.0 5.1 %collective-permute-start.35 = (f32[3,32,256]{2,1,0:T(8,128)S(1)}, f32[3,32,256]{2,1,0:T(8,128)S(1)}, u32[]{:S(2)}, u32[]{:S(2)}) collective-permute-start(f32[3,32,256]{2,1,0:T(8,128)S(1)} %y_sum.1.a), channel_id=1, source_target_pairs={{0,16},{8,24},{16,0},{24,8},{1,17},{9,25},{17,1},{25,9},{2,18},{10... | collective-permute-start | bytes 294920 | tf_op jit(solution)/shard_map/ppermute | solution.py:318
  155.2 5.7 %collective-permute-start.34 = (f32[3,32,256]{2,1,0:T(8,128)S(1)}, f32[3,32,256]{2,1,0:T(8,128)S(1)}, u32[]{:S(2)}, u32[]{:S(2)}) collective-permute-start(f32[3,32,256]{2,1,0:T(8,128)S(1)} %y_sum.1.a), channel_id=1, source_target_pairs={{0,8},{8,16},{16,24},{24,0},{1,9},{9,17},{17,25},{25,1},{2,10},{10... | collective-permute-start | bytes 294920 | tf_op jit(solution)/shard_map/ppermute | solution.py:318
  160.9 7.0 %collective-permute-start.39 = (f32[2,32,256]{2,1,0:T(8,128)S(1)}, f32[2,32,256]{2,1,0:T(8,128)S(1)}, u32[]{:S(2)}, u32[]{:S(2)}) collective-permute-start(f32[2,32,256]{2,1,0:T(8,128)S(1)} %z_sum.3.a), channel_id=1, source_target_pairs={{0,96},{32,0},{64,32},{96,64},{1,97},{33,1},{65,33},{97,65},{2,98}... | collective-permute-start | bytes 196616 | tf_op jit(solution)/shard_map/ppermute | solution.py:318
  163.2 4.7 %collective-permute-start.38 = (f32[2,32,256]{2,1,0:T(8,128)S(1)}, f32[2,32,256]{2,1,0:T(8,128)S(1)}, u32[]{:S(2)}, u32[]{:S(2)}) collective-permute-start(f32[2,32,256]{2,1,0:T(8,128)S(1)} %z_sum.3.a), channel_id=1, source_target_pairs={{0,64},{32,96},{64,0},{96,32},{1,65},{33,97},{65,1},{97,33},{2,66}... | collective-permute-start | bytes 196616 | tf_op jit(solution)/shard_map/ppermute | solution.py:318
  164.8 4.3 %collective-permute-start.37 = (f32[2,32,256]{2,1,0:T(8,128)S(1)}, f32[2,32,256]{2,1,0:T(8,128)S(1)}, u32[]{:S(2)}, u32[]{:S(2)}) collective-permute-start(f32[2,32,256]{2,1,0:T(8,128)S(1)} %z_sum.3.a), channel_id=1, source_target_pairs={{0,32},{32,64},{64,96},{96,0},{1,33},{33,65},{65,97},{97,1},{2,34}... | collective-permute-start | bytes 196616 | tf_op jit(solution)/shard_map/ppermute | solution.py:318
  169.2 8.3 %copy-start.5 = (f32[4,2,32,256]{3,2,1,0:T(8,128)}, f32[4,2,32,256]{3,2,1,0:T(8,128)S(1)}, u32[]{:S(2)}) copy-start(f32[4,2,32,256]{3,2,1,0:T(8,128)S(1)} %half_probe.3.mine) | copy-start | bytes 786436
  169.2 8.3 %collective-permute-start.40 = (f32[4,2,32,256]{3,2,1,0:T(8,128)S(1)}, f32[4,2,32,256]{3,2,1,0:T(8,128)S(1)}, u32[]{:S(2)}, u32[]{:S(2)}) collective-permute-start(f32[4,2,32,256]{3,2,1,0:T(8,128)S(1)} %half_probe.3.mine), channel_id=1, source_target_pairs={{0,1},{1,0},{2,3},{3,2},{4,5},{5,4},{6,7},{7,6},{8,9},{9,8},{10,11... | collective-permute-start | bytes 786440 | tf_op jit(solution)/shard_map/ppermute | solution.py:322
  177.5 0.7 copy-start.9

commit v7 on v5

--- a/solution.py
+++ b/solution.py
@@ -14,7 +14,7 @@
 ALPHA = 0.5
 LANES = 128
 CHUNK = 32
-GROUPS = (4, 2, 1)
+GROUPS = (6, 2, 1)
 N_X, N_Z, N_Y, N_CORE = 4, 4, 4, 2
 N_ROW, N_COL = N_X * N_Z, N_Y * N_CORE
 ROW, COL = ("x", "z"), ("y", "core")
@@ -280,6 +280,16 @@
     obj_out[:, size:, size:] = obj[:, size:, size:] - alpha * own[:, size:, size:]
 
 
+def last_kernel(obj, own, left, down, step, obj_out, done):
+    object_step(obj, own, left, down, step, obj_out)
+    done[...] = obj_out[0, :8, :LANES]
+
+
+def stack_kernel(a, b, c, d, *rest):
+    for j, chunk in enumerate((a, b, c, d)):
+        rest[-1][j] = chunk[...]
+
+
 def both_kernel(a, b, c, d, mine, obj, own, left, down, step, fresh, obj_out, below, right):
     probe_step(a, b, c, d, mine, fresh)
     object_step(obj, own, left, down, step, obj_out)
@@ -296,18 +306,6 @@
         for j in range(N_X):
             at = pl.multiple_of(side * half + lax.rem(x - j + N_X, N_X) * quarter, quarter)
             out[:, pl.ds(at, quarter), :] = piece[j]
-
-
-def run_probe(place, mine, other):
-    vmem = pl.BlockSpec(memory_space=pltpu.VMEM)
-    size = mine.shape[-1]
-    return pl.pallas_call(
-        probe_kernel,
-        out_shape=jax.ShapeDtypeStruct((2, size, size), F32),
-        in_specs=[pl.BlockSpec(memory_space=pltpu.SMEM), vmem, vmem],
-        out_specs=vmem,
-        name="probe_whole",
-    )(place, mine, other)
 
 
 def moved(value, axis, count, steps):
@@ -351,8 +349,10 @@
     lows = [obj[:, :size, :size].astype(BF), obj[:, :size, size:].astype(BF)]
     right = obj[:, :, :size].astype(BF)
     pieces = (probe,)
+    row = jax.ShapeDtypeStruct((8, LANES), F32)
+    half_probe = jax.ShapeDtypeStruct((N_X, *mine.shape), F32)
+    halos = halo(lows, right)
     for iteration in range(ITERS):
-        halos = halo(lows, right)
         own, low_left, low_right, right, corner, keep, send, step = run_frames(
             place, counts[iteration, 0], positions[iteration], obj, halos, pieces, amps, tables, iteration
         )
@@ -365,15 +365,20 @@
         (total,) = small_call(y_kernel, [share], (around(total, "y"), [left]), "y_sum")
         sums = around(total, "z") + [mine]
         if iteration < ITERS - 1:
-            mine, obj, *lows, right = small_call(
+            mine, obj, below, right = small_call(
                 both_kernel, [part, whole, flat, tall], ([*sums, obj, own, left, down, step], []), "z_sum_object"
             )
+            halos = halo([below], right)
+            waited = [halos[2]]
         else:
             (mine,) = small_call(z_kernel, [part], (sums, [down]), "z_sum")
-            (obj,) = small_call(object_step, [whole], ([obj, own, left, down, step], []), "object_update")
-        stack = jnp.stack(around(mine, "x"))
+            obj, done = small_call(last_kernel, [whole, row], ([obj, own, left, down, step], []), "object_update")
+            waited = [done]
+        (stack,) = small_call(stack_kernel, [half_probe], (around(mine, "x"), waited), "half_probe")
         pieces = (stack, swapped(stack))
-    return (obj, run_probe(place, *pieces))
+    shape = jax.ShapeDtypeStruct((2, size, size), F32)
+    (probe,) = small_call(probe_kernel, [shape], ([place, *pieces], []), "probe_whole")
+    return (obj, probe)
 
 
 def solution(mesh):

time: 163 us -> 163 us (level)
  starting transfers between devices: 76.8 us -> 83.3 us
  Pallas kernels: 21.4 us -> 17.6 us
  waiting for transfers between devices: 56.9 us -> 54.4 us
    ppermute x24, waiting for transfers between devices: 43.2 us -> 36.7 us  [turned(): return lax.ppermute(value, axis, [(s, (s + steps) % 4) for s in range(4)])]
    ppermute x13, starting transfers between devices: 35.3 us -> 38.7 us  [moved(): lax.ppermute(value, axis, [(s, s + steps) for s in range(first, last)])]
    pallas_call x2, Pallas kernels: 15 us -> 11.6 us  [run_frames(): pl.pallas_call(functools.partial(frames_kernel, iteration, len(lows), len...]
    ppermute x24, starting transfers between devices: 35 us -> 37.9 us  [turned(): return lax.ppermute(value, axis, [(s, (s + steps) % 4) for s in range(4)])]
    ppermute x13, waiting for transfers between devices: 13.7 us -> 16.6 us  [moved(): lax.ppermute(value, axis, [(s, s + steps) for s in range(first, last)])]
    pallas_call x1 -> x0, Pallas kernels: 1.87 us -> none  [run_probe(): pl.pallas_call(probe_kernel, out_shape=jax.ShapeDtypeStruct((2, size, siz...]
    pallas_call x7 -> x10, Pallas kernels: 4.59 us -> 5.95 us  [small_call(): pl.pallas_call(body, out_shape=shapes, in_specs=[spec(space) for space in...]
    unnamed x22 -> x16, local copies, waits for them, and re-layouts: 3.38 us -> 2.66 us
  transfers between devices with their start and end apart: 41 -> 41, of which waited for: 26 -> 25; matrix products, arithmetic and copies ran while one was open for 1% -> 1% of each run, Pallas kernels for 2% -> 2%
where the time goes in v7:
time: 163 us; the launch traced here: 162 us
  starting transfers between devices  83.3 us (51%)
  waiting for transfers between devices  54.4 us (33%)
  Pallas kernels  17.6 us (11%)
  local copies, waits for them, and re-layouts  4.19 us (3%)
  other arithmetic  1.83 us (1%)
    ppermute x13, starting transfers between devices, moved(): lax.ppermute(value, axis, [(s, s + steps) for s in range(first, last)])  38.7 us
    ppermute x24, starting transfers between devices, turned(): return lax.ppermute(value, axis, [(s, (s + steps) % 4) for s in range(4)])  37.9 us
    ppermute x24, waiting for transfers between devices, turned(): return lax.ppermute(value, axis, [(s, (s + steps) % 4) for s in range(4)])  36.7 us
    ppermute x13, waiting for transfers between devices, moved(): lax.ppermute(value, axis, [(s, s + steps) for s in range(first, last)])  16.6 us
    pallas_call x2, Pallas kernels, run_frames(): pl.pallas_call(functools.partial(frames_kernel, iteration, len(lows), len...  11.6 us
    ppermute x4, starting transfers between devices, swapped(): return lax.ppermute(value, 'core', [(0, 1), (1, 0)])  6.63 us
    pallas_call x10, Pallas kernels, small_call(): pl.pallas_call(body, out_shape=shapes, in_specs=[spec(space) for space in...  5.95 us
  transfers between devices with their start and end apart: 41, of which 25 were waited for; matrix products, arithmetic and copies ran while one was open for 1% of the time, Pallas kernels for 2%

profile of v7, /device:TPU:1, one launch (start us, length us, event | category | flops | bytes accessed | tf_op | source)
XLA Modules:
  0.0 162.2 jit_solution(6826477537024325467)
XLA Ops:
  0.7 1.6 %convert.5 = bf16[2,512,384]{2,1,0:T(8,128)(2,1)S(1)} convert(f32[2,512,384]{2,1,0:T(8,128)} %obj.3) | non-fusion elementwise | flops 393216 | bytes 2359296 | tf_op jit(solution)/shard_map/convert.2
  2.3 1.3 collective-permute-start
  3.6 0.8 slice.69
  4.5 3.3 %collective-permute-start.2 = (bf16[2,512,256]{2,1,0:T(8,128)(2,1)}, bf16[2,512,256]{2,1,0:T(8,128)(2,1)S(1)}, u32[]{:S(2)}, u32[]{:S(2)}) collective-permute-start(bf16[2,512,256]{2,1,0:T(8,128)(2,1)} %slice.69), channel_id=1, source_target_pairs={{1,0},{2,1},{3,2},{4,3},{5,4},{6,5},{7,6},{9,8},{10,9},{11,10},{12... | collective-permute-start | bytes 1572872 | tf_op jit(solution)/shard_map/ppermute | solution.py:313
  7.8 1.3 collective-permute-start.1
  9.1 3.6 %collective-permute-done.rest_0_ = bf16[2,256,256]{2,1,0:T(8,128)(2,1)S(1)} collective-permute-done((bf16[2,256,256]{2,1,0:T(8,128)(2,1)S(1)}, bf16[2,256,256]{2,1,0:T(8,128)(2,1)S(1)}, u32[]{:S(2)}, u32[]{:S(2)}) %collective-permute-start) | collective-permute-done | bytes 262176 | tf_op jit(solution)/shard_map/ppermute | solution.py:313
  12.7 3.3 %collective-permute-start.3 = (bf16[2,256,256]{2,1,0:T(8,128)(2,1)S(1)}, bf16[2,256,256]{2,1,0:T(8,128)(2,1)S(1)}, u32[]{:S(2)}, u32[]{:S(2)}) collective-permute-start(bf16[2,256,256]{2,1,0:T(8,128)(2,1)S(1)} %collective-permute-done.rest_0_), channel_id=1, source_target_pairs={{1,0},{2,1},{3,2},{4,3},{5,4},{6,5},{7,6},{9,8},{10,9},{11,10},{12... | collective-permute-start | bytes 786440 | tf_op jit(solution)/shard_map/ppermute | solution.py:313
  16.2 0.6 fusion
  16.7 4.4 %collective-permute-done.3.rest_3_ = bf16[2,256,256]{2,1,0:T(8,128)(2,1)S(1)} collective-permute-done((bf16[2,256,256]{2,1,0:T(8,128)(2,1)S(1)}, bf16[2,256,256]{2,1,0:T(8,128)(2,1)S(1)}, u32[]{:S(2)}, u32[]{:S(2)}) %collective-permute-start.3) | collective-permute-done | bytes 262176 | tf_op jit(solution)/shard_map/ppermute | solution.py:313
  21.2 1.2 copy-done.4
  22.4 5.9 %frames.2 = (f32[2,512,384]{2,1,0:T(8,128)S(1)}, f32[2,256,256]{2,1,0:T(8,128)S(1)}, bf16[2,256,128]{2,1,0:T(8,128)(2,1)S(1)}, bf16[2,512,256]{2,1,0:T(8,128)(2,...) custom-call(s32[2]{0:T(128)S(1)} %pad_add_fusion.place, ...), custom_call_target="tpu_custom_call" | custom-call | flops 6000000000 | bytes 8000000 | tf_op jit(solution)/shard_map/frames/pallas_call | solution.py:225
  28.4 3.6 %collective-permute-start.8 = (bf16[2,256,256]{2,1,0:T(8,128)(2,1)S(1)}, bf16[2,256,256]{2,1,0:T(8,128)(2,1)S(1)}, u32[]{:S(2)}, u32[]{:S(2)}) collective-permute-start(bf16[2,256,256]{2,1,0:T(8,128)(2,1)S(1)} %get-tuple-element.32), channel_id=1, source_target_pairs={{0,1},{1,2},{2,3},{3,4},{4,5},{5,6},{6,7},{8,9},{9,10},{10,11},{11... | collective-permute-start | bytes 786440 | tf_op jit(solution)/shard_map/ppermute | solution.py:313
  32.0 2.3 %collective-permute-start.12 = (bf16[2,512,256]{2,1,0:T(8,128)(2,1)}, bf16[2,512,256]{2,1,0:T(8,128)(2,1)S(1)}, u32[]{:S(2)}, u32[]{:S(2)}) collective-permute-start(bf16[2,512,256]{2,1,0:T(8,128)(2,1)} %get-tuple-element.34), channel_id=1, source_target_pairs={{0,1},{1,2},{2,3},{3,4},{4,5},{5,6},{6,7},{8,9},{9,10},{10,11},{11... | collective-permute-start | bytes 1572872 | tf_op jit(solution)/shard_map/ppermute | solution.py:313
  34.5 6.6 %collective-permute-start.7 = (f32[3,32,256]{2,1,0:T(8,128)S(1)}, f32[3,32,256]{2,1,0:T(8,128)S(1)}, u32[]{:S(2)}, u32[]{:S(2)}) collective-permute-start(f32[3,32,256]{2,1,0:T(8,128)S(1)} %get-tuple-element.58), channel_id=1, source_target_pairs={{0,96},{32,0},{64,32},{96,64},{1,97},{33,1},{65,33},{97,65},{2,98}... | collective-permute-start | bytes 294920 | tf_op jit(solution)/shard_map/ppermute | solution.py:317
  41.1 0.7 collective-permute-start.5
  41.9 3.4 %collective-permute-done.7.d = f32[3,32,256]{2,1,0:T(8,128)S(1)} collective-permute-done((f32[3,32,256]{2,1,0:T(8,128)S(1)}, f32[3,32,256]{2,1,0:T(8,128)S(1)}, u32[]{:S(2)}, u32[]{:S(2)}) %collective-permute-start.7) | collective-permute-done | bytes 98336 | tf_op jit(solution)/shard_map/ppermute | solution.py:317
  45.3 1.5 collective-permute-done.6.c
  46.7 2.1 %collective-permute-done.5.b = f32[3,32,256]{2,1,0:T(8,128)S(1)} collective-permute-done((f32[3,32,256]{2,1,0:T(8,128)S(1)}, f32[3,32,256]{2,1,0:T(8,128)S(1)}, u32[]{:S(2)}, u32[]{:S(2)}) %collective-permute-start.5) | collective-permute-done | bytes 98336 | tf_op jit(solution)/shard_map/ppermute | solution.py:317
  48.8 0.9 x_sum.2
  49.7 5.7 %collective-permute-start.16 = (bf16[2,256,384]{2,1,0:T(8,128)(2,1)}, bf16[2,256,384]{2,1,0:T(8,128)(2,1)S(1)}, u32[]{:S(2)}, u32[]{:S(2)}) collective-permute-start(bf16[2,256,384]{2,1,0:T(8,128)(2,1)} %get-tuple-element.36), channel_id=1, source_target_pairs={{0,8},{8,16},{16,24},{24,32},{32,40},{40,48},{48,56},{56,64},{64,7... | collective-permute-start | bytes 1179656 | tf_op jit(solution)/shard_map/ppermute | solution.py:313
  55.7 4.7 %collective-permute-start.10 = (f32[3,32,256]{2,1,0:T(8,128)S(1)}, f32[3,32,256]{2,1,0:T(8,128)S(1)}, u32[]{:S(2)}, u32[]{:S(2)}) collective-permute-start(f32[3,32,256]{2,1,0:T(8,128)S(1)} %get-tuple-element.33.a), channel_id=1, source_target_pairs={{0,4},{2,6},{4,0},{6,2},{1,5},{3,7},{5,1},{7,3},{8,12},{10,14},{12... | collective-permute-start | bytes 294920 | tf_op jit(solution)/shard_map/ppermute | solution.py:317
  60.6 1.8 %collective-permute-done.10.c = f32[3,32,256]{2,1,0:T(8,128)S(1)} collective-permute-done((f32[3,32,256]{2,1,0:T(8,128)S(1)}, f32[3,32,256]{2,1,0:T(8,128)S(1)}, u32[]{:S(2)}, u32[]{:S(2)}) %collective-permute-start.10) | collective-permute-done | bytes 98336 | tf_op jit(solution)/shard_map/ppermute | solution.py:317
  62.4 3.1 %collective-permute-done.9.b = f32[3,32,256]{2,1,0:T(8,128)S(1)} collective-permute-done((f32[3,32,256]{2,1,0:T(8,128)S(1)}, f32[3,32,256]{2,1,0:T(8,128)S(1)}, u32[]{:S(2)}, u32[]{:S(2)}) %collective-permute-start.9) | collective-permute-done | bytes 98336 | tf_op jit(solution)/shard_map/ppermute | solution.py:317
  65.6 2.0 %collective-permute-start.14 = (f32[3,32,256]{2,1,0:T(8,128)S(1)}, f32[3,32,256]{2,1,0:T(8,128)S(1)}, u32[]{:S(2)}, u32[]{:S(2)}) collective-permute-start(f32[3,32,256]{2,1,0:T(8,128)S(1)} %y_sum.2.a), channel_id=1, source_target_pairs={{0,16},{8,24},{16,0},{24,8},{1,17},{9,25},{17,1},{25,9},{2,18},{10... | collective-permute-start | bytes 294920 | tf_op jit(solution)/shard_map/ppermute | solution.py:317
  67.6 1.5 collective-permute-done.15.d
  69.1 1.6 collective-permute-done.14.c
  70.7 1.6 collective-permute-done.13.b
  72.2 1.4 copy-done.2
  73.6 1.2 z_sum_object.1
  74.9 1.3 collective-permute-start.17
  76.2 7.2 %collective-permute-done.17.rest_0_ = bf16[2,256,384]{2,1,0:T(8,128)(2,1)S(1)} collective-permute-done((bf16[2,256,384]{2,1,0:T(8,128)(2,1)S(1)}, bf16[2,256,384]{2,1,0:T(8,128)(2,1)S(1)}, u32[]{:S(2)}, u32[]{:S(2)}) %collective-permute-start.17) | collective-permute-done | bytes 393248 | tf_op jit(solution)/shard_map/ppermute | solution.py:313
  83.4 6.8 %collective-permute-start.19 = (bf16[2,256,256]{2,1,0:T(8,128)(2,1)S(1)}, bf16[2,256,256]{2,1,0:T(8,128)(2,1)S(1)}, u32[]{:S(2)}, u32[]{:S(2)}) collective-permute-start(bf16[2,256,256]{2,1,0:T(8,128)(2,1)S(1)} %slice.74), channel_id=1, source_target_pairs={{1,0},{2,1},{3,2},{4,3},{5,4},{6,5},{7,6},{9,8},{10,9},{11,10},{12... | collective-permute-start | bytes 786440 | tf_op jit(solution)/shard_map/ppermute | solution.py:313
  90.3 1.9 %collective-permute-start.18 = (bf16[2,512,256]{2,1,0:T(8,128)(2,1)S(1)}, bf16[2,512,256]{2,1,0:T(8,128)(2,1)S(1)}, u32[]{:S(2)}, u32[]{:S(2)}) collective-permute-start(bf16[2,512,256]{2,1,0:T(8,128)(2,1)S(1)} %get-tuple-element.40), channel_id=1, source_target_pairs={{1,0},{2,1},{3,2},{4,3},{5,4},{6,5},{7,6},{9,8},{10,9},{11,10},{12... | collective-permute-start | bytes 1572872 | tf_op jit(solution)/shard_map/ppermute | solution.py:313
  92.6 1.5 collective-permute-start.21
  94.5 1.3 collective-permute-done.22.d
  95.8 1.6 collective-permute-done.21.c
  97.4 1.6 collective-permute-done.20.b
  99.5 1.3 collective-permute-done.18.rest_1_
  100.8 5.7 %frames.3 = (f32[2,512,384]{2,1,0:T(8,128)S(1)}, f32[2,256,256]{2,1,0:T(8,128)S(1)}, bf16[2,256,128]{2,1,0:T(8,128)(2,1)S(1)}, bf16[2,512,256]{2,1,0:T(8,128)(2,...) custom-call(s32[2]{0:T(128)S(1)} %pad_add_fusion.place, ...), custom_call_target="tpu_custom_call" | custom-call | flops 6000000000 | bytes 8000000 | tf_op jit(solution)/shard_map/frames/pallas_call | solution.py:225
  106.8 4.5 %collective-permute-start.29 = (bf16[2,256,256]{2,1,0:T(8,128)(2,1)S(1)}, bf16[2,256,256]{2,1,0:T(8,128)(2,1)S(1)}, u32[]{:S(2)}, u32[]{:S(2)}) collective-permute-start(bf16[2,256,256]{2,1,0:T(8,128)(2,1)S(1)} %get-tuple-element.48), channel_id=1, source_target_pairs={{0,1},{1,2},{2,3},{3,4},{4,5},{5,6},{6,7},{8,9},{9,10},{10,11},{11... | collective-permute-start | bytes 786440 | tf_op jit(solution)/shard_map/ppermute | solution.py:313
  111.4 1.9 %collective-permute-start.24 = (bf16[2,512,256]{2,1,0:T(8,128)(2,1)S(1)}, bf16[2,512,256]{2,1,0:T(8,128)(2,1)S(1)}, u32[]{:S(2)}, u32[]{:S(2)}) collective-permute-start(bf16[2,512,256]{2,1,0:T(8,128)(2,1)S(1)} %get-tuple-element.43), channel_id=1, source_target_pairs={{0,1},{1,2},{2,3},{3,4},{4,5},{5,6},{6,7},{8,9},{9,10},{10,11},{11... | collective-permute-start | bytes 1572872 | tf_op jit(solution)/shard_map/ppermute | solution.py:313
  113.4 3.7 %collective-permute-start.28 = (f32[3,32,256]{2,1,0:T(8,128)S(1)}, f32[3,32,256]{2,1,0:T(8,128)S(1)}, u32[]{:S(2)}, u32[]{:S(2)}) collective-permute-start(f32[3,32,256]{2,1,0:T(8,128)S(1)} %get-tuple-element.54), channel_id=1, source_target_pairs={{0,96},{32,0},{64,32},{96,64},{1,97},{33,1},{65,33},{97,65},{2,98}... | collective-permute-start | bytes 294920 | tf_op jit(solution)/shard_map/ppermute | solution.py:317
  117.2 6.0 %collective-permute-start.27 = (f32[3,32,256]{2,1,0:T(8,128)S(1)}, f32[3,32,256]{2,1,0:T(8,128)S(1)}, u32[]{:S(2)}, u32[]{:S(2)}) collective-permute-start(f32[3,32,256]{2,1,0:T(8,128)S(1)} %get-tuple-element.55), channel_id=1, source_target_pairs={{0,64},{32,96},{64,0},{96,32},{1,65},{33,97},{65,1},{97,33},{2,66}... | collective-permute-start | bytes 294920 | tf_op jit(solution)/shard_map/ppermute | solution.py:317
  123.1 0.8 collective-permute-start.26
  123.9 2.3 %collective-permute-done.27.c = f32[3,32,256]{2,1,0:T(8,128)S(1)} collective-permute-done((f32[3,32,256]{2,1,0:T(8,128)S(1)}, f32[3,32,256]{2,1,0:T(8,128)S(1)}, u32[]{:S(2)}, u32[]{:S(2)}) %collective-permute-start.27) | collective-permute-done | bytes 98336 | tf_op jit(solution)/shard_map/ppermute | solution.py:317
  126.2 2.1 %collective-permute-done.26.b = f32[3,32,256]{2,1,0:T(8,128)S(1)} collective-permute-done((f32[3,32,256]{2,1,0:T(8,128)S(1)}, f32[3,32,256]{2,1,0:T(8,128)S(1)}, u32[]{:S(2)}, u32[]{:S(2)}) %collective-permute-start.26) | collective-permute-done | bytes 98336 | tf_op jit(solution)/shard_map/ppermute | solution.py:317
  128.5 1.3 collective-permute-start.30
  129.9 3.3 %collective-permute-start.32 = (f32[3,32,256]{2,1,0:T(8,128)S(1)}, f32[3,32,256]{2,1,0:T(8,128)S(1)}, u32[]{:S(2)}, u32[]{:S(2)}) collective-permute-start(f32[3,32,256]{2,1,0:T(8,128)S(1)} %get-tuple-element.52.a), channel_id=1, source_target_pairs={{0,4},{2,6},{4,0},{6,2},{1,5},{3,7},{5,1},{7,3},{8,12},{10,14},{12... | collective-permute-start | bytes 294920 | tf_op jit(solution)/shard_map/ppermute | solution.py:317
  133.1 0.8 collective-permute-start.31
  133.9 1.2 collective-permute-done.32.c
  135.1 3.8 %collective-permute-done.31.b = f32[3,32,256]{2,1,0:T(8,128)S(1)} collective-permute-done((f32[3,32,256]{2,1,0:T(8,128)S(1)}, f32[3,32,256]{2,1,0:T(8,128)S(1)}, u32[]{:S(2)}, u32[]{:S(2)}) %collective-permute-start.31) | collective-permute-done | bytes 98336 | tf_op jit(solution)/shard_map/ppermute | solution.py:317
  138.9 1.9 %collective-permute-start.36 = (f32[3,32,256]{2,1,0:T(8,128)S(1)}, f32[3,32,256]{2,1,0:T(8,128)S(1)}, u32[]{:S(2)}, u32[]{:S(2)}) collective-permute-start(f32[3,32,256]{2,1,0:T(8,128)S(1)} %y_sum.3.a), channel_id=1, source_target_pairs={{0,24},{8,0},{16,8},{24,16},{1,25},{9,1},{17,9},{25,17},{2,26},{10... | collective-permute-start | bytes 294920 | tf_op jit(solution)/shard_map/ppermute | solution.py:317
  140.8 1.4 collective-permute-start.35
  142.2 1.2 collective-permute-done.36.d
  143.4 2.4 %collective-permute-done.35.c = f32[3,32,256]{2,1,0:T(8,128)S(1)} collective-permute-done((f32[3,32,256]{2,1,0:T(8,128)S(1)}, f32[3,32,256]{2,1,0:T(8,128)S(1)}, u32[]{:S(2)}, u32[]{:S(2)}) %collective-permute-start.35) | collective-permute-done | bytes 98336 | tf_op jit(solution)/shard_map/ppermute | solution.py:317
  145.8 1.1 collective-permute-done.34.b
  146.9 0.6 collective-permute-start.39
  147.5 2.1 %collective-permute-start.38 = (f32[2,32,256]{2,1,0:T(8,128)S(1)}, f32[2,32,256]{2,1,0:T(8,128)S(1)}, u32[]{:S(2)}, u32[]{:S(2)}) collective-permute-start(f32[2,32,256]{2,1,0:T(8,128)S(1)} %z_sum.1.a), channel_id=1, source_target_pairs={{0,64},{32,96},{64,0},{96,32},{1,65},{33,97},{65,1},{97,33},{2,66}... | collective-permute-start | bytes 196616 | tf_op jit(solution)/shard_map/ppermute | solution.py:317
  149.6 0.8 collective-permute-start.37
  150.4 2.3 %object_update.1 = (f32[2,512,384]{2,1,0:T(8,128)}, f32[8,128]{1,0:T(8,128)S(1)}) custom-call(f32[2,512,384]{2,1,0:T(8,128)S(1)} %get-tuple-element.38.obj, f32[2,512,384]{2,1,0:T(8,128)S(1)} %get-tuple-element.42.own, bf16[2,512,256]{2,1,0:T(8,128)(2,1)S(1)} %collective-permute-done.24.left.waited, ...), custom_call_target="tpu_custom_call" | custom-call | flops 2000000 | bytes 4000000 | tf_op jit(solution)/shard_map/object_update/pallas_call | solution.py:243
  152.7 1.3 collective-permute-done.37.b
  154.0 5.7 %collective-permute-start.40 = (f32[4,2,32,256]{3,2,1,0:T(8,128)S(1)}, f32[4,2,32,256]{3,2,1,0:T(8,128)S(1)}, u32[]{:S(2)}, u32[]{:S(2)}) collective-permute-start(f32[4,2,32,256]{3,2,1,0:T(8,128)S(1)} %half_probe.3.mine), channel_id=1, source_target_pairs={{0,1},{1,0},{2,3},{3,2},{4,5},{5,4},{6,7},{7,6},{8,9},{9,8},{10,11... | collective-permute-start | bytes 786440 | tf_op jit(solution)/shard_map/ppermute | solution.py:321
  159.7 1.2 collective-permute-done.40.other
  160.9 1.4 probe_whole.1
  (59 shorter events, 2.9 us)
Async XLA Ops:
  0.6 20.6 %copy-start = (f32[2,512,384]{2,1,0:T(8,128)S(1)}, f32[2,512,384]{2,1,0:T(8,128)}, u32[]{:S(2)}) copy-start(f32[2,512,384]{2,1,0:T(8,128)} %obj.3) | copy-start | bytes 4718596
  0.6 15.4 %copy-start.6 = (s32[2,2,12]{2,1,0:T(2,128)S(1)}, s32[2,2,12]{2,1,0:T(2,128)}, u32[]{:S(2)}) copy-start(s32[2,2,12]{2,1,0:T(2,128)} %param.9) | copy-start | bytes 580
  0.7 15.5 %copy-start.7 = (s32[2,1,1]{0,2,1:T(1,128)S(1)}, s32[2,1,1]{0,2,1:T(1,128)}, u32[]{:S(2)}) copy-start(s32[2,1,1]{0,2,1:T(1,128)} %param.10) | copy-start | bytes 28
  0.7 20.5 %copy-start.3 = (f32[2,256,256]{2,1,0:T(8,128)S(1)}, f32[2,256,256]{2,1,0:T(8,128)}, u32[]{:S(2)}) copy-start(f32[2,256,256]{2,1,0:T(8,128)} %rest_4_.1) | copy-start | bytes 1572868
  2.3 10.4 %collective-permute-start = (bf16[2,256,256]{2,1,0:T(8,128)(2,1)S(1)}, bf16[2,256,256]{2,1,0:T(8,128)(2,1)S(1)}, u32[]{:S(2)}, u32[]{:S(2)}) collective-permute-start(bf16[2,256,256]{2,1,0:T(8,128)(2,1)S(1)} %slice.67), channel_id=1, source_target_pairs={{8,0},{16,8},{24,16},{32,24},{40,32},{48,40},{56,48},{64,56},{72,6... | collective-permute-start | bytes 786440 | tf_op jit(solution)/shard_map/ppermute | solution.py:313
  4.5 16.7 %collective-permute-start.2 = (bf16[2,512,256]{2,1,0:T(8,128)(2,1)}, bf16[2,512,256]{2,1,0:T(8,128)(2,1)S(1)}, u32[]{:S(2)}, u32[]{:S(2)}) collective-permute-start(bf16[2,512,256]{2,1,0:T(8,128)(2,1)} %slice.69), channel_id=1, source_target_pairs={{1,0},{2,1},{3,2},{4,3},{5,4},{6,5},{7,6},{9,8},{10,9},{11,10},{12... | collective-permute-start | bytes 1572872 | tf_op jit(solution)/shard_map/ppermute | solution.py:313
  7.8 8.9 %collective-permute-start.1 = (bf16[2,256,128]{2,1,0:T(8,128)(2,1)S(1)}, bf16[2,256,128]{2,1,0:T(8,128)(2,1)S(1)}, u32[]{:S(2)}, u32[]{:S(2)}) collective-permute-start(bf16[2,256,128]{2,1,0:T(8,128)(2,1)S(1)} %slice.68), channel_id=1, source_target_pairs={{8,0},{16,8},{24,16},{32,24},{40,32},{48,40},{56,48},{64,56},{72,6... | collective-permute-start | bytes 393224 | tf_op jit(solution)/shard_map/ppermute | solution.py:313
  12.7 8.5 %collective-permute-start.3 = (bf16[2,256,256]{2,1,0:T(8,128)(2,1)S(1)}, bf16[2,256,256]{2,1,0:T(8,128)(2,1)S(1)}, u32[]{:S(2)}, u32[]{:S(2)}) collective-permute-start(bf16[2,256,256]{2,1,0:T(8,128)(2,1)S(1)} %collective-permute-done.rest_0_), channel_id=1, source_target_pairs={{1,0},{2,1},{3,2},{4,3},{5,4},{6,5},{7,6},{9,8},{10,9},{11,10},{12... | collective-permute-start | bytes 786440 | tf_op jit(solution)/shard_map/ppermute | solution.py:313
  21.2 1.2 copy-start.4
  28.3 21.4 %copy-start.1 = (f32[2,512,384]{2,1,0:T(8,128)}, f32[2,512,384]{2,1,0:T(8,128)S(1)}, u32[]{:S(2)}) copy-start(f32[2,512,384]{2,1,0:T(8,128)S(1)} %get-tuple-element.35.own) | copy-start | bytes 4718596
  28.3 6.0 %collective-permute-start.4 = (f32[4,3,32,256]{3,2,1,0:T(8,128)S(1)}, f32[4,3,32,256]{3,2,1,0:T(8,128)S(1)}, u32[]{:S(2)}, u32[]{:S(2)}) collective-permute-start(f32[4,3,32,256]{3,2,1,0:T(8,128)S(1)} %get-tuple-element.29), channel_id=1, source_target_pairs={{0,1},{1,0},{2,3},{3,2},{4,5},{5,4},{6,7},{7,6},{8,9},{9,8},{10,11... | collective-permute-start | bytes 1179656 | tf_op jit(solution)/shard_map/ppermute | solution.py:321
  28.4 13.4 %collective-permute-start.8 = (bf16[2,256,256]{2,1,0:T(8,128)(2,1)S(1)}, bf16[2,256,256]{2,1,0:T(8,128)(2,1)S(1)}, u32[]{:S(2)}, u32[]{:S(2)}) collective-permute-start(bf16[2,256,256]{2,1,0:T(8,128)(2,1)S(1)} %get-tuple-element.32), channel_id=1, source_target_pairs={{0,1},{1,2},{2,3},{3,4},{4,5},{5,6},{6,7},{8,9},{9,10},{10,11},{11... | collective-permute-start | bytes 786440 | tf_op jit(solution)/shard_map/ppermute | solution.py:313
  32.0 28.4 %collective-permute-start.12 = (bf16[2,512,256]{2,1,0:T(8,128)(2,1)}, bf16[2,512,256]{2,1,0:T(8,128)(2,1)S(1)}, u32[]{:S(2)}, u32[]{:S(2)}) collective-permute-start(bf16[2,512,256]{2,1,0:T(8,128)(2,1)} %get-tuple-element.34), channel_id=1, source_target_pairs={{0,1},{1,2},{2,3},{3,4},{4,5},{5,6},{6,7},{8,9},{9,10},{10,11},{11... | collective-permute-start | bytes 1572872 | tf_op jit(solution)/shard_map/ppermute | solution.py:313
  34.5 10.8 %collective-permute-start.7 = (f32[3,32,256]{2,1,0:T(8,128)S(1)}, f32[3,32,256]{2,1,0:T(8,128)S(1)}, u32[]{:S(2)}, u32[]{:S(2)}) collective-permute-start(f32[3,32,256]{2,1,0:T(8,128)S(1)} %get-tuple-element.58), channel_id=1, source_target_pairs={{0,96},{32,0},{64,32},{96,64},{1,97},{33,1},{65,33},{97,65},{2,98}... | collective-permute-start | bytes 294920 | tf_op jit(solution)/shard_map/ppermute | solution.py:317
  41.1 5.6 %collective-permute-start.6 = (f32[3,32,256]{2,1,0:T(8,128)S(1)}, f32[3,32,256]{2,1,0:T(8,128)S(1)}, u32[]{:S(2)}, u32[]{:S(2)}) collective-permute-start(f32[3,32,256]{2,1,0:T(8,128)S(1)} %get-tuple-element.59), channel_id=1, source_target_pairs={{0,64},{32,96},{64,0},{96,32},{1,65},{33,97},{65,1},{97,33},{2,66}... | collective-permute-start | bytes 294920 | tf_op jit(solution)/shard_map/ppermute | solution.py:317
  41.1 7.7 %collective-permute-start.5 = (f32[3,32,256]{2,1,0:T(8,128)S(1)}, f32[3,32,256]{2,1,0:T(8,128)S(1)}, u32[]{:S(2)}, u32[]{:S(2)}) collective-permute-start(f32[3,32,256]{2,1,0:T(8,128)S(1)} %get-tuple-element.60), channel_id=1, source_target_pairs={{0,32},{32,64},{64,96},{96,0},{1,33},{33,65},{65,97},{97,1},{2,34}... | collective-permute-start | bytes 294920 | tf_op jit(solution)/shard_map/ppermute | solution.py:317
  49.7 22.5 %collective-permute-start.16 = (bf16[2,256,384]{2,1,0:T(8,128)(2,1)}, bf16[2,256,384]{2,1,0:T(8,128)(2,1)S(1)}, u32[]{:S(2)}, u32[]{:S(2)}) collective-permute-start(bf16[2,256,384]{2,1,0:T(8,128)(2,1)} %get-tuple-element.36), channel_id=1, source_target_pairs={{0,8},{8,16},{16,24},{24,32},{32,40},{40,48},{48,56},{56,64},{64,7... | collective-permute-start | bytes 1179656 | tf_op jit(solution)/shard_map/ppermute | solution.py:313
  55.5 5.1 %collective-permute-start.11 = (f32[3,32,256]{2,1,0:T(8,128)S(1)}, f32[3,32,256]{2,1,0:T(8,128)S(1)}, u32[]{:S(2)}, u32[]{:S(2)}) collective-permute-start(f32[3,32,256]{2,1,0:T(8,128)S(1)} %get-tuple-element.33.a), channel_id=1, source_target_pairs={{0,6},{2,0},{4,2},{6,4},{1,7},{3,1},{5,3},{7,5},{8,14},{10,8},{12,... | collective-permute-start | bytes 294920 | tf_op jit(solution)/shard_map/ppermute | solution.py:317
  55.7 6.7 %collective-permute-start.10 = (f32[3,32,256]{2,1,0:T(8,128)S(1)}, f32[3,32,256]{2,1,0:T(8,128)S(1)}, u32[]{:S(2)}, u32[]{:S(2)}) collective-permute-start(f32[3,32,256]{2,1,0:T(8,128)S(1)} %get-tuple-element.33.a), channel_id=1, source_target_pairs={{0,4},{2,6},{4,0},{6,2},{1,5},{3,7},{5,1},{7,3},{8,12},{10,14},{12... | collective-permute-start | bytes 294920 | tf_op jit(solution)/shard_map/ppermute | solution.py:317
  60.4 5.1 %collective-permute-start.9 = (f32[3,32,256]{2,1,0:T(8,128)S(1)}, f32[3,32,256]{2,1,0:T(8,128)S(1)}, u32[]{:S(2)}, u32[]{:S(2)}) collective-permute-start(f32[3,32,256]{2,1,0:T(8,128)S(1)} %get-tuple-element.33.a), channel_id=1, source_target_pairs={{0,2},{2,4},{4,6},{6,0},{1,3},{3,5},{5,7},{7,1},{8,10},{10,12},{12... | collective-permute-start | bytes 294920 | tf_op jit(solution)/shard_map/ppermute | solution.py:317
  65.5 3.5 %collective-permute-start.15 = (f32[3,32,256]{2,1,0:T(8,128)S(1)}, f32[3,32,256]{2,1,0:T(8,128)S(1)}, u32[]{:S(2)}, u32[]{:S(2)}) collective-permute-start(f32[3,32,256]{2,1,0:T(8,128)S(1)} %y_sum.2.a), channel_id=1, source_target_pairs={{0,24},{8,0},{16,8},{24,16},{1,25},{9,1},{17,9},{25,17},{2,26},{10... | collective-permute-start | bytes 294920 | tf_op jit(solution)/shard_map/ppermute | solution.py:317
  65.6 5.1 %collective-permute-start.14 = (f32[3,32,256]{2,1,0:T(8,128)S(1)}, f32[3,32,256]{2,1,0:T(8,128)S(1)}, u32[]{:S(2)}, u32[]{:S(2)}) collective-permute-start(f32[3,32,256]{2,1,0:T(8,128)S(1)} %y_sum.2.a), channel_id=1, source_target_pairs={{0,16},{8,24},{16,0},{24,8},{1,17},{9,25},{17,1},{25,9},{2,18},{10... | collective-permute-start | bytes 294920 | tf_op jit(solution)/shard_map/ppermute | solution.py:317
  67.6 4.7 %collective-permute-start.13 = (f32[3,32,256]{2,1,0:T(8,128)S(1)}, f32[3,32,256]{2,1,0:T(8,128)S(1)}, u32[]{:S(2)}, u32[]{:S(2)}) collective-permute-start(f32[3,32,256]{2,1,0:T(8,128)S(1)} %y_sum.2.a), channel_id=1, source_target_pairs={{0,8},{8,16},{16,24},{24,0},{1,9},{9,17},{17,25},{25,1},{2,10},{10... | collective-permute-start | bytes 294920 | tf_op jit(solution)/shard_map/ppermute | solution.py:317
  72.2 1.4 copy-start.2
  73.6 27.1 %copy-start.5 = (bf16[2,512,512]{2,1,0:T(8,128)(2,1)S(1)}, bf16[2,512,512]{2,1,0:T(8,128)(2,1)}, u32[]{:S(2)}) copy-start(bf16[2,512,512]{2,1,0:T(8,128)(2,1)} %constant.20.clone.rest_6_) | copy-start | bytes 3145732
  74.9 8.5 %collective-permute-start.17 = (bf16[2,256,384]{2,1,0:T(8,128)(2,1)S(1)}, bf16[2,256,384]{2,1,0:T(8,128)(2,1)S(1)}, u32[]{:S(2)}, u32[]{:S(2)}) collective-permute-start(bf16[2,256,384]{2,1,0:T(8,128)(2,1)S(1)} %get-tuple-element.39), channel_id=1, source_target_pairs={{8,0},{16,8},{24,16},{32,24},{40,32},{48,40},{56,48},{64,56},{72,6... | collective-permute-start | bytes 1179656 | tf_op jit(solution)/shard_map/ppermute | solution.py:313
  83.4 15.6 %collective-permute-start.19 = (bf16[2,256,256]{2,1,0:T(8,128)(2,1)S(1)}, bf16[2,256,256]{2,1,0:T(8,128)(2,1)S(1)}, u32[]{:S(2)}, u32[]{:S(2)}) collective-permute-start(bf16[2,256,256]{2,1,0:T(8,128)(2,1)S(1)} %slice.74), channel_id=1, source_target_pairs={{1,0},{2,1},{3,2},{4,3},{5,4},{6,5},{7,6},{9,8},{10,9},{11,10},{12... | collective-permute-start | bytes 786440 | tf_op jit(solution)/shard_map/ppermute | solution.py:313
  90.3 10.5 %collective-permute-start.18 = (bf16[2,512,256]{2,1,0:T(8,128)(2,1)S(1)}, bf16[2,512,256]{2,1,0:T(8,128)(2,1)S(1)}, u32[]{:S(2)}, u32[]{:S(2)}) collective-permute-start(bf16[2,512,256]{2,1,0:T(8,128)(2,1)S(1)} %get-tuple-element.40), channel_id=1, source_target_pairs={{1,0},{2,1},{3,2},{4,3},{5,4},{6,5},{7,6},{9,8},{10,9},{11,10},{12... | collective-permute-start | bytes 1572872 | tf_op jit(solution)/shard_map/ppermute | solution.py:313
  92.2 3.6 %collective-permute-start.22 = (f32[2,32,256]{2,1,0:T(8,128)S(1)}, f32[2,32,256]{2,1,0:T(8,128)S(1)}, u32[]{:S(2)}, u32[]{:S(2)}) collective-permute-start(f32[2,32,256]{2,1,0:T(8,128)S(1)} %get-tuple-element.41.a.mine), channel_id=1, source_target_pairs={{0,96},{32,0},{64,32},{96,64},{1,97},{33,1},{65,33},{97,65},{2,98}... | collective-permute-start | bytes 196616 | tf_op jit(solution)/shard_map/ppermute | solution.py:317
  92.6 4.8 %collective-permute-start.21 = (f32[2,32,256]{2,1,0:T(8,128)S(1)}, f32[2,32,256]{2,1,0:T(8,128)S(1)}, u32[]{:S(2)}, u32[]{:S(2)}) collective-permute-start(f32[2,32,256]{2,1,0:T(8,128)S(1)} %get-tuple-element.41.a.mine), channel_id=1, source_target_pairs={{0,64},{32,96},{64,0},{96,32},{1,65},{33,97},{65,1},{97,33},{2,66}... | collective-permute-start | bytes 196616 | tf_op jit(solution)/shard_map/ppermute | solution.py:317
  94.1 4.9 %collective-permute-start.20 = (f32[2,32,256]{2,1,0:T(8,128)S(1)}, f32[2,32,256]{2,1,0:T(8,128)S(1)}, u32[]{:S(2)}, u32[]{:S(2)}) collective-permute-start(f32[2,32,256]{2,1,0:T(8,128)S(1)} %get-tuple-element.41.a.mine), channel_id=1, source_target_pairs={{0,32},{32,64},{64,96},{96,0},{1,33},{33,65},{65,97},{97,1},{2,34}... | collective-permute-start | bytes 196616 | tf_op jit(solution)/shard_map/ppermute | solution.py:317
  99.0 1.7 %collective-permute-start.23 = (f32[4,2,32,256]{3,2,1,0:T(8,128)S(1)}, f32[4,2,32,256]{3,2,1,0:T(8,128)S(1)}, u32[]{:S(2)}, u32[]{:S(2)}) collective-permute-start(f32[4,2,32,256]{3,2,1,0:T(8,128)S(1)} %half_probe.2.rest_3_), channel_id=1, source_target_pairs={{0,1},{1,0},{2,3},{3,2},{4,5},{5,4},{6,7},{7,6},{8,9},{9,8},{10,11... | collective-permute-start | bytes 786440 | tf_op jit(solution)/shard_map/ppermute | solution.py:321
  106.5 6.8 %collective-permute-start.25 = (f32[4,3,32,256]{3,2,1,0:T(8,128)S(1)}, f32[4,3,32,256]{3,2,1,0:T(8,128)S(1)}, u32[]{:S(2)}, u32[]{:S(2)}) collective-permute-start(f32[4,3,32,256]{3,2,1,0:T(8,128)S(1)} %get-tuple-element.45), channel_id=1, source_target_pairs={{0,1},{1,0},{2,3},{3,2},{4,5},{5,4},{6,7},{7,6},{8,9},{9,8},{10,11... | collective-permute-start | bytes 1179656 | tf_op jit(solution)/shard_map/ppermute | solution.py:321
  106.8 17.1 %collective-permute-start.29 = (bf16[2,256,256]{2,1,0:T(8,128)(2,1)S(1)}, bf16[2,256,256]{2,1,0:T(8,128)(2,1)S(1)}, u32[]{:S(2)}, u32[]{:S(2)}) collective-permute-start(bf16[2,256,256]{2,1,0:T(8,128)(2,1)S(1)} %get-tuple-element.48), channel_id=1, source_target_pairs={{0,1},{1,2},{2,3},{3,4},{4,5},{5,6},{6,7},{8,9},{9,10},{10,11},{11... | collective-permute-start | bytes 786440 | tf_op jit(solution)/shard_map/ppermute | solution.py:313
  111.4 22.5 %collective-permute-start.24 = (bf16[2,512,256]{2,1,0:T(8,128)(2,1)S(1)}, bf16[2,512,256]{2,1,0:T(8,128)(2,1)S(1)}, u32[]{:S(2)}, u32[]{:S(2)}) collective-permute-start(bf16[2,512,256]{2,1,0:T(8,128)(2,1)S(1)} %get-tuple-element.43), channel_id=1, source_target_pairs={{0,1},{1,2},{2,3},{3,4},{4,5},{5,6},{6,7},{8,9},{9,10},{10,11},{11... | collective-permute-start | bytes 1572872 | tf_op jit(solution)/shard_map/ppermute | solution.py:313
  113.4 10.5 %collective-permute-start.28 = (f32[3,32,256]{2,1,0:T(8,128)S(1)}, f32[3,32,256]{2,1,0:T(8,128)S(1)}, u32[]{:S(2)}, u32[]{:S(2)}) collective-permute-start(f32[3,32,256]{2,1,0:T(8,128)S(1)} %get-tuple-element.54), channel_id=1, source_target_pairs={{0,96},{32,0},{64,32},{96,64},{1,97},{33,1},{65,33},{97,65},{2,98}... | collective-permute-start | bytes 294920 | tf_op jit(solution)/shard_map/ppermute | solution.py:317
  117.2 9.1 %collective-permute-start.27 = (f32[3,32,256]{2,1,0:T(8,128)S(1)}, f32[3,32,256]{2,1,0:T(8,128)S(1)}, u32[]{:S(2)}, u32[]{:S(2)}) collective-permute-start(f32[3,32,256]{2,1,0:T(8,128)S(1)} %get-tuple-element.55), channel_id=1, source_target_pairs={{0,64},{32,96},{64,0},{96,32},{1,65},{33,97},{65,1},{97,33},{2,66}... | collective-permute-start | bytes 294920 | tf_op jit(solution)/shard_map/ppermute | solution.py:317
  123.1 5.3 %collective-permute-start.26 = (f32[3,32,256]{2,1,0:T(8,128)S(1)}, f32[3,32,256]{2,1,0:T(8,128)S(1)}, u32[]{:S(2)}, u32[]{:S(2)}) collective-permute-start(f32[3,32,256]{2,1,0:T(8,128)S(1)} %get-tuple-element.56), channel_id=1, source_target_pairs={{0,32},{32,64},{64,96},{96,0},{1,33},{33,65},{65,97},{97,1},{2,34}... | collective-permute-start | bytes 294920 | tf_op jit(solution)/shard_map/ppermute | solution.py:317
  128.5 18.4 %collective-permute-start.30 = (bf16[2,256,384]{2,1,0:T(8,128)(2,1)S(1)}, bf16[2,256,384]{2,1,0:T(8,128)(2,1)S(1)}, u32[]{:S(2)}, u32[]{:S(2)}) collective-permute-start(bf16[2,256,384]{2,1,0:T(8,128)(2,1)S(1)} %get-tuple-element.49), channel_id=1, source_target_pairs={{0,8},{8,16},{16,24},{24,32},{32,40},{40,48},{48,56},{56,64},{64,7... | collective-permute-start | bytes 1179656 | tf_op jit(solution)/shard_map/ppermute | solution.py:313
  129.8 4.1 %collective-permute-start.33 = (f32[3,32,256]{2,1,0:T(8,128)S(1)}, f32[3,32,256]{2,1,0:T(8,128)S(1)}, u32[]{:S(2)}, u32[]{:S(2)}) collective-permute-start(f32[3,32,256]{2,1,0:T(8,128)S(1)} %get-tuple-element.52.a), channel_id=1, source_target_pairs={{0,6},{2,0},{4,2},{6,4},{1,7},{3,1},{5,3},{7,5},{8,14},{10,8},{12,... | collective-permute-start | bytes 294920 | tf_op jit(solution)/shard_map/ppermute | solution.py:317
  129.9 5.3 %collective-permute-start.32 = (f32[3,32,256]{2,1,0:T(8,128)S(1)}, f32[3,32,256]{2,1,0:T(8,128)S(1)}, u32[]{:S(2)}, u32[]{:S(2)}) collective-permute-start(f32[3,32,256]{2,1,0:T(8,128)S(1)} %get-tuple-element.52.a), channel_id=1, source_target_pairs={{0,4},{2,6},{4,0},{6,2},{1,5},{3,7},{5,1},{7,3},{8,12},{10,14},{12... | collective-permute-start | bytes 294920 | tf_op jit(solution)/shard_map/ppermute | solution.py:317
  133.1 5.8 %collective-permute-start.31 = (f32[3,32,256]{2,1,0:T(8,128)S(1)}, f32[3,32,256]{2,1,0:T(8,128)S(1)}, u32[]{:S(2)}, u32[]{:S(2)}) collective-permute-start(f32[3,32,256]{2,1,0:T(8,128)S(1)} %get-tuple-element.52.a), channel_id=1, source_target_pairs={{0,2},{2,4},{4,6},{6,0},{1,3},{3,5},{5,7},{7,1},{8,10},{10,12},{12... | collective-permute-start | bytes 294920 | tf_op jit(solution)/shard_map/ppermute | solution.py:317
  138.9 4.5 %collective-permute-start.36 = (f32[3,32,256]{2,1,0:T(8,128)S(1)}, f32[3,32,256]{2,1,0:T(8,128)S(1)}, u32[]{:S(2)}, u32[]{:S(2)}) collective-permute-start(f32[3,32,256]{2,1,0:T(8,128)S(1)} %y_sum.3.a), channel_id=1, source_target_pairs={{0,24},{8,0},{16,8},{24,16},{1,25},{9,1},{17,9},{25,17},{2,26},{10... | collective-permute-start | bytes 294920 | tf_op jit(solution)/shard_map/ppermute | solution.py:317
  140.8 5.0 %collective-permute-start.35 = (f32[3,32,256]{2,1,0:T(8,128)S(1)}, f32[3,32,256]{2,1,0:T(8,128)S(1)}, u32[]{:S(2)}, u32[]{:S(2)}) collective-permute-start(f32[3,32,256]{2,1,0:T(8,128)S(1)} %y_sum.3.a), channel_id=1, source_target_pairs={{0,16},{8,24},{16,0},{24,8},{1,17},{9,25},{17,1},{25,9},{2,18},{10... | collective-permute-start | bytes 294920 | tf_op jit(solution)/shard_map/ppermute | solution.py:317
  142.2 4.7 %collective-permute-start.34 = (f32[3,32,256]{2,1,0:T(8,128)S(1)}, f32[3,32,256]{2,1,0:T(8,128)S(1)}, u32[]{:S(2)}, u32[]{:S(2)}) collective-permute-start(f32[3,32,256]{2,1,0:T(8,128)S(1)} %y_sum.3.a), channel_id=1, source_target_pairs={{0,8},{8,16},{16,24},{24,0},{1,9},{9,17},{17,25},{25,1},{2,10},{10... | collective-permute-start | bytes 294920 | tf_op jit(solution)/shard_map/ppermute | solution.py:317
  146.9 5.8 %collective-permute-start.39 = (f32[2,32,256]{2,1,0:T(8,128)S(1)}, f32[2,32,256]{2,1,0:T(8,128)S(1)}, u32[]{:S(2)}, u32[]{:S(2)}) collective-permute-start(f32[2,32,256]{2,1,0:T(8,128)S(1)} %z_sum.1.a), channel_id=1, source_target_pairs={{0,96},{32,0},{64,32},{96,64},{1,97},{33,1},{65,33},{97,65},{2,98}... | collective-permute-start | bytes 196616 | tf_op jit(solution)/shard_map/ppermute | solution.py:317
  147.5 5.1 %collective-permute-start.38 = (f32[2,32,256]{2,1,0:T(8,128)S(1)}, f32[2,32,256]{2,1,0:T(8,128)S(1)}, u32[]{:S(2)}, u32[]{:S(2)}) collective-permute-start(f32[2,32,256]{2,1,0:T(8,128)S(1)} %z_sum.1.a), channel_id=1, source_target_pairs={{0,64},{32,96},{64,0},{96,32},{1,65},{33,97},{65,1},{97,33},{2,66}... | collective-permute-start | bytes 196616 | tf_op jit(solution)/shard_map/ppermute | solution.py:317
  149.6 4.3 %collective-permute-start.37 = (f32[2,32,256]{2,1,0:T(8,128)S(1)}, f32[2,32,256]{2,1,0:T(8,128)S(1)}, u32[]{:S(2)}, u32[]{:S(2)}) collective-permute-start(f32[2,32,256]{2,1,0:T(8,128)S(1)} %z_sum.1.a), channel_id=1, source_target_pairs={{0,32},{32,64},{64,96},{96,0},{1,33},{33,65},{65,97},{97,1},{2,34}... | collective-permute-start | bytes 196616 | tf_op jit(solution)/shard_map/ppermute | solution.py:317
  154.0 6.9 %collective-permute-start.40 = (f32[4,2,32,256]{3,2,1,0:T(8,128)S(1)}, f32[4,2,32,256]{3,2,1,0:T(8,128)S(1)}, u32[]{:S(2)}, u32[]{:S(2)}) collective-permute-start(f32[4,2,32,256]{3,2,1,0:T(8,128)S(1)} %half_probe.3.mine), channel_id=1, source_target_pairs={{0,1},{1,0},{2,3},{3,2},{4,5},{5,4},{6,7},{7,6},{8,9},{9,8},{10,11... | collective-permute-start | bytes 786440 | tf_op jit(solution)/shard_map/ppermute | solution.py:321

commit v8 on v7

--- a/solution.py
+++ b/solution.py
@@ -33,13 +33,14 @@
 
 
 def frames_kernel(
-    iteration, n_low, n_pieces,
+    middle, iteration, n_low, n_pieces,
     place, counts, pos, obj, *rest,
 ):
     lows, (right, corner), rest = rest[:n_low], rest[n_low : n_low + 2], rest[n_low + 2 :]
     pieces, (amps, tables), rest = rest[:n_pieces], rest[n_pieces : n_pieces + 2], rest[n_pieces + 2 :]
-    own_out, low_left, low_right, right_out, corner_out, keep_out, send_out, step_out = rest[:8]
-    ext, acc, sums, wave, mis, patch, levels, arrived, here, *rest = rest[8:]
+    n_grads = 3 if middle else 5
+    grads_out, (keep_out, send_out, step_out) = rest[:n_grads], rest[n_grads : n_grads + 3]
+    ext, acc, sums, wave, mis, patch, levels, arrived, here, *rest = rest[n_grads + 3 :]
     landing, probe_scratch = rest[: 5 + n_pieces], rest[5 + n_pieces :]
     count = counts[0]
     low_parts, at = [], 0
@@ -174,14 +175,26 @@
 
         lax.fori_loop(0, times, several, 0)
         done = done + times * group
-    for j in range(all_tiles):
-        inside = j < inner_tiles
-        at = (j if inside else j - inner_tiles) * LANES
-        upper = own_out if inside else right_out
-        upper[:, :, at : at + LANES] = acc[:, j, :rows, :].astype(upper.dtype)
-        lower = (low_left if j < left_tiles else low_right) if inside else corner_out
-        at = at if j < left_tiles or not inside else at - size
-        lower[:, :, at : at + LANES] = acc[:, j, rows:, :].astype(lower.dtype)
+    if middle:
+        all_out, to_right, to_left = grads_out
+        for j in range(all_tiles):
+            at = j * LANES
+            all_out[:, :, at : at + LANES] = acc[:, j]
+            if j < left_tiles:
+                to_left[:, :, at : at + LANES] = acc[:, j].astype(BF)
+            if j >= inner_tiles:
+                at = at - cols
+                to_right[:, :, at : at + LANES] = acc[:, j].astype(BF)
+    else:
+        own_out, low_left, low_right, right_out, corner_out = grads_out
+        for j in range(all_tiles):
+            inside = j < inner_tiles
+            at = (j if inside else j - inner_tiles) * LANES
+            upper = own_out if inside else right_out
+            upper[:, :, at : at + LANES] = acc[:, j, :rows, :].astype(upper.dtype)
+            lower = (low_left if j < left_tiles else low_right) if inside else corner_out
+            at = at if j < left_tiles or not inside else at - size
+            lower[:, :, at : at + LANES] = acc[:, j, rows:, :].astype(lower.dtype)
     for j in range(N_X):
         inner = lax.rem(x + j, N_X) * quarter
         keep_at = pl.multiple_of(core * half + inner, quarter)
@@ -190,18 +203,27 @@
         send_out[j] = sums[:, pl.ds(send_at, quarter), :]
 
 
-def run_frames(place, counts, pos, obj, halos, pieces, amps, tables, iteration):
+def run_frames(place, counts, pos, obj, halos, pieces, amps, tables, iteration, middle):
     rows, cols = obj.shape[1], obj.shape[2]
     slots, size = amps.shape[1], amps.shape[2]
     vmem = pl.BlockSpec(memory_space=pltpu.VMEM)
     smem = pl.BlockSpec(memory_space=pltpu.SMEM)
     quarter = size // (N_CORE * N_X)
-    shapes = [
-        jax.ShapeDtypeStruct((2, rows, cols), F32),
-        jax.ShapeDtypeStruct((2, size, size), F32),
-        jax.ShapeDtypeStruct((2, size, cols - size), BF),
-        jax.ShapeDtypeStruct((2, rows, size), BF),
-        jax.ShapeDtypeStruct((2, size, size), BF),
+    if middle:
+        shapes = [
+            jax.ShapeDtypeStruct((2, rows + size, cols + size), F32),
+            jax.ShapeDtypeStruct((2, rows + size, size), BF),
+            jax.ShapeDtypeStruct((2, rows + size, size), BF),
+        ]
+    else:
+        shapes = [
+            jax.ShapeDtypeStruct((2, rows, cols), F32),
+            jax.ShapeDtypeStruct((2, size, size), F32),
+            jax.ShapeDtypeStruct((2, size, cols - size), BF),
+            jax.ShapeDtypeStruct((2, rows, size), BF),
+            jax.ShapeDtypeStruct((2, size, size), BF),
+        ]
+    shapes += [
         jax.ShapeDtypeStruct((N_X, 3, quarter, size), F32),
         jax.ShapeDtypeStruct((N_X, 3, quarter, size), F32),
         jax.ShapeDtypeStruct((1, 1), F32),
@@ -223,10 +245,10 @@
     if len(pieces) > 1:
         scratch.append(pltpu.VMEM((2, size, size), F32))
     return pl.pallas_call(
-        functools.partial(frames_kernel, iteration, len(lows), len(pieces)),
+        functools.partial(frames_kernel, middle, iteration, len(lows), len(pieces)),
         out_shape=shapes,
         in_specs=[smem] * 3 + [pl.BlockSpec(memory_space=pltpu.HBM)] * (5 + len(lows) + len(pieces)),
-        out_specs=[vmem] * 7 + [smem],
+        out_specs=[vmem] * (len(shapes) - 1) + [smem],
         scratch_shapes=scratch,
         compiler_params=pltpu.CompilerParams(vmem_limit_bytes=44 << 20),
         cost_estimate=pl.CostEstimate(flops=6_000_000_000, bytes_accessed=8_000_000, transcendentals=0),
@@ -290,12 +312,50 @@
         rest[-1][j] = chunk[...]
 
 
-def both_kernel(a, b, c, d, mine, obj, own, left, down, step, fresh, obj_out, below, right):
-    probe_step(a, b, c, d, mine, fresh)
-    object_step(obj, own, left, down, step, obj_out)
-    size = left.shape[2]
-    below[...] = obj_out[:, :size, :].astype(BF)
-    right[...] = obj_out[:, :, :size].astype(BF)
+def sum_kernel(a, b, c, d, *rest):
+    total = rest[-1]
+    total[...] = a[...].reshape(total.shape) + b[...] + c[...] + d[...]
+
+
+def rim_kernel(a, b, c, d, grads, from_left, from_right, total, down, up):
+    sum_kernel(a, b, c, d, total)
+    size = down.shape[1]
+    cols = grads.shape[2] - size
+    rows = grads.shape[1] - size
+    for out, span in ((down, slice(rows, rows + size)), (up, slice(0, size))):
+        out[:, :, :size] = (grads[:, span, :size] + from_left[:, span].astype(F32)).astype(BF)
+        out[:, :, size:cols] = grads[:, span, size:cols].astype(BF)
+        out[:, :, cols:] = (grads[:, span, cols:] + from_right[:, span].astype(F32)).astype(BF)
+
+
+def wide_kernel(
+    obj, low_left, low_right, right, corner, grads, from_left, from_right, above, under, step,
+    obj_out, below_out, right_out, corner_out,
+):
+    size = corner.shape[1]
+    rows, cols = obj.shape[1], obj.shape[2]
+    alpha = step[0, 0]
+    for r in (slice(0, size), slice(size, rows), slice(rows, rows + size)):
+        for c in (slice(0, size), slice(size, cols), slice(cols, cols + size)):
+            outside_r, outside_c = r.start == rows, c.start == cols
+            total = grads[:, r, c]
+            if c.start == 0:
+                total = total + from_left[:, r].astype(F32)
+            if outside_c:
+                total = total + from_right[:, r].astype(F32)
+            if r.start == 0:
+                total = total + above[:, :, c].astype(F32)
+            if outside_r:
+                total = total + under[:, :, c].astype(F32)
+            if outside_r and outside_c:
+                corner_out[...] = (corner[...].astype(F32) - alpha * total).astype(BF)
+            elif outside_r:
+                low = low_left if c.start == 0 else low_right
+                below_out[:, :, c] = (low[...].astype(F32) - alpha * total).astype(BF)
+            elif outside_c:
+                right_out[:, r, :] = (right[:, r, :].astype(F32) - alpha * total).astype(BF)
+            else:
+                obj_out[:, r, c] = obj[:, r, c] - alpha * total
 
 
 def probe_kernel(place, mine, other, out):
@@ -352,26 +412,43 @@
     row = jax.ShapeDtypeStruct((8, LANES), F32)
     half_probe = jax.ShapeDtypeStruct((N_X, *mine.shape), F32)
     halos = halo(lows, right)
+    square = jax.ShapeDtypeStruct((2, size, size), BF)
+    wide = jax.ShapeDtypeStruct((2, size, cols + size), BF)
     for iteration in range(ITERS):
-        own, low_left, low_right, right, corner, keep, send, step = run_frames(
-            place, counts[iteration, 0], positions[iteration], obj, halos, pieces, amps, tables, iteration
+        middle = iteration < ITERS - 1
+        *grads, keep, send, step = run_frames(
+            place, counts[iteration, 0], positions[iteration], obj, halos, pieces, amps, tables, iteration, middle
         )
-        corner = moved(corner, COL, N_COL, 1)
-        left = moved(right, COL, N_COL, 1)
+        if middle:
+            grads, to_right, to_left = grads
+            from_left, from_right = moved(to_right, COL, N_COL, 1), moved(to_left, COL, N_COL, -1)
+        else:
+            own, low_left, low_right, right, corner = grads
+            corner = moved(corner, COL, N_COL, 1)
+            left = moved(right, COL, N_COL, 1)
         sums = keep + swapped(send)
         sums = [sums[:1]] + [turned(sums[j], "x", j) for j in (1, 2, 3)]
-        total, down = small_call(x_kernel, [share, flat], ([*sums, low_left, low_right, corner], []), "x_sum")
-        down = moved(down, ROW, N_ROW, 1)
-        (total,) = small_call(y_kernel, [share], (around(total, "y"), [left]), "y_sum")
-        sums = around(total, "z") + [mine]
-        if iteration < ITERS - 1:
-            mine, obj, below, right = small_call(
-                both_kernel, [part, whole, flat, tall], ([*sums, obj, own, left, down, step], []), "z_sum_object"
+        if middle:
+            (total,) = small_call(sum_kernel, [share], (sums, []), "x_sum")
+            total, down, up = small_call(
+                rim_kernel, [share, wide, wide], ([*around(total, "z"), grads, from_left, from_right], []), "z_sum_rims"
             )
-            halos = halo([below], right)
-            waited = [halos[2]]
+            above, under = moved(down, ROW, N_ROW, 1), moved(up, ROW, N_ROW, -1)
+            (mine,) = small_call(probe_step, [part], ([*around(total, "y"), mine], []), "y_sum")
+            lows, right, corner = halos
+            obj, below, right, corner = small_call(
+                wide_kernel,
+                [whole, flat, tall, square],
+                ([obj, *lows, right, corner, grads, from_left, from_right, above, under, step], []),
+                "wide_update",
+                24,
+            )
+            halos, waited = ((below,), right, corner), [above, under]
         else:
-            (mine,) = small_call(z_kernel, [part], (sums, [down]), "z_sum")
+            total, down = small_call(x_kernel, [share, flat], ([*sums, low_left, low_right, corner], []), "x_sum")
+            down = moved(down, ROW, N_ROW, 1)
+            (total,) = small_call(y_kernel, [share], (around(total, "y"), [left]), "y_sum")
+            (mine,) = small_call(z_kernel, [part], ([*around(total, "z"), mine], [down]), "z_sum")
             obj, done = small_call(last_kernel, [whole, row], ([obj, own, left, down, step], []), "object_update")
             waited = [done]
         (stack,) = small_call(stack_kernel, [half_probe], (around(mine, "x"), waited), "half_probe")

time: 163 us -> 161 us (0.988)
  waiting for transfers between devices: 54.4 us -> 36 us
  local copies, waits for them, and re-layouts: 4.19 us -> 11.4 us
  Pallas kernels: 17.6 us -> 22.8 us
  starting transfers between devices: 83.3 us -> 87 us
    ppermute x24, waiting for transfers between devices: 36.7 us -> 25.8 us  [turned(): return lax.ppermute(value, axis, [(s, (s + steps) % 4) for s in range(4)])]
    ppermute x24, starting transfers between devices: 37.9 us -> 47.9 us  [turned(): return lax.ppermute(value, axis, [(s, (s + steps) % 4) for s in range(4)])]
    ppermute x13 -> x11, waiting for transfers between devices: 16.6 us -> 9.03 us  [moved(): lax.ppermute(value, axis, [(s, s + steps) for s in range(first, last)])]
    ppermute x13 -> x11, starting transfers between devices: 38.7 us -> 31.8 us  [moved(): lax.ppermute(value, axis, [(s, s + steps) for s in range(first, last)])]
    unnamed x16 -> x30, local copies, waits for them, and re-layouts: 2.66 us -> 9 us
    pallas_call x2, Pallas kernels: 11.6 us -> 14.9 us  [run_frames(): pl.pallas_call(functools.partial(frames_kernel, middle, iteration, len(lo...]
    pallas_call x10 -> x11, Pallas kernels: 5.95 us -> 7.9 us  [small_call(): pl.pallas_call(body, out_shape=shapes, in_specs=[spec(space) for space in...]
  transfers between devices with their start and end apart: 41 -> 39, of which waited for: 25 -> 21; matrix products, arithmetic and copies ran while one was open for 1% -> 2% of each run, Pallas kernels for 2% -> 3%
where the time goes in v8:
time: 161 us; the launch traced here: 160 us
  starting transfers between devices  87 us (54%)
  waiting for transfers between devices  36 us (22%)
  Pallas kernels  22.8 us (14%)
  local copies, waits for them, and re-layouts  11.4 us (7%)
  other arithmetic  1.82 us (1%)
    ppermute x24, starting transfers between devices, turned(): return lax.ppermute(value, axis, [(s, (s + steps) % 4) for s in range(4)])  47.9 us
    ppermute x11, starting transfers between devices, moved(): lax.ppermute(value, axis, [(s, s + steps) for s in range(first, last)])  31.8 us
    ppermute x24, waiting for transfers between devices, turned(): return lax.ppermute(value, axis, [(s, (s + steps) % 4) for s in range(4)])  25.8 us
    pallas_call x2, Pallas kernels, run_frames(): pl.pallas_call(functools.partial(frames_kernel, middle, iteration, len(lo...  14.9 us
    ppermute x11, waiting for transfers between devices, moved(): lax.ppermute(value, axis, [(s, s + steps) for s in range(first, last)])  9.03 us
    unnamed x30, local copies, waits for them, and re-layouts  9 us
    pallas_call x11, Pallas kernels, small_call(): pl.pallas_call(body, out_shape=shapes, in_specs=[spec(space) for space in...  7.9 us
    ppermute x4, starting transfers between devices, swapped(): return lax.ppermute(value, 'core', [(0, 1), (1, 0)])  7.32 us
  transfers between devices with their start and end apart: 39, of which 21 were waited for; matrix products, arithmetic and copies ran while one was open for 2% of the time, Pallas kernels for 3%

profile of v8, /device:TPU:1, one launch (start us, length us, event | category | flops | bytes accessed | tf_op | source)
XLA Modules:
  0.0 160.0 jit_solution(302738612157436903)
XLA Ops:
  0.7 1.6 %convert.5 = bf16[2,512,384]{2,1,0:T(8,128)(2,1)S(1)} convert(f32[2,512,384]{2,1,0:T(8,128)} %obj.3) | non-fusion elementwise | flops 393216 | bytes 2359296 | tf_op jit(solution)/shard_map/convert.2
  2.3 1.3 collective-permute-start
  3.6 0.8 slice.65
  4.5 3.3 %collective-permute-start.2 = (bf16[2,512,256]{2,1,0:T(8,128)(2,1)}, bf16[2,512,256]{2,1,0:T(8,128)(2,1)S(1)}, u32[]{:S(2)}, u32[]{:S(2)}) collective-permute-start(bf16[2,512,256]{2,1,0:T(8,128)(2,1)} %slice.65), channel_id=1, source_target_pairs={{1,0},{2,1},{3,2},{4,3},{5,4},{6,5},{7,6},{9,8},{10,9},{11,10},{12... | collective-permute-start | bytes 1572872 | tf_op jit(solution)/shard_map/ppermute | solution.py:373
  7.8 1.3 collective-permute-start.1
  9.1 3.6 %collective-permute-done.rest_0_.low_left = bf16[2,256,256]{2,1,0:T(8,128)(2,1)S(1)} collective-permute-done((bf16[2,256,256]{2,1,0:T(8,128)(2,1)S(1)}, bf16[2,256,256]{2,1,0:T(8,128)(2,1)S(1)}, u32[]{:S(2)}, u32[]{:S(2)}) %collective-permute-start) | collective-permute-done | bytes 262176 | tf_op jit(solution)/shard_map/ppermute | solution.py:373
  12.7 3.3 %collective-permute-start.3 = (bf16[2,256,256]{2,1,0:T(8,128)(2,1)S(1)}, bf16[2,256,256]{2,1,0:T(8,128)(2,1)S(1)}, u32[]{:S(2)}, u32[]{:S(2)}) collective-permute-start(bf16[2,256,256]{2,1,0:T(8,128)(2,1)S(1)} %collective-permute-done.rest_0_.low_left), channel_id=1, source_target_pairs={{1,0},{2,1},{3,2},{4,3},{5,4},{6,5},{7,6},{9,8},{10,9},{11,10},{12... | collective-permute-start | bytes 786440 | tf_op jit(solution)/shard_map/ppermute | solution.py:373
  16.2 0.6 fusion
  16.8 4.4 %collective-permute-done.3.rest_3_.corner = bf16[2,256,256]{2,1,0:T(8,128)(2,1)S(1)} collective-permute-done((bf16[2,256,256]{2,1,0:T(8,128)(2,1)S(1)}, bf16[2,256,256]{2,1,0:T(8,128)(2,1)S(1)}, u32[]{:S(2)}, u32[]{:S(2)}) %collective-permute-start.3) | collective-permute-done | bytes 262176 | tf_op jit(solution)/shard_map/ppermute | solution.py:373
  21.2 2.0 %copy-done.10 = bf16[2,12,256,256]{3,2,1,0:T(8,128)(2,1)S(1)} copy-done((bf16[2,12,256,256]{3,2,1,0:T(8,128)(2,1)S(1)}, bf16[2,12,256,256]{3,2,1,0:T(8,128)(2,1)}, u32[]{:S(2)}) %copy-start.10) | copy-done | bytes 3145752
  23.2 1.2 copy-done.11
  24.4 9.3 %frames.2 = (f32[2,768,640]{2,1,0:T(8,128)}, bf16[2,768,256]{2,1,0:T(8,128)(2,1)S(1)}, bf16[2,768,256]{2,1,0:T(8,128)(2,1)S(1)}, f32[4,3,32,256]{3,2,1,0:T(8,128...) custom-call(s32[2]{0:T(128)S(1)} %pad_add_fusion.place, s32[1]{0:T(128)} %bitcast.2.counts, ...), custom_call_target="tpu_custom_call" | custom-call | flops 6000000000 | bytes 8000000 | tf_op jit(solution)/shard_map/frames/pallas_call | solution.py:247
  33.9 1.9 %collective-permute-start.4 = (bf16[2,768,256]{2,1,0:T(8,128)(2,1)S(1)}, bf16[2,768,256]{2,1,0:T(8,128)(2,1)S(1)}, u32[]{:S(2)}, u32[]{:S(2)}) collective-permute-start(bf16[2,768,256]{2,1,0:T(8,128)(2,1)S(1)} %get-tuple-element.28), channel_id=1, source_target_pairs={{0,1},{1,2},{2,3},{3,4},{4,5},{5,6},{6,7},{8,9},{9,10},{10,11},{11... | collective-permute-start | bytes 2359304 | tf_op jit(solution)/shard_map/ppermute | solution.py:373
  35.8 2.5 %collective-permute-start.5 = (bf16[2,768,256]{2,1,0:T(8,128)(2,1)S(1)}, bf16[2,768,256]{2,1,0:T(8,128)(2,1)S(1)}, u32[]{:S(2)}, u32[]{:S(2)}) collective-permute-start(bf16[2,768,256]{2,1,0:T(8,128)(2,1)S(1)} %get-tuple-element.29), channel_id=1, source_target_pairs={{1,0},{2,1},{3,2},{4,3},{5,4},{6,5},{7,6},{9,8},{10,9},{11,10},{12... | collective-permute-start | bytes 2359304 | tf_op jit(solution)/shard_map/ppermute | solution.py:373
  38.3 2.8 %collective-permute-start.7 = (f32[3,32,256]{2,1,0:T(8,128)S(1)}, f32[3,32,256]{2,1,0:T(8,128)S(1)}, u32[]{:S(2)}, u32[]{:S(2)}) collective-permute-start(f32[3,32,256]{2,1,0:T(8,128)S(1)} %get-tuple-element.58), channel_id=1, source_target_pairs={{0,32},{32,64},{64,96},{96,0},{1,33},{33,65},{65,97},{97,1},{2,34}... | collective-permute-start | bytes 294920 | tf_op jit(solution)/shard_map/ppermute | solution.py:377
  41.1 2.8 %collective-permute-start.8 = (f32[3,32,256]{2,1,0:T(8,128)S(1)}, f32[3,32,256]{2,1,0:T(8,128)S(1)}, u32[]{:S(2)}, u32[]{:S(2)}) collective-permute-start(f32[3,32,256]{2,1,0:T(8,128)S(1)} %get-tuple-element.57), channel_id=1, source_target_pairs={{0,64},{32,96},{64,0},{96,32},{1,65},{33,97},{65,1},{97,33},{2,66}... | collective-permute-start | bytes 294920 | tf_op jit(solution)/shard_map/ppermute | solution.py:377
  44.1 1.3 collective-permute-done.7.b
  45.4 3.7 %collective-permute-done.8.c = f32[3,32,256]{2,1,0:T(8,128)S(1)} collective-permute-done((f32[3,32,256]{2,1,0:T(8,128)S(1)}, f32[3,32,256]{2,1,0:T(8,128)S(1)}, u32[]{:S(2)}, u32[]{:S(2)}) %collective-permute-start.8) | collective-permute-done | bytes 98336 | tf_op jit(solution)/shard_map/ppermute | solution.py:377
  49.1 8.9 %collective-permute-start.10 = (f32[3,32,256]{2,1,0:T(8,128)S(1)}, f32[3,32,256]{2,1,0:T(8,128)S(1)}, u32[]{:S(2)}, u32[]{:S(2)}) collective-permute-start(f32[3,32,256]{2,1,0:T(8,128)S(1)} %x_sum.2.a), channel_id=1, source_target_pairs={{0,8},{8,16},{16,24},{24,0},{1,9},{9,17},{17,25},{25,1},{2,10},{10... | collective-permute-start | bytes 294920 | tf_op jit(solution)/shard_map/ppermute | solution.py:377
  58.0 0.5 collective-permute-start.11
  58.5 2.0 %collective-permute-start.12 = (f32[3,32,256]{2,1,0:T(8,128)S(1)}, f32[3,32,256]{2,1,0:T(8,128)S(1)}, u32[]{:S(2)}, u32[]{:S(2)}) collective-permute-start(f32[3,32,256]{2,1,0:T(8,128)S(1)} %x_sum.2.a), channel_id=1, source_target_pairs={{0,24},{8,0},{16,8},{24,16},{1,25},{9,1},{17,9},{25,17},{2,26},{10... | collective-permute-start | bytes 294920 | tf_op jit(solution)/shard_map/ppermute | solution.py:377
  60.5 2.5 %collective-permute-done.11.c = f32[3,32,256]{2,1,0:T(8,128)S(1)} collective-permute-done((f32[3,32,256]{2,1,0:T(8,128)S(1)}, f32[3,32,256]{2,1,0:T(8,128)S(1)}, u32[]{:S(2)}, u32[]{:S(2)}) %collective-permute-start.11) | collective-permute-done | bytes 98336 | tf_op jit(solution)/shard_map/ppermute | solution.py:377
  63.2 2.1 %copy-done = f32[2,768,640]{2,1,0:T(8,128)S(1)} copy-done((f32[2,768,640]{2,1,0:T(8,128)S(1)}, f32[2,768,640]{2,1,0:T(8,128)}, u32[]{:S(2)}) %copy-start) | copy-done | bytes 3932184
  65.3 1.2 z_sum_rims.1
  66.5 0.6 copy-done.7
  67.2 5.1 %collective-permute-start.13 = (bf16[2,256,640]{2,1,0:T(8,128)(2,1)}, bf16[2,256,640]{2,1,0:T(8,128)(2,1)}, u32[]{:S(2)}, u32[]{:S(2)}) collective-permute-start(bf16[2,256,640]{2,1,0:T(8,128)(2,1)} %get-tuple-element.32), channel_id=1, source_target_pairs={{0,8},{8,16},{16,24},{24,32},{32,40},{40,48},{48,56},{56,64},{64,7... | collective-permute-start | bytes 1966088 | tf_op jit(solution)/shard_map/ppermute | solution.py:373
  72.3 1.3 collective-permute-start.14
  74.1 2.5 %collective-permute-start.17 = (f32[3,32,256]{2,1,0:T(8,128)}, f32[3,32,256]{2,1,0:T(8,128)S(1)}, u32[]{:S(2)}, u32[]{:S(2)}) collective-permute-start(f32[3,32,256]{2,1,0:T(8,128)} %copy-done.7), channel_id=1, source_target_pairs={{0,6},{2,0},{4,2},{6,4},{1,7},{3,1},{5,3},{7,5},{8,14},{10,8},{12,... | collective-permute-start | bytes 294920 | tf_op jit(solution)/shard_map/ppermute | solution.py:377
  76.5 0.8 constant_dynamic-slice_fusion.mine
  77.4 1.6 collective-permute-done.15.b
  79.0 1.4 collective-permute-done.16.c
  80.8 0.9 copy-done.8
  81.7 1.9 %collective-permute-start.18 = (f32[2,32,256]{2,1,0:T(8,128)S(1)}, f32[2,32,256]{2,1,0:T(8,128)S(1)}, u32[]{:S(2)}, u32[]{:S(2)}) collective-permute-start(f32[2,32,256]{2,1,0:T(8,128)S(1)} %y_sum.2.a.mine), channel_id=1, source_target_pairs={{0,32},{32,64},{64,96},{96,0},{1,33},{33,65},{65,97},{97,1},{2,34}... | collective-permute-start | bytes 196616 | tf_op jit(solution)/shard_map/ppermute | solution.py:377
  83.7 3.2 %collective-permute-start.19 = (f32[2,32,256]{2,1,0:T(8,128)S(1)}, f32[2,32,256]{2,1,0:T(8,128)S(1)}, u32[]{:S(2)}, u32[]{:S(2)}) collective-permute-start(f32[2,32,256]{2,1,0:T(8,128)S(1)} %y_sum.2.a.mine), channel_id=1, source_target_pairs={{0,64},{32,96},{64,0},{96,32},{1,65},{33,97},{65,1},{97,33},{2,66}... | collective-permute-start | bytes 196616 | tf_op jit(solution)/shard_map/ppermute | solution.py:377
  87.4 1.9 %collective-permute-done.19.c = f32[2,32,256]{2,1,0:T(8,128)S(1)} collective-permute-done((f32[2,32,256]{2,1,0:T(8,128)S(1)}, f32[2,32,256]{2,1,0:T(8,128)S(1)}, u32[]{:S(2)}, u32[]{:S(2)}) %collective-permute-start.19) | collective-permute-done | bytes 65568 | tf_op jit(solution)/shard_map/ppermute | solution.py:377
  89.2 2.0 %collective-permute-done.20.d = f32[2,32,256]{2,1,0:T(8,128)S(1)} collective-permute-done((f32[2,32,256]{2,1,0:T(8,128)S(1)}, f32[2,32,256]{2,1,0:T(8,128)S(1)}, u32[]{:S(2)}, u32[]{:S(2)}) %collective-permute-start.20) | collective-permute-done | bytes 65568 | tf_op jit(solution)/shard_map/ppermute | solution.py:377
  91.2 4.1 %collective-permute-start.21 = (f32[4,2,32,256]{3,2,1,0:T(8,128)S(1)}, f32[4,2,32,256]{3,2,1,0:T(8,128)S(1)}, u32[]{:S(2)}, u32[]{:S(2)}) collective-permute-start(f32[4,2,32,256]{3,2,1,0:T(8,128)S(1)} %half_probe.2.rest_3_), channel_id=1, source_target_pairs={{0,1},{1,0},{2,3},{3,2},{4,5},{5,4},{6,7},{7,6},{8,9},{9,8},{10,11... | collective-permute-start | bytes 786440 | tf_op jit(solution)/shard_map/ppermute | solution.py:381
  95.3 2.1 %copy-done.1 = f32[2,768,640]{2,1,0:T(8,128)S(1)} copy-done((f32[2,768,640]{2,1,0:T(8,128)S(1)}, f32[2,768,640]{2,1,0:T(8,128)}, u32[]{:S(2)}) %copy-start.1) | copy-done | bytes 3932184
  97.5 2.8 %wide_update.1 = (f32[2,512,384]{2,1,0:T(8,128)S(1)}, bf16[2,256,384]{2,1,0:T(8,128)(2,1)S(1)}, bf16[2,512,256]{2,1,0:T(8,128)(2,1)S(1)}, bf16[2,256,256]{2,1,0:T(8,128)(2,1)S(1)}) custom-call(f32[2,512,384]{2,1,0:T(8,128)S(1)} %copy-done.2, bf16[2,256,256]{2,1,0:T(8,128)(2,1)S(1)} %collective-permute-done.rest_0_.low_left, ...), custom_call_target="tpu_custom_call" | custom-call | flops 2000000 | bytes 4000000 | tf_op jit(solution)/shard_map/wide_update/pallas_call | solution.py:265
  100.3 5.6 %frames.3 = (f32[2,512,384]{2,1,0:T(8,128)S(1)}, f32[2,256,256]{2,1,0:T(8,128)S(1)}, bf16[2,256,128]{2,1,0:T(8,128)(2,1)S(1)}, bf16[2,512,256]{2,1,0:T(8,128)(2,...) custom-call(s32[2]{0:T(128)S(1)} %pad_add_fusion.place, ...), custom_call_target="tpu_custom_call" | custom-call | flops 6000000000 | bytes 8000000 | tf_op jit(solution)/shard_map/frames/pallas_call | solution.py:247
  106.0 3.1 %collective-permute-start.22 = (bf16[2,512,256]{2,1,0:T(8,128)(2,1)S(1)}, bf16[2,512,256]{2,1,0:T(8,128)(2,1)S(1)}, u32[]{:S(2)}, u32[]{:S(2)}) collective-permute-start(bf16[2,512,256]{2,1,0:T(8,128)(2,1)S(1)} %get-tuple-element.41), channel_id=1, source_target_pairs={{0,1},{1,2},{2,3},{3,4},{4,5},{5,6},{6,7},{8,9},{9,10},{10,11},{11... | collective-permute-start | bytes 1572872 | tf_op jit(solution)/shard_map/ppermute | solution.py:373
  109.1 2.0 %collective-permute-start.27 = (bf16[2,256,256]{2,1,0:T(8,128)(2,1)S(1)}, bf16[2,256,256]{2,1,0:T(8,128)(2,1)S(1)}, u32[]{:S(2)}, u32[]{:S(2)}) collective-permute-start(bf16[2,256,256]{2,1,0:T(8,128)(2,1)S(1)} %get-tuple-element.46), channel_id=1, source_target_pairs={{0,1},{1,2},{2,3},{3,4},{4,5},{5,6},{6,7},{8,9},{9,10},{10,11},{11... | collective-permute-start | bytes 786440 | tf_op jit(solution)/shard_map/ppermute | solution.py:373
  111.2 3.4 %collective-permute-start.24 = (f32[3,32,256]{2,1,0:T(8,128)S(1)}, f32[3,32,256]{2,1,0:T(8,128)S(1)}, u32[]{:S(2)}, u32[]{:S(2)}) collective-permute-start(f32[3,32,256]{2,1,0:T(8,128)S(1)} %get-tuple-element.54), channel_id=1, source_target_pairs={{0,32},{32,64},{64,96},{96,0},{1,33},{33,65},{65,97},{97,1},{2,34}... | collective-permute-start | bytes 294920 | tf_op jit(solution)/shard_map/ppermute | solution.py:377
  114.6 2.0 %collective-permute-start.25 = (f32[3,32,256]{2,1,0:T(8,128)S(1)}, f32[3,32,256]{2,1,0:T(8,128)S(1)}, u32[]{:S(2)}, u32[]{:S(2)}) collective-permute-start(f32[3,32,256]{2,1,0:T(8,128)S(1)} %get-tuple-element.53), channel_id=1, source_target_pairs={{0,64},{32,96},{64,0},{96,32},{1,65},{33,97},{65,1},{97,33},{2,66}... | collective-permute-start | bytes 294920 | tf_op jit(solution)/shard_map/ppermute | solution.py:377
  117.1 1.0 collective-permute-done.27.corner
  118.0 0.5 collective-permute-done.24.b
  118.6 3.1 %collective-permute-done.25.c = f32[3,32,256]{2,1,0:T(8,128)S(1)} collective-permute-done((f32[3,32,256]{2,1,0:T(8,128)S(1)}, f32[3,32,256]{2,1,0:T(8,128)S(1)}, u32[]{:S(2)}, u32[]{:S(2)}) %collective-permute-start.25) | collective-permute-done | bytes 98336 | tf_op jit(solution)/shard_map/ppermute | solution.py:377
  121.7 6.8 %collective-permute-start.28 = (bf16[2,256,384]{2,1,0:T(8,128)(2,1)S(1)}, bf16[2,256,384]{2,1,0:T(8,128)(2,1)S(1)}, u32[]{:S(2)}, u32[]{:S(2)}) collective-permute-start(bf16[2,256,384]{2,1,0:T(8,128)(2,1)S(1)} %get-tuple-element.47), channel_id=1, source_target_pairs={{0,8},{8,16},{16,24},{24,32},{32,40},{40,48},{48,56},{56,64},{64,7... | collective-permute-start | bytes 1179656 | tf_op jit(solution)/shard_map/ppermute | solution.py:373
  128.5 1.0 collective-permute-start.29
  129.5 3.1 %collective-permute-start.30 = (f32[3,32,256]{2,1,0:T(8,128)S(1)}, f32[3,32,256]{2,1,0:T(8,128)S(1)}, u32[]{:S(2)}, u32[]{:S(2)}) collective-permute-start(f32[3,32,256]{2,1,0:T(8,128)S(1)} %get-tuple-element.50.a), channel_id=1, source_target_pairs={{0,4},{2,6},{4,0},{6,2},{1,5},{3,7},{5,1},{7,3},{8,12},{10,14},{12... | collective-permute-start | bytes 294920 | tf_op jit(solution)/shard_map/ppermute | solution.py:377
  132.6 2.0 %collective-permute-start.31 = (f32[3,32,256]{2,1,0:T(8,128)S(1)}, f32[3,32,256]{2,1,0:T(8,128)S(1)}, u32[]{:S(2)}, u32[]{:S(2)}) collective-permute-start(f32[3,32,256]{2,1,0:T(8,128)S(1)} %get-tuple-element.50.a), channel_id=1, source_target_pairs={{0,6},{2,0},{4,2},{6,4},{1,7},{3,1},{5,3},{7,5},{8,14},{10,8},{12,... | collective-permute-start | bytes 294920 | tf_op jit(solution)/shard_map/ppermute | solution.py:377
  134.6 1.1 collective-permute-done.30.c
  135.7 1.4 collective-permute-done.31.d
  137.1 0.6 collective-permute-start.32
  137.8 4.2 %collective-permute-start.33 = (f32[3,32,256]{2,1,0:T(8,128)S(1)}, f32[3,32,256]{2,1,0:T(8,128)S(1)}, u32[]{:S(2)}, u32[]{:S(2)}) collective-permute-start(f32[3,32,256]{2,1,0:T(8,128)S(1)} %y_sum.3.a), channel_id=1, source_target_pairs={{0,16},{8,24},{16,0},{24,8},{1,17},{9,25},{17,1},{25,9},{2,18},{10... | collective-permute-start | bytes 294920 | tf_op jit(solution)/shard_map/ppermute | solution.py:377
  142.0 0.8 collective-permute-done.32.b
  142.8 2.3 %collective-permute-done.33.c = f32[3,32,256]{2,1,0:T(8,128)S(1)} collective-permute-done((f32[3,32,256]{2,1,0:T(8,128)S(1)}, f32[3,32,256]{2,1,0:T(8,128)S(1)}, u32[]{:S(2)}, u32[]{:S(2)}) %collective-permute-start.33) | collective-permute-done | bytes 98336 | tf_op jit(solution)/shard_map/ppermute | solution.py:377
  145.1 1.1 collective-permute-done.34.d
  146.3 3.8 %collective-permute-start.36 = (f32[2,32,256]{2,1,0:T(8,128)S(1)}, f32[2,32,256]{2,1,0:T(8,128)S(1)}, u32[]{:S(2)}, u32[]{:S(2)}) collective-permute-start(f32[2,32,256]{2,1,0:T(8,128)S(1)} %z_sum.1.a), channel_id=1, source_target_pairs={{0,64},{32,96},{64,0},{96,32},{1,65},{33,97},{65,1},{97,33},{2,66}... | collective-permute-start | bytes 196616 | tf_op jit(solution)/shard_map/ppermute | solution.py:377
  150.1 2.0 %collective-permute-start.37 = (f32[2,32,256]{2,1,0:T(8,128)S(1)}, f32[2,32,256]{2,1,0:T(8,128)S(1)}, u32[]{:S(2)}, u32[]{:S(2)}) collective-permute-start(f32[2,32,256]{2,1,0:T(8,128)S(1)} %z_sum.1.a), channel_id=1, source_target_pairs={{0,96},{32,0},{64,32},{96,64},{1,97},{33,1},{65,33},{97,65},{2,98}... | collective-permute-start | bytes 196616 | tf_op jit(solution)/shard_map/ppermute | solution.py:377
  152.1 2.3 %object_update.1 = (f32[2,512,384]{2,1,0:T(8,128)}, f32[8,128]{1,0:T(8,128)S(1)}) custom-call(f32[2,512,384]{2,1,0:T(8,128)S(1)} %get-tuple-element.35.obj, f32[2,512,384]{2,1,0:T(8,128)S(1)} %get-tuple-element.40.own, bf16[2,512,256]{2,1,0:T(8,128)(2,1)S(1)} %collective-permute-done.22.left.waited, ...), custom_call_target="tpu_custom_call" | custom-call | flops 2000000 | bytes 4000000 | tf_op jit(solution)/shard_map/object_update/pallas_call | solution.py:265
  154.4 3.0 %collective-permute-start.38 = (f32[4,2,32,256]{3,2,1,0:T(8,128)S(1)}, f32[4,2,32,256]{3,2,1,0:T(8,128)S(1)}, u32[]{:S(2)}, u32[]{:S(2)}) collective-permute-start(f32[4,2,32,256]{3,2,1,0:T(8,128)S(1)} %half_probe.3.mine), channel_id=1, source_target_pairs={{0,1},{1,0},{2,3},{3,2},{4,5},{5,4},{6,7},{7,6},{8,9},{9,8},{10,11... | collective-permute-start | bytes 786440 | tf_op jit(solution)/shard_map/ppermute | solution.py:381
  157.5 1.2 collective-permute-done.38.other
  158.6 1.4 probe_whole.1
  (69 shorter events, 3.1 us)
Async XLA Ops:
  0.6 20.6 %copy-start.2 = (f32[2,512,384]{2,1,0:T(8,128)S(1)}, f32[2,512,384]{2,1,0:T(8,128)}, u32[]{:S(2)}) copy-start(f32[2,512,384]{2,1,0:T(8,128)} %obj.3) | copy-start | bytes 4718596
  0.6 15.4 %copy-start.13 = (s32[2,2,12]{2,1,0:T(2,128)S(1)}, s32[2,2,12]{2,1,0:T(2,128)}, u32[]{:S(2)}) copy-start(s32[2,2,12]{2,1,0:T(2,128)} %param.9) | copy-start | bytes 580
  0.6 15.5 %copy-start.14 = (s32[2,1,1]{0,2,1:T(1,128)S(1)}, s32[2,1,1]{0,2,1:T(1,128)}, u32[]{:S(2)}) copy-start(s32[2,1,1]{0,2,1:T(1,128)} %param.10) | copy-start | bytes 28
  0.7 20.5 %copy-start.9 = (f32[2,256,256]{2,1,0:T(8,128)S(1)}, f32[2,256,256]{2,1,0:T(8,128)}, u32[]{:S(2)}) copy-start(f32[2,256,256]{2,1,0:T(8,128)} %rest_4_.1) | copy-start | bytes 1572868
  2.3 10.4 %collective-permute-start = (bf16[2,256,256]{2,1,0:T(8,128)(2,1)S(1)}, bf16[2,256,256]{2,1,0:T(8,128)(2,1)S(1)}, u32[]{:S(2)}, u32[]{:S(2)}) collective-permute-start(bf16[2,256,256]{2,1,0:T(8,128)(2,1)S(1)} %slice.63), channel_id=1, source_target_pairs={{8,0},{16,8},{24,16},{32,24},{40,32},{48,40},{56,48},{64,56},{72,6... | collective-permute-start | bytes 786440 | tf_op jit(solution)/shard_map/ppermute | solution.py:373
  4.5 12.3 %collective-permute-start.2 = (bf16[2,512,256]{2,1,0:T(8,128)(2,1)}, bf16[2,512,256]{2,1,0:T(8,128)(2,1)S(1)}, u32[]{:S(2)}, u32[]{:S(2)}) collective-permute-start(bf16[2,512,256]{2,1,0:T(8,128)(2,1)} %slice.65), channel_id=1, source_target_pairs={{1,0},{2,1},{3,2},{4,3},{5,4},{6,5},{7,6},{9,8},{10,9},{11,10},{12... | collective-permute-start | bytes 1572872 | tf_op jit(solution)/shard_map/ppermute | solution.py:373
  7.8 8.9 %collective-permute-start.1 = (bf16[2,256,128]{2,1,0:T(8,128)(2,1)S(1)}, bf16[2,256,128]{2,1,0:T(8,128)(2,1)S(1)}, u32[]{:S(2)}, u32[]{:S(2)}) collective-permute-start(bf16[2,256,128]{2,1,0:T(8,128)(2,1)S(1)} %slice.64), channel_id=1, source_target_pairs={{8,0},{16,8},{24,16},{32,24},{40,32},{48,40},{56,48},{64,56},{72,6... | collective-permute-start | bytes 393224 | tf_op jit(solution)/shard_map/ppermute | solution.py:373
  12.7 8.5 %collective-permute-start.3 = (bf16[2,256,256]{2,1,0:T(8,128)(2,1)S(1)}, bf16[2,256,256]{2,1,0:T(8,128)(2,1)S(1)}, u32[]{:S(2)}, u32[]{:S(2)}) collective-permute-start(bf16[2,256,256]{2,1,0:T(8,128)(2,1)S(1)} %collective-permute-done.rest_0_.low_left), channel_id=1, source_target_pairs={{1,0},{2,1},{3,2},{4,3},{5,4},{6,5},{7,6},{9,8},{10,9},{11,10},{12... | collective-permute-start | bytes 786440 | tf_op jit(solution)/shard_map/ppermute | solution.py:373
  16.8 17.0 %copy-start.3 = (bf16[2,512,256]{2,1,0:T(8,128)(2,1)}, bf16[2,512,256]{2,1,0:T(8,128)(2,1)S(1)}, u32[]{:S(2)}) copy-start(bf16[2,512,256]{2,1,0:T(8,128)(2,1)S(1)} %collective-permute-done.2.rest_2_.right) | copy-start | bytes 1572868
  21.2 12.6 %copy-start.5 = (bf16[2,256,256]{2,1,0:T(8,128)(2,1)}, bf16[2,256,256]{2,1,0:T(8,128)(2,1)S(1)}, u32[]{:S(2)}) copy-start(bf16[2,256,256]{2,1,0:T(8,128)(2,1)S(1)} %collective-permute-done.3.rest_3_.corner) | copy-start | bytes 786436
  21.2 2.0 %copy-start.10 = (bf16[2,12,256,256]{3,2,1,0:T(8,128)(2,1)S(1)}, bf16[2,12,256,256]{3,2,1,0:T(8,128)(2,1)}, u32[]{:S(2)}) copy-start(bf16[2,12,256,256]{3,2,1,0:T(8,128)(2,1)} %rest_5_.3) | copy-start | bytes 9437188
  23.2 1.2 copy-start.11
  33.8 4.5 %collective-permute-start.6 = (f32[4,3,32,256]{3,2,1,0:T(8,128)S(1)}, f32[4,3,32,256]{3,2,1,0:T(8,128)S(1)}, u32[]{:S(2)}, u32[]{:S(2)}) collective-permute-start(f32[4,3,32,256]{3,2,1,0:T(8,128)S(1)} %get-tuple-element.31), channel_id=1, source_target_pairs={{0,1},{1,0},{2,3},{3,2},{4,5},{5,4},{6,7},{7,6},{8,9},{9,8},{10,11... | collective-permute-start | bytes 1179656 | tf_op jit(solution)/shard_map/ppermute | solution.py:381
  33.9 29.3 %collective-permute-start.4 = (bf16[2,768,256]{2,1,0:T(8,128)(2,1)S(1)}, bf16[2,768,256]{2,1,0:T(8,128)(2,1)S(1)}, u32[]{:S(2)}, u32[]{:S(2)}) collective-permute-start(bf16[2,768,256]{2,1,0:T(8,128)(2,1)S(1)} %get-tuple-element.28), channel_id=1, source_target_pairs={{0,1},{1,2},{2,3},{3,4},{4,5},{5,6},{6,7},{8,9},{9,10},{10,11},{11... | collective-permute-start | bytes 2359304 | tf_op jit(solution)/shard_map/ppermute | solution.py:373
  35.8 27.4 %collective-permute-start.5 = (bf16[2,768,256]{2,1,0:T(8,128)(2,1)S(1)}, bf16[2,768,256]{2,1,0:T(8,128)(2,1)S(1)}, u32[]{:S(2)}, u32[]{:S(2)}) collective-permute-start(bf16[2,768,256]{2,1,0:T(8,128)(2,1)S(1)} %get-tuple-element.29), channel_id=1, source_target_pairs={{1,0},{2,1},{3,2},{4,3},{5,4},{6,5},{7,6},{9,8},{10,9},{11,10},{12... | collective-permute-start | bytes 2359304 | tf_op jit(solution)/shard_map/ppermute | solution.py:373
  38.3 7.0 %collective-permute-start.7 = (f32[3,32,256]{2,1,0:T(8,128)S(1)}, f32[3,32,256]{2,1,0:T(8,128)S(1)}, u32[]{:S(2)}, u32[]{:S(2)}) collective-permute-start(f32[3,32,256]{2,1,0:T(8,128)S(1)} %get-tuple-element.58), channel_id=1, source_target_pairs={{0,32},{32,64},{64,96},{96,0},{1,33},{33,65},{65,97},{97,1},{2,34}... | collective-permute-start | bytes 294920 | tf_op jit(solution)/shard_map/ppermute | solution.py:377
  41.1 7.9 %collective-permute-start.8 = (f32[3,32,256]{2,1,0:T(8,128)S(1)}, f32[3,32,256]{2,1,0:T(8,128)S(1)}, u32[]{:S(2)}, u32[]{:S(2)}) collective-permute-start(f32[3,32,256]{2,1,0:T(8,128)S(1)} %get-tuple-element.57), channel_id=1, source_target_pairs={{0,64},{32,96},{64,0},{96,32},{1,65},{33,97},{65,1},{97,33},{2,66}... | collective-permute-start | bytes 294920 | tf_op jit(solution)/shard_map/ppermute | solution.py:377
  43.9 5.1 %collective-permute-start.9 = (f32[3,32,256]{2,1,0:T(8,128)S(1)}, f32[3,32,256]{2,1,0:T(8,128)S(1)}, u32[]{:S(2)}, u32[]{:S(2)}) collective-permute-start(f32[3,32,256]{2,1,0:T(8,128)S(1)} %get-tuple-element.56), channel_id=1, source_target_pairs={{0,96},{32,0},{64,32},{96,64},{1,97},{33,1},{65,33},{97,65},{2,98}... | collective-permute-start | bytes 294920 | tf_op jit(solution)/shard_map/ppermute | solution.py:377
  49.1 11.3 %collective-permute-start.10 = (f32[3,32,256]{2,1,0:T(8,128)S(1)}, f32[3,32,256]{2,1,0:T(8,128)S(1)}, u32[]{:S(2)}, u32[]{:S(2)}) collective-permute-start(f32[3,32,256]{2,1,0:T(8,128)S(1)} %x_sum.2.a), channel_id=1, source_target_pairs={{0,8},{8,16},{16,24},{24,0},{1,9},{9,17},{17,25},{25,1},{2,10},{10... | collective-permute-start | bytes 294920 | tf_op jit(solution)/shard_map/ppermute | solution.py:377
  58.0 5.0 %collective-permute-start.11 = (f32[3,32,256]{2,1,0:T(8,128)S(1)}, f32[3,32,256]{2,1,0:T(8,128)S(1)}, u32[]{:S(2)}, u32[]{:S(2)}) collective-permute-start(f32[3,32,256]{2,1,0:T(8,128)S(1)} %x_sum.2.a), channel_id=1, source_target_pairs={{0,16},{8,24},{16,0},{24,8},{1,17},{9,25},{17,1},{25,9},{2,18},{10... | collective-permute-start | bytes 294920 | tf_op jit(solution)/shard_map/ppermute | solution.py:377
  58.5 4.7 %collective-permute-start.12 = (f32[3,32,256]{2,1,0:T(8,128)S(1)}, f32[3,32,256]{2,1,0:T(8,128)S(1)}, u32[]{:S(2)}, u32[]{:S(2)}) collective-permute-start(f32[3,32,256]{2,1,0:T(8,128)S(1)} %x_sum.2.a), channel_id=1, source_target_pairs={{0,24},{8,0},{16,8},{24,16},{1,25},{9,1},{17,9},{25,17},{2,26},{10... | collective-permute-start | bytes 294920 | tf_op jit(solution)/shard_map/ppermute | solution.py:377
  63.2 2.1 %copy-start = (f32[2,768,640]{2,1,0:T(8,128)S(1)}, f32[2,768,640]{2,1,0:T(8,128)}, u32[]{:S(2)}) copy-start(f32[2,768,640]{2,1,0:T(8,128)} %get-tuple-element.27.grads) | copy-start | bytes 11796484
  66.5 0.6 copy-start.7
  67.2 24.1 %collective-permute-start.13 = (bf16[2,256,640]{2,1,0:T(8,128)(2,1)}, bf16[2,256,640]{2,1,0:T(8,128)(2,1)}, u32[]{:S(2)}, u32[]{:S(2)}) collective-permute-start(bf16[2,256,640]{2,1,0:T(8,128)(2,1)} %get-tuple-element.32), channel_id=1, source_target_pairs={{0,8},{8,16},{16,24},{24,32},{32,40},{40,48},{48,56},{56,64},{64,7... | collective-permute-start | bytes 1966088 | tf_op jit(solution)/shard_map/ppermute | solution.py:373
  72.3 18.9 %collective-permute-start.14 = (bf16[2,256,640]{2,1,0:T(8,128)(2,1)}, bf16[2,256,640]{2,1,0:T(8,128)(2,1)}, u32[]{:S(2)}, u32[]{:S(2)}) collective-permute-start(bf16[2,256,640]{2,1,0:T(8,128)(2,1)} %get-tuple-element.33), channel_id=1, source_target_pairs={{8,0},{16,8},{24,16},{32,24},{40,32},{48,40},{56,48},{64,56},{72,6... | collective-permute-start | bytes 1966088 | tf_op jit(solution)/shard_map/ppermute | solution.py:373
  73.6 21.7 %copy-start.4 = (bf16[2,512,256]{2,1,0:T(8,128)(2,1)S(1)}, bf16[2,512,256]{2,1,0:T(8,128)(2,1)}, u32[]{:S(2)}) copy-start(bf16[2,512,256]{2,1,0:T(8,128)(2,1)} %copy-done.3) | copy-start | bytes 1572868
  73.6 21.7 %copy-start.6 = (bf16[2,256,256]{2,1,0:T(8,128)(2,1)S(1)}, bf16[2,256,256]{2,1,0:T(8,128)(2,1)}, u32[]{:S(2)}) copy-start(bf16[2,256,256]{2,1,0:T(8,128)(2,1)} %copy-done.5) | copy-start | bytes 786436
  73.6 5.3 %collective-permute-start.15 = (f32[3,32,256]{2,1,0:T(8,128)}, f32[3,32,256]{2,1,0:T(8,128)S(1)}, u32[]{:S(2)}, u32[]{:S(2)}) collective-permute-start(f32[3,32,256]{2,1,0:T(8,128)} %copy-done.7), channel_id=1, source_target_pairs={{0,2},{2,4},{4,6},{6,0},{1,3},{3,5},{5,7},{7,1},{8,10},{10,12},{12... | collective-permute-start | bytes 294920 | tf_op jit(solution)/shard_map/ppermute | solution.py:377
  74.1 6.3 %collective-permute-start.16 = (f32[3,32,256]{2,1,0:T(8,128)}, f32[3,32,256]{2,1,0:T(8,128)S(1)}, u32[]{:S(2)}, u32[]{:S(2)}) collective-permute-start(f32[3,32,256]{2,1,0:T(8,128)} %copy-done.7), channel_id=1, source_target_pairs={{0,4},{2,6},{4,0},{6,2},{1,5},{3,7},{5,1},{7,3},{8,12},{10,14},{12... | collective-permute-start | bytes 294920 | tf_op jit(solution)/shard_map/ppermute | solution.py:377
  74.1 6.7 %collective-permute-start.17 = (f32[3,32,256]{2,1,0:T(8,128)}, f32[3,32,256]{2,1,0:T(8,128)S(1)}, u32[]{:S(2)}, u32[]{:S(2)}) collective-permute-start(f32[3,32,256]{2,1,0:T(8,128)} %copy-done.7), channel_id=1, source_target_pairs={{0,6},{2,0},{4,2},{6,4},{1,7},{3,1},{5,3},{7,5},{8,14},{10,8},{12,... | collective-permute-start | bytes 294920 | tf_op jit(solution)/shard_map/ppermute | solution.py:377
  80.8 0.9 copy-start.8
  81.7 5.6 %collective-permute-start.18 = (f32[2,32,256]{2,1,0:T(8,128)S(1)}, f32[2,32,256]{2,1,0:T(8,128)S(1)}, u32[]{:S(2)}, u32[]{:S(2)}) collective-permute-start(f32[2,32,256]{2,1,0:T(8,128)S(1)} %y_sum.2.a.mine), channel_id=1, source_target_pairs={{0,32},{32,64},{64,96},{96,0},{1,33},{33,65},{65,97},{97,1},{2,34}... | collective-permute-start | bytes 196616 | tf_op jit(solution)/shard_map/ppermute | solution.py:377
  83.7 5.6 %collective-permute-start.19 = (f32[2,32,256]{2,1,0:T(8,128)S(1)}, f32[2,32,256]{2,1,0:T(8,128)S(1)}, u32[]{:S(2)}, u32[]{:S(2)}) collective-permute-start(f32[2,32,256]{2,1,0:T(8,128)S(1)} %y_sum.2.a.mine), channel_id=1, source_target_pairs={{0,64},{32,96},{64,0},{96,32},{1,65},{33,97},{65,1},{97,33},{2,66}... | collective-permute-start | bytes 196616 | tf_op jit(solution)/shard_map/ppermute | solution.py:377
  86.9 4.3 %collective-permute-start.20 = (f32[2,32,256]{2,1,0:T(8,128)S(1)}, f32[2,32,256]{2,1,0:T(8,128)S(1)}, u32[]{:S(2)}, u32[]{:S(2)}) collective-permute-start(f32[2,32,256]{2,1,0:T(8,128)S(1)} %y_sum.2.a.mine), channel_id=1, source_target_pairs={{0,96},{32,0},{64,32},{96,64},{1,97},{33,1},{65,33},{97,65},{2,98}... | collective-permute-start | bytes 196616 | tf_op jit(solution)/shard_map/ppermute | solution.py:377
  91.2 9.0 %collective-permute-start.21 = (f32[4,2,32,256]{3,2,1,0:T(8,128)S(1)}, f32[4,2,32,256]{3,2,1,0:T(8,128)S(1)}, u32[]{:S(2)}, u32[]{:S(2)}) collective-permute-start(f32[4,2,32,256]{3,2,1,0:T(8,128)S(1)} %half_probe.2.rest_3_), channel_id=1, source_target_pairs={{0,1},{1,0},{2,3},{3,2},{4,5},{5,4},{6,7},{7,6},{8,9},{9,8},{10,11... | collective-permute-start | bytes 786440 | tf_op jit(solution)/shard_map/ppermute | solution.py:381
  95.3 2.1 %copy-start.1 = (f32[2,768,640]{2,1,0:T(8,128)S(1)}, f32[2,768,640]{2,1,0:T(8,128)}, u32[]{:S(2)}) copy-start(f32[2,768,640]{2,1,0:T(8,128)} %get-tuple-element.27.grads) | copy-start | bytes 11796484
  97.5 2.8 %copy-start.12 = (bf16[2,512,512]{2,1,0:T(8,128)(2,1)S(1)}, bf16[2,512,512]{2,1,0:T(8,128)(2,1)}, u32[]{:S(2)}) copy-start(bf16[2,512,512]{2,1,0:T(8,128)(2,1)} %constant.20.clone.rest_6_) | copy-start | bytes 3145732
  105.9 5.2 %collective-permute-start.23 = (f32[4,3,32,256]{3,2,1,0:T(8,128)S(1)}, f32[4,3,32,256]{3,2,1,0:T(8,128)S(1)}, u32[]{:S(2)}, u32[]{:S(2)}) collective-permute-start(f32[4,3,32,256]{3,2,1,0:T(8,128)S(1)} %get-tuple-element.43), channel_id=1, source_target_pairs={{0,1},{1,0},{2,3},{3,2},{4,5},{5,4},{6,7},{7,6},{8,9},{9,8},{10,11... | collective-permute-start | bytes 1179656 | tf_op jit(solution)/shard_map/ppermute | solution.py:381
  106.0 28.5 %collective-permute-start.22 = (bf16[2,512,256]{2,1,0:T(8,128)(2,1)S(1)}, bf16[2,512,256]{2,1,0:T(8,128)(2,1)S(1)}, u32[]{:S(2)}, u32[]{:S(2)}) collective-permute-start(bf16[2,512,256]{2,1,0:T(8,128)(2,1)S(1)} %get-tuple-element.41), channel_id=1, source_target_pairs={{0,1},{1,2},{2,3},{3,4},{4,5},{5,6},{6,7},{8,9},{9,10},{10,11},{11... | collective-permute-start | bytes 1572872 | tf_op jit(solution)/shard_map/ppermute | solution.py:373
  109.1 8.9 %collective-permute-start.27 = (bf16[2,256,256]{2,1,0:T(8,128)(2,1)S(1)}, bf16[2,256,256]{2,1,0:T(8,128)(2,1)S(1)}, u32[]{:S(2)}, u32[]{:S(2)}) collective-permute-start(bf16[2,256,256]{2,1,0:T(8,128)(2,1)S(1)} %get-tuple-element.46), channel_id=1, source_target_pairs={{0,1},{1,2},{2,3},{3,4},{4,5},{5,6},{6,7},{8,9},{9,10},{10,11},{11... | collective-permute-start | bytes 786440 | tf_op jit(solution)/shard_map/ppermute | solution.py:373
  111.2 7.4 %collective-permute-start.24 = (f32[3,32,256]{2,1,0:T(8,128)S(1)}, f32[3,32,256]{2,1,0:T(8,128)S(1)}, u32[]{:S(2)}, u32[]{:S(2)}) collective-permute-start(f32[3,32,256]{2,1,0:T(8,128)S(1)} %get-tuple-element.54), channel_id=1, source_target_pairs={{0,32},{32,64},{64,96},{96,0},{1,33},{33,65},{65,97},{97,1},{2,34}... | collective-permute-start | bytes 294920 | tf_op jit(solution)/shard_map/ppermute | solution.py:377
  114.6 7.1 %collective-permute-start.25 = (f32[3,32,256]{2,1,0:T(8,128)S(1)}, f32[3,32,256]{2,1,0:T(8,128)S(1)}, u32[]{:S(2)}, u32[]{:S(2)}) collective-permute-start(f32[3,32,256]{2,1,0:T(8,128)S(1)} %get-tuple-element.53), channel_id=1, source_target_pairs={{0,64},{32,96},{64,0},{96,32},{1,65},{33,97},{65,1},{97,33},{2,66}... | collective-permute-start | bytes 294920 | tf_op jit(solution)/shard_map/ppermute | solution.py:377
  116.6 5.0 %collective-permute-start.26 = (f32[3,32,256]{2,1,0:T(8,128)S(1)}, f32[3,32,256]{2,1,0:T(8,128)S(1)}, u32[]{:S(2)}, u32[]{:S(2)}) collective-permute-start(f32[3,32,256]{2,1,0:T(8,128)S(1)} %get-tuple-element.52), channel_id=1, source_target_pairs={{0,96},{32,0},{64,32},{96,64},{1,97},{33,1},{65,33},{97,65},{2,98}... | collective-permute-start | bytes 294920 | tf_op jit(solution)/shard_map/ppermute | solution.py:377
  121.7 24.5 %collective-permute-start.28 = (bf16[2,256,384]{2,1,0:T(8,128)(2,1)S(1)}, bf16[2,256,384]{2,1,0:T(8,128)(2,1)S(1)}, u32[]{:S(2)}, u32[]{:S(2)}) collective-permute-start(bf16[2,256,384]{2,1,0:T(8,128)(2,1)S(1)} %get-tuple-element.47), channel_id=1, source_target_pairs={{0,8},{8,16},{16,24},{24,32},{32,40},{40,48},{48,56},{56,64},{64,7... | collective-permute-start | bytes 1179656 | tf_op jit(solution)/shard_map/ppermute | solution.py:373
  128.5 6.1 %collective-permute-start.29 = (f32[3,32,256]{2,1,0:T(8,128)S(1)}, f32[3,32,256]{2,1,0:T(8,128)S(1)}, u32[]{:S(2)}, u32[]{:S(2)}) collective-permute-start(f32[3,32,256]{2,1,0:T(8,128)S(1)} %get-tuple-element.50.a), channel_id=1, source_target_pairs={{0,2},{2,4},{4,6},{6,0},{1,3},{3,5},{5,7},{7,1},{8,10},{10,12},{12... | collective-permute-start | bytes 294920 | tf_op jit(solution)/shard_map/ppermute | solution.py:377
  129.5 6.2 %collective-permute-start.30 = (f32[3,32,256]{2,1,0:T(8,128)S(1)}, f32[3,32,256]{2,1,0:T(8,128)S(1)}, u32[]{:S(2)}, u32[]{:S(2)}) collective-permute-start(f32[3,32,256]{2,1,0:T(8,128)S(1)} %get-tuple-element.50.a), channel_id=1, source_target_pairs={{0,4},{2,6},{4,0},{6,2},{1,5},{3,7},{5,1},{7,3},{8,12},{10,14},{12... | collective-permute-start | bytes 294920 | tf_op jit(solution)/shard_map/ppermute | solution.py:377
  132.6 4.5 %collective-permute-start.31 = (f32[3,32,256]{2,1,0:T(8,128)S(1)}, f32[3,32,256]{2,1,0:T(8,128)S(1)}, u32[]{:S(2)}, u32[]{:S(2)}) collective-permute-start(f32[3,32,256]{2,1,0:T(8,128)S(1)} %get-tuple-element.50.a), channel_id=1, source_target_pairs={{0,6},{2,0},{4,2},{6,4},{1,7},{3,1},{5,3},{7,5},{8,14},{10,8},{12,... | collective-permute-start | bytes 294920 | tf_op jit(solution)/shard_map/ppermute | solution.py:377
  137.1 5.7 %collective-permute-start.32 = (f32[3,32,256]{2,1,0:T(8,128)S(1)}, f32[3,32,256]{2,1,0:T(8,128)S(1)}, u32[]{:S(2)}, u32[]{:S(2)}) collective-permute-start(f32[3,32,256]{2,1,0:T(8,128)S(1)} %y_sum.3.a), channel_id=1, source_target_pairs={{0,8},{8,16},{16,24},{24,0},{1,9},{9,17},{17,25},{25,1},{2,10},{10... | collective-permute-start | bytes 294920 | tf_op jit(solution)/shard_map/ppermute | solution.py:377
  137.8 7.3 %collective-permute-start.33 = (f32[3,32,256]{2,1,0:T(8,128)S(1)}, f32[3,32,256]{2,1,0:T(8,128)S(1)}, u32[]{:S(2)}, u32[]{:S(2)}) collective-permute-start(f32[3,32,256]{2,1,0:T(8,128)S(1)} %y_sum.3.a), channel_id=1, source_target_pairs={{0,16},{8,24},{16,0},{24,8},{1,17},{9,25},{17,1},{25,9},{2,18},{10... | collective-permute-start | bytes 294920 | tf_op jit(solution)/shard_map/ppermute | solution.py:377
  142.0 4.2 %collective-permute-start.34 = (f32[3,32,256]{2,1,0:T(8,128)S(1)}, f32[3,32,256]{2,1,0:T(8,128)S(1)}, u32[]{:S(2)}, u32[]{:S(2)}) collective-permute-start(f32[3,32,256]{2,1,0:T(8,128)S(1)} %y_sum.3.a), channel_id=1, source_target_pairs={{0,24},{8,0},{16,8},{24,16},{1,25},{9,1},{17,9},{25,17},{2,26},{10... | collective-permute-start | bytes 294920 | tf_op jit(solution)/shard_map/ppermute | solution.py:377
  146.2 8.2 %collective-permute-start.35 = (f32[2,32,256]{2,1,0:T(8,128)S(1)}, f32[2,32,256]{2,1,0:T(8,128)S(1)}, u32[]{:S(2)}, u32[]{:S(2)}) collective-permute-start(f32[2,32,256]{2,1,0:T(8,128)S(1)} %z_sum.1.a), channel_id=1, source_target_pairs={{0,32},{32,64},{64,96},{96,0},{1,33},{33,65},{65,97},{97,1},{2,34}... | collective-permute-start | bytes 196616 | tf_op jit(solution)/shard_map/ppermute | solution.py:377
  146.3 8.1 %collective-permute-start.36 = (f32[2,32,256]{2,1,0:T(8,128)S(1)}, f32[2,32,256]{2,1,0:T(8,128)S(1)}, u32[]{:S(2)}, u32[]{:S(2)}) collective-permute-start(f32[2,32,256]{2,1,0:T(8,128)S(1)} %z_sum.1.a), channel_id=1, source_target_pairs={{0,64},{32,96},{64,0},{96,32},{1,65},{33,97},{65,1},{97,33},{2,66}... | collective-permute-start | bytes 196616 | tf_op jit(solution)/shard_map/ppermute | solution.py:377
  150.1 4.2 %collective-permute-start.37 = (f32[2,32,256]{2,1,0:T(8,128)S(1)}, f32[2,32,256]{2,1,0:T(8,128)S(1)}, u32[]{:S(2)}, u32[]{:S(2)}) collective-permute-start(f32[2,32,256]{2,1,0:T(8,128)S(1)} %z_sum.1.a), channel_id=1, source_target_pairs={{0,96},{32,0},{64,32},{96,64},{1,97},{33,1},{65,33},{97,65},{2,98}... | collective-permute-start | bytes 196616 | tf_op jit(solution)/shard_map/ppermute | solution.py:377
  154.4 4.2 %collective-permute-start.38 = (f32[4,2,32,256]{3,2,1,0:T(8,128)S(1)}, f32[4,2,32,256]{3,2,1,0:T(8,128)S(1)}, u32[]{:S(2)}, u32[]{:S(2)}) collective-permute-start(f32[4,2,32,256]{3,2,1,0:T(8,128)S(1)} %half_probe.3.mine), channel_id=1, source_target_pairs={{0,1},{1,0},{2,3},{3,2},{4,5},{5,4},{6,7},{7,6},{8,9},{9,8},{10,11... | collective-permute-start | bytes 786440 | tf_op jit(solution)/shard_map/ppermute | solution.py:381

commit v9 on v8

--- a/solution.py
+++ b/solution.py
@@ -250,7 +250,7 @@
         in_specs=[smem] * 3 + [pl.BlockSpec(memory_space=pltpu.HBM)] * (5 + len(lows) + len(pieces)),
         out_specs=[vmem] * (len(shapes) - 1) + [smem],
         scratch_shapes=scratch,
-        compiler_params=pltpu.CompilerParams(vmem_limit_bytes=44 << 20),
+        compiler_params=pltpu.CompilerParams(vmem_limit_bytes=46 << 20),
         cost_estimate=pl.CostEstimate(flops=6_000_000_000, bytes_accessed=8_000_000, transcendentals=0),
         name="frames",
     )(place, counts, pos, obj, *lows, right, corner, *pieces, amps, tables)

time: 161 us -> 156 us (0.969)
  Pallas kernels: 22.8 us -> 20.6 us
  local copies, waits for them, and re-layouts: 11.4 us -> 9.54 us
    pallas_call x2, Pallas kernels: 14.9 us -> 12.8 us  [run_frames(): pl.pallas_call(functools.partial(frames_kernel, middle, iteration, len(lo...]
    unnamed x30 -> x28, local copies, waits for them, and re-layouts: 9 us -> 7.12 us
  transfers between devices with their start and end apart: 39 -> 39, of which waited for: 21 -> 18; matrix products, arithmetic and copies ran while one was open for 2% -> 2% of each run, Pallas kernels for 3% -> 3%
where the time goes in v9:
time: 156 us; the launch traced here: 155 us
  starting transfers between devices  85.9 us (55%)
  waiting for transfers between devices  36.4 us (23%)
  Pallas kernels  20.6 us (13%)
  local copies, waits for them, and re-layouts  9.54 us (6%)
  other arithmetic  1.82 us (1%)
    ppermute x24, starting transfers between devices, turned(): return lax.ppermute(value, axis, [(s, (s + steps) % 4) for s in range(4)])  46.7 us
    ppermute x11, starting transfers between devices, moved(): lax.ppermute(value, axis, [(s, s + steps) for s in range(first, last)])  31.6 us
    ppermute x24, waiting for transfers between devices, turned(): return lax.ppermute(value, axis, [(s, (s + steps) % 4) for s in range(4)])  25 us
    pallas_call x2, Pallas kernels, run_frames(): pl.pallas_call(functools.partial(frames_kernel, middle, iteration, len(lo...  12.8 us
    ppermute x11, waiting for transfers between devices, moved(): lax.ppermute(value, axis, [(s, s + steps) for s in range(first, last)])  10.3 us
    pallas_call x11, Pallas kernels, small_call(): pl.pallas_call(body, out_shape=shapes, in_specs=[spec(space) for space in...  7.76 us
    ppermute x4, starting transfers between devices, swapped(): return lax.ppermute(value, 'core', [(0, 1), (1, 0)])  7.63 us
    unnamed x28, local copies, waits for them, and re-layouts  7.12 us
  transfers between devices with their start and end apart: 39, of which 18 were waited for; matrix products, arithmetic and copies ran while one was open for 2% of the time, Pallas kernels for 3%

profile of v9, /device:TPU:1, one launch (start us, length us, event | category | flops | bytes accessed | tf_op | source)
XLA Modules:
  0.0 155.3 jit_solution(16842317755213332874)
XLA Ops:
  0.7 1.6 %convert.5 = bf16[2,512,384]{2,1,0:T(8,128)(2,1)S(1)} convert(f32[2,512,384]{2,1,0:T(8,128)} %obj.3) | non-fusion elementwise | flops 393216 | bytes 2359296 | tf_op jit(solution)/shard_map/convert.2
  2.3 1.3 collective-permute-start
  3.6 0.8 slice.65
  4.5 3.3 %collective-permute-start.2 = (bf16[2,512,256]{2,1,0:T(8,128)(2,1)}, bf16[2,512,256]{2,1,0:T(8,128)(2,1)S(1)}, u32[]{:S(2)}, u32[]{:S(2)}) collective-permute-start(bf16[2,512,256]{2,1,0:T(8,128)(2,1)} %slice.65), channel_id=1, source_target_pairs={{1,0},{2,1},{3,2},{4,3},{5,4},{6,5},{7,6},{9,8},{10,9},{11,10},{12... | collective-permute-start | bytes 1572872 | tf_op jit(solution)/shard_map/ppermute | solution.py:373
  7.8 1.3 collective-permute-start.1
  9.1 3.6 %collective-permute-done.rest_0_.low_left = bf16[2,256,256]{2,1,0:T(8,128)(2,1)S(1)} collective-permute-done((bf16[2,256,256]{2,1,0:T(8,128)(2,1)S(1)}, bf16[2,256,256]{2,1,0:T(8,128)(2,1)S(1)}, u32[]{:S(2)}, u32[]{:S(2)}) %collective-permute-start) | collective-permute-done | bytes 262176 | tf_op jit(solution)/shard_map/ppermute | solution.py:373
  12.7 3.3 %collective-permute-start.3 = (bf16[2,256,256]{2,1,0:T(8,128)(2,1)S(1)}, bf16[2,256,256]{2,1,0:T(8,128)(2,1)S(1)}, u32[]{:S(2)}, u32[]{:S(2)}) collective-permute-start(bf16[2,256,256]{2,1,0:T(8,128)(2,1)S(1)} %collective-permute-done.rest_0_.low_left), channel_id=1, source_target_pairs={{1,0},{2,1},{3,2},{4,3},{5,4},{6,5},{7,6},{9,8},{10,9},{11,10},{12... | collective-permute-start | bytes 786440 | tf_op jit(solution)/shard_map/ppermute | solution.py:373
  16.2 0.7 fusion
  16.8 4.4 %collective-permute-done.3.rest_3_.corner = bf16[2,256,256]{2,1,0:T(8,128)(2,1)S(1)} collective-permute-done((bf16[2,256,256]{2,1,0:T(8,128)(2,1)S(1)}, bf16[2,256,256]{2,1,0:T(8,128)(2,1)S(1)}, u32[]{:S(2)}, u32[]{:S(2)}) %collective-permute-start.3) | collective-permute-done | bytes 262176 | tf_op jit(solution)/shard_map/ppermute | solution.py:373
  21.2 1.3 copy-done.10
  22.5 7.2 %frames.2 = (f32[2,768,640]{2,1,0:T(8,128)}, bf16[2,768,256]{2,1,0:T(8,128)(2,1)S(1)}, bf16[2,768,256]{2,1,0:T(8,128)(2,1)S(1)}, f32[4,3,32,256]{3,2,1,0:T(8,128...) custom-call(s32[2]{0:T(128)S(1)} %pad_add_fusion.place, s32[1]{0:T(128)} %bitcast.2.counts, ...), custom_call_target="tpu_custom_call" | custom-call | flops 6000000000 | bytes 8000000 | tf_op jit(solution)/shard_map/frames/pallas_call | solution.py:247
  29.7 0.1 collective-permute-start.6
  29.8 3.6 %collective-permute-start.4 = (bf16[2,768,256]{2,1,0:T(8,128)(2,1)S(1)}, bf16[2,768,256]{2,1,0:T(8,128)(2,1)S(1)}, u32[]{:S(2)}, u32[]{:S(2)}) collective-permute-start(bf16[2,768,256]{2,1,0:T(8,128)(2,1)S(1)} %get-tuple-element.28), channel_id=1, source_target_pairs={{0,1},{1,2},{2,3},{3,4},{4,5},{5,6},{6,7},{8,9},{9,10},{10,11},{11... | collective-permute-start | bytes 2359304 | tf_op jit(solution)/shard_map/ppermute | solution.py:373
  33.4 1.9 %collective-permute-start.5 = (bf16[2,768,256]{2,1,0:T(8,128)(2,1)S(1)}, bf16[2,768,256]{2,1,0:T(8,128)(2,1)S(1)}, u32[]{:S(2)}, u32[]{:S(2)}) collective-permute-start(bf16[2,768,256]{2,1,0:T(8,128)(2,1)S(1)} %get-tuple-element.29), channel_id=1, source_target_pairs={{1,0},{2,1},{3,2},{4,3},{5,4},{6,5},{7,6},{9,8},{10,9},{11,10},{12... | collective-permute-start | bytes 2359304 | tf_op jit(solution)/shard_map/ppermute | solution.py:373
  35.4 10.9 %collective-permute-start.7 = (f32[3,32,256]{2,1,0:T(8,128)S(1)}, f32[3,32,256]{2,1,0:T(8,128)S(1)}, u32[]{:S(2)}, u32[]{:S(2)}) collective-permute-start(f32[3,32,256]{2,1,0:T(8,128)S(1)} %get-tuple-element.58), channel_id=1, source_target_pairs={{0,32},{32,64},{64,96},{96,0},{1,33},{33,65},{65,97},{97,1},{2,34}... | collective-permute-start | bytes 294920 | tf_op jit(solution)/shard_map/ppermute | solution.py:377
  46.4 2.8 %collective-permute-start.8 = (f32[3,32,256]{2,1,0:T(8,128)S(1)}, f32[3,32,256]{2,1,0:T(8,128)S(1)}, u32[]{:S(2)}, u32[]{:S(2)}) collective-permute-start(f32[3,32,256]{2,1,0:T(8,128)S(1)} %get-tuple-element.57), channel_id=1, source_target_pairs={{0,64},{32,96},{64,0},{96,32},{1,65},{33,97},{65,1},{97,33},{2,66}... | collective-permute-start | bytes 294920 | tf_op jit(solution)/shard_map/ppermute | solution.py:377
  49.1 2.0 %collective-permute-start.9 = (f32[3,32,256]{2,1,0:T(8,128)S(1)}, f32[3,32,256]{2,1,0:T(8,128)S(1)}, u32[]{:S(2)}, u32[]{:S(2)}) collective-permute-start(f32[3,32,256]{2,1,0:T(8,128)S(1)} %get-tuple-element.56), channel_id=1, source_target_pairs={{0,96},{32,0},{64,32},{96,64},{1,97},{33,1},{65,33},{97,65},{2,98}... | collective-permute-start | bytes 294920 | tf_op jit(solution)/shard_map/ppermute | solution.py:377
  51.1 2.0 %collective-permute-done.8.c = f32[3,32,256]{2,1,0:T(8,128)S(1)} collective-permute-done((f32[3,32,256]{2,1,0:T(8,128)S(1)}, f32[3,32,256]{2,1,0:T(8,128)S(1)}, u32[]{:S(2)}, u32[]{:S(2)}) %collective-permute-start.8) | collective-permute-done | bytes 98336 | tf_op jit(solution)/shard_map/ppermute | solution.py:377
  53.3 0.1 collective-permute-start.11
  53.4 2.6 %collective-permute-start.12 = (f32[3,32,256]{2,1,0:T(8,128)S(1)}, f32[3,32,256]{2,1,0:T(8,128)S(1)}, u32[]{:S(2)}, u32[]{:S(2)}) collective-permute-start(f32[3,32,256]{2,1,0:T(8,128)S(1)} %x_sum.2.a), channel_id=1, source_target_pairs={{0,24},{8,0},{16,8},{24,16},{1,25},{9,1},{17,9},{25,17},{2,26},{10... | collective-permute-start | bytes 294920 | tf_op jit(solution)/shard_map/ppermute | solution.py:377
  55.9 5.1 %collective-permute-done.10.b = f32[3,32,256]{2,1,0:T(8,128)S(1)} collective-permute-done((f32[3,32,256]{2,1,0:T(8,128)S(1)}, f32[3,32,256]{2,1,0:T(8,128)S(1)}, u32[]{:S(2)}, u32[]{:S(2)}) %collective-permute-start.10) | collective-permute-done | bytes 98336 | tf_op jit(solution)/shard_map/ppermute | solution.py:377
  61.0 0.3 collective-permute-done.12.d
  61.3 2.1 %copy-done = f32[2,768,640]{2,1,0:T(8,128)S(1)} copy-done((f32[2,768,640]{2,1,0:T(8,128)S(1)}, f32[2,768,640]{2,1,0:T(8,128)}, u32[]{:S(2)}) %copy-start) | copy-done | bytes 3932184
  63.4 1.3 z_sum_rims.1
  64.7 0.6 copy-done.7
  65.4 3.0 %collective-permute-start.13 = (bf16[2,256,640]{2,1,0:T(8,128)(2,1)}, bf16[2,256,640]{2,1,0:T(8,128)(2,1)}, u32[]{:S(2)}, u32[]{:S(2)}) collective-permute-start(bf16[2,256,640]{2,1,0:T(8,128)(2,1)} %get-tuple-element.32), channel_id=1, source_target_pairs={{0,8},{8,16},{16,24},{24,32},{32,40},{40,48},{48,56},{56,64},{64,7... | collective-permute-start | bytes 1966088 | tf_op jit(solution)/shard_map/ppermute | solution.py:373
  68.4 1.3 collective-permute-start.14
  69.9 2.6 %collective-permute-start.17 = (f32[3,32,256]{2,1,0:T(8,128)}, f32[3,32,256]{2,1,0:T(8,128)S(1)}, u32[]{:S(2)}, u32[]{:S(2)}) collective-permute-start(f32[3,32,256]{2,1,0:T(8,128)} %copy-done.7), channel_id=1, source_target_pairs={{0,6},{2,0},{4,2},{6,4},{1,7},{3,1},{5,3},{7,5},{8,14},{10,8},{12,... | collective-permute-start | bytes 294920 | tf_op jit(solution)/shard_map/ppermute | solution.py:377
  72.5 0.8 constant_dynamic-slice_fusion.mine
  73.3 3.2 %collective-permute-done.15.b = f32[3,32,256]{2,1,0:T(8,128)S(1)} collective-permute-done((f32[3,32,256]{2,1,0:T(8,128)}, f32[3,32,256]{2,1,0:T(8,128)S(1)}, u32[]{:S(2)}, u32[]{:S(2)}) %collective-permute-start.15) | collective-permute-done | bytes 98336 | tf_op jit(solution)/shard_map/ppermute | solution.py:377
  76.5 0.5 collective-permute-done.17.d
  77.1 0.9 copy-done.8
  78.0 3.7 %collective-permute-start.18 = (f32[2,32,256]{2,1,0:T(8,128)S(1)}, f32[2,32,256]{2,1,0:T(8,128)S(1)}, u32[]{:S(2)}, u32[]{:S(2)}) collective-permute-start(f32[2,32,256]{2,1,0:T(8,128)S(1)} %y_sum.2.a.mine), channel_id=1, source_target_pairs={{0,32},{32,64},{64,96},{96,0},{1,33},{33,65},{65,97},{97,1},{2,34}... | collective-permute-start | bytes 196616 | tf_op jit(solution)/shard_map/ppermute | solution.py:377
  81.6 3.9 %collective-permute-start.19 = (f32[2,32,256]{2,1,0:T(8,128)S(1)}, f32[2,32,256]{2,1,0:T(8,128)S(1)}, u32[]{:S(2)}, u32[]{:S(2)}) collective-permute-start(f32[2,32,256]{2,1,0:T(8,128)S(1)} %y_sum.2.a.mine), channel_id=1, source_target_pairs={{0,64},{32,96},{64,0},{96,32},{1,65},{33,97},{65,1},{97,33},{2,66}... | collective-permute-start | bytes 196616 | tf_op jit(solution)/shard_map/ppermute | solution.py:377
  85.6 0.5 collective-permute-done.18.b
  86.0 1.9 %collective-permute-done.19.c = f32[2,32,256]{2,1,0:T(8,128)S(1)} collective-permute-done((f32[2,32,256]{2,1,0:T(8,128)S(1)}, f32[2,32,256]{2,1,0:T(8,128)S(1)}, u32[]{:S(2)}, u32[]{:S(2)}) %collective-permute-start.19) | collective-permute-done | bytes 65568 | tf_op jit(solution)/shard_map/ppermute | solution.py:377
  87.9 1.5 collective-permute-done.20.d
  89.5 3.6 %collective-permute-start.21 = (f32[4,2,32,256]{3,2,1,0:T(8,128)S(1)}, f32[4,2,32,256]{3,2,1,0:T(8,128)S(1)}, u32[]{:S(2)}, u32[]{:S(2)}) collective-permute-start(f32[4,2,32,256]{3,2,1,0:T(8,128)S(1)} %half_probe.2.rest_3_), channel_id=1, source_target_pairs={{0,1},{1,0},{2,3},{3,2},{4,5},{5,4},{6,7},{7,6},{8,9},{9,8},{10,11... | collective-permute-start | bytes 786440 | tf_op jit(solution)/shard_map/ppermute | solution.py:381
  93.0 2.1 %copy-done.1 = f32[2,768,640]{2,1,0:T(8,128)S(1)} copy-done((f32[2,768,640]{2,1,0:T(8,128)S(1)}, f32[2,768,640]{2,1,0:T(8,128)}, u32[]{:S(2)}) %copy-start.1) | copy-done | bytes 3932184
  95.2 2.7 %wide_update.1 = (f32[2,512,384]{2,1,0:T(8,128)S(1)}, bf16[2,256,384]{2,1,0:T(8,128)(2,1)S(1)}, bf16[2,512,256]{2,1,0:T(8,128)(2,1)S(1)}, bf16[2,256,256]{2,1,0:T(8,128)(2,1)S(1)}) custom-call(f32[2,512,384]{2,1,0:T(8,128)S(1)} %copy-done.2, bf16[2,256,256]{2,1,0:T(8,128)(2,1)S(1)} %collective-permute-done.rest_0_.low_left, ...), custom_call_target="tpu_custom_call" | custom-call | flops 2000000 | bytes 4000000 | tf_op jit(solution)/shard_map/wide_update/pallas_call | solution.py:265
  97.8 5.7 %frames.3 = (f32[2,512,384]{2,1,0:T(8,128)S(1)}, f32[2,256,256]{2,1,0:T(8,128)S(1)}, bf16[2,256,128]{2,1,0:T(8,128)(2,1)S(1)}, bf16[2,512,256]{2,1,0:T(8,128)(2,...) custom-call(s32[2]{0:T(128)S(1)} %pad_add_fusion.place, ...), custom_call_target="tpu_custom_call" | custom-call | flops 6000000000 | bytes 8000000 | tf_op jit(solution)/shard_map/frames/pallas_call | solution.py:247
  103.5 0.1 collective-permute-start.23
  103.7 5.4 %collective-permute-start.22 = (bf16[2,512,256]{2,1,0:T(8,128)(2,1)S(1)}, bf16[2,512,256]{2,1,0:T(8,128)(2,1)S(1)}, u32[]{:S(2)}, u32[]{:S(2)}) collective-permute-start(bf16[2,512,256]{2,1,0:T(8,128)(2,1)S(1)} %get-tuple-element.41), channel_id=1, source_target_pairs={{0,1},{1,2},{2,3},{3,4},{4,5},{5,6},{6,7},{8,9},{9,10},{10,11},{11... | collective-permute-start | bytes 1572872 | tf_op jit(solution)/shard_map/ppermute | solution.py:373
  109.0 2.0 %collective-permute-start.27 = (bf16[2,256,256]{2,1,0:T(8,128)(2,1)S(1)}, bf16[2,256,256]{2,1,0:T(8,128)(2,1)S(1)}, u32[]{:S(2)}, u32[]{:S(2)}) collective-permute-start(bf16[2,256,256]{2,1,0:T(8,128)(2,1)S(1)} %get-tuple-element.46), channel_id=1, source_target_pairs={{0,1},{1,2},{2,3},{3,4},{4,5},{5,6},{6,7},{8,9},{9,10},{10,11},{11... | collective-permute-start | bytes 786440 | tf_op jit(solution)/shard_map/ppermute | solution.py:373
  111.2 4.5 %collective-permute-start.25 = (f32[3,32,256]{2,1,0:T(8,128)S(1)}, f32[3,32,256]{2,1,0:T(8,128)S(1)}, u32[]{:S(2)}, u32[]{:S(2)}) collective-permute-start(f32[3,32,256]{2,1,0:T(8,128)S(1)} %get-tuple-element.53), channel_id=1, source_target_pairs={{0,64},{32,96},{64,0},{96,32},{1,65},{33,97},{65,1},{97,33},{2,66}... | collective-permute-start | bytes 294920 | tf_op jit(solution)/shard_map/ppermute | solution.py:377
  115.7 2.3 %collective-permute-done.27.corner = bf16[2,256,256]{2,1,0:T(8,128)(2,1)S(1)} collective-permute-done((bf16[2,256,256]{2,1,0:T(8,128)(2,1)S(1)}, bf16[2,256,256]{2,1,0:T(8,128)(2,1)S(1)}, u32[]{:S(2)}, u32[]{:S(2)}) %collective-permute-start.27) | collective-permute-done | bytes 262176 | tf_op jit(solution)/shard_map/ppermute | solution.py:373
  118.0 2.2 %collective-permute-done.25.c = f32[3,32,256]{2,1,0:T(8,128)S(1)} collective-permute-done((f32[3,32,256]{2,1,0:T(8,128)S(1)}, f32[3,32,256]{2,1,0:T(8,128)S(1)}, u32[]{:S(2)}, u32[]{:S(2)}) %collective-permute-start.25) | collective-permute-done | bytes 98336 | tf_op jit(solution)/shard_map/ppermute | solution.py:377
  120.3 5.2 %collective-permute-start.28 = (bf16[2,256,384]{2,1,0:T(8,128)(2,1)S(1)}, bf16[2,256,384]{2,1,0:T(8,128)(2,1)S(1)}, u32[]{:S(2)}, u32[]{:S(2)}) collective-permute-start(bf16[2,256,384]{2,1,0:T(8,128)(2,1)S(1)} %get-tuple-element.47), channel_id=1, source_target_pairs={{0,8},{8,16},{16,24},{24,32},{32,40},{40,48},{48,56},{56,64},{64,7... | collective-permute-start | bytes 1179656 | tf_op jit(solution)/shard_map/ppermute | solution.py:373
  125.5 0.6 collective-permute-start.29
  126.1 2.5 %collective-permute-start.31 = (f32[3,32,256]{2,1,0:T(8,128)S(1)}, f32[3,32,256]{2,1,0:T(8,128)S(1)}, u32[]{:S(2)}, u32[]{:S(2)}) collective-permute-start(f32[3,32,256]{2,1,0:T(8,128)S(1)} %get-tuple-element.50.a), channel_id=1, source_target_pairs={{0,6},{2,0},{4,2},{6,4},{1,7},{3,1},{5,3},{7,5},{8,14},{10,8},{12,... | collective-permute-start | bytes 294920 | tf_op jit(solution)/shard_map/ppermute | solution.py:377
  128.6 4.2 %collective-permute-done.29.b = f32[3,32,256]{2,1,0:T(8,128)S(1)} collective-permute-done((f32[3,32,256]{2,1,0:T(8,128)S(1)}, f32[3,32,256]{2,1,0:T(8,128)S(1)}, u32[]{:S(2)}, u32[]{:S(2)}) %collective-permute-start.29) | collective-permute-done | bytes 98336 | tf_op jit(solution)/shard_map/ppermute | solution.py:377
  132.8 0.5 collective-permute-start.32
  133.3 4.0 %collective-permute-start.33 = (f32[3,32,256]{2,1,0:T(8,128)S(1)}, f32[3,32,256]{2,1,0:T(8,128)S(1)}, u32[]{:S(2)}, u32[]{:S(2)}) collective-permute-start(f32[3,32,256]{2,1,0:T(8,128)S(1)} %y_sum.3.a), channel_id=1, source_target_pairs={{0,16},{8,24},{16,0},{24,8},{1,17},{9,25},{17,1},{25,9},{2,18},{10... | collective-permute-start | bytes 294920 | tf_op jit(solution)/shard_map/ppermute | solution.py:377
  137.3 1.8 %collective-permute-start.34 = (f32[3,32,256]{2,1,0:T(8,128)S(1)}, f32[3,32,256]{2,1,0:T(8,128)S(1)}, u32[]{:S(2)}, u32[]{:S(2)}) collective-permute-start(f32[3,32,256]{2,1,0:T(8,128)S(1)} %y_sum.3.a), channel_id=1, source_target_pairs={{0,24},{8,0},{16,8},{24,16},{1,25},{9,1},{17,9},{25,17},{2,26},{10... | collective-permute-start | bytes 294920 | tf_op jit(solution)/shard_map/ppermute | solution.py:377
  139.1 1.3 collective-permute-done.33.c
  140.4 1.3 collective-permute-done.34.d
  141.7 0.7 collective-permute-start.35
  142.5 3.3 %collective-permute-start.36 = (f32[2,32,256]{2,1,0:T(8,128)S(1)}, f32[2,32,256]{2,1,0:T(8,128)S(1)}, u32[]{:S(2)}, u32[]{:S(2)}) collective-permute-start(f32[2,32,256]{2,1,0:T(8,128)S(1)} %z_sum.1.a), channel_id=1, source_target_pairs={{0,64},{32,96},{64,0},{96,32},{1,65},{33,97},{65,1},{97,33},{2,66}... | collective-permute-start | bytes 196616 | tf_op jit(solution)/shard_map/ppermute | solution.py:377
  145.8 2.3 %object_update.1 = (f32[2,512,384]{2,1,0:T(8,128)}, f32[8,128]{1,0:T(8,128)S(1)}) custom-call(f32[2,512,384]{2,1,0:T(8,128)S(1)} %get-tuple-element.35.obj, f32[2,512,384]{2,1,0:T(8,128)S(1)} %get-tuple-element.40.own, bf16[2,512,256]{2,1,0:T(8,128)(2,1)S(1)} %collective-permute-done.22.left.waited, ...), custom_call_target="tpu_custom_call" | custom-call | flops 2000000 | bytes 4000000 | tf_op jit(solution)/shard_map/object_update/pallas_call | solution.py:265
  148.1 0.1 collective-permute-done.36.c
  148.1 0.8 collective-permute-done.37.d
  148.9 3.9 %collective-permute-start.38 = (f32[4,2,32,256]{3,2,1,0:T(8,128)S(1)}, f32[4,2,32,256]{3,2,1,0:T(8,128)S(1)}, u32[]{:S(2)}, u32[]{:S(2)}) collective-permute-start(f32[4,2,32,256]{3,2,1,0:T(8,128)S(1)} %half_probe.3.mine), channel_id=1, source_target_pairs={{0,1},{1,0},{2,3},{3,2},{4,5},{5,4},{6,7},{7,6},{8,9},{9,8},{10,11... | collective-permute-start | bytes 786440 | tf_op jit(solution)/shard_map/ppermute | solution.py:381
  152.8 1.2 collective-permute-done.38.other
  153.9 1.4 probe_whole.1
  (67 shorter events, 0.9 us)
Async XLA Ops:
  0.6 20.6 %copy-start.2 = (f32[2,512,384]{2,1,0:T(8,128)S(1)}, f32[2,512,384]{2,1,0:T(8,128)}, u32[]{:S(2)}) copy-start(f32[2,512,384]{2,1,0:T(8,128)} %obj.3) | copy-start | bytes 4718596
  0.6 15.4 %copy-start.12 = (s32[2,2,12]{2,1,0:T(2,128)S(1)}, s32[2,2,12]{2,1,0:T(2,128)}, u32[]{:S(2)}) copy-start(s32[2,2,12]{2,1,0:T(2,128)} %param.9) | copy-start | bytes 580
  0.6 15.5 %copy-start.13 = (s32[2,1,1]{0,2,1:T(1,128)S(1)}, s32[2,1,1]{0,2,1:T(1,128)}, u32[]{:S(2)}) copy-start(s32[2,1,1]{0,2,1:T(1,128)} %param.10) | copy-start | bytes 28
  0.7 20.5 %copy-start.9 = (f32[2,256,256]{2,1,0:T(8,128)S(1)}, f32[2,256,256]{2,1,0:T(8,128)}, u32[]{:S(2)}) copy-start(f32[2,256,256]{2,1,0:T(8,128)} %rest_4_.1) | copy-start | bytes 1572868
  2.3 10.4 %collective-permute-start = (bf16[2,256,256]{2,1,0:T(8,128)(2,1)S(1)}, bf16[2,256,256]{2,1,0:T(8,128)(2,1)S(1)}, u32[]{:S(2)}, u32[]{:S(2)}) collective-permute-start(bf16[2,256,256]{2,1,0:T(8,128)(2,1)S(1)} %slice.63), channel_id=1, source_target_pairs={{8,0},{16,8},{24,16},{32,24},{40,32},{48,40},{56,48},{64,56},{72,6... | collective-permute-start | bytes 786440 | tf_op jit(solution)/shard_map/ppermute | solution.py:373
  4.5 12.4 %collective-permute-start.2 = (bf16[2,512,256]{2,1,0:T(8,128)(2,1)}, bf16[2,512,256]{2,1,0:T(8,128)(2,1)S(1)}, u32[]{:S(2)}, u32[]{:S(2)}) collective-permute-start(bf16[2,512,256]{2,1,0:T(8,128)(2,1)} %slice.65), channel_id=1, source_target_pairs={{1,0},{2,1},{3,2},{4,3},{5,4},{6,5},{7,6},{9,8},{10,9},{11,10},{12... | collective-permute-start | bytes 1572872 | tf_op jit(solution)/shard_map/ppermute | solution.py:373
  7.8 9.0 %collective-permute-start.1 = (bf16[2,256,128]{2,1,0:T(8,128)(2,1)S(1)}, bf16[2,256,128]{2,1,0:T(8,128)(2,1)S(1)}, u32[]{:S(2)}, u32[]{:S(2)}) collective-permute-start(bf16[2,256,128]{2,1,0:T(8,128)(2,1)S(1)} %slice.64), channel_id=1, source_target_pairs={{8,0},{16,8},{24,16},{32,24},{40,32},{48,40},{56,48},{64,56},{72,6... | collective-permute-start | bytes 393224 | tf_op jit(solution)/shard_map/ppermute | solution.py:373
  12.7 8.5 %collective-permute-start.3 = (bf16[2,256,256]{2,1,0:T(8,128)(2,1)S(1)}, bf16[2,256,256]{2,1,0:T(8,128)(2,1)S(1)}, u32[]{:S(2)}, u32[]{:S(2)}) collective-permute-start(bf16[2,256,256]{2,1,0:T(8,128)(2,1)S(1)} %collective-permute-done.rest_0_.low_left), channel_id=1, source_target_pairs={{1,0},{2,1},{3,2},{4,3},{5,4},{6,5},{7,6},{9,8},{10,9},{11,10},{12... | collective-permute-start | bytes 786440 | tf_op jit(solution)/shard_map/ppermute | solution.py:373
  16.8 12.9 %copy-start.3 = (bf16[2,512,256]{2,1,0:T(8,128)(2,1)}, bf16[2,512,256]{2,1,0:T(8,128)(2,1)S(1)}, u32[]{:S(2)}) copy-start(bf16[2,512,256]{2,1,0:T(8,128)(2,1)S(1)} %collective-permute-done.2.rest_2_.right) | copy-start | bytes 1572868
  21.2 8.5 %copy-start.5 = (bf16[2,256,256]{2,1,0:T(8,128)(2,1)}, bf16[2,256,256]{2,1,0:T(8,128)(2,1)S(1)}, u32[]{:S(2)}) copy-start(bf16[2,256,256]{2,1,0:T(8,128)(2,1)S(1)} %collective-permute-done.3.rest_3_.corner) | copy-start | bytes 786436
  21.2 1.3 copy-start.10
  29.7 5.6 %collective-permute-start.6 = (f32[4,3,32,256]{3,2,1,0:T(8,128)S(1)}, f32[4,3,32,256]{3,2,1,0:T(8,128)S(1)}, u32[]{:S(2)}, u32[]{:S(2)}) collective-permute-start(f32[4,3,32,256]{3,2,1,0:T(8,128)S(1)} %get-tuple-element.31), channel_id=1, source_target_pairs={{0,1},{1,0},{2,3},{3,2},{4,5},{5,4},{6,7},{7,6},{8,9},{9,8},{10,11... | collective-permute-start | bytes 1179656 | tf_op jit(solution)/shard_map/ppermute | solution.py:381
  29.8 31.5 %collective-permute-start.4 = (bf16[2,768,256]{2,1,0:T(8,128)(2,1)S(1)}, bf16[2,768,256]{2,1,0:T(8,128)(2,1)S(1)}, u32[]{:S(2)}, u32[]{:S(2)}) collective-permute-start(bf16[2,768,256]{2,1,0:T(8,128)(2,1)S(1)} %get-tuple-element.28), channel_id=1, source_target_pairs={{0,1},{1,2},{2,3},{3,4},{4,5},{5,6},{6,7},{8,9},{9,10},{10,11},{11... | collective-permute-start | bytes 2359304 | tf_op jit(solution)/shard_map/ppermute | solution.py:373
  33.4 27.9 %collective-permute-start.5 = (bf16[2,768,256]{2,1,0:T(8,128)(2,1)S(1)}, bf16[2,768,256]{2,1,0:T(8,128)(2,1)S(1)}, u32[]{:S(2)}, u32[]{:S(2)}) collective-permute-start(bf16[2,768,256]{2,1,0:T(8,128)(2,1)S(1)} %get-tuple-element.29), channel_id=1, source_target_pairs={{1,0},{2,1},{3,2},{4,3},{5,4},{6,5},{7,6},{9,8},{10,9},{11,10},{12... | collective-permute-start | bytes 2359304 | tf_op jit(solution)/shard_map/ppermute | solution.py:373
  35.4 15.7 %collective-permute-start.7 = (f32[3,32,256]{2,1,0:T(8,128)S(1)}, f32[3,32,256]{2,1,0:T(8,128)S(1)}, u32[]{:S(2)}, u32[]{:S(2)}) collective-permute-start(f32[3,32,256]{2,1,0:T(8,128)S(1)} %get-tuple-element.58), channel_id=1, source_target_pairs={{0,32},{32,64},{64,96},{96,0},{1,33},{33,65},{65,97},{97,1},{2,34}... | collective-permute-start | bytes 294920 | tf_op jit(solution)/shard_map/ppermute | solution.py:377
  46.4 6.8 %collective-permute-start.8 = (f32[3,32,256]{2,1,0:T(8,128)S(1)}, f32[3,32,256]{2,1,0:T(8,128)S(1)}, u32[]{:S(2)}, u32[]{:S(2)}) collective-permute-start(f32[3,32,256]{2,1,0:T(8,128)S(1)} %get-tuple-element.57), channel_id=1, source_target_pairs={{0,64},{32,96},{64,0},{96,32},{1,65},{33,97},{65,1},{97,33},{2,66}... | collective-permute-start | bytes 294920 | tf_op jit(solution)/shard_map/ppermute | solution.py:377
  49.1 4.0 %collective-permute-start.9 = (f32[3,32,256]{2,1,0:T(8,128)S(1)}, f32[3,32,256]{2,1,0:T(8,128)S(1)}, u32[]{:S(2)}, u32[]{:S(2)}) collective-permute-start(f32[3,32,256]{2,1,0:T(8,128)S(1)} %get-tuple-element.56), channel_id=1, source_target_pairs={{0,96},{32,0},{64,32},{96,64},{1,97},{33,1},{65,33},{97,65},{2,98}... | collective-permute-start | bytes 294920 | tf_op jit(solution)/shard_map/ppermute | solution.py:377
  53.2 7.9 %collective-permute-start.10 = (f32[3,32,256]{2,1,0:T(8,128)S(1)}, f32[3,32,256]{2,1,0:T(8,128)S(1)}, u32[]{:S(2)}, u32[]{:S(2)}) collective-permute-start(f32[3,32,256]{2,1,0:T(8,128)S(1)} %x_sum.2.a), channel_id=1, source_target_pairs={{0,8},{8,16},{16,24},{24,0},{1,9},{9,17},{17,25},{25,1},{2,10},{10... | collective-permute-start | bytes 294920 | tf_op jit(solution)/shard_map/ppermute | solution.py:377
  53.3 7.8 %collective-permute-start.11 = (f32[3,32,256]{2,1,0:T(8,128)S(1)}, f32[3,32,256]{2,1,0:T(8,128)S(1)}, u32[]{:S(2)}, u32[]{:S(2)}) collective-permute-start(f32[3,32,256]{2,1,0:T(8,128)S(1)} %x_sum.2.a), channel_id=1, source_target_pairs={{0,16},{8,24},{16,0},{24,8},{1,17},{9,25},{17,1},{25,9},{2,18},{10... | collective-permute-start | bytes 294920 | tf_op jit(solution)/shard_map/ppermute | solution.py:377
  53.4 8.0 %collective-permute-start.12 = (f32[3,32,256]{2,1,0:T(8,128)S(1)}, f32[3,32,256]{2,1,0:T(8,128)S(1)}, u32[]{:S(2)}, u32[]{:S(2)}) collective-permute-start(f32[3,32,256]{2,1,0:T(8,128)S(1)} %x_sum.2.a), channel_id=1, source_target_pairs={{0,24},{8,0},{16,8},{24,16},{1,25},{9,1},{17,9},{25,17},{2,26},{10... | collective-permute-start | bytes 294920 | tf_op jit(solution)/shard_map/ppermute | solution.py:377
  61.3 2.1 %copy-start = (f32[2,768,640]{2,1,0:T(8,128)S(1)}, f32[2,768,640]{2,1,0:T(8,128)}, u32[]{:S(2)}) copy-start(f32[2,768,640]{2,1,0:T(8,128)} %get-tuple-element.27.grads) | copy-start | bytes 11796484
  64.7 0.7 copy-start.7
  65.4 24.1 %collective-permute-start.13 = (bf16[2,256,640]{2,1,0:T(8,128)(2,1)}, bf16[2,256,640]{2,1,0:T(8,128)(2,1)}, u32[]{:S(2)}, u32[]{:S(2)}) collective-permute-start(bf16[2,256,640]{2,1,0:T(8,128)(2,1)} %get-tuple-element.32), channel_id=1, source_target_pairs={{0,8},{8,16},{16,24},{24,32},{32,40},{40,48},{48,56},{56,64},{64,7... | collective-permute-start | bytes 1966088 | tf_op jit(solution)/shard_map/ppermute | solution.py:373
  68.4 21.1 %collective-permute-start.14 = (bf16[2,256,640]{2,1,0:T(8,128)(2,1)}, bf16[2,256,640]{2,1,0:T(8,128)(2,1)}, u32[]{:S(2)}, u32[]{:S(2)}) collective-permute-start(bf16[2,256,640]{2,1,0:T(8,128)(2,1)} %get-tuple-element.33), channel_id=1, source_target_pairs={{8,0},{16,8},{24,16},{32,24},{40,32},{48,40},{56,48},{64,56},{72,6... | collective-permute-start | bytes 1966088 | tf_op jit(solution)/shard_map/ppermute | solution.py:373
  69.7 23.4 %copy-start.4 = (bf16[2,512,256]{2,1,0:T(8,128)(2,1)S(1)}, bf16[2,512,256]{2,1,0:T(8,128)(2,1)}, u32[]{:S(2)}) copy-start(bf16[2,512,256]{2,1,0:T(8,128)(2,1)} %copy-done.3) | copy-start | bytes 1572868
  69.7 23.3 %copy-start.6 = (bf16[2,256,256]{2,1,0:T(8,128)(2,1)S(1)}, bf16[2,256,256]{2,1,0:T(8,128)(2,1)}, u32[]{:S(2)}) copy-start(bf16[2,256,256]{2,1,0:T(8,128)(2,1)} %copy-done.5) | copy-start | bytes 786436
  69.7 6.8 %collective-permute-start.15 = (f32[3,32,256]{2,1,0:T(8,128)}, f32[3,32,256]{2,1,0:T(8,128)S(1)}, u32[]{:S(2)}, u32[]{:S(2)}) collective-permute-start(f32[3,32,256]{2,1,0:T(8,128)} %copy-done.7), channel_id=1, source_target_pairs={{0,2},{2,4},{4,6},{6,0},{1,3},{3,5},{5,7},{7,1},{8,10},{10,12},{12... | collective-permute-start | bytes 294920 | tf_op jit(solution)/shard_map/ppermute | solution.py:377
  69.8 6.7 %collective-permute-start.16 = (f32[3,32,256]{2,1,0:T(8,128)}, f32[3,32,256]{2,1,0:T(8,128)S(1)}, u32[]{:S(2)}, u32[]{:S(2)}) collective-permute-start(f32[3,32,256]{2,1,0:T(8,128)} %copy-done.7), channel_id=1, source_target_pairs={{0,4},{2,6},{4,0},{6,2},{1,5},{3,7},{5,1},{7,3},{8,12},{10,14},{12... | collective-permute-start | bytes 294920 | tf_op jit(solution)/shard_map/ppermute | solution.py:377
  69.9 7.2 %collective-permute-start.17 = (f32[3,32,256]{2,1,0:T(8,128)}, f32[3,32,256]{2,1,0:T(8,128)S(1)}, u32[]{:S(2)}, u32[]{:S(2)}) collective-permute-start(f32[3,32,256]{2,1,0:T(8,128)} %copy-done.7), channel_id=1, source_target_pairs={{0,6},{2,0},{4,2},{6,4},{1,7},{3,1},{5,3},{7,5},{8,14},{10,8},{12,... | collective-permute-start | bytes 294920 | tf_op jit(solution)/shard_map/ppermute | solution.py:377
  77.1 0.9 copy-start.8
  78.0 8.0 %collective-permute-start.18 = (f32[2,32,256]{2,1,0:T(8,128)S(1)}, f32[2,32,256]{2,1,0:T(8,128)S(1)}, u32[]{:S(2)}, u32[]{:S(2)}) collective-permute-start(f32[2,32,256]{2,1,0:T(8,128)S(1)} %y_sum.2.a.mine), channel_id=1, source_target_pairs={{0,32},{32,64},{64,96},{96,0},{1,33},{33,65},{65,97},{97,1},{2,34}... | collective-permute-start | bytes 196616 | tf_op jit(solution)/shard_map/ppermute | solution.py:377
  81.6 6.3 %collective-permute-start.19 = (f32[2,32,256]{2,1,0:T(8,128)S(1)}, f32[2,32,256]{2,1,0:T(8,128)S(1)}, u32[]{:S(2)}, u32[]{:S(2)}) collective-permute-start(f32[2,32,256]{2,1,0:T(8,128)S(1)} %y_sum.2.a.mine), channel_id=1, source_target_pairs={{0,64},{32,96},{64,0},{96,32},{1,65},{33,97},{65,1},{97,33},{2,66}... | collective-permute-start | bytes 196616 | tf_op jit(solution)/shard_map/ppermute | solution.py:377
  85.5 3.9 %collective-permute-start.20 = (f32[2,32,256]{2,1,0:T(8,128)S(1)}, f32[2,32,256]{2,1,0:T(8,128)S(1)}, u32[]{:S(2)}, u32[]{:S(2)}) collective-permute-start(f32[2,32,256]{2,1,0:T(8,128)S(1)} %y_sum.2.a.mine), channel_id=1, source_target_pairs={{0,96},{32,0},{64,32},{96,64},{1,97},{33,1},{65,33},{97,65},{2,98}... | collective-permute-start | bytes 196616 | tf_op jit(solution)/shard_map/ppermute | solution.py:377
  89.5 8.4 %collective-permute-start.21 = (f32[4,2,32,256]{3,2,1,0:T(8,128)S(1)}, f32[4,2,32,256]{3,2,1,0:T(8,128)S(1)}, u32[]{:S(2)}, u32[]{:S(2)}) collective-permute-start(f32[4,2,32,256]{3,2,1,0:T(8,128)S(1)} %half_probe.2.rest_3_), channel_id=1, source_target_pairs={{0,1},{1,0},{2,3},{3,2},{4,5},{5,4},{6,7},{7,6},{8,9},{9,8},{10,11... | collective-permute-start | bytes 786440 | tf_op jit(solution)/shard_map/ppermute | solution.py:381
  93.0 2.1 %copy-start.1 = (f32[2,768,640]{2,1,0:T(8,128)S(1)}, f32[2,768,640]{2,1,0:T(8,128)}, u32[]{:S(2)}) copy-start(f32[2,768,640]{2,1,0:T(8,128)} %get-tuple-element.27.grads) | copy-start | bytes 11796484
  95.2 2.7 %copy-start.11 = (bf16[2,512,512]{2,1,0:T(8,128)(2,1)S(1)}, bf16[2,512,512]{2,1,0:T(8,128)(2,1)}, u32[]{:S(2)}) copy-start(bf16[2,512,512]{2,1,0:T(8,128)(2,1)} %constant.20.clone.rest_6_) | copy-start | bytes 3145732
  103.5 7.5 %collective-permute-start.23 = (f32[4,3,32,256]{3,2,1,0:T(8,128)S(1)}, f32[4,3,32,256]{3,2,1,0:T(8,128)S(1)}, u32[]{:S(2)}, u32[]{:S(2)}) collective-permute-start(f32[4,3,32,256]{3,2,1,0:T(8,128)S(1)} %get-tuple-element.43), channel_id=1, source_target_pairs={{0,1},{1,0},{2,3},{3,2},{4,5},{5,4},{6,7},{7,6},{8,9},{9,8},{10,11... | collective-permute-start | bytes 1179656 | tf_op jit(solution)/shard_map/ppermute | solution.py:381
  103.7 24.9 %collective-permute-start.22 = (bf16[2,512,256]{2,1,0:T(8,128)(2,1)S(1)}, bf16[2,512,256]{2,1,0:T(8,128)(2,1)S(1)}, u32[]{:S(2)}, u32[]{:S(2)}) collective-permute-start(bf16[2,512,256]{2,1,0:T(8,128)(2,1)S(1)} %get-tuple-element.41), channel_id=1, source_target_pairs={{0,1},{1,2},{2,3},{3,4},{4,5},{5,6},{6,7},{8,9},{9,10},{10,11},{11... | collective-permute-start | bytes 1572872 | tf_op jit(solution)/shard_map/ppermute | solution.py:373
  109.0 8.9 %collective-permute-start.27 = (bf16[2,256,256]{2,1,0:T(8,128)(2,1)S(1)}, bf16[2,256,256]{2,1,0:T(8,128)(2,1)S(1)}, u32[]{:S(2)}, u32[]{:S(2)}) collective-permute-start(bf16[2,256,256]{2,1,0:T(8,128)(2,1)S(1)} %get-tuple-element.46), channel_id=1, source_target_pairs={{0,1},{1,2},{2,3},{3,4},{4,5},{5,6},{6,7},{8,9},{9,10},{10,11},{11... | collective-permute-start | bytes 786440 | tf_op jit(solution)/shard_map/ppermute | solution.py:373
  111.1 6.8 %collective-permute-start.24 = (f32[3,32,256]{2,1,0:T(8,128)S(1)}, f32[3,32,256]{2,1,0:T(8,128)S(1)}, u32[]{:S(2)}, u32[]{:S(2)}) collective-permute-start(f32[3,32,256]{2,1,0:T(8,128)S(1)} %get-tuple-element.54), channel_id=1, source_target_pairs={{0,32},{32,64},{64,96},{96,0},{1,33},{33,65},{65,97},{97,1},{2,34}... | collective-permute-start | bytes 294920 | tf_op jit(solution)/shard_map/ppermute | solution.py:377
  111.2 9.0 %collective-permute-start.25 = (f32[3,32,256]{2,1,0:T(8,128)S(1)}, f32[3,32,256]{2,1,0:T(8,128)S(1)}, u32[]{:S(2)}, u32[]{:S(2)}) collective-permute-start(f32[3,32,256]{2,1,0:T(8,128)S(1)} %get-tuple-element.53), channel_id=1, source_target_pairs={{0,64},{32,96},{64,0},{96,32},{1,65},{33,97},{65,1},{97,33},{2,66}... | collective-permute-start | bytes 294920 | tf_op jit(solution)/shard_map/ppermute | solution.py:377
  115.7 4.5 %collective-permute-start.26 = (f32[3,32,256]{2,1,0:T(8,128)S(1)}, f32[3,32,256]{2,1,0:T(8,128)S(1)}, u32[]{:S(2)}, u32[]{:S(2)}) collective-permute-start(f32[3,32,256]{2,1,0:T(8,128)S(1)} %get-tuple-element.52), channel_id=1, source_target_pairs={{0,96},{32,0},{64,32},{96,64},{1,97},{33,1},{65,33},{97,65},{2,98}... | collective-permute-start | bytes 294920 | tf_op jit(solution)/shard_map/ppermute | solution.py:377
  120.3 21.4 %collective-permute-start.28 = (bf16[2,256,384]{2,1,0:T(8,128)(2,1)S(1)}, bf16[2,256,384]{2,1,0:T(8,128)(2,1)S(1)}, u32[]{:S(2)}, u32[]{:S(2)}) collective-permute-start(bf16[2,256,384]{2,1,0:T(8,128)(2,1)S(1)} %get-tuple-element.47), channel_id=1, source_target_pairs={{0,8},{8,16},{16,24},{24,32},{32,40},{40,48},{48,56},{56,64},{64,7... | collective-permute-start | bytes 1179656 | tf_op jit(solution)/shard_map/ppermute | solution.py:373
  125.5 7.3 %collective-permute-start.29 = (f32[3,32,256]{2,1,0:T(8,128)S(1)}, f32[3,32,256]{2,1,0:T(8,128)S(1)}, u32[]{:S(2)}, u32[]{:S(2)}) collective-permute-start(f32[3,32,256]{2,1,0:T(8,128)S(1)} %get-tuple-element.50.a), channel_id=1, source_target_pairs={{0,2},{2,4},{4,6},{6,0},{1,3},{3,5},{5,7},{7,1},{8,10},{10,12},{12... | collective-permute-start | bytes 294920 | tf_op jit(solution)/shard_map/ppermute | solution.py:377
  126.1 6.7 %collective-permute-start.30 = (f32[3,32,256]{2,1,0:T(8,128)S(1)}, f32[3,32,256]{2,1,0:T(8,128)S(1)}, u32[]{:S(2)}, u32[]{:S(2)}) collective-permute-start(f32[3,32,256]{2,1,0:T(8,128)S(1)} %get-tuple-element.50.a), channel_id=1, source_target_pairs={{0,4},{2,6},{4,0},{6,2},{1,5},{3,7},{5,1},{7,3},{8,12},{10,14},{12... | collective-permute-start | bytes 294920 | tf_op jit(solution)/shard_map/ppermute | solution.py:377
  126.1 6.7 %collective-permute-start.31 = (f32[3,32,256]{2,1,0:T(8,128)S(1)}, f32[3,32,256]{2,1,0:T(8,128)S(1)}, u32[]{:S(2)}, u32[]{:S(2)}) collective-permute-start(f32[3,32,256]{2,1,0:T(8,128)S(1)} %get-tuple-element.50.a), channel_id=1, source_target_pairs={{0,6},{2,0},{4,2},{6,4},{1,7},{3,1},{5,3},{7,5},{8,14},{10,8},{12,... | collective-permute-start | bytes 294920 | tf_op jit(solution)/shard_map/ppermute | solution.py:377
  132.8 6.3 %collective-permute-start.32 = (f32[3,32,256]{2,1,0:T(8,128)S(1)}, f32[3,32,256]{2,1,0:T(8,128)S(1)}, u32[]{:S(2)}, u32[]{:S(2)}) collective-permute-start(f32[3,32,256]{2,1,0:T(8,128)S(1)} %y_sum.3.a), channel_id=1, source_target_pairs={{0,8},{8,16},{16,24},{24,0},{1,9},{9,17},{17,25},{25,1},{2,10},{10... | collective-permute-start | bytes 294920 | tf_op jit(solution)/shard_map/ppermute | solution.py:377
  133.3 7.2 %collective-permute-start.33 = (f32[3,32,256]{2,1,0:T(8,128)S(1)}, f32[3,32,256]{2,1,0:T(8,128)S(1)}, u32[]{:S(2)}, u32[]{:S(2)}) collective-permute-start(f32[3,32,256]{2,1,0:T(8,128)S(1)} %y_sum.3.a), channel_id=1, source_target_pairs={{0,16},{8,24},{16,0},{24,8},{1,17},{9,25},{17,1},{25,9},{2,18},{10... | collective-permute-start | bytes 294920 | tf_op jit(solution)/shard_map/ppermute | solution.py:377
  137.3 4.4 %collective-permute-start.34 = (f32[3,32,256]{2,1,0:T(8,128)S(1)}, f32[3,32,256]{2,1,0:T(8,128)S(1)}, u32[]{:S(2)}, u32[]{:S(2)}) collective-permute-start(f32[3,32,256]{2,1,0:T(8,128)S(1)} %y_sum.3.a), channel_id=1, source_target_pairs={{0,24},{8,0},{16,8},{24,16},{1,25},{9,1},{17,9},{25,17},{2,26},{10... | collective-permute-start | bytes 294920 | tf_op jit(solution)/shard_map/ppermute | solution.py:377
  141.7 6.3 %collective-permute-start.35 = (f32[2,32,256]{2,1,0:T(8,128)S(1)}, f32[2,32,256]{2,1,0:T(8,128)S(1)}, u32[]{:S(2)}, u32[]{:S(2)}) collective-permute-start(f32[2,32,256]{2,1,0:T(8,128)S(1)} %z_sum.1.a), channel_id=1, source_target_pairs={{0,32},{32,64},{64,96},{96,0},{1,33},{33,65},{65,97},{97,1},{2,34}... | collective-permute-start | bytes 196616 | tf_op jit(solution)/shard_map/ppermute | solution.py:377
  142.5 5.7 %collective-permute-start.36 = (f32[2,32,256]{2,1,0:T(8,128)S(1)}, f32[2,32,256]{2,1,0:T(8,128)S(1)}, u32[]{:S(2)}, u32[]{:S(2)}) collective-permute-start(f32[2,32,256]{2,1,0:T(8,128)S(1)} %z_sum.1.a), channel_id=1, source_target_pairs={{0,64},{32,96},{64,0},{96,32},{1,65},{33,97},{65,1},{97,33},{2,66}... | collective-permute-start | bytes 196616 | tf_op jit(solution)/shard_map/ppermute | solution.py:377
  145.8 3.1 %collective-permute-start.37 = (f32[2,32,256]{2,1,0:T(8,128)S(1)}, f32[2,32,256]{2,1,0:T(8,128)S(1)}, u32[]{:S(2)}, u32[]{:S(2)}) collective-permute-start(f32[2,32,256]{2,1,0:T(8,128)S(1)} %z_sum.1.a), channel_id=1, source_target_pairs={{0,96},{32,0},{64,32},{96,64},{1,97},{33,1},{65,33},{97,65},{2,98}... | collective-permute-start | bytes 196616 | tf_op jit(solution)/shard_map/ppermute | solution.py:377
  148.9 5.0 %collective-permute-start.38 = (f32[4,2,32,256]{3,2,1,0:T(8,128)S(1)}, f32[4,2,32,256]{3,2,1,0:T(8,128)S(1)}, u32[]{:S(2)}, u32[]{:S(2)}) collective-permute-start(f32[4,2,32,256]{3,2,1,0:T(8,128)S(1)} %half_probe.3.mine), channel_id=1, source_target_pairs={{0,1},{1,0},{2,3},{3,2},{4,5},{5,4},{6,7},{7,6},{8,9},{9,8},{10,11... | collective-permute-start | bytes 786440 | tf_op jit(solution)/shard_map/ppermute | solution.py:381

commit v10 on v9

--- a/solution.py
+++ b/solution.py
@@ -302,6 +302,13 @@
     obj_out[:, size:, size:] = obj[:, size:, size:] - alpha * own[:, size:, size:]
 
 
+def strips_kernel(obj, low_left, low_right, right):
+    size = right.shape[2]
+    low_left[...] = obj[:, :size, :size].astype(BF)
+    low_right[...] = obj[:, :size, size:].astype(BF)
+    right[...] = obj[:, :, :size].astype(BF)
+
+
 def last_kernel(obj, own, left, down, step, obj_out, done):
     object_step(obj, own, left, down, step, obj_out)
     done[...] = obj_out[0, :8, :LANES]
@@ -406,8 +413,9 @@
     tall = jax.ShapeDtypeStruct((2, rows, size), BF)
     share = jax.ShapeDtypeStruct((3, quarter, size), F32)
     part = jax.ShapeDtypeStruct(mine.shape, F32)
-    lows = [obj[:, :size, :size].astype(BF), obj[:, :size, size:].astype(BF)]
-    right = obj[:, :, :size].astype(BF)
+    square = jax.ShapeDtypeStruct((2, size, size), BF)
+    narrow = jax.ShapeDtypeStruct((2, size, cols - size), BF)
+    *lows, right = small_call(strips_kernel, [square, narrow, tall], ([obj], []), "strips")
     pieces = (probe,)
     row = jax.ShapeDtypeStruct((8, LANES), F32)
     half_probe = jax.ShapeDtypeStruct((N_X, *mine.shape), F32)

time: 156 us -> 160 us (1.026)
  waiting for transfers between devices: 36.4 us -> 39.6 us
  other arithmetic: 1.82 us -> 0.18 us
    ppermute x24, starting transfers between devices: 46.7 us -> 39 us  [turned(): return lax.ppermute(value, axis, [(s, (s + steps) % 4) for s in range(4)])]
    ppermute x11, starting transfers between devices: 31.6 us -> 39.1 us  [moved(): lax.ppermute(value, axis, [(s, s + steps) for s in range(first, last)])]
    ppermute x11, waiting for transfers between devices: 10.3 us -> 12.8 us  [moved(): lax.ppermute(value, axis, [(s, s + steps) for s in range(first, last)])]
    unnamed x28 -> x30, local copies, waits for them, and re-layouts: 7.12 us -> 9.55 us
    another operation x1 -> x0, other arithmetic: 1.64 us -> none
    pallas_call x11 -> x12, Pallas kernels: 7.76 us -> 7.87 us  [small_call(): pl.pallas_call(body, out_shape=shapes, in_specs=[spec(space) for space in...]
  transfers between devices with their start and end apart: 39 -> 39, of which waited for: 18 -> 22; matrix products, arithmetic and copies ran while one was open for 2% -> 1% of each run, Pallas kernels for 3% -> 3%
where the time goes in v10:
time: 160 us; the launch traced here: 159 us
  starting transfers between devices  86.7 us (54%)
  waiting for transfers between devices  39.6 us (25%)
  Pallas kernels  20.6 us (13%)
  local copies, waits for them, and re-layouts  11 us (7%)
    ppermute x11, starting transfers between devices, moved(): lax.ppermute(value, axis, [(s, s + steps) for s in range(first, last)])  39.1 us
    ppermute x24, starting transfers between devices, turned(): return lax.ppermute(value, axis, [(s, (s + steps) % 4) for s in range(4)])  39 us
    ppermute x24, waiting for transfers between devices, turned(): return lax.ppermute(value, axis, [(s, (s + steps) % 4) for s in range(4)])  25.6 us
    ppermute x11, waiting for transfers between devices, moved(): lax.ppermute(value, axis, [(s, s + steps) for s in range(first, last)])  12.8 us
    pallas_call x2, Pallas kernels, run_frames(): pl.pallas_call(functools.partial(frames_kernel, middle, iteration, len(lo...  12.7 us
    unnamed x30, local copies, waits for them, and re-layouts  9.55 us
    ppermute x4, starting transfers between devices, swapped(): return lax.ppermute(value, 'core', [(0, 1), (1, 0)])  8.58 us
    pallas_call x12, Pallas kernels, small_call(): pl.pallas_call(body, out_shape=shapes, in_specs=[spec(space) for space in...  7.87 us
  transfers between devices with their start and end apart: 39, of which 22 were waited for; matrix products, arithmetic and copies ran while one was open for 1% of the time, Pallas kernels for 3%

profile of v10, /device:TPU:1, one launch (start us, length us, event | category | flops | bytes accessed | tf_op | source)
XLA Modules:
  0.0 159.0 jit_solution(13877381315165604603)
XLA Ops:
  0.6 1.4 copy-done.2
  2.1 1.4 collective-permute-start
  3.6 3.3 %collective-permute-start.2 = (bf16[2,512,256]{2,1,0:T(8,128)(2,1)S(1)}, bf16[2,512,256]{2,1,0:T(8,128)(2,1)S(1)}, u32[]{:S(2)}, u32[]{:S(2)}) collective-permute-start(bf16[2,512,256]{2,1,0:T(8,128)(2,1)S(1)} %get-tuple-element.32), channel_id=1, source_target_pairs={{1,0},{2,1},{3,2},{4,3},{5,4},{6,5},{7,6},{9,8},{10,9},{11,10},{12... | collective-permute-start | bytes 1572872 | tf_op jit(solution)/shard_map/ppermute | solution.py:380
  6.9 1.3 collective-permute-start.1
  8.2 4.4 %collective-permute-done.rest_0_.low_left = bf16[2,256,256]{2,1,0:T(8,128)(2,1)S(1)} collective-permute-done((bf16[2,256,256]{2,1,0:T(8,128)(2,1)S(1)}, bf16[2,256,256]{2,1,0:T(8,128)(2,1)S(1)}, u32[]{:S(2)}, u32[]{:S(2)}) %collective-permute-start) | collective-permute-done | bytes 262176 | tf_op jit(solution)/shard_map/ppermute | solution.py:380
  12.6 4.0 %collective-permute-start.3 = (bf16[2,256,256]{2,1,0:T(8,128)(2,1)S(1)}, bf16[2,256,256]{2,1,0:T(8,128)(2,1)S(1)}, u32[]{:S(2)}, u32[]{:S(2)}) collective-permute-start(bf16[2,256,256]{2,1,0:T(8,128)(2,1)S(1)} %collective-permute-done.rest_0_.low_left), channel_id=1, source_target_pairs={{1,0},{2,1},{3,2},{4,3},{5,4},{6,5},{7,6},{9,8},{10,9},{11,10},{12... | collective-permute-start | bytes 786440 | tf_op jit(solution)/shard_map/ppermute | solution.py:380
  16.7 0.6 fusion
  17.3 4.6 %collective-permute-done.3.rest_3_.corner = bf16[2,256,256]{2,1,0:T(8,128)(2,1)S(1)} collective-permute-done((bf16[2,256,256]{2,1,0:T(8,128)(2,1)S(1)}, bf16[2,256,256]{2,1,0:T(8,128)(2,1)S(1)}, u32[]{:S(2)}, u32[]{:S(2)}) %collective-permute-start.3) | collective-permute-done | bytes 262176 | tf_op jit(solution)/shard_map/ppermute | solution.py:380
  22.0 1.1 copy-done.10
  23.1 1.2 copy-done.11
  24.3 7.2 %frames.2 = (f32[2,768,640]{2,1,0:T(8,128)}, bf16[2,768,256]{2,1,0:T(8,128)(2,1)S(1)}, bf16[2,768,256]{2,1,0:T(8,128)(2,1)S(1)}, f32[4,3,32,256]{3,2,1,0:T(8,128...) custom-call(s32[2]{0:T(128)S(1)} %pad_add_fusion.place, s32[1]{0:T(128)} %bitcast.2.counts, ...), custom_call_target="tpu_custom_call" | custom-call | flops 6000000000 | bytes 8000000 | tf_op jit(solution)/shard_map/frames/pallas_call | solution.py:247
  31.6 8.6 %collective-permute-start.4 = (bf16[2,768,256]{2,1,0:T(8,128)(2,1)S(1)}, bf16[2,768,256]{2,1,0:T(8,128)(2,1)S(1)}, u32[]{:S(2)}, u32[]{:S(2)}) collective-permute-start(bf16[2,768,256]{2,1,0:T(8,128)(2,1)S(1)} %get-tuple-element.34), channel_id=1, source_target_pairs={{0,1},{1,2},{2,3},{3,4},{4,5},{5,6},{6,7},{8,9},{9,10},{10,11},{11... | collective-permute-start | bytes 2359304 | tf_op jit(solution)/shard_map/ppermute | solution.py:380
  40.2 1.9 %collective-permute-start.5 = (bf16[2,768,256]{2,1,0:T(8,128)(2,1)S(1)}, bf16[2,768,256]{2,1,0:T(8,128)(2,1)S(1)}, u32[]{:S(2)}, u32[]{:S(2)}) collective-permute-start(bf16[2,768,256]{2,1,0:T(8,128)(2,1)S(1)} %get-tuple-element.35), channel_id=1, source_target_pairs={{1,0},{2,1},{3,2},{4,3},{5,4},{6,5},{7,6},{9,8},{10,9},{11,10},{12... | collective-permute-start | bytes 2359304 | tf_op jit(solution)/shard_map/ppermute | solution.py:380
  42.3 1.8 %collective-permute-start.8 = (f32[3,32,256]{2,1,0:T(8,128)S(1)}, f32[3,32,256]{2,1,0:T(8,128)S(1)}, u32[]{:S(2)}, u32[]{:S(2)}) collective-permute-start(f32[3,32,256]{2,1,0:T(8,128)S(1)} %get-tuple-element.63), channel_id=1, source_target_pairs={{0,64},{32,96},{64,0},{96,32},{1,65},{33,97},{65,1},{97,33},{2,66}... | collective-permute-start | bytes 294920 | tf_op jit(solution)/shard_map/ppermute | solution.py:384
  44.1 0.9 collective-permute-start.9
  45.0 3.0 %collective-permute-done.7.b = f32[3,32,256]{2,1,0:T(8,128)S(1)} collective-permute-done((f32[3,32,256]{2,1,0:T(8,128)S(1)}, f32[3,32,256]{2,1,0:T(8,128)S(1)}, u32[]{:S(2)}, u32[]{:S(2)}) %collective-permute-start.7) | collective-permute-done | bytes 98336 | tf_op jit(solution)/shard_map/ppermute | solution.py:384
  48.0 0.6 collective-permute-done.9.d
  48.7 1.4 collective-permute-start.10
  50.1 9.1 %collective-permute-start.11 = (f32[3,32,256]{2,1,0:T(8,128)S(1)}, f32[3,32,256]{2,1,0:T(8,128)S(1)}, u32[]{:S(2)}, u32[]{:S(2)}) collective-permute-start(f32[3,32,256]{2,1,0:T(8,128)S(1)} %x_sum.2.a), channel_id=1, source_target_pairs={{0,16},{8,24},{16,0},{24,8},{1,17},{9,25},{17,1},{25,9},{2,18},{10... | collective-permute-start | bytes 294920 | tf_op jit(solution)/shard_map/ppermute | solution.py:384
  59.2 1.0 collective-permute-done.10.b
  60.2 2.0 %collective-permute-done.11.c = f32[3,32,256]{2,1,0:T(8,128)S(1)} collective-permute-done((f32[3,32,256]{2,1,0:T(8,128)S(1)}, f32[3,32,256]{2,1,0:T(8,128)S(1)}, u32[]{:S(2)}, u32[]{:S(2)}) %collective-permute-start.11) | collective-permute-done | bytes 98336 | tf_op jit(solution)/shard_map/ppermute | solution.py:384
  62.2 0.4 collective-permute-done.12.d
  62.6 2.1 %copy-done = f32[2,768,640]{2,1,0:T(8,128)S(1)} copy-done((f32[2,768,640]{2,1,0:T(8,128)S(1)}, f32[2,768,640]{2,1,0:T(8,128)}, u32[]{:S(2)}) %copy-start) | copy-done | bytes 3932184
  64.7 1.2 z_sum_rims.1
  66.0 0.6 copy-done.8
  66.6 2.4 %collective-permute-start.13 = (bf16[2,256,640]{2,1,0:T(8,128)(2,1)}, bf16[2,256,640]{2,1,0:T(8,128)(2,1)}, u32[]{:S(2)}, u32[]{:S(2)}) collective-permute-start(bf16[2,256,640]{2,1,0:T(8,128)(2,1)} %get-tuple-element.38), channel_id=1, source_target_pairs={{0,8},{8,16},{16,24},{24,32},{32,40},{40,48},{48,56},{56,64},{64,7... | collective-permute-start | bytes 1966088 | tf_op jit(solution)/shard_map/ppermute | solution.py:380
  69.0 1.3 collective-permute-start.14
  70.6 3.1 %collective-permute-start.16 = (f32[3,32,256]{2,1,0:T(8,128)}, f32[3,32,256]{2,1,0:T(8,128)S(1)}, u32[]{:S(2)}, u32[]{:S(2)}) collective-permute-start(f32[3,32,256]{2,1,0:T(8,128)} %copy-done.8), channel_id=1, source_target_pairs={{0,4},{2,6},{4,0},{6,2},{1,5},{3,7},{5,1},{7,3},{8,12},{10,14},{12... | collective-permute-start | bytes 294920 | tf_op jit(solution)/shard_map/ppermute | solution.py:384
  73.7 0.5 collective-permute-start.17
  74.2 0.8 constant_dynamic-slice_fusion.mine
  75.0 0.3 collective-permute-done.15.b
  75.3 1.7 %collective-permute-done.16.c = f32[3,32,256]{2,1,0:T(8,128)S(1)} collective-permute-done((f32[3,32,256]{2,1,0:T(8,128)}, f32[3,32,256]{2,1,0:T(8,128)S(1)}, u32[]{:S(2)}, u32[]{:S(2)}) %collective-permute-start.16) | collective-permute-done | bytes 98336 | tf_op jit(solution)/shard_map/ppermute | solution.py:384
  77.0 0.7 collective-permute-done.17.d
  77.7 0.9 copy-done.9
  78.7 3.8 %collective-permute-start.18 = (f32[2,32,256]{2,1,0:T(8,128)S(1)}, f32[2,32,256]{2,1,0:T(8,128)S(1)}, u32[]{:S(2)}, u32[]{:S(2)}) collective-permute-start(f32[2,32,256]{2,1,0:T(8,128)S(1)} %y_sum.2.a.mine), channel_id=1, source_target_pairs={{0,32},{32,64},{64,96},{96,0},{1,33},{33,65},{65,97},{97,1},{2,34}... | collective-permute-start | bytes 196616 | tf_op jit(solution)/shard_map/ppermute | solution.py:384
  82.5 2.5 %collective-permute-start.19 = (f32[2,32,256]{2,1,0:T(8,128)S(1)}, f32[2,32,256]{2,1,0:T(8,128)S(1)}, u32[]{:S(2)}, u32[]{:S(2)}) collective-permute-start(f32[2,32,256]{2,1,0:T(8,128)S(1)} %y_sum.2.a.mine), channel_id=1, source_target_pairs={{0,64},{32,96},{64,0},{96,32},{1,65},{33,97},{65,1},{97,33},{2,66}... | collective-permute-start | bytes 196616 | tf_op jit(solution)/shard_map/ppermute | solution.py:384
  85.0 0.5 collective-permute-done.18.b
  85.5 1.9 %collective-permute-done.19.c = f32[2,32,256]{2,1,0:T(8,128)S(1)} collective-permute-done((f32[2,32,256]{2,1,0:T(8,128)S(1)}, f32[2,32,256]{2,1,0:T(8,128)S(1)}, u32[]{:S(2)}, u32[]{:S(2)}) %collective-permute-start.19) | collective-permute-done | bytes 65568 | tf_op jit(solution)/shard_map/ppermute | solution.py:384
  87.3 1.4 collective-permute-done.20.d
  88.8 6.3 %collective-permute-start.21 = (f32[4,2,32,256]{3,2,1,0:T(8,128)S(1)}, f32[4,2,32,256]{3,2,1,0:T(8,128)S(1)}, u32[]{:S(2)}, u32[]{:S(2)}) collective-permute-start(f32[4,2,32,256]{3,2,1,0:T(8,128)S(1)} %half_probe.2.rest_3_), channel_id=1, source_target_pairs={{0,1},{1,0},{2,3},{3,2},{4,5},{5,4},{6,7},{7,6},{8,9},{9,8},{10,11... | collective-permute-start | bytes 786440 | tf_op jit(solution)/shard_map/ppermute | solution.py:388
  95.2 2.1 %copy-done.1 = f32[2,768,640]{2,1,0:T(8,128)S(1)} copy-done((f32[2,768,640]{2,1,0:T(8,128)S(1)}, f32[2,768,640]{2,1,0:T(8,128)}, u32[]{:S(2)}) %copy-start.1) | copy-done | bytes 3932184
  97.3 2.7 %wide_update.1 = (f32[2,512,384]{2,1,0:T(8,128)S(1)}, bf16[2,256,384]{2,1,0:T(8,128)(2,1)S(1)}, bf16[2,512,256]{2,1,0:T(8,128)(2,1)S(1)}, bf16[2,256,256]{2,1,0:T(8,128)(2,1)S(1)}) custom-call(f32[2,512,384]{2,1,0:T(8,128)S(1)} %copy-done.3, bf16[2,256,256]{2,1,0:T(8,128)(2,1)S(1)} %collective-permute-done.rest_0_.low_left, ...), custom_call_target="tpu_custom_call" | custom-call | flops 2000000 | bytes 4000000 | tf_op jit(solution)/shard_map/wide_update/pallas_call | solution.py:265
  100.0 5.6 %frames.3 = (f32[2,512,384]{2,1,0:T(8,128)S(1)}, f32[2,256,256]{2,1,0:T(8,128)S(1)}, bf16[2,256,128]{2,1,0:T(8,128)(2,1)S(1)}, bf16[2,512,256]{2,1,0:T(8,128)(2,...) custom-call(s32[2]{0:T(128)S(1)} %pad_add_fusion.place, ...), custom_call_target="tpu_custom_call" | custom-call | flops 6000000000 | bytes 8000000 | tf_op jit(solution)/shard_map/frames/pallas_call | solution.py:247
  105.7 11.2 %collective-permute-start.22 = (bf16[2,512,256]{2,1,0:T(8,128)(2,1)S(1)}, bf16[2,512,256]{2,1,0:T(8,128)(2,1)S(1)}, u32[]{:S(2)}, u32[]{:S(2)}) collective-permute-start(bf16[2,512,256]{2,1,0:T(8,128)(2,1)S(1)} %get-tuple-element.47), channel_id=1, source_target_pairs={{0,1},{1,2},{2,3},{3,4},{4,5},{5,6},{6,7},{8,9},{9,10},{10,11},{11... | collective-permute-start | bytes 1572872 | tf_op jit(solution)/shard_map/ppermute | solution.py:380
  116.8 2.4 %collective-permute-start.27 = (bf16[2,256,256]{2,1,0:T(8,128)(2,1)S(1)}, bf16[2,256,256]{2,1,0:T(8,128)(2,1)S(1)}, u32[]{:S(2)}, u32[]{:S(2)}) collective-permute-start(bf16[2,256,256]{2,1,0:T(8,128)(2,1)S(1)} %get-tuple-element.52), channel_id=1, source_target_pairs={{0,1},{1,2},{2,3},{3,4},{4,5},{5,6},{6,7},{8,9},{9,10},{10,11},{11... | collective-permute-start | bytes 786440 | tf_op jit(solution)/shard_map/ppermute | solution.py:380
  119.6 2.5 %collective-permute-start.26 = (f32[3,32,256]{2,1,0:T(8,128)S(1)}, f32[3,32,256]{2,1,0:T(8,128)S(1)}, u32[]{:S(2)}, u32[]{:S(2)}) collective-permute-start(f32[3,32,256]{2,1,0:T(8,128)S(1)} %get-tuple-element.58), channel_id=1, source_target_pairs={{0,96},{32,0},{64,32},{96,64},{1,97},{33,1},{65,33},{97,65},{2,98}... | collective-permute-start | bytes 294920 | tf_op jit(solution)/shard_map/ppermute | solution.py:384
  122.1 3.7 %collective-permute-done.27.corner = bf16[2,256,256]{2,1,0:T(8,128)(2,1)S(1)} collective-permute-done((bf16[2,256,256]{2,1,0:T(8,128)(2,1)S(1)}, bf16[2,256,256]{2,1,0:T(8,128)(2,1)S(1)}, u32[]{:S(2)}, u32[]{:S(2)}) %collective-permute-start.27) | collective-permute-done | bytes 262176 | tf_op jit(solution)/shard_map/ppermute | solution.py:380
  125.8 1.4 collective-permute-done.24.b
  127.1 0.3 collective-permute-done.26.d
  127.5 1.3 collective-permute-start.28
  129.0 2.6 %collective-permute-start.31 = (f32[3,32,256]{2,1,0:T(8,128)S(1)}, f32[3,32,256]{2,1,0:T(8,128)S(1)}, u32[]{:S(2)}, u32[]{:S(2)}) collective-permute-start(f32[3,32,256]{2,1,0:T(8,128)S(1)} %get-tuple-element.56.a), channel_id=1, source_target_pairs={{0,6},{2,0},{4,2},{6,4},{1,7},{3,1},{5,3},{7,5},{8,14},{10,8},{12,... | collective-permute-start | bytes 294920 | tf_op jit(solution)/shard_map/ppermute | solution.py:384
  131.6 4.8 %collective-permute-done.29.b = f32[3,32,256]{2,1,0:T(8,128)S(1)} collective-permute-done((f32[3,32,256]{2,1,0:T(8,128)S(1)}, f32[3,32,256]{2,1,0:T(8,128)S(1)}, u32[]{:S(2)}, u32[]{:S(2)}) %collective-permute-start.29) | collective-permute-done | bytes 98336 | tf_op jit(solution)/shard_map/ppermute | solution.py:384
  136.5 4.3 %collective-permute-start.33 = (f32[3,32,256]{2,1,0:T(8,128)S(1)}, f32[3,32,256]{2,1,0:T(8,128)S(1)}, u32[]{:S(2)}, u32[]{:S(2)}) collective-permute-start(f32[3,32,256]{2,1,0:T(8,128)S(1)} %y_sum.3.a), channel_id=1, source_target_pairs={{0,16},{8,24},{16,0},{24,8},{1,17},{9,25},{17,1},{25,9},{2,18},{10... | collective-permute-start | bytes 294920 | tf_op jit(solution)/shard_map/ppermute | solution.py:384
  140.8 0.8 collective-permute-done.32.b
  141.6 2.3 %collective-permute-done.33.c = f32[3,32,256]{2,1,0:T(8,128)S(1)} collective-permute-done((f32[3,32,256]{2,1,0:T(8,128)S(1)}, f32[3,32,256]{2,1,0:T(8,128)S(1)}, u32[]{:S(2)}, u32[]{:S(2)}) %collective-permute-start.33) | collective-permute-done | bytes 98336 | tf_op jit(solution)/shard_map/ppermute | solution.py:384
  144.0 1.5 collective-permute-done.34.d
  145.5 1.4 collective-permute-start.35
  146.8 3.7 %collective-permute-start.36 = (f32[2,32,256]{2,1,0:T(8,128)S(1)}, f32[2,32,256]{2,1,0:T(8,128)S(1)}, u32[]{:S(2)}, u32[]{:S(2)}) collective-permute-start(f32[2,32,256]{2,1,0:T(8,128)S(1)} %z_sum.1.a), channel_id=1, source_target_pairs={{0,64},{32,96},{64,0},{96,32},{1,65},{33,97},{65,1},{97,33},{2,66}... | collective-permute-start | bytes 196616 | tf_op jit(solution)/shard_map/ppermute | solution.py:384
  150.5 0.8 collective-permute-start.37
  151.3 2.3 %object_update.1 = (f32[2,512,384]{2,1,0:T(8,128)}, f32[8,128]{1,0:T(8,128)S(1)}) custom-call(f32[2,512,384]{2,1,0:T(8,128)S(1)} %get-tuple-element.41.obj, f32[2,512,384]{2,1,0:T(8,128)S(1)} %get-tuple-element.46.own, bf16[2,512,256]{2,1,0:T(8,128)(2,1)S(1)} %collective-permute-done.22.left.waited, ...), custom_call_target="tpu_custom_call" | custom-call | flops 2000000 | bytes 4000000 | tf_op jit(solution)/shard_map/object_update/pallas_call | solution.py:265
  153.6 0.8 collective-permute-done.37.d
  154.4 2.1 %collective-permute-start.38 = (f32[4,2,32,256]{3,2,1,0:T(8,128)S(1)}, f32[4,2,32,256]{3,2,1,0:T(8,128)S(1)}, u32[]{:S(2)}, u32[]{:S(2)}) collective-permute-start(f32[4,2,32,256]{3,2,1,0:T(8,128)S(1)} %half_probe.3.mine), channel_id=1, source_target_pairs={{0,1},{1,0},{2,3},{3,2},{4,5},{5,4},{6,7},{7,6},{8,9},{9,8},{10,11... | collective-permute-start | bytes 786440 | tf_op jit(solution)/shard_map/ppermute | solution.py:388
  156.5 1.2 collective-permute-done.38.other
  157.7 1.4 probe_whole.1
  (66 shorter events, 1.6 us)
Async XLA Ops:
  0.6 1.4 copy-start.2
  2.0 14.6 %copy-start.13 = (s32[2,2,12]{2,1,0:T(2,128)S(1)}, s32[2,2,12]{2,1,0:T(2,128)}, u32[]{:S(2)}) copy-start(s32[2,2,12]{2,1,0:T(2,128)} %param.9) | copy-start | bytes 580
  2.0 14.7 %copy-start.14 = (s32[2,1,1]{0,2,1:T(1,128)S(1)}, s32[2,1,1]{0,2,1:T(1,128)}, u32[]{:S(2)}) copy-start(s32[2,1,1]{0,2,1:T(1,128)} %param.10) | copy-start | bytes 28
  2.0 19.9 %copy-start.3 = (f32[2,512,384]{2,1,0:T(8,128)S(1)}, f32[2,512,384]{2,1,0:T(8,128)}, u32[]{:S(2)}) copy-start(f32[2,512,384]{2,1,0:T(8,128)} %obj.5) | copy-start | bytes 4718596
  2.1 10.5 %collective-permute-start = (bf16[2,256,256]{2,1,0:T(8,128)(2,1)S(1)}, bf16[2,256,256]{2,1,0:T(8,128)(2,1)S(1)}, u32[]{:S(2)}, u32[]{:S(2)}) collective-permute-start(bf16[2,256,256]{2,1,0:T(8,128)(2,1)S(1)} %get-tuple-element.30), channel_id=1, source_target_pairs={{8,0},{16,8},{24,16},{32,24},{40,32},{48,40},{56,48},{64,56},{72,6... | collective-permute-start | bytes 786440 | tf_op jit(solution)/shard_map/ppermute | solution.py:380
  3.6 13.7 %collective-permute-start.2 = (bf16[2,512,256]{2,1,0:T(8,128)(2,1)S(1)}, bf16[2,512,256]{2,1,0:T(8,128)(2,1)S(1)}, u32[]{:S(2)}, u32[]{:S(2)}) collective-permute-start(bf16[2,512,256]{2,1,0:T(8,128)(2,1)S(1)} %get-tuple-element.32), channel_id=1, source_target_pairs={{1,0},{2,1},{3,2},{4,3},{5,4},{6,5},{7,6},{9,8},{10,9},{11,10},{12... | collective-permute-start | bytes 1572872 | tf_op jit(solution)/shard_map/ppermute | solution.py:380
  6.9 10.4 %collective-permute-start.1 = (bf16[2,256,128]{2,1,0:T(8,128)(2,1)S(1)}, bf16[2,256,128]{2,1,0:T(8,128)(2,1)S(1)}, u32[]{:S(2)}, u32[]{:S(2)}) collective-permute-start(bf16[2,256,128]{2,1,0:T(8,128)(2,1)S(1)} %get-tuple-element.31), channel_id=1, source_target_pairs={{8,0},{16,8},{24,16},{32,24},{40,32},{48,40},{56,48},{64,56},{72,6... | collective-permute-start | bytes 393224 | tf_op jit(solution)/shard_map/ppermute | solution.py:380
  12.6 9.3 %collective-permute-start.3 = (bf16[2,256,256]{2,1,0:T(8,128)(2,1)S(1)}, bf16[2,256,256]{2,1,0:T(8,128)(2,1)S(1)}, u32[]{:S(2)}, u32[]{:S(2)}) collective-permute-start(bf16[2,256,256]{2,1,0:T(8,128)(2,1)S(1)} %collective-permute-done.rest_0_.low_left), channel_id=1, source_target_pairs={{1,0},{2,1},{3,2},{4,3},{5,4},{6,5},{7,6},{9,8},{10,9},{11,10},{12... | collective-permute-start | bytes 786440 | tf_op jit(solution)/shard_map/ppermute | solution.py:380
  17.3 14.2 %copy-start.4 = (bf16[2,512,256]{2,1,0:T(8,128)(2,1)}, bf16[2,512,256]{2,1,0:T(8,128)(2,1)S(1)}, u32[]{:S(2)}) copy-start(bf16[2,512,256]{2,1,0:T(8,128)(2,1)S(1)} %collective-permute-done.2.rest_2_.right) | copy-start | bytes 1572868
  22.0 9.6 %copy-start.6 = (bf16[2,256,256]{2,1,0:T(8,128)(2,1)}, bf16[2,256,256]{2,1,0:T(8,128)(2,1)S(1)}, u32[]{:S(2)}) copy-start(bf16[2,256,256]{2,1,0:T(8,128)(2,1)S(1)} %collective-permute-done.3.rest_3_.corner) | copy-start | bytes 786436
  22.0 1.1 copy-start.10
  23.1 1.2 copy-start.11
  31.5 10.6 %collective-permute-start.6 = (f32[4,3,32,256]{3,2,1,0:T(8,128)S(1)}, f32[4,3,32,256]{3,2,1,0:T(8,128)S(1)}, u32[]{:S(2)}, u32[]{:S(2)}) collective-permute-start(f32[4,3,32,256]{3,2,1,0:T(8,128)S(1)} %get-tuple-element.37), channel_id=1, source_target_pairs={{0,1},{1,0},{2,3},{3,2},{4,5},{5,4},{6,7},{7,6},{8,9},{9,8},{10,11... | collective-permute-start | bytes 1179656 | tf_op jit(solution)/shard_map/ppermute | solution.py:388
  31.6 31.0 %collective-permute-start.4 = (bf16[2,768,256]{2,1,0:T(8,128)(2,1)S(1)}, bf16[2,768,256]{2,1,0:T(8,128)(2,1)S(1)}, u32[]{:S(2)}, u32[]{:S(2)}) collective-permute-start(bf16[2,768,256]{2,1,0:T(8,128)(2,1)S(1)} %get-tuple-element.34), channel_id=1, source_target_pairs={{0,1},{1,2},{2,3},{3,4},{4,5},{5,6},{6,7},{8,9},{9,10},{10,11},{11... | collective-permute-start | bytes 2359304 | tf_op jit(solution)/shard_map/ppermute | solution.py:380
  40.2 22.4 %collective-permute-start.5 = (bf16[2,768,256]{2,1,0:T(8,128)(2,1)S(1)}, bf16[2,768,256]{2,1,0:T(8,128)(2,1)S(1)}, u32[]{:S(2)}, u32[]{:S(2)}) collective-permute-start(bf16[2,768,256]{2,1,0:T(8,128)(2,1)S(1)} %get-tuple-element.35), channel_id=1, source_target_pairs={{1,0},{2,1},{3,2},{4,3},{5,4},{6,5},{7,6},{9,8},{10,9},{11,10},{12... | collective-permute-start | bytes 2359304 | tf_op jit(solution)/shard_map/ppermute | solution.py:380
  42.2 5.8 %collective-permute-start.7 = (f32[3,32,256]{2,1,0:T(8,128)S(1)}, f32[3,32,256]{2,1,0:T(8,128)S(1)}, u32[]{:S(2)}, u32[]{:S(2)}) collective-permute-start(f32[3,32,256]{2,1,0:T(8,128)S(1)} %get-tuple-element.64), channel_id=1, source_target_pairs={{0,32},{32,64},{64,96},{96,0},{1,33},{33,65},{65,97},{97,1},{2,34}... | collective-permute-start | bytes 294920 | tf_op jit(solution)/shard_map/ppermute | solution.py:384
  42.3 5.7 %collective-permute-start.8 = (f32[3,32,256]{2,1,0:T(8,128)S(1)}, f32[3,32,256]{2,1,0:T(8,128)S(1)}, u32[]{:S(2)}, u32[]{:S(2)}) collective-permute-start(f32[3,32,256]{2,1,0:T(8,128)S(1)} %get-tuple-element.63), channel_id=1, source_target_pairs={{0,64},{32,96},{64,0},{96,32},{1,65},{33,97},{65,1},{97,33},{2,66}... | collective-permute-start | bytes 294920 | tf_op jit(solution)/shard_map/ppermute | solution.py:384
  44.1 4.6 %collective-permute-start.9 = (f32[3,32,256]{2,1,0:T(8,128)S(1)}, f32[3,32,256]{2,1,0:T(8,128)S(1)}, u32[]{:S(2)}, u32[]{:S(2)}) collective-permute-start(f32[3,32,256]{2,1,0:T(8,128)S(1)} %get-tuple-element.62), channel_id=1, source_target_pairs={{0,96},{32,0},{64,32},{96,64},{1,97},{33,1},{65,33},{97,65},{2,98}... | collective-permute-start | bytes 294920 | tf_op jit(solution)/shard_map/ppermute | solution.py:384
  48.7 11.5 %collective-permute-start.10 = (f32[3,32,256]{2,1,0:T(8,128)S(1)}, f32[3,32,256]{2,1,0:T(8,128)S(1)}, u32[]{:S(2)}, u32[]{:S(2)}) collective-permute-start(f32[3,32,256]{2,1,0:T(8,128)S(1)} %x_sum.2.a), channel_id=1, source_target_pairs={{0,8},{8,16},{16,24},{24,0},{1,9},{9,17},{17,25},{25,1},{2,10},{10... | collective-permute-start | bytes 294920 | tf_op jit(solution)/shard_map/ppermute | solution.py:384
  50.1 12.1 %collective-permute-start.11 = (f32[3,32,256]{2,1,0:T(8,128)S(1)}, f32[3,32,256]{2,1,0:T(8,128)S(1)}, u32[]{:S(2)}, u32[]{:S(2)}) collective-permute-start(f32[3,32,256]{2,1,0:T(8,128)S(1)} %x_sum.2.a), channel_id=1, source_target_pairs={{0,16},{8,24},{16,0},{24,8},{1,17},{9,25},{17,1},{25,9},{2,18},{10... | collective-permute-start | bytes 294920 | tf_op jit(solution)/shard_map/ppermute | solution.py:384
  59.1 3.5 %collective-permute-start.12 = (f32[3,32,256]{2,1,0:T(8,128)S(1)}, f32[3,32,256]{2,1,0:T(8,128)S(1)}, u32[]{:S(2)}, u32[]{:S(2)}) collective-permute-start(f32[3,32,256]{2,1,0:T(8,128)S(1)} %x_sum.2.a), channel_id=1, source_target_pairs={{0,24},{8,0},{16,8},{24,16},{1,25},{9,1},{17,9},{25,17},{2,26},{10... | collective-permute-start | bytes 294920 | tf_op jit(solution)/shard_map/ppermute | solution.py:384
  62.6 2.1 %copy-start = (f32[2,768,640]{2,1,0:T(8,128)S(1)}, f32[2,768,640]{2,1,0:T(8,128)}, u32[]{:S(2)}) copy-start(f32[2,768,640]{2,1,0:T(8,128)} %get-tuple-element.33.grads) | copy-start | bytes 11796484
  66.0 0.6 copy-start.8
  66.6 22.2 %collective-permute-start.13 = (bf16[2,256,640]{2,1,0:T(8,128)(2,1)}, bf16[2,256,640]{2,1,0:T(8,128)(2,1)}, u32[]{:S(2)}, u32[]{:S(2)}) collective-permute-start(bf16[2,256,640]{2,1,0:T(8,128)(2,1)} %get-tuple-element.38), channel_id=1, source_target_pairs={{0,8},{8,16},{16,24},{24,32},{32,40},{40,48},{48,56},{56,64},{64,7... | collective-permute-start | bytes 1966088 | tf_op jit(solution)/shard_map/ppermute | solution.py:380
  69.0 19.8 %collective-permute-start.14 = (bf16[2,256,640]{2,1,0:T(8,128)(2,1)}, bf16[2,256,640]{2,1,0:T(8,128)(2,1)}, u32[]{:S(2)}, u32[]{:S(2)}) collective-permute-start(bf16[2,256,640]{2,1,0:T(8,128)(2,1)} %get-tuple-element.39), channel_id=1, source_target_pairs={{8,0},{16,8},{24,16},{32,24},{40,32},{48,40},{56,48},{64,56},{72,6... | collective-permute-start | bytes 1966088 | tf_op jit(solution)/shard_map/ppermute | solution.py:380
  70.3 24.8 %copy-start.5 = (bf16[2,512,256]{2,1,0:T(8,128)(2,1)S(1)}, bf16[2,512,256]{2,1,0:T(8,128)(2,1)}, u32[]{:S(2)}) copy-start(bf16[2,512,256]{2,1,0:T(8,128)(2,1)} %copy-done.4) | copy-start | bytes 1572868
  70.3 24.8 %copy-start.7 = (bf16[2,256,256]{2,1,0:T(8,128)(2,1)S(1)}, bf16[2,256,256]{2,1,0:T(8,128)(2,1)}, u32[]{:S(2)}) copy-start(bf16[2,256,256]{2,1,0:T(8,128)(2,1)} %copy-done.6) | copy-start | bytes 786436
  70.3 5.0 %collective-permute-start.15 = (f32[3,32,256]{2,1,0:T(8,128)}, f32[3,32,256]{2,1,0:T(8,128)S(1)}, u32[]{:S(2)}, u32[]{:S(2)}) collective-permute-start(f32[3,32,256]{2,1,0:T(8,128)} %copy-done.8), channel_id=1, source_target_pairs={{0,2},{2,4},{4,6},{6,0},{1,3},{3,5},{5,7},{7,1},{8,10},{10,12},{12... | collective-permute-start | bytes 294920 | tf_op jit(solution)/shard_map/ppermute | solution.py:384
  70.6 6.4 %collective-permute-start.16 = (f32[3,32,256]{2,1,0:T(8,128)}, f32[3,32,256]{2,1,0:T(8,128)S(1)}, u32[]{:S(2)}, u32[]{:S(2)}) collective-permute-start(f32[3,32,256]{2,1,0:T(8,128)} %copy-done.8), channel_id=1, source_target_pairs={{0,4},{2,6},{4,0},{6,2},{1,5},{3,7},{5,1},{7,3},{8,12},{10,14},{12... | collective-permute-start | bytes 294920 | tf_op jit(solution)/shard_map/ppermute | solution.py:384
  73.7 4.1 %collective-permute-start.17 = (f32[3,32,256]{2,1,0:T(8,128)}, f32[3,32,256]{2,1,0:T(8,128)S(1)}, u32[]{:S(2)}, u32[]{:S(2)}) collective-permute-start(f32[3,32,256]{2,1,0:T(8,128)} %copy-done.8), channel_id=1, source_target_pairs={{0,6},{2,0},{4,2},{6,4},{1,7},{3,1},{5,3},{7,5},{8,14},{10,8},{12,... | collective-permute-start | bytes 294920 | tf_op jit(solution)/shard_map/ppermute | solution.py:384
  77.7 0.9 copy-start.9
  78.7 6.8 %collective-permute-start.18 = (f32[2,32,256]{2,1,0:T(8,128)S(1)}, f32[2,32,256]{2,1,0:T(8,128)S(1)}, u32[]{:S(2)}, u32[]{:S(2)}) collective-permute-start(f32[2,32,256]{2,1,0:T(8,128)S(1)} %y_sum.2.a.mine), channel_id=1, source_target_pairs={{0,32},{32,64},{64,96},{96,0},{1,33},{33,65},{65,97},{97,1},{2,34}... | collective-permute-start | bytes 196616 | tf_op jit(solution)/shard_map/ppermute | solution.py:384
  82.5 4.9 %collective-permute-start.19 = (f32[2,32,256]{2,1,0:T(8,128)S(1)}, f32[2,32,256]{2,1,0:T(8,128)S(1)}, u32[]{:S(2)}, u32[]{:S(2)}) collective-permute-start(f32[2,32,256]{2,1,0:T(8,128)S(1)} %y_sum.2.a.mine), channel_id=1, source_target_pairs={{0,64},{32,96},{64,0},{96,32},{1,65},{33,97},{65,1},{97,33},{2,66}... | collective-permute-start | bytes 196616 | tf_op jit(solution)/shard_map/ppermute | solution.py:384
  85.0 3.8 %collective-permute-start.20 = (f32[2,32,256]{2,1,0:T(8,128)S(1)}, f32[2,32,256]{2,1,0:T(8,128)S(1)}, u32[]{:S(2)}, u32[]{:S(2)}) collective-permute-start(f32[2,32,256]{2,1,0:T(8,128)S(1)} %y_sum.2.a.mine), channel_id=1, source_target_pairs={{0,96},{32,0},{64,32},{96,64},{1,97},{33,1},{65,33},{97,65},{2,98}... | collective-permute-start | bytes 196616 | tf_op jit(solution)/shard_map/ppermute | solution.py:384
  88.8 11.2 %collective-permute-start.21 = (f32[4,2,32,256]{3,2,1,0:T(8,128)S(1)}, f32[4,2,32,256]{3,2,1,0:T(8,128)S(1)}, u32[]{:S(2)}, u32[]{:S(2)}) collective-permute-start(f32[4,2,32,256]{3,2,1,0:T(8,128)S(1)} %half_probe.2.rest_3_), channel_id=1, source_target_pairs={{0,1},{1,0},{2,3},{3,2},{4,5},{5,4},{6,7},{7,6},{8,9},{9,8},{10,11... | collective-permute-start | bytes 786440 | tf_op jit(solution)/shard_map/ppermute | solution.py:388
  95.2 2.1 %copy-start.1 = (f32[2,768,640]{2,1,0:T(8,128)S(1)}, f32[2,768,640]{2,1,0:T(8,128)}, u32[]{:S(2)}) copy-start(f32[2,768,640]{2,1,0:T(8,128)} %get-tuple-element.33.grads) | copy-start | bytes 11796484
  97.3 2.7 %copy-start.12 = (bf16[2,512,512]{2,1,0:T(8,128)(2,1)S(1)}, bf16[2,512,512]{2,1,0:T(8,128)(2,1)}, u32[]{:S(2)}) copy-start(bf16[2,512,512]{2,1,0:T(8,128)(2,1)} %constant.20.clone.rest_6_) | copy-start | bytes 3145732
  105.6 13.7 %collective-permute-start.23 = (f32[4,3,32,256]{3,2,1,0:T(8,128)S(1)}, f32[4,3,32,256]{3,2,1,0:T(8,128)S(1)}, u32[]{:S(2)}, u32[]{:S(2)}) collective-permute-start(f32[4,3,32,256]{3,2,1,0:T(8,128)S(1)} %get-tuple-element.49), channel_id=1, source_target_pairs={{0,1},{1,0},{2,3},{3,2},{4,5},{5,4},{6,7},{7,6},{8,9},{9,8},{10,11... | collective-permute-start | bytes 1179656 | tf_op jit(solution)/shard_map/ppermute | solution.py:388
  105.7 25.9 %collective-permute-start.22 = (bf16[2,512,256]{2,1,0:T(8,128)(2,1)S(1)}, bf16[2,512,256]{2,1,0:T(8,128)(2,1)S(1)}, u32[]{:S(2)}, u32[]{:S(2)}) collective-permute-start(bf16[2,512,256]{2,1,0:T(8,128)(2,1)S(1)} %get-tuple-element.47), channel_id=1, source_target_pairs={{0,1},{1,2},{2,3},{3,4},{4,5},{5,6},{6,7},{8,9},{9,10},{10,11},{11... | collective-permute-start | bytes 1572872 | tf_op jit(solution)/shard_map/ppermute | solution.py:380
  116.8 8.9 %collective-permute-start.27 = (bf16[2,256,256]{2,1,0:T(8,128)(2,1)S(1)}, bf16[2,256,256]{2,1,0:T(8,128)(2,1)S(1)}, u32[]{:S(2)}, u32[]{:S(2)}) collective-permute-start(bf16[2,256,256]{2,1,0:T(8,128)(2,1)S(1)} %get-tuple-element.52), channel_id=1, source_target_pairs={{0,1},{1,2},{2,3},{3,4},{4,5},{5,6},{6,7},{8,9},{9,10},{10,11},{11... | collective-permute-start | bytes 786440 | tf_op jit(solution)/shard_map/ppermute | solution.py:380
  119.4 7.8 %collective-permute-start.24 = (f32[3,32,256]{2,1,0:T(8,128)S(1)}, f32[3,32,256]{2,1,0:T(8,128)S(1)}, u32[]{:S(2)}, u32[]{:S(2)}) collective-permute-start(f32[3,32,256]{2,1,0:T(8,128)S(1)} %get-tuple-element.60), channel_id=1, source_target_pairs={{0,32},{32,64},{64,96},{96,0},{1,33},{33,65},{65,97},{97,1},{2,34}... | collective-permute-start | bytes 294920 | tf_op jit(solution)/shard_map/ppermute | solution.py:384
  119.4 7.7 %collective-permute-start.25 = (f32[3,32,256]{2,1,0:T(8,128)S(1)}, f32[3,32,256]{2,1,0:T(8,128)S(1)}, u32[]{:S(2)}, u32[]{:S(2)}) collective-permute-start(f32[3,32,256]{2,1,0:T(8,128)S(1)} %get-tuple-element.59), channel_id=1, source_target_pairs={{0,64},{32,96},{64,0},{96,32},{1,65},{33,97},{65,1},{97,33},{2,66}... | collective-permute-start | bytes 294920 | tf_op jit(solution)/shard_map/ppermute | solution.py:384
  119.6 7.9 %collective-permute-start.26 = (f32[3,32,256]{2,1,0:T(8,128)S(1)}, f32[3,32,256]{2,1,0:T(8,128)S(1)}, u32[]{:S(2)}, u32[]{:S(2)}) collective-permute-start(f32[3,32,256]{2,1,0:T(8,128)S(1)} %get-tuple-element.58), channel_id=1, source_target_pairs={{0,96},{32,0},{64,32},{96,64},{1,97},{33,1},{65,33},{97,65},{2,98}... | collective-permute-start | bytes 294920 | tf_op jit(solution)/shard_map/ppermute | solution.py:384
  127.5 17.9 %collective-permute-start.28 = (bf16[2,256,384]{2,1,0:T(8,128)(2,1)S(1)}, bf16[2,256,384]{2,1,0:T(8,128)(2,1)S(1)}, u32[]{:S(2)}, u32[]{:S(2)}) collective-permute-start(bf16[2,256,384]{2,1,0:T(8,128)(2,1)S(1)} %get-tuple-element.53), channel_id=1, source_target_pairs={{0,8},{8,16},{16,24},{24,32},{32,40},{40,48},{48,56},{56,64},{64,7... | collective-permute-start | bytes 1179656 | tf_op jit(solution)/shard_map/ppermute | solution.py:380
  128.8 7.6 %collective-permute-start.29 = (f32[3,32,256]{2,1,0:T(8,128)S(1)}, f32[3,32,256]{2,1,0:T(8,128)S(1)}, u32[]{:S(2)}, u32[]{:S(2)}) collective-permute-start(f32[3,32,256]{2,1,0:T(8,128)S(1)} %get-tuple-element.56.a), channel_id=1, source_target_pairs={{0,2},{2,4},{4,6},{6,0},{1,3},{3,5},{5,7},{7,1},{8,10},{10,12},{12... | collective-permute-start | bytes 294920 | tf_op jit(solution)/shard_map/ppermute | solution.py:384
  128.9 7.5 %collective-permute-start.30 = (f32[3,32,256]{2,1,0:T(8,128)S(1)}, f32[3,32,256]{2,1,0:T(8,128)S(1)}, u32[]{:S(2)}, u32[]{:S(2)}) collective-permute-start(f32[3,32,256]{2,1,0:T(8,128)S(1)} %get-tuple-element.56.a), channel_id=1, source_target_pairs={{0,4},{2,6},{4,0},{6,2},{1,5},{3,7},{5,1},{7,3},{8,12},{10,14},{12... | collective-permute-start | bytes 294920 | tf_op jit(solution)/shard_map/ppermute | solution.py:384
  129.0 7.4 %collective-permute-start.31 = (f32[3,32,256]{2,1,0:T(8,128)S(1)}, f32[3,32,256]{2,1,0:T(8,128)S(1)}, u32[]{:S(2)}, u32[]{:S(2)}) collective-permute-start(f32[3,32,256]{2,1,0:T(8,128)S(1)} %get-tuple-element.56.a), channel_id=1, source_target_pairs={{0,6},{2,0},{4,2},{6,4},{1,7},{3,1},{5,3},{7,5},{8,14},{10,8},{12,... | collective-permute-start | bytes 294920 | tf_op jit(solution)/shard_map/ppermute | solution.py:384
  136.5 5.2 %collective-permute-start.32 = (f32[3,32,256]{2,1,0:T(8,128)S(1)}, f32[3,32,256]{2,1,0:T(8,128)S(1)}, u32[]{:S(2)}, u32[]{:S(2)}) collective-permute-start(f32[3,32,256]{2,1,0:T(8,128)S(1)} %y_sum.3.a), channel_id=1, source_target_pairs={{0,8},{8,16},{16,24},{24,0},{1,9},{9,17},{17,25},{25,1},{2,10},{10... | collective-permute-start | bytes 294920 | tf_op jit(solution)/shard_map/ppermute | solution.py:384
  136.5 7.4 %collective-permute-start.33 = (f32[3,32,256]{2,1,0:T(8,128)S(1)}, f32[3,32,256]{2,1,0:T(8,128)S(1)}, u32[]{:S(2)}, u32[]{:S(2)}) collective-permute-start(f32[3,32,256]{2,1,0:T(8,128)S(1)} %y_sum.3.a), channel_id=1, source_target_pairs={{0,16},{8,24},{16,0},{24,8},{1,17},{9,25},{17,1},{25,9},{2,18},{10... | collective-permute-start | bytes 294920 | tf_op jit(solution)/shard_map/ppermute | solution.py:384
  140.8 4.6 %collective-permute-start.34 = (f32[3,32,256]{2,1,0:T(8,128)S(1)}, f32[3,32,256]{2,1,0:T(8,128)S(1)}, u32[]{:S(2)}, u32[]{:S(2)}) collective-permute-start(f32[3,32,256]{2,1,0:T(8,128)S(1)} %y_sum.3.a), channel_id=1, source_target_pairs={{0,24},{8,0},{16,8},{24,16},{1,25},{9,1},{17,9},{25,17},{2,26},{10... | collective-permute-start | bytes 294920 | tf_op jit(solution)/shard_map/ppermute | solution.py:384
  145.5 8.1 %collective-permute-start.35 = (f32[2,32,256]{2,1,0:T(8,128)S(1)}, f32[2,32,256]{2,1,0:T(8,128)S(1)}, u32[]{:S(2)}, u32[]{:S(2)}) collective-permute-start(f32[2,32,256]{2,1,0:T(8,128)S(1)} %z_sum.1.a), channel_id=1, source_target_pairs={{0,32},{32,64},{64,96},{96,0},{1,33},{33,65},{65,97},{97,1},{2,34}... | collective-permute-start | bytes 196616 | tf_op jit(solution)/shard_map/ppermute | solution.py:384
  146.8 6.7 %collective-permute-start.36 = (f32[2,32,256]{2,1,0:T(8,128)S(1)}, f32[2,32,256]{2,1,0:T(8,128)S(1)}, u32[]{:S(2)}, u32[]{:S(2)}) collective-permute-start(f32[2,32,256]{2,1,0:T(8,128)S(1)} %z_sum.1.a), channel_id=1, source_target_pairs={{0,64},{32,96},{64,0},{96,32},{1,65},{33,97},{65,1},{97,33},{2,66}... | collective-permute-start | bytes 196616 | tf_op jit(solution)/shard_map/ppermute | solution.py:384
  150.5 3.9 %collective-permute-start.37 = (f32[2,32,256]{2,1,0:T(8,128)S(1)}, f32[2,32,256]{2,1,0:T(8,128)S(1)}, u32[]{:S(2)}, u32[]{:S(2)}) collective-permute-start(f32[2,32,256]{2,1,0:T(8,128)S(1)} %z_sum.1.a), channel_id=1, source_target_pairs={{0,96},{32,0},{64,32},{96,64},{1,97},{33,1},{65,33},{97,65},{2,98}... | collective-permute-start | bytes 196616 | tf_op jit(solution)/shard_map/ppermute | solution.py:384
  154.4 3.2 %collective-permute-start.38 = (f32[4,2,32,256]{3,2,1,0:T(8,128)S(1)}, f32[4,2,32,256]{3,2,1,0:T(8,128)S(1)}, u32[]{:S(2)}, u32[]{:S(2)}) collective-permute-start(f32[4,2,32,256]{3,2,1,0:T(8,128)S(1)} %half_probe.3.mine), channel_id=1, source_target_pairs={{0,1},{1,0},{2,3},{3,2},{4,5},{5,4},{6,7},{7,6},{8,9},{9,8},{10,11... | collective-permute-start | bytes 786440 | tf_op jit(solution)/shard_map/ppermute | solution.py:388
